TPU v7x, 32 devices: a whole 2x2x4 slice. The times are simulated.
32 devices in a mesh: dp: 8 (over z, core), fsdp: 4 (over y, x).
Axes of the slice: x: 2, y: 2, z: 4, core: 2. Of those that a mesh axis runs over, the one named last changes fastest.
Arguments:
- tokens: bfloat16 [16384, 1024], P(('dp', 'fsdp')), may hold values from -6 to 6
- cotangent: bfloat16 [16384, 1024], P(('dp', 'fsdp')), may hold values from -6 to 6
- doc_ids: int32 [8, 8], P('dp'), may hold values from 0 to 2, as said below
- norm1_gain: bfloat16 [1024], P(('dp', 'fsdp')), may hold values from 0.099609375 to 1.8984375
- norm1_bias: bfloat16 [1024], P(('dp', 'fsdp')), may hold values from -1.75 to 1.75
- norm2_gain: bfloat16 [1024], P(('dp', 'fsdp')), may hold values from 0.099609375 to 1.8984375
- norm2_bias: bfloat16 [1024], P(('dp', 'fsdp')), may hold values from -1.75 to 1.75
- qkv_weight: bfloat16 [1024, 3072], P(('dp', 'fsdp')), may hold values from -0.25 to 0.25
- qkv_bias: bfloat16 [3072], P(('dp', 'fsdp')), may hold values from -3 to 3
- out_weight: bfloat16 [1024, 1024], P(('dp', 'fsdp')), may hold values from -0.5 to 0.5
- out_bias: bfloat16 [1024], P(('dp', 'fsdp')), may hold values from -3 to 3
- up_weight: bfloat16 [1024, 4096], P(('dp', 'fsdp')), may hold values from -0.1875 to 0.1875
- up_bias: bfloat16 [4096], P(('dp', 'fsdp')), may hold values from -3 to 3
- down_weight: bfloat16 [4096, 1024], P(('dp', 'fsdp')), may hold values from -0.09375 to 0.09375
- down_bias: bfloat16 [1024], P(('dp', 'fsdp')), may hold values from -3 to 3
Outputs:
- output: bfloat16 [16384, 1024], P(('dp', 'fsdp'))
- grad_tokens: bfloat16 [16384, 1024], P(('dp', 'fsdp'))
- grad_norm1_gain: float32 [1024], P(('dp', 'fsdp'))
- grad_norm1_bias: float32 [1024], P(('dp', 'fsdp'))
- grad_norm2_gain: float32 [1024], P(('dp', 'fsdp'))
- grad_norm2_bias: float32 [1024], P(('dp', 'fsdp'))
- grad_qkv_weight: float32 [1024, 3072], P(('dp', 'fsdp'))
- grad_qkv_bias: float32 [3072], P(('dp', 'fsdp'))
- grad_out_weight: float32 [1024, 1024], P(('dp', 'fsdp'))
- grad_out_bias: float32 [1024], P(('dp', 'fsdp'))
- grad_up_weight: float32 [1024, 4096], P(('dp', 'fsdp'))
- grad_up_bias: float32 [4096], P(('dp', 'fsdp'))
- grad_down_weight: float32 [4096, 1024], P(('dp', 'fsdp'))
- grad_down_bias: float32 [1024], P(('dp', 'fsdp'))
Inputs may be any that keep to these rules, and one draw needn't show every extreme that they name: `doc_ids`: document numbers never fall along a row. In each row one document spans from the block that holds position 511 to the block that holds position (3) * 512.
All inputs are finite; a program needn't handle non-finite values.
Results may differ from a plain program's by a relative error of at most 0.012.
The roundings to bfloat16 on the way count: a program that leaves them out, or rounds other values in their place, can miss the bound.
Values may be sent and summed in bfloat16 or wider, within the bound.
No kernel may reach another device: no remote copies, remote signals or barrier semaphores. Data moves between devices by JAX's collectives and lax.ppermute only.
A program may use at most 256 MiB of HBM per device.

v0:
```python
import jax
import jax.numpy as jnp
from jax import lax
from jax.sharding import PartitionSpec as P

HEADS = 16
HEAD = 64
ROT = 16
BLOCK = 256


EPS = 1e-05


def gelu(values_in):
    return jax.nn.gelu(values_in, approximate=False)


def norm(values_in, gain_vec, bias_vec):
    centre = values_in - jnp.mean(values_in, axis=-1, keepdims=True)
    spread = jnp.mean(centre * centre, axis=-1, keepdims=True)
    return centre * lax.rsqrt(spread + EPS) * gain_vec + bias_vec


def rotate(matrix, positions):
    row_count = matrix.shape[0]
    by_head = matrix.reshape(row_count, HEADS, HEAD)
    half_rot = ROT // 2
    frequency = 10000.0 ** (-(jnp.arange(half_rot, dtype=jnp.float32) * 2.0) / ROT)
    angles = positions.astype(jnp.float32)[:, None] * frequency[None, :]
    cosine = jnp.cos(angles)[:, None, :]
    sine_vals = jnp.sin(angles)[:, None, :]
    leading = by_head[:, :, :half_rot]
    trailing = by_head[:, :, half_rot:ROT]
    turned = jnp.concatenate(
        [
            leading * cosine - trailing * sine_vals,
            trailing * cosine + leading * sine_vals,
            by_head[:, :, ROT:],
        ],
        axis=-1,
    )
    return turned.reshape(row_count, HEADS * HEAD)


def outer(left, right):
    return lax.dot_general(
        left, right, (((0,), (0,)), ((), ())), preferred_element_type=jnp.float32
    )


def back_through(left, weight_mat):
    return lax.dot_general(
        left, weight_mat, (((1,), (1,)), ((), ())), preferred_element_type=jnp.float32
    )


def local(
    tokens,
    cotangent,
    doc_ids,
    norm1_gain,
    norm1_bias,
    norm2_gain,
    norm2_bias,
    qkv_weight,
    qkv_bias,
    out_weight,
    out_bias,
    up_weight,
    up_bias,
    down_weight,
    down_bias,
):
    gathered = (
        lax.all_gather(norm1_gain, ("dp", "fsdp"), axis=0, tiled=True),
        lax.all_gather(norm1_bias, ("dp", "fsdp"), axis=0, tiled=True),
        lax.all_gather(norm2_gain, ("dp", "fsdp"), axis=0, tiled=True),
        lax.all_gather(norm2_bias, ("dp", "fsdp"), axis=0, tiled=True),
        lax.all_gather(qkv_weight, ("dp", "fsdp"), axis=0, tiled=True),
        lax.all_gather(qkv_bias, ("dp", "fsdp"), axis=0, tiled=True),
        lax.all_gather(out_weight, ("dp", "fsdp"), axis=0, tiled=True),
        lax.all_gather(out_bias, ("dp", "fsdp"), axis=0, tiled=True),
        lax.all_gather(up_weight, ("dp", "fsdp"), axis=0, tiled=True),
        lax.all_gather(up_bias, ("dp", "fsdp"), axis=0, tiled=True),
        lax.all_gather(down_weight, ("dp", "fsdp"), axis=0, tiled=True),
        lax.all_gather(down_bias, ("dp", "fsdp"), axis=0, tiled=True),
    )
    gain_one = gathered[0].astype(jnp.float32)
    bias_one = gathered[1].astype(jnp.float32)
    gain_two = gathered[2].astype(jnp.float32)
    bias_two = gathered[3].astype(jnp.float32)
    full_qkv = gathered[4]
    shift_qkv = gathered[5].astype(jnp.float32)
    full_out = gathered[6]
    shift_out = gathered[7].astype(jnp.float32)
    full_up = gathered[8]
    shift_up = gathered[9].astype(jnp.float32)
    full_down = gathered[10]
    shift_down = gathered[11].astype(jnp.float32)
    rows = tokens.shape[0]
    width = tokens.shape[1]
    group = lax.axis_size("fsdp")
    member = lax.axis_index("fsdp")
    stream_len = rows * group
    x_rows = tokens.astype(jnp.float32)
    normed_one, norm_pull_one = jax.vjp(norm, x_rows, gain_one, bias_one)
    normed_two, norm_pull_two = jax.vjp(norm, x_rows, gain_two, bias_two)
    h_one = normed_one.astype(jnp.bfloat16)
    h_two = normed_two.astype(jnp.bfloat16)
    qkv_rows = jnp.dot(h_one, full_qkv, preferred_element_type=jnp.float32) + shift_qkv
    places = member * rows + jnp.arange(rows, dtype=jnp.int32)

    def turn(query_raw, key_raw):
        return (rotate(query_raw, places) * 0.125, rotate(key_raw, places))

    (query_rot, key_rot), turn_pull = jax.vjp(
        turn, qkv_rows[:, :width], qkv_rows[:, width : 2 * width]
    )
    queries = query_rot.astype(jnp.bfloat16)
    keys_own = key_rot.astype(jnp.bfloat16)
    values_own = qkv_rows[:, 2 * width :].astype(jnp.bfloat16)
    key_all, value_all = (
        lax.all_gather(keys_own, "fsdp", axis=0, tiled=True),
        lax.all_gather(values_own, "fsdp", axis=0, tiled=True),
    )
    block_span = 2 * BLOCK
    block_count = stream_len // block_span
    doc_row = doc_ids[0]
    table = jnp.arange(doc_row.shape[0], dtype=jnp.int32)

    def owner_of(block_ids):
        return jnp.sum(jnp.where(block_ids[:, None] == table[None, :], doc_row[None, :], 0), axis=1)

    own_block = places // BLOCK
    own_doc = owner_of(own_block)
    key_block = jnp.arange(stream_len, dtype=jnp.int32) // BLOCK
    key_doc = owner_of(key_block)
    tiles = (
        key_all.reshape(block_count, block_span, HEADS, HEAD),
        value_all.reshape(block_count, block_span, HEADS, HEAD),
        key_block.reshape(block_count, block_span),
        key_doc.reshape(block_count, block_span),
    )
    query_heads = queries.reshape(rows, HEADS, HEAD)
    tile_count = (member * rows + rows - 1) // block_span + 1

    def tile_at(index):
        return tuple(
            (lax.dynamic_index_in_dim(member_arr, index, 0, keepdims=False) for member_arr in tiles)
        )

    def tile_scores(tile):
        raw = jnp.einsum("qhd,khd->hqk", query_heads, tile[0], preferred_element_type=jnp.float32)
        allowed = (tile[2][None, :] <= own_block[:, None]) & (tile[3][None, :] == own_doc[:, None])
        return (raw, allowed[None])

    def max_step(index, carry):
        top, total = carry
        raw, allowed = tile_scores(tile_at(index))
        new_top = jnp.maximum(top, jnp.max(jnp.where(allowed, raw, -1e30), axis=-1))
        total = total * jnp.exp(top - new_top) + jnp.sum(
            jnp.where(allowed, jnp.exp(raw - new_top[:, :, None]), 0.0), axis=-1
        )
        return (new_top, total)

    start = (jnp.full((HEADS, rows), -1e30, jnp.float32), jnp.zeros((HEADS, rows), jnp.float32))
    top, total = lax.fori_loop(0, tile_count, max_step, start)
    log_total = top + jnp.log(total)

    def probs_of(raw, allowed):
        return jnp.where(allowed, jnp.exp(raw - log_total[:, :, None]), 0.0)

    d_attended = back_through(cotangent, full_out).astype(jnp.bfloat16)
    grad_heads = d_attended.reshape(rows, HEADS, HEAD)

    def mix_step(index, carry):
        summed, delta_sum = carry
        tile = tile_at(index)
        raw, allowed = tile_scores(tile)
        probs_now = probs_of(raw, allowed)
        summed = summed + jnp.einsum(
            "hqk,khd->qhd",
            probs_now.astype(jnp.bfloat16),
            tile[1],
            preferred_element_type=jnp.float32,
        )
        d_probs = jnp.einsum(
            "qhd,khd->hqk", grad_heads, tile[1], preferred_element_type=jnp.float32
        )
        delta_sum = delta_sum + jnp.sum(probs_now * d_probs, axis=-1)
        return (summed, delta_sum)

    head_zeros = jnp.zeros((rows, HEADS, HEAD), jnp.float32)
    mixed, delta = lax.fori_loop(
        0, tile_count, mix_step, (head_zeros, jnp.zeros((HEADS, rows), jnp.float32))
    )
    attended = mixed.reshape(rows, width).astype(jnp.bfloat16)
    up_rows = jnp.dot(h_two, full_up, preferred_element_type=jnp.float32) + shift_up
    active_f, gelu_pull = jax.vjp(gelu, up_rows)
    active = active_f.astype(jnp.bfloat16)
    result = (
        x_rows
        + jnp.dot(attended, full_out, preferred_element_type=jnp.float32)
        + shift_out
        + jnp.dot(active, full_down, preferred_element_type=jnp.float32)
        + shift_down
    )
    output = result.astype(jnp.bfloat16)
    back_qkv, back_up, back_down = (
        lax.all_gather(qkv_weight, ("dp", "fsdp"), axis=0, tiled=True),
        lax.all_gather(up_weight, ("dp", "fsdp"), axis=0, tiled=True),
        lax.all_gather(down_weight, ("dp", "fsdp"), axis=0, tiled=True),
    )
    d_rows = cotangent.astype(jnp.float32)
    grad_end_bias = jnp.sum(d_rows, axis=0)
    grad_down = outer(active, cotangent)
    grad_out = outer(attended, cotangent)
    d_active = back_through(cotangent, back_down)
    d_up = gelu_pull(d_active)[0].astype(jnp.bfloat16)
    grad_up_shift = jnp.sum(d_up.astype(jnp.float32), axis=0)
    grad_up = outer(h_two, d_up)
    d_two = back_through(d_up, back_up)

    def score_grads(tile):
        raw, allowed = tile_scores(tile)
        probs_now = probs_of(raw, allowed)
        d_probs = jnp.einsum(
            "qhd,khd->hqk", grad_heads, tile[1], preferred_element_type=jnp.float32
        )
        d_scores = (probs_now * (d_probs - delta[:, :, None])).astype(jnp.bfloat16)
        return (probs_now, d_scores)

    def grad_step(index, carry):
        d_query_sum, key_parts, value_parts = carry
        tile = tile_at(index)
        probs_now, d_scores = score_grads(tile)
        d_query_sum = d_query_sum + jnp.einsum(
            "hqk,khd->qhd", d_scores, tile[0], preferred_element_type=jnp.float32
        )
        d_key_tile = jnp.einsum(
            "hqk,qhd->khd", d_scores, query_heads, preferred_element_type=jnp.float32
        )
        d_value_tile = jnp.einsum(
            "hqk,qhd->khd",
            probs_now.astype(jnp.bfloat16),
            grad_heads,
            preferred_element_type=jnp.float32,
        )
        key_parts = lax.dynamic_update_index_in_dim(key_parts, d_key_tile, index, 0)
        value_parts = lax.dynamic_update_index_in_dim(value_parts, d_value_tile, index, 0)
        return (d_query_sum, key_parts, value_parts)

    part_zeros = jnp.zeros((block_count, block_span, HEADS, HEAD), jnp.float32)
    d_queries, key_parts, value_parts = lax.fori_loop(
        0, tile_count, grad_step, (head_zeros, part_zeros, part_zeros)
    )
    d_keys, d_values = (
        lax.psum_scatter(
            key_parts.reshape(stream_len, width), "fsdp", scatter_dimension=0, tiled=True
        ),
        lax.psum_scatter(
            value_parts.reshape(stream_len, width), "fsdp", scatter_dimension=0, tiled=True
        ),
    )
    d_query_raw, d_key_raw = turn_pull((d_queries.reshape(rows, width), d_keys))
    d_qkv = jnp.concatenate([d_query_raw, d_key_raw, d_values], axis=1).astype(jnp.bfloat16)
    grad_qkv_shift = jnp.sum(d_qkv.astype(jnp.float32), axis=0)
    grad_qkv = outer(h_one, d_qkv)
    d_one = back_through(d_qkv, back_qkv)
    d_x_one, grad_gain_one, grad_bias_one = norm_pull_one(d_one)
    d_x_two, grad_gain_two, grad_bias_two = norm_pull_two(d_two)
    grad_tokens = (d_rows + d_x_one + d_x_two).astype(jnp.bfloat16)
    shards = (
        lax.psum_scatter(grad_gain_one, ("dp", "fsdp"), scatter_dimension=0, tiled=True),
        lax.psum_scatter(grad_bias_one, ("dp", "fsdp"), scatter_dimension=0, tiled=True),
        lax.psum_scatter(grad_gain_two, ("dp", "fsdp"), scatter_dimension=0, tiled=True),
        lax.psum_scatter(grad_bias_two, ("dp", "fsdp"), scatter_dimension=0, tiled=True),
        lax.psum_scatter(grad_qkv, ("dp", "fsdp"), scatter_dimension=0, tiled=True),
        lax.psum_scatter(grad_qkv_shift, ("dp", "fsdp"), scatter_dimension=0, tiled=True),
        lax.psum_scatter(grad_out, ("dp", "fsdp"), scatter_dimension=0, tiled=True),
        lax.psum_scatter(grad_end_bias, ("dp", "fsdp"), scatter_dimension=0, tiled=True),
        lax.psum_scatter(grad_up, ("dp", "fsdp"), scatter_dimension=0, tiled=True),
        lax.psum_scatter(grad_up_shift, ("dp", "fsdp"), scatter_dimension=0, tiled=True),
        lax.psum_scatter(grad_down, ("dp", "fsdp"), scatter_dimension=0, tiled=True),
        lax.psum_scatter(grad_end_bias, ("dp", "fsdp"), scatter_dimension=0, tiled=True),
    )
    return (
        output,
        grad_tokens,
        shards[0],
        shards[1],
        shards[2],
        shards[3],
        shards[4],
        shards[5],
        shards[6],
        shards[7],
        shards[8],
        shards[9],
        shards[10],
        shards[11],
    )


def solution(mesh):
    placed = (
        P(("dp", "fsdp"), None),
        P(("dp", "fsdp"), None),
        P("dp", None),
        P(("dp", "fsdp")),
        P(("dp", "fsdp")),
        P(("dp", "fsdp")),
        P(("dp", "fsdp")),
        P(("dp", "fsdp"), None),
        P(("dp", "fsdp")),
        P(("dp", "fsdp"), None),
        P(("dp", "fsdp")),
        P(("dp", "fsdp"), None),
        P(("dp", "fsdp")),
        P(("dp", "fsdp"), None),
        P(("dp", "fsdp")),
    )
    return jax.shard_map(
        local,
        mesh=mesh,
        in_specs=placed,
        out_specs=(
            P(("dp", "fsdp"), None),
            P(("dp", "fsdp"), None),
            P(("dp", "fsdp")),
            P(("dp", "fsdp")),
            P(("dp", "fsdp")),
            P(("dp", "fsdp")),
            P(("dp", "fsdp"), None),
            P(("dp", "fsdp")),
            P(("dp", "fsdp"), None),
            P(("dp", "fsdp")),
            P(("dp", "fsdp"), None),
            P(("dp", "fsdp")),
            P(("dp", "fsdp"), None),
            P(("dp", "fsdp")),
        ),
        check_vma=False,
    )
```

profile of v0, /device:TPU:0, one launch (start us, length us, event | category | flops | bytes accessed | tf_op | source)
XLA Modules:
  0.0 2141.3 jit_solution(5805465102954182040)
XLA Ops:
  14.6 42.9 %all-reduce.21 = (bf16[1024]{0:T(1024)(128)(2,1)}, bf16[1024]{0:T(1024)(128)(2,1)}, bf16[3072]{0:T(1024)(128)(2,1)S(1)}, bf16[1024]{0:T(1024)(128)(2,1)S(1)}, bf...) all-reduce(bf16[1024]{0:T(1024)(128)(2,1)S(1)} %dynamic-update-slic, ...), channel_id=1, replica_groups=mesh['dp'=8,'fsdp'=4] {'dp','fsdp'}, use_global_device_ids=true, to_apply=%add.11 | all-reduce | flops 9216 | bytes 36864
  61.6 21.7 %all-gather.8.cloned.1.call-done = bf16[1024,3072]{1,0:T(8,128)(2,1)} async-done(((bf16[32,3072]{1,0:T(8,128)(2,1)}), bf16[1024,3072]{1,0:T(8,128)(2,1)}) %all-gather.8.cloned.1.call-update) | async-done | bytes 6291472 | tf_op jit(solution)/shard_map/all_gather | solution.py:80
  104.6 36.5 %all-gather.14.cloned.1.call-done = bf16[1024,1024]{1,0:T(8,128)(2,1)} async-done(((bf16[32,1024]{1,0:T(8,128)(2,1)}), bf16[1024,1024]{1,0:T(8,128)(2,1)}) %all-gather.14.cloned.1.call-update) | async-done | bytes 2097168 | tf_op jit(solution)/shard_map/all_gather | solution.py:82
  148.1 46.9 %all-gather.12.cloned.1.call-done = bf16[2048,1024]{0,1:T(8,128)(2,1)} async-done(((bf16[512,1024]{0,1:T(8,128)(2,1)}), bf16[2048,1024]{0,1:T(8,128)(2,1)}) %all-gather.12.cloned.1.call-update) | async-done | bytes 4194320 | tf_op jit(solution)/shard_map/all_gather | solution.py:124
  208.5 18.8 while.42
  227.3 22.7 %all-gather.10.cloned.1.call-done = bf16[2048,1024]{1,0:T(8,128)(2,1)} async-done(((bf16[512,1024]{1,0:T(8,128)(2,1)}), bf16[2048,1024]{1,0:T(8,128)(2,1)}) %all-gather.10.cloned.1.call-update) | async-done | bytes 4194320 | tf_op jit(solution)/shard_map/all_gather | solution.py:125
  250.0 11.6 reshape.425
  271.7 35.5 %while.43 = (s32[]{:T(128)}, f32[512,16,64]{0,2,1:T(8,128)S(1)}, f32[16,512]{1,0:T(8,128)S(1)}, s32[]{:T(128)}, bf16[4,512,16,64]{1,3,2,0:T(8,128)(2,1)}, /*inde...) while((s32[]{:T(128)}, f32[512,16,64]{0,2,1:T(8,128)S(1)}, ...), condition=%wide.region_10.11_spmd.clone, body=%wide.region_8.10_spmd.clone.sunk | while | flops 1641291776 | bytes 132073736 | solution.py:195
  317.4 129.0 %while.44 = (s32[]{:T(128)}, f32[512,16,64]{0,2,1:T(8,128)S(1)}, f32[4,512,16,64]{1,0,3,2:T(4,128)}, f32[4,512,16,64]{1,0,3,2:T(4,128)}, s32[]{:T(128)}, /*index...) while((s32[]{:T(128)}, f32[512,16,64]{0,2,1:T(8,128)S(1)}, ...), condition=%wide.region_12.13_spmd.clone, body=%wide.region_11.12_spmd.clone.sunk | while | flops 2719227904 | bytes 146655520 | solution.py:255
  343.3 41.1 %dynamic_update_slice.11 = f32[4,512,16,64]{1,0,3,2:T(4,128)} dynamic-update-slice(f32[4,512,16,64]{1,0,3,2:T(4,128)} %get-tuple-element.973, f32[1,512,16,64]{1,0,3,2:T(1,128)} %copy.122, s32[]{:T(128)S(6)} %select_n.154, s32[]{:T(128)} %constant.157.clone.1..sunk.2, s32[]{:T(128)} %constant.157.clone.1..sunk.2, s32[]{:T(128)} %constant.157.clone.1..sunk.2) | dynamic-update-slice | bytes 4194308 | tf_op jit(solution)/shard_map/while/body/jit(dynamic_update_index_in_dim)/dynamic_update_slice | solution.py:250
  399.8 41.0 %dynamic_update_slice.12 = f32[4,512,16,64]{1,0,3,2:T(4,128)} dynamic-update-slice(f32[4,512,16,64]{1,0,3,2:T(4,128)} %get-tuple-element.974, f32[1,512,16,64]{1,0,3,2:T(1,128)} %copy.123, s32[]{:T(128)S(6)} %select_n.154, s32[]{:T(128)} %constant.157.clone.1..sunk.2, s32[]{:T(128)} %constant.157.clone.1..sunk.2, s32[]{:T(128)} %constant.157.clone.1..sunk.2) | dynamic-update-slice | bytes 4194308 | tf_op jit(solution)/shard_map/while/body/jit(dynamic_update_index_in_dim)/dynamic_update_slice | solution.py:251
  446.5 10.9 copy.118
  457.4 10.8 copy.119
  468.9 538.5 %all-gather = bf16[32,1,128]{2,1,0:T(2,128)(2,1)S(1)} all-gather(bf16[1,1,128]{2,1,0:T(2,128)(2,1)S(1)} %bitcast.224), channel_id=1, replica_groups=mesh['dp'=8,'fsdp'=4] {'dp','fsdp'}, dimensions={0}, use_global_device_ids=true | all-gather | bytes 8448 | tf_op jit(solution)/shard_map/all_gather | solution.py:85
  1007.5 10.7 fusion.109
  1022.6 27.9 %convert_reduce_fusion = (f32[4096]{0:T(1024)S(1)}, bf16[512,4096]{1,0:T(8,128)(2,1)}, f32[512,4096]{1,0:T(8,128)}) fusion(f32[512,4096]{1,0:T(8,128)} %fusion.109, f32[4096]{0:T(1024)S(1)} %bitcast.220, bf16[512,1024]{1,0:T(8,128)(2,1)} %param.22, bf16[4096,1024]{1,0:T(8,128)(2,1)} %all-gather.18.cloned.1.call-done), kind=kOutput, calls=%fused_computation.94 | convolution fusion | flops 4452249600 | bytes 30441472 | tf_op jit(solution)/shard_map/dot_general | solution.py:53
  1060.9 10.5 fusion.124
  1071.6 10.7 fusion.107
  1086.9 18.4 reduce-scatter.9.cloned.1.call-done
  1147.7 40.9 %all-reduce.20 = (f32[1024]{0:T(1024)S(1)}, f32[1024]{0:T(1024)S(1)}, f32[1024]{0:T(1024)S(1)}, f32[1024]{0:T(1024)S(1)}, f32[3072]{0:T(1024)S(1)}, /*index=5*/f32[1024]{0:T(1024)S(1)}, f32[4096]{0:T(1024)S(1)}) all-reduce(f32[1024]{0:T(1024)S(1)} %get-tuple-element.489, ...), channel_id=4, replica_groups=mesh['dp'=8,'fsdp'=4] {'dp','fsdp'}, use_global_device_ids=true, to_apply=%region_20.21.clone | all-reduce | flops 12288 | bytes 98304
  1192.2 57.6 %reduce-scatter.13.cloned.1.call-done = f32[32,1024]{1,0:T(8,128)} async-done(((f32[1024,1024]{1,0:T(8,128)}), f32[32,1024]{1,0:T(8,128)}) %reduce-scatter.13.cloned.1.call-update) | async-done | bytes 131088 | tf_op jit(solution)/shard_map/reduce_scatter | solution.py:281
  1249.8 358.1 %reduce-scatter.17.cloned.1.call-done = f32[128,1024]{1,0:T(8,128)} async-done(((f32[4096,1024]{1,0:T(8,128)}), f32[128,1024]{1,0:T(8,128)}) %reduce-scatter.17.cloned.1.call-update) | async-done | bytes 524304 | tf_op jit(solution)/shard_map/reduce_scatter | solution.py:285
  1608.0 361.9 %reduce-scatter.15.cloned.1.call-done = f32[32,4096]{1,0:T(8,128)} async-done(((f32[1024,4096]{1,0:T(8,128)}), f32[32,4096]{1,0:T(8,128)}) %reduce-scatter.15.cloned.1.call-update) | async-done | bytes 524304 | tf_op jit(solution)/shard_map/reduce_scatter | solution.py:283
  1969.9 163.7 %reduce-scatter.11.cloned.1.call-done = f32[32,3072]{1,0:T(8,128)} async-done(((f32[1024,3072]{1,0:T(8,128)}), f32[32,3072]{1,0:T(8,128)}) %reduce-scatter.11.cloned.1.call-update) | async-done | bytes 393232 | tf_op jit(solution)/shard_map/reduce_scatter | solution.py:279
  (226 shorter events, 224.3 us)
Async XLA Ops:
  7.2 76.1 %all-gather.8.cloned.1.call-start = ((), (), s32[]{:S(2)}) async-start(), calls=%async_computation.6 | async-start | bytes 6488064 | tf_op jit(solution)/shard_map/all_gather | solution.py:80
  7.9 133.2 %all-gather.14.cloned.1.call-start = ((), (), s32[]{:S(2)}) async-start(), calls=%async_computation.9 | async-start | bytes 2162688 | tf_op jit(solution)/shard_map/all_gather | solution.py:82
  8.7 186.3 %all-gather.12.cloned.1.call-start = ((), (), s32[]{:S(2)}) async-start(), calls=%async_computation.8 | async-start | bytes 5242880 | tf_op jit(solution)/shard_map/all_gather | solution.py:124
  57.5 25.8 %copy-start.23 = (f32[1024]{0:T(1024)}, f32[1024]{0:T(1024)S(1)}, u32[]{:S(2)}) copy-start(f32[1024]{0:T(1024)S(1)} %convert_element_type.91) | copy-start | bytes 12292
  57.5 25.8 %copy-start.31 = (f32[1024]{0:T(1024)}, f32[1024]{0:T(1024)S(1)}, u32[]{:S(2)}) copy-start(f32[1024]{0:T(1024)S(1)} %convert_element_type.92) | copy-start | bytes 12292
  59.0 24.3 %copy-start.25 = (f32[512]{0:T(512)}, f32[512]{0:T(512)S(1)}, u32[]{:S(2)}) copy-start(f32[512]{0:T(512)S(1)} %broadcast_multiply_fusion.1) | copy-start | bytes 6148
  61.6 36.5 %copy-start.19 = (f32[512,8]{0,1:T(8,128)}, f32[512,8]{0,1:T(8,128)S(1)}, u32[]{:S(2)}) copy-start(f32[512,8]{0,1:T(8,128)S(1)} %get-tuple-element.609) | copy-start | bytes 49156
  61.6 36.5 %copy-start.21 = (f32[512,8]{0,1:T(8,128)}, f32[512,8]{0,1:T(8,128)S(1)}, u32[]{:S(2)}) copy-start(f32[512,8]{0,1:T(8,128)S(1)} %get-tuple-element.610) | copy-start | bytes 49156
  100.3 149.7 %all-gather.10.cloned.1.call-start = ((), (), s32[]{:S(2)}) async-start(), calls=%async_computation.7 | async-start | bytes 5242880 | tf_op jit(solution)/shard_map/all_gather | solution.py:125
  103.1 904.3 %all-gather.16.cloned.1.call-start = ((), (), s32[]{:S(2)}) async-start(), calls=%async_computation.10 | async-start | bytes 8650752 | tf_op jit(solution)/shard_map/all_gather | solution.py:84
  103.7 918.9 %all-gather.18.cloned.1.call-start = ((), (), s32[]{:S(2)}) async-start(), calls=%async_computation.11 | async-start | bytes 8650752 | tf_op jit(solution)/shard_map/all_gather | solution.py:86
  104.3 979.7 %reduce-scatter.7.cloned.1.call-start = ((), (), s32[]{:S(2)}) async-start(), calls=%async_computation.12 | async-start | bytes 10485760 | tf_op jit(solution)/shard_map/reduce_scatter | solution.py:259
  457.3 648.0 %reduce-scatter.9.cloned.1.call-start = ((), (), s32[]{:S(2)}) async-start(), calls=%async_computation.13 | async-start | bytes 10485760 | tf_op jit(solution)/shard_map/reduce_scatter | solution.py:262
  468.2 539.2 %copy-start.4 = (bf16[512,1024]{1,0:T(8,128)(2,1)S(1)}, bf16[512,1024]{1,0:T(8,128)(2,1)}, u32[]{:S(2)}) copy-start(bf16[512,1024]{1,0:T(8,128)(2,1)} %param.21) | copy-start | bytes 3145732
  468.2 539.2 %copy-start.26 = (f32[512]{0:T(512)S(1)}, f32[512]{0:T(512)}, u32[]{:S(2)}) copy-start(f32[512]{0:T(512)} %copy-done.25) | copy-start | bytes 6148
  468.2 539.2 %copy-start.28 = (f32[512]{0:T(512)S(1)}, f32[512]{0:T(512)}, u32[]{:S(2)}) copy-start(f32[512]{0:T(512)} %copy-done.27) | copy-start | bytes 6148
  468.2 781.6 %reduce-scatter.13.cloned.1.call-start = ((), (), s32[]{:S(2)}) async-start(), calls=%async_computation.15 | async-start | bytes 4325376 | tf_op jit(solution)/shard_map/reduce_scatter | solution.py:281
  1022.5 585.4 %reduce-scatter.17.cloned.1.call-start = ((), (), s32[]{:S(2)}) async-start(), calls=%async_computation.17 | async-start | bytes 17301504 | tf_op jit(solution)/shard_map/reduce_scatter | solution.py:285
  1071.4 898.5 %reduce-scatter.15.cloned.1.call-start = ((), (), s32[]{:S(2)}) async-start(), calls=%async_computation.16 | async-start | bytes 17301504 | tf_op jit(solution)/shard_map/reduce_scatter | solution.py:283
  1082.4 1051.2 %reduce-scatter.11.cloned.1.call-start = ((), (), s32[]{:S(2)}) async-start(), calls=%async_computation.14 | async-start | bytes 12976128 | tf_op jit(solution)/shard_map/reduce_scatter | solution.py:279
  1084.0 23.3 %copy-start.20 = (f32[512,8]{0,1:T(8,128)S(1)}, f32[512,8]{0,1:T(8,128)}, u32[]{:S(2)}) copy-start(f32[512,8]{0,1:T(8,128)} %copy-done.19) | copy-start | bytes 49156
  1084.0 23.3 %copy-start.22 = (f32[512,8]{0,1:T(8,128)S(1)}, f32[512,8]{0,1:T(8,128)}, u32[]{:S(2)}) copy-start(f32[512,8]{0,1:T(8,128)} %copy-done.21) | copy-start | bytes 49156
  1084.0 23.3 %copy-start.6 = (f32[512,16,64]{0,2,1:T(8,128)S(1)}, f32[512,16,64]{0,2,1:T(8,128)}, u32[]{:S(2)}) copy-start(f32[512,16,64]{0,2,1:T(8,128)} %copy-done.5) | copy-start | bytes 6291460
  1188.7 945.3 %copy-start.40 = (f32[32]{0:T(128)}, f32[32]{0:T(128)S(1)}, u32[]{:S(2)}) copy-start(f32[32]{0:T(128)S(1)} %dynamic-slice.5) | copy-start | bytes 388
  (32 other events, 175.2 us)
Sparse Core Ops, SparseCore 0:
  10.9 72.3 all-gather.7
  86.2 54.8 all-gather.13
  143.5 51.4 all-gather.11
  197.3 52.6 all-gather.9
  252.7 77.2 all-gather.15
  332.8 76.1 all-gather.17
  457.5 558.1 reduce-scatter.6
  1019.0 86.3 reduce-scatter.8
  1108.2 141.5 reduce-scatter.12
  1252.5 355.3 reduce-scatter.16
  1610.8 358.9 reduce-scatter.14
  1976.3 157.1 reduce-scatter.10
where the time goes:
time: 2160 us; the launch traced here: 2140 us
  waiting for transfers between devices  1090 us (50%)
  blocking collectives  622 us (29%)
  local copies, waits for them, and re-layouts  190 us (9%)
  matrix products  170 us (8%)
  other arithmetic  35.6 us (2%)
    all_gather x1, blocking collectives, local(): lax.all_gather(up_bias, ('dp', 'fsdp'), axis=0, tiled=True)  538 us
    reduce_scatter x1, waiting for transfers between devices, local(): lax.psum_scatter(grad_up, ('dp', 'fsdp'), scatter_dimension=0, tiled=True)  362 us
    reduce_scatter x1, waiting for transfers between devices, local(): lax.psum_scatter(grad_down, ('dp', 'fsdp'), scatter_dimension=0, tiled=True)  358 us
    reduce_scatter x1, waiting for transfers between devices, local(): lax.psum_scatter(grad_qkv, ('dp', 'fsdp'), scatter_dimension=0, tiled=True)  164 us
    unnamed x2, blocking collectives  83.8 us
    reduce_scatter x1, waiting for transfers between devices, local(): lax.psum_scatter(grad_out, ('dp', 'fsdp'), scatter_dimension=0, tiled=True)  57.6 us
    unnamed x104, local copies, waits for them, and re-layouts  52.5 us
    all_gather x1, waiting for transfers between devices, local(): lax.all_gather(keys_own, 'fsdp', axis=0, tiled=True)  46.9 us
  transfers between devices with their start and end apart: 12, of which 9 were waited for; matrix products, arithmetic and copies ran while one was open for 18% of the time, Pallas kernels for 0%

commit v1 on v0

v1 whole, which is shorter than its diff:
```python
import functools

import jax
import jax.numpy as jnp
import numpy as np
from jax import lax
from jax.experimental import pallas as pl
from jax.experimental.pallas import tpu as pltpu
from jax.sharding import PartitionSpec as P

HEADS = 16
HEAD = 64
ROT = 16
BLOCK = 256
EPS = 1e-05
VMEM = 60 * 1024 * 1024
ALL = ("dp", "fsdp")
F32 = jnp.float32
LOW = jnp.bfloat16


def dot(left, right, contract=((1,), (0,))):
    return lax.dot_general(left, right, (contract, ((), ())), preferred_element_type=F32)


NT = ((1,), (1,))
TN = ((0,), (0,))


def normed(x_rows):
    centre = x_rows - jnp.mean(x_rows, axis=-1, keepdims=True)
    spread = jnp.mean(centre * centre, axis=-1, keepdims=True)
    scale = lax.rsqrt(spread + EPS)
    return centre * scale, scale


def turned(z, cosine, sine_a, sine_b, sign):
    groups = []
    for start in range(0, z.shape[1], 128):
        part = z[:, start : start + 128]
        ahead = pltpu.roll(part, 128 - ROT // 2, 1)
        behind = pltpu.roll(part, ROT // 2, 1)
        groups.append(part * cosine + sign * (ahead * sine_a + behind * sine_b))
    return groups[0] if len(groups) == 1 else jnp.concatenate(groups, axis=1)


def head_only(array, head):
    lane = lax.broadcasted_iota(jnp.int32, array.shape, 1)
    keep = (lane >= head * HEAD) & (lane < (head + 1) * HEAD)
    return jnp.where(keep, array, jnp.zeros_like(array))


def params(*order):
    return pltpu.CompilerParams(vmem_limit_bytes=VMEM, dimension_semantics=order)


def whole(shape):
    return pl.BlockSpec(shape, lambda *_: (0,) * len(shape))


def qkv_kernel(order, x, gain, bias, weight, shift, cosine, sine_a, sine_b, q, k, v):
    width = q.shape[1]
    n, _ = normed(x[...].astype(F32))
    h = (n * gain[...] + bias[...]).astype(LOW)
    rows = dot(h, weight[...]) + shift[...]
    tables = (cosine[...], sine_a[...], sine_b[...])
    q[...] = (turned(rows[:, :width], *tables, 1.0) * 0.125).astype(LOW)
    k[...] = turned(rows[:, width : 2 * width], *tables, 1.0).astype(LOW)
    v[...] = rows[:, 2 * width :].astype(LOW)


def call_qkv(order, x, gain, bias, weight, shift, tables, span):
    rows, model = x.shape
    width = shift.shape[1] // 3
    here = lambda i, o: (i, 0)
    there = lambda i, o: (o[i], 0)
    return pl.pallas_call(
        qkv_kernel,
        grid_spec=pltpu.PrefetchScalarGridSpec(
            num_scalar_prefetch=1,
            grid=(rows // span,),
            in_specs=[
                pl.BlockSpec((span, model), here),
                whole((1, model)),
                whole((1, model)),
                whole((model, 3 * width)),
                whole((1, 3 * width)),
            ]
            + [pl.BlockSpec((span, 128), there)] * 3,
            out_specs=[pl.BlockSpec((span, width), there)] * 3,
        ),
        out_shape=[jax.ShapeDtypeStruct((rows, width), LOW)] * 3,
        compiler_params=params("arbitrary"),
        cost_estimate=pl.CostEstimate(flops=6 * rows * model * width, bytes_accessed=4 * rows * model, transcendentals=0),
        name="qkv",
    )(order, x, gain, bias, weight, shift, *tables)


def fwd_kernel(first, q, k, v, mixed, low_mixed, lse, keys, values_t, scores, top, total, out_t):
    step = pl.program_id(0)
    width = q.shape[1]
    heads = width // HEAD
    own = pl.ds(pl.multiple_of(step * BLOCK, BLOCK), BLOCK)
    k_own = k[own, :]
    for head in range(heads):
        keys[step, head] = head_only(k_own, head)
    values_t[step] = v[own, :].T
    q_t = q[own, :].T
    top[...] = jnp.full_like(top, -1e30)
    total[...] = jnp.zeros_like(total)
    out_t[...] = jnp.zeros_like(out_t)

    def score(at, _):
        for head in range(heads):
            s = dot(keys[at, head], q_t)
            scores[at, head] = s
            top[head] = jnp.maximum(top[head], jnp.max(s.reshape(BLOCK // 8, 8, BLOCK), axis=0))
        return 0

    lax.fori_loop(first[step], step + 1, score, 0)
    peak = [jnp.max(top[head], axis=0, keepdims=True) for head in range(heads)]

    def mix(at, _):
        for head in range(heads):
            e = jnp.exp(scores[at, head] - peak[head])
            total[head] += jnp.sum(e.reshape(BLOCK // 8, 8, BLOCK), axis=0)
            span = slice(head * HEAD, (head + 1) * HEAD)
            out_t[span, :] += dot(values_t[at, span, :], e.astype(LOW))
        return 0

    lax.fori_loop(first[step], step + 1, mix, 0)
    for head in range(heads):
        sums = jnp.sum(total[head], axis=0, keepdims=True)
        lse[head : head + 1, :] = peak[head] + jnp.log(sums)
        span = slice(head * HEAD, (head + 1) * HEAD)
        out_t[span, :] = out_t[span, :] * (1.0 / sums)
    result = out_t[...].T
    mixed[...] = result
    low_mixed[...] = result.astype(LOW)


def call_fwd(first, q, k, v):
    rows, width = q.shape
    heads = width // HEAD
    blocks = rows // BLOCK
    return pl.pallas_call(
        fwd_kernel,
        grid_spec=pltpu.PrefetchScalarGridSpec(
            num_scalar_prefetch=1,
            grid=(blocks,),
            in_specs=[whole((rows, width))] * 3,
            out_specs=[
                pl.BlockSpec((BLOCK, width), lambda i, o: (i, 0)),
                pl.BlockSpec((BLOCK, width), lambda i, o: (i, 0)),
                pl.BlockSpec((heads, BLOCK), lambda i, o: (0, i)),
            ],
            scratch_shapes=[
                pltpu.VMEM((blocks, heads, BLOCK, width), LOW),
                pltpu.VMEM((blocks, width, BLOCK), LOW),
                pltpu.VMEM((blocks, heads, BLOCK, BLOCK), F32),
                pltpu.VMEM((heads, 8, BLOCK), F32),
                pltpu.VMEM((heads, 8, BLOCK), F32),
                pltpu.VMEM((width, BLOCK), F32),
            ],
        ),
        out_shape=[
            jax.ShapeDtypeStruct((rows, width), F32),
            jax.ShapeDtypeStruct((rows, width), LOW),
            jax.ShapeDtypeStruct((heads, rows), F32),
        ],
        compiler_params=params("arbitrary"),
        cost_estimate=pl.CostEstimate(flops=8 * rows * rows * width, bytes_accessed=16 * rows * width, transcendentals=rows * rows * heads),
        name="attend",
    )(first, q, k, v)


def mlp_kernel(
    order, x, cot, mixed, gain, bias, w_up, b_up, w_down, w_out,
    part, d_mixed, to_norm, g_up, g_down, g_out, sums, acc_up, acc_down, acc_out,
):
    step = pl.program_id(0)

    @pl.when(step == 0)
    def _():
        acc_up[...] = jnp.zeros_like(acc_up)
        acc_down[...] = jnp.zeros_like(acc_down)
        acc_out[...] = jnp.zeros_like(acc_out)
        sums[...] = jnp.zeros_like(sums)

    n, _ = normed(x[...].astype(F32))
    h = (n * gain[...] + bias[...]).astype(LOW)
    u = dot(h, w_up[...]) + b_up[...]
    cdf = 0.5 * (1.0 + lax.erf(u * np.float32(np.sqrt(0.5))))
    slope = cdf + u * (jnp.exp(-0.5 * u * u) * np.float32(1.0 / np.sqrt(2.0 * np.pi)))
    active = (u * cdf).astype(LOW)
    dy = cot[...]
    part[...] = (dot(active, w_down[...]) + dot(mixed[...], w_out[...])).astype(LOW)
    d_mixed[...] = dot(dy, w_out[...], NT).astype(LOW)
    acc_down[...] += dot(active, dy, TN)
    acc_out[...] += dot(mixed[...], dy, TN)
    d_up32 = dot(dy, w_down[...], NT) * slope
    d_up = d_up32.astype(LOW)
    sums[0:1, : d_up.shape[1]] += jnp.sum(d_up.astype(F32), axis=0, keepdims=True)
    acc_up[...] += dot(h, d_up, TN)
    d_h = dot(d_up, w_up[...], NT)
    sums[1:2, : n.shape[1]] += jnp.sum(d_h, axis=0, keepdims=True)
    sums[2:3, : n.shape[1]] += jnp.sum(d_h * n, axis=0, keepdims=True)
    to_norm[...] = d_h * gain[...]

    @pl.when(step == pl.num_programs(0) - 1)
    def _():
        g_up[...] = acc_up[...].astype(LOW)
        g_down[...] = acc_down[...].astype(LOW)
        g_out[...] = acc_out[...].astype(LOW)


def call_mlp(order, x, cot, mixed, gain, bias, w_up, b_up, w_down, w_out, span):
    rows, model = x.shape
    units = w_up.shape[1]
    width = mixed.shape[1]
    here = lambda i, o: (i, 0)
    there = lambda i, o: (o[i], 0)
    return pl.pallas_call(
        mlp_kernel,
        grid_spec=pltpu.PrefetchScalarGridSpec(
            num_scalar_prefetch=1,
            grid=(rows // span,),
            in_specs=[
                pl.BlockSpec((span, model), here),
                pl.BlockSpec((span, model), here),
                pl.BlockSpec((span, width), there),
                whole((1, model)),
                whole((1, model)),
                whole((model, units)),
                whole((1, units)),
                whole((units, model)),
                whole((width, model)),
            ],
            out_specs=[
                pl.BlockSpec((span, model), here),
                pl.BlockSpec((span, width), there),
                pl.BlockSpec((span, model), here),
                whole((model, units)),
                whole((units, model)),
                whole((width, model)),
                whole((8, max(model, units))),
            ],
            scratch_shapes=[
                pltpu.VMEM((model, units), F32),
                pltpu.VMEM((units, model), F32),
                pltpu.VMEM((width, model), F32),
            ],
        ),
        out_shape=[
            jax.ShapeDtypeStruct((rows, model), LOW),
            jax.ShapeDtypeStruct((rows, width), LOW),
            jax.ShapeDtypeStruct((rows, model), F32),
            jax.ShapeDtypeStruct((model, units), LOW),
            jax.ShapeDtypeStruct((units, model), LOW),
            jax.ShapeDtypeStruct((width, model), LOW),
            jax.ShapeDtypeStruct((8, max(model, units)), F32),
        ],
        compiler_params=params("arbitrary"),
        cost_estimate=pl.CostEstimate(flops=12 * rows * model * (units + width // 2), bytes_accessed=12 * rows * model, transcendentals=rows * units * 2),
        name="mlp",
    )(order, x, cot, mixed, gain, bias, w_up, b_up, w_down, w_out)


def bwd_kernel(
    first, q, k, v, d_mixed, mixed, lse, cosine, sine_a, sine_b,
    d_qkv, keys, values, keys_t, d_q_t, d_k, d_v, queries, seeds,
):
    step = pl.program_id(0)
    width = q.shape[1]
    heads = width // HEAD
    own = pl.ds(pl.multiple_of(step * BLOCK, BLOCK), BLOCK)
    k_own = k[own, :]
    v_own = v[own, :]
    q_own = q[own, :]
    s_own = d_mixed[own, :]
    for head in range(heads):
        keys[step, head] = head_only(k_own, head)
        values[step, head] = head_only(v_own, head)
        queries[head] = head_only(q_own, head)
        seeds[head] = head_only(s_own, head)
    keys_t[step] = k_own.T
    q_t = q_own.T
    s_t = s_own.T
    product_t = (s_own.astype(F32) * mixed[own, :]).T
    delta = [
        jnp.sum(product_t[head * HEAD : (head + 1) * HEAD, :], axis=0, keepdims=True) for head in range(heads)
    ]
    log_total = lse[...]
    d_q_t[...] = jnp.zeros_like(d_q_t)
    d_k[own, :] = jnp.zeros((BLOCK, width), F32)
    d_v[own, :] = jnp.zeros((BLOCK, width), F32)

    def body(at, _):
        rows = pl.ds(pl.multiple_of(at * BLOCK, BLOCK), BLOCK)
        low_probs = []
        low_scores = []
        for head in range(heads):
            s = dot(keys[at, head], q_t)
            probs = jnp.exp(s - log_total[head : head + 1, :])
            d_probs = dot(values[at, head], s_t)
            d_scores = (probs * (d_probs - delta[head])).astype(LOW)
            low_probs.append(probs.astype(LOW))
            low_scores.append(d_scores)
            span = slice(head * HEAD, (head + 1) * HEAD)
            d_q_t[span, :] += dot(keys_t[at, span, :], d_scores)
        d_v[rows, :] += dot(jnp.concatenate(low_probs, axis=1), seeds[...].reshape(heads * BLOCK, width))
        d_k[rows, :] += dot(jnp.concatenate(low_scores, axis=1), queries[...].reshape(heads * BLOCK, width))
        return 0

    lax.fori_loop(first[step], step + 1, body, 0)
    d_qkv[own, :width] = (turned(d_q_t[...].T, cosine[own, :], sine_a[own, :], sine_b[own, :], -1.0) * 0.125).astype(LOW)

    @pl.when(step == pl.num_programs(0) - 1)
    def _():
        def close(at, _):
            rows = pl.ds(pl.multiple_of(at * BLOCK, BLOCK), BLOCK)
            d_qkv[rows, width : 2 * width] = turned(d_k[rows, :], cosine[rows, :], sine_a[rows, :], sine_b[rows, :], -1.0).astype(LOW)
            d_qkv[rows, 2 * width :] = d_v[rows, :].astype(LOW)
            return 0

        lax.fori_loop(0, q.shape[0] // BLOCK, close, 0)


def call_bwd(first, q, k, v, d_mixed, mixed, lse, tables):
    rows, width = q.shape
    heads = width // HEAD
    blocks = rows // BLOCK
    return pl.pallas_call(
        bwd_kernel,
        grid_spec=pltpu.PrefetchScalarGridSpec(
            num_scalar_prefetch=1,
            grid=(blocks,),
            in_specs=[whole((rows, width))] * 5
            + [pl.BlockSpec((heads, BLOCK), lambda i, o: (0, i))]
            + [whole((rows, 128))] * 3,
            out_specs=whole((rows, 3 * width)),
            scratch_shapes=[
                pltpu.VMEM((blocks, heads, BLOCK, width), LOW),
                pltpu.VMEM((blocks, heads, BLOCK, width), LOW),
                pltpu.VMEM((blocks, width, BLOCK), LOW),
                pltpu.VMEM((width, BLOCK), F32),
                pltpu.VMEM((rows, width), F32),
                pltpu.VMEM((rows, width), F32),
                pltpu.VMEM((heads, BLOCK, width), LOW),
                pltpu.VMEM((heads, BLOCK, width), LOW),
            ],
        ),
        out_shape=jax.ShapeDtypeStruct((rows, 3 * width), LOW),
        compiler_params=params("arbitrary"),
        cost_estimate=pl.CostEstimate(flops=20 * rows * rows * width, bytes_accessed=24 * rows * width, transcendentals=rows * rows * heads),
        name="attend_back",
    )(first, q, k, v, d_mixed, mixed, lse, *tables)


def close_kernel(order, x, d_qkv, to_norm, gain, bias, weight, part, g_qkv, sums, acc):
    step = pl.program_id(0)

    @pl.when(step == 0)
    def _():
        acc[...] = jnp.zeros_like(acc)
        sums[...] = jnp.zeros_like(sums)

    width3 = d_qkv.shape[1]
    n, scale = normed(x[...].astype(F32))
    h = (n * gain[...] + bias[...]).astype(LOW)
    d_rows = d_qkv[...]
    acc[...] += dot(h, d_rows, TN)
    sums[0:1, :width3] += jnp.sum(d_rows.astype(F32), axis=0, keepdims=True)
    d_h = dot(d_rows, weight[...], NT)
    sums[1:2, : n.shape[1]] += jnp.sum(d_h, axis=0, keepdims=True)
    sums[2:3, : n.shape[1]] += jnp.sum(d_h * n, axis=0, keepdims=True)
    e = d_h * gain[...] + to_norm[...]
    e = e - jnp.mean(e, axis=-1, keepdims=True) - n * jnp.mean(e * n, axis=-1, keepdims=True)
    part[...] = (e * scale).astype(LOW)

    @pl.when(step == pl.num_programs(0) - 1)
    def _():
        g_qkv[...] = acc[...].astype(LOW)


def call_close(order, x, d_qkv, to_norm, gain, bias, weight, span):
    rows, model = x.shape
    width3 = d_qkv.shape[1]
    here = lambda i, o: (i, 0)
    there = lambda i, o: (o[i], 0)
    return pl.pallas_call(
        close_kernel,
        grid_spec=pltpu.PrefetchScalarGridSpec(
            num_scalar_prefetch=1,
            grid=(rows // span,),
            in_specs=[
                pl.BlockSpec((span, model), here),
                pl.BlockSpec((span, width3), there),
                pl.BlockSpec((span, model), here),
                whole((1, model)),
                whole((1, model)),
                whole((model, width3)),
            ],
            out_specs=[
                pl.BlockSpec((span, model), here),
                whole((model, width3)),
                whole((8, max(model, width3))),
            ],
            scratch_shapes=[pltpu.VMEM((model, width3), F32)],
        ),
        out_shape=[
            jax.ShapeDtypeStruct((rows, model), LOW),
            jax.ShapeDtypeStruct((model, width3), LOW),
            jax.ShapeDtypeStruct((8, max(model, width3)), F32),
        ],
        compiler_params=params("arbitrary"),
        cost_estimate=pl.CostEstimate(flops=4 * rows * model * width3, bytes_accessed=10 * rows * model, transcendentals=0),
        name="close",
    )(order, x, d_qkv, to_norm, gain, bias, weight)


def across(array, bit):
    size = lax.axis_size("fsdp")
    return lax.ppermute(array, "fsdp", [(i, i ^ bit) for i in range(size)])


def exchange(pieces):
    size = lax.axis_size("fsdp")
    if size != 4:
        return lax.all_to_all(pieces, "fsdp", split_axis=0, concat_axis=0, tiled=True)
    member = lax.axis_index("fsdp")
    out = pieces
    for bit in range(1, size):
        mine = lax.dynamic_index_in_dim(pieces, member ^ bit, 0, keepdims=False)
        out = lax.dynamic_update_index_in_dim(out, across(mine, bit), member ^ bit, 0)
    return out


def gather_rows(rows):
    if lax.axis_size("fsdp") != 4:
        return lax.all_gather(rows, "fsdp", axis=0, tiled=True)
    half = rows.shape[0] // 2
    one = across(rows, 1)
    two = across(rows, 2)
    low_half = across(one[:half], 2)
    high_half = across(two[half:], 1)
    return jnp.concatenate([rows, one, two, low_half, high_half], axis=0)


def reduce_rows(parts):
    size = lax.axis_size("fsdp")
    if size != 4:
        return lax.psum_scatter(parts, "fsdp", scatter_dimension=0, tiled=True).astype(F32)
    own, one, two, three = jnp.split(parts, 4, axis=0)
    half = own.shape[0] // 2
    from_one = across(three[:half], 1)
    from_two = across(three[half:], 2)
    one = jnp.concatenate([one[:half], (one[half:].astype(F32) + from_two.astype(F32)).astype(LOW)], axis=0)
    two = jnp.concatenate([(two[:half].astype(F32) + from_one.astype(F32)).astype(LOW), two[half:]], axis=0)
    return own.astype(F32) + across(one, 1).astype(F32) + across(two, 2).astype(F32)


def total_over_all(vector):
    count = lax.axis_size("dp") * lax.axis_size("fsdp")
    step = 1
    while step < count:
        vector = vector + lax.ppermute(vector, ALL, [(i, i ^ step) for i in range(count)])
        step *= 2
    return vector


def swap_owner(array, back):
    groups, members = lax.axis_size("dp"), lax.axis_size("fsdp")
    pairs = [(m * groups + g, g * members + m) for g in range(groups) for m in range(members)]
    if back:
        pairs = [(b, a) for a, b in pairs]
    return lax.ppermute(array, ALL, pairs)


def gather_dp(array):
    return lax.all_gather(array, "dp", axis=0, tiled=True)


def scatter_dp(array):
    return lax.psum_scatter(array, "dp", scatter_dimension=0, tiled=True)


def rotary_tables(length):
    half = ROT // 2
    frequency = (np.float32(10000.0) ** (-(np.arange(half, dtype=np.float32) * np.float32(2.0)) / np.float32(ROT))).astype(np.float32)
    angles = (np.arange(length, dtype=np.float32)[:, None] * frequency[None, :]).astype(np.float32)
    cosine = np.cos(angles).astype(np.float32)
    sine = np.sin(angles).astype(np.float32)
    cos_row = np.ones((length, 128), np.float32)
    ahead = np.zeros((length, 128), np.float32)
    behind = np.zeros((length, 128), np.float32)
    for start in range(0, 128, HEAD):
        cos_row[:, start : start + half] = cosine
        cos_row[:, start + half : start + ROT] = cosine
        ahead[:, start : start + half] = -sine
        behind[:, start + half : start + ROT] = sine
    return tuple(jnp.asarray(t) for t in (cos_row, ahead, behind))


def local(
    tokens, cotangent, doc_ids, norm1_gain, norm1_bias, norm2_gain, norm2_bias, qkv_weight, qkv_bias,
    out_weight, out_bias, up_weight, up_bias, down_weight, down_bias,
):
    groups, members = lax.axis_size("dp"), lax.axis_size("fsdp")
    group, member = lax.axis_index("dp"), lax.axis_index("fsdp")
    devices = groups * members
    rows, model = tokens.shape
    stream = rows * members
    shard = qkv_weight.shape[0]
    width = model // members
    units_dev = up_bias.shape[0]
    units = groups * units_dev

    small = jnp.concatenate([norm1_gain, norm1_bias, norm2_gain, norm2_bias, qkv_bias, out_bias, down_bias, up_bias])
    sizes = [norm1_gain.shape[0]] * 4 + [qkv_bias.shape[0], out_bias.shape[0], down_bias.shape[0], units_dev]
    small = jnp.pad(small, (0, shard * 128 - small.shape[0])).reshape(shard, 128)
    qkv_cut = qkv_weight.reshape(shard, 3, members, width).transpose(2, 0, 1, 3).reshape(members, shard, 3 * width)
    up_cut = up_weight.reshape(shard, groups, members, units_dev).transpose(2, 0, 1, 3).reshape(members, shard, units)
    small_cut = jnp.broadcast_to(small[None], (members, shard, 128))
    arrived = exchange(jnp.concatenate([qkv_cut, small_cut, up_cut], axis=2)).reshape(members * shard, -1)
    x_all = gather_rows(tokens)
    qkv_all = gather_dp(arrived[:, : 3 * width + 128])
    up_all = gather_dp(arrived[:, 3 * width + 128 :])
    down_all = gather_dp(down_weight)
    out_all = gather_dp(swap_owner(out_weight, False))
    cot_all = gather_rows(cotangent)

    packed = qkv_all[:, 3 * width :].reshape(devices, shard * 128).astype(F32)
    ends = np.cumsum([0] + sizes)
    gain_one, bias_one, gain_two, bias_two, shift_qkv, shift_out, shift_down, shift_up = (
        packed[:, ends[i] : ends[i + 1]] for i in range(8)
    )
    gain_one, bias_one, gain_two, bias_two = (a.reshape(1, model) for a in (gain_one, bias_one, gain_two, bias_two))
    shift_qkv = lax.dynamic_index_in_dim(shift_qkv.reshape(3, members, width), member, 1, keepdims=False).reshape(1, 3 * width)
    shift_up = lax.dynamic_index_in_dim(shift_up.reshape(groups, members, units_dev), member, 1, keepdims=False).reshape(1, units)

    sources = jnp.arange(members, dtype=jnp.int32)
    order = sources ^ member if members == 4 else sources
    doc_row = doc_ids[0]
    first = jnp.sum((doc_row[None, :] < doc_row[:, None]).astype(jnp.int32), axis=1)
    tables = rotary_tables(stream)

    q, k, v = call_qkv(order, x_all, gain_one, bias_one, qkv_all, shift_qkv, tables, rows)
    mixed, low_mixed, lse = call_fwd(first, q, k, v)
    part, d_mixed, to_norm, g_up, g_down, g_out, sums_two = call_mlp(
        order, x_all, cot_all, low_mixed, gain_two, bias_two, up_all, shift_up, down_all, out_all, rows
    )
    x_rows = tokens.astype(F32)
    d_rows = cotangent.astype(F32)
    output = (
        x_rows + reduce_rows(part) + shift_out.reshape(1, model) + shift_down.reshape(1, model)
    ).astype(LOW)
    g_down = scatter_dp(g_down).astype(F32)
    g_up = exchange(scatter_dp(g_up).reshape(members, shard, units))
    g_up = g_up.reshape(members, shard, groups, units_dev).transpose(1, 2, 0, 3).reshape(shard, -1).astype(F32)
    g_out = swap_owner(scatter_dp(g_out), True).astype(F32)

    d_qkv = call_bwd(first, q, k, v, d_mixed, mixed, lse, tables)
    part, g_qkv, sums_one = call_close(order, x_all, d_qkv, to_norm, gain_one, bias_one, qkv_all, rows)
    grad_tokens = (d_rows + reduce_rows(part)).astype(LOW)
    g_qkv = exchange(scatter_dp(g_qkv).reshape(members, shard, 3 * width))
    g_qkv = g_qkv.reshape(members, shard, 3, width).transpose(1, 2, 0, 3).reshape(shard, -1).astype(F32)

    wide_qkv = lax.dynamic_update_index_in_dim(
        jnp.zeros((3, members, width), F32), sums_one[0, : 3 * width].reshape(3, 1, width), member, 1
    )
    wide_up = lax.dynamic_update_index_in_dim(
        jnp.zeros((groups, members, units_dev), F32), sums_two[0, :units].reshape(groups, 1, units_dev), member, 1
    )
    vectors = [
        sums_one[2, :model], sums_one[1, :model], sums_two[2, :model], sums_two[1, :model],
        jnp.sum(d_rows, axis=0), wide_qkv.reshape(-1), wide_up.reshape(-1),
    ]
    summed = total_over_all(jnp.concatenate(vectors))
    place = group * members + member
    mine = []
    start = 0
    for vector in vectors:
        size = vector.shape[0] // devices
        mine.append(lax.dynamic_slice_in_dim(summed, start + place * size, size))
        start += vector.shape[0]
    gain_1, bias_1, gain_2, bias_2, end_bias, qkv_shift, up_shift = mine
    return (
        output, grad_tokens, gain_1, bias_1, gain_2, bias_2, g_qkv, qkv_shift, g_out, end_bias, g_up, up_shift, g_down, end_bias,
    )


def solution(mesh):
    row, vec = P(ALL, None), P(ALL)
    return jax.shard_map(
        local,
        mesh=mesh,
        in_specs=(row, row, P("dp", None), vec, vec, vec, vec, row, vec, row, vec, row, vec, row, vec),
        out_specs=(row, row, vec, vec, vec, vec, row, vec, row, vec, row, vec, row, vec),
        check_vma=False,
    )
```

time: 2160 us -> 417 us (0.19)
  waiting for transfers between devices: 1090 us -> 89 us
  blocking collectives: 622 us -> 54 us
  matrix products: 170 us -> 0 us
  Pallas kernels: 0 us -> 152 us
  local copies, waits for them, and re-layouts: 190 us -> 49.3 us
  starting transfers between devices: 0.69 us -> 38.7 us
    reduce_scatter x6 -> x4, waiting for transfers between devices: 960 us -> 0.04 us  [scatter_dp(): return lax.psum_scatter(array, 'dp', scatter_dimension=0, tiled=True)]
    all_gather x1, blocking collectives: 538 us -> 54 us  [gather_dp(): return lax.all_gather(array, 'dp', axis=0, tiled=True)]
    dot_general x21 -> x0, matrix products: 170 us -> none  [the longest x4 44.8 us: back_through(): lax.dot_general(left, weight_mat, (((1,), (1,)), ((), ())), preferred_ele...]
    pallas_call x0 -> x5, Pallas kernels: none -> 152 us  [the longest x1 57.8 us: call_bwd(): pl.pallas_call(bwd_kernel, grid_spec=pltpu.PrefetchScalarGridSpec(num_sca...]
    all_gather x6 -> x3, waiting for transfers between devices: 128 us -> 0.01 us  [gather_dp(): return lax.all_gather(array, 'dp', axis=0, tiled=True)]
    dynamic_update_slice x4 -> x8, local copies, waits for them, and re-layouts: 90.9 us -> 2.59 us  [the longest x6 2.5 us: exchange(): lax.dynamic_update_index_in_dim(out, across(mine, bit), member ^ bit, 0)]
    ppermute x0 -> x32, waiting for transfers between devices: none -> 87.6 us  [the longest x25 54 us: across(): return lax.ppermute(array, 'fsdp', [(i, i ^ bit) for i in range(size)])]
    unnamed x2 -> x0, blocking collectives: 83.8 us -> none
  transfers between devices with their start and end apart: 12 -> 39, of which waited for: 9 -> 18; matrix products, arithmetic and copies ran while one was open for 18% -> 14% of each run, Pallas kernels for 0% -> 26%
where the time goes in v1:
time: 417 us; the launch traced here: 418 us
  Pallas kernels  152 us (36%)
  waiting for transfers between devices  89 us (21%)
  blocking collectives  54 us (13%)
  local copies, waits for them, and re-layouts  49.3 us (12%)
  starting transfers between devices  38.7 us (9%)
  other arithmetic  21 us (5%)
  between operations  14.5 us (3%)
    pallas_call x1, Pallas kernels, call_bwd(): pl.pallas_call(bwd_kernel, grid_spec=pltpu.PrefetchScalarGridSpec(num_sca...  57.8 us
    all_gather x1, blocking collectives, gather_dp(): return lax.all_gather(array, 'dp', axis=0, tiled=True)  54 us
    ppermute x25, waiting for transfers between devices, across(): return lax.ppermute(array, 'fsdp', [(i, i ^ bit) for i in range(size)])  54 us
    pallas_call x1, Pallas kernels, call_mlp(): pl.pallas_call(mlp_kernel, grid_spec=pltpu.PrefetchScalarGridSpec(num_sca...  41.1 us
    ppermute x5, waiting for transfers between devices, total_over_all(): lax.ppermute(vector, ALL, [(i, i ^ step) for i in range(count)])  33.6 us
    ppermute x25, starting transfers between devices, across(): return lax.ppermute(array, 'fsdp', [(i, i ^ bit) for i in range(size)])  30.4 us
    pallas_call x1, Pallas kernels, call_fwd(): pl.pallas_call(fwd_kernel, grid_spec=pltpu.PrefetchScalarGridSpec(num_sca...  24.5 us
    pallas_call x1, Pallas kernels, call_close(): pl.pallas_call(close_kernel, grid_spec=pltpu.PrefetchScalarGridSpec(num_s...  17.5 us
  transfers between devices with their start and end apart: 39, of which 18 were waited for; matrix products, arithmetic and copies ran while one was open for 14% of the time, Pallas kernels for 26%

profile of v1, /device:TPU:0, one launch (start us, length us, event | category | flops | bytes accessed | tf_op | source)
XLA Modules:
  0.0 418.3 jit_solution(4981182710837992179)
XLA Ops:
  10.1 5.4 %concatenate.29 = bf16[416]{0:T(512)(128)(2,1)S(1)} concatenate(bf16[32]{0:T(256)(128)(2,1)} %param.21, bf16[32]{0:T(256)(128)(2,1)} %param.22, bf16[32]{0:T(256)(128)(2,1)} %param.23, bf16[32]{0:T(256)(128)(2,1)} %param.24, bf16[96]{0:T(256)(128)(2,1)} %param.26, bf16[32]{0:T(256)(128)(2,1)} %param.28, bf16[32]{0:T(256)(128)(2,1)} %param.32, bf16[128]{0:T(256)(128)(2,1)} %param.30), dimensions={0} | concatenate | bytes 1664 | tf_op jit(solution)/shard_map/concatenate | solution.py:519
  15.6 3.0 collective-permute-start.8
  18.6 3.3 collective-permute-done.8
  25.3 3.0 collective-permute-done.9
  39.2 54.0 %all_gather.15.w_out = bf16[256,1024]{1,0:T(8,128)(2,1)} all-gather(bf16[32,1024]{1,0:T(8,128)(2,1)S(1)} %collective-permute-done.11), channel_id=1, replica_groups=mesh['dp'=8,'fsdp'=4] {'dp'}, dimensions={0}, use_global_device_ids=true | all-gather | bytes 589824 | tf_op jit(solution)/shard_map/all_gather | solution.py:481
  109.6 2.5 collective-permute-done.3
  112.2 7.7 %collective-permute-done.6 = bf16[256,1024]{1,0:T(8,128)(2,1)S(1)} collective-permute-done((bf16[256,1024]{1,0:T(8,128)(2,1)S(1)}, bf16[256,1024]{1,0:T(8,128)(2,1)S(1)}, u32[]{:S(2)}, u32[]{:S(2)}) %collective-permute-start.6) | collective-permute-done | bytes 524320 | tf_op jit(solution)/shard_map/ppermute | solution.py:424
  128.5 10.8 %qkv.1 = (bf16[2048,256]{1,0:T(8,128)(2,1)}, bf16[2048,256]{1,0:T(8,128)(2,1)}, bf16[2048,256]{1,0:T(8,128)(2,1)}) custom-call(s32[4]{0:T(128)} %iota_xor_fusion.order, bf16[2048,1024]{1,0:T(8,128)(2,1)} %copy-done.4, f32[1,1024]{1,0:T(1,128)} %reshape.107.gain, f32[1,1024]{1,0:T(1,128)} %reshape.108.bias, ...), custom_call_target="tpu_custom_call" | custom-call | flops 3221225472 | bytes 8388608 | tf_op jit(solution)/shard_map/qkv/pallas_call | solution.py:77
  139.4 24.5 %attend.1 = (f32[2048,256]{1,0:T(8,128)}, bf16[2048,256]{1,0:T(8,128)(2,1)}, f32[4,2048]{1,0:T(4,128)}) custom-call(s32[8]{0:T(128)} %convert_reduce_fusion.1.first, bf16[2048,256]{1,0:T(8,128)(2,1)} %get-tuple-element.30.q, bf16[2048,256]{1,0:T(8,128)(2,1)} %get-tuple-element.31.k, bf16[2048,256]{1,0:T(8,128)(2,1)} %get-tuple-element.32.v), custom_call_target="tpu_custom_call" | custom-call | flops 8589934592 | bytes 8388608 | tf_op jit(solution)/shard_map/attend/pallas_call | solution.py:146
  163.9 41.1 %mlp.1 = (bf16[2048,1024]{1,0:T(8,128)(2,1)}, bf16[2048,256]{1,0:T(8,128)(2,1)}, f32[2048,1024]{1,0:T(8,128)}, bf16[1024,1024]{1,0:T(8,128)(2,1)}, bf16[1024,102...) custom-call(s32[4]{0:T(128)} %iota_xor_fusion.order, bf16[2048,1024]{1,0:T(8,128)(2,1)} %copy-done.4, ...), custom_call_target="tpu_custom_call" | custom-call | flops 28991029248 | bytes 25165824 | tf_op jit(solution)/shard_map/mlp/pallas_call | solution.py:223
  205.1 57.8 %attend_back.1.d_qkv = bf16[2048,768]{1,0:T(8,128)(2,1)} custom-call(s32[8]{0:T(128)} %convert_reduce_fusion.1.first, bf16[2048,256]{1,0:T(8,128)(2,1)} %get-tuple-element.30.q, bf16[2048,256]{1,0:T(8,128)(2,1)} %get-tuple-element.31.k, bf16[2048,256]{1,0:T(8,128)(2,1)} %get-tuple-element.32.v, bf16[2048,256]{1,0:T(8,128)(2,1)} %get-tuple-element.35.d_mixed, ...), custom_call_target="tpu_custom_call" | custom-call | flops 21474836480 | bytes 12582912 | tf_op jit(solution)/shard_map/attend_back/pallas_call | solution.py:333
  262.9 17.5 %close.1 = (bf16[2048,1024]{1,0:T(8,128)(2,1)}, bf16[1024,768]{1,0:T(8,128)(2,1)}, f32[8,1024]{1,0:T(8,128)}) custom-call(s32[4]{0:T(128)} %iota_xor_fusion.order, bf16[2048,1024]{1,0:T(8,128)(2,1)} %copy-done.4, bf16[2048,768]{1,0:T(8,128)(2,1)} %attend_back.1.d_qkv, f32[2048,1024]{1,0:T(8,128)} %get-tuple-element.38.to_norm, f32[1,1024]{1,0:T(1,128)} %reshape.107.gain, ...), custom_call_target="tpu_custom_call" | custom-call | flops 6442450944 | bytes 20971520 | tf_op jit(solution)/shard_map/close/pallas_call | solution.py:391
  281.0 3.0 fusion.2
  290.2 9.0 %collective-permute-done.16 = bf16[256,1024]{1,0:T(8,128)(2,1)} collective-permute-done((bf16[256,1024]{1,0:T(8,128)(2,1)}, bf16[256,1024]{1,0:T(8,128)(2,1)}, u32[]{:S(2)}, u32[]{:S(2)}) %collective-permute-start.16) | collective-permute-done | bytes 524320 | tf_op jit(solution)/shard_map/ppermute | solution.py:424
  318.3 15.5 %collective-permute-done.17 = bf16[512,1024]{1,0:T(8,128)(2,1)} collective-permute-done((bf16[512,1024]{1,0:T(8,128)(2,1)}, bf16[512,1024]{1,0:T(8,128)(2,1)}, u32[]{:S(2)}, u32[]{:S(2)}) %collective-permute-start.17) | collective-permute-done | bytes 1048608 | tf_op jit(solution)/shard_map/ppermute | solution.py:424
  333.8 3.8 convert_reduce_fusion
  339.4 16.2 %collective-permute-done.20 = f32[12288]{0:T(1024)S(1)} collective-permute-done((f32[12288]{0:T(1024)S(1)}, f32[12288]{0:T(1024)S(1)}, u32[]{:S(2)}, u32[]{:S(2)}) %collective-permute-start.20) | collective-permute-done | bytes 49184 | tf_op jit(solution)/shard_map/ppermute | solution.py:467
  356.5 3.3 collective-permute-done.21
  361.4 3.0 collective-permute-start.23
  365.2 10.7 %collective-permute-done.23 = f32[12288]{0:T(1024)S(1)} collective-permute-done((f32[12288]{0:T(1024)S(1)}, f32[12288]{0:T(1024)S(1)}, u32[]{:S(2)}, u32[]{:S(2)}) %collective-permute-start.23) | collective-permute-done | bytes 49184 | tf_op jit(solution)/shard_map/ppermute | solution.py:467
  376.0 3.5 add_convert_fusion
  379.5 3.5 collective-permute-done.24
  385.6 2.3 collective-permute-done.25
  402.8 2.9 collective-permute-start.31
  (179 shorter events, 96.3 us)
Async XLA Ops:
  7.2 116.1 %all-gather.4.cloned.1.call-start = ((), (), s32[]{:S(2)}) async-start(), calls=%async_computation.4 | async-start | bytes 2064384 | tf_op jit(solution)/shard_map/all_gather | solution.py:481
  30.4 133.5 %all-gather.8.cloned.1.call-start = ((), (), s32[]{:S(2)}) async-start(), calls=%async_computation.6 | async-start | bytes 2359296 | tf_op jit(solution)/shard_map/all_gather | solution.py:481
  31.1 132.8 %all-gather.6.cloned.1.call-start = ((), (), s32[]{:S(2)}) async-start(), calls=%async_computation.5 | async-start | bytes 2359296 | tf_op jit(solution)/shard_map/all_gather | solution.py:481
  31.2 62.0 %collective-permute-start = (bf16[512,1024]{1,0:T(8,128)(2,1)S(1)}, bf16[512,1024]{1,0:T(8,128)(2,1)}, u32[]{:S(2)}, u32[]{:S(2)}) collective-permute-start(bf16[512,1024]{1,0:T(8,128)(2,1)S(1)} %copy-done.1), channel_id=1, source_target_pairs={{0,1},{1,0},{2,3},{3,2},{4,5},{5,4},{6,7},{7,6},{8,9},{9,8},{10,11... | collective-permute-start | bytes 3145736 | tf_op jit(solution)/shard_map/ppermute | solution.py:424
  33.0 63.2 %collective-permute-start.1 = (bf16[512,1024]{1,0:T(8,128)(2,1)S(1)}, bf16[512,1024]{1,0:T(8,128)(2,1)}, u32[]{:S(2)}, u32[]{:S(2)}) collective-permute-start(bf16[512,1024]{1,0:T(8,128)(2,1)S(1)} %copy-done.1), channel_id=1, source_target_pairs={{0,2},{1,3},{2,0},{3,1},{4,6},{5,7},{6,4},{7,5},{8,10},{9,11},{10,... | collective-permute-start | bytes 3145736 | tf_op jit(solution)/shard_map/ppermute | solution.py:424
  33.8 64.2 %collective-permute-start.4 = (bf16[512,1024]{1,0:T(8,128)(2,1)S(1)}, bf16[512,1024]{1,0:T(8,128)(2,1)}, u32[]{:S(2)}, u32[]{:S(2)}) collective-permute-start(bf16[512,1024]{1,0:T(8,128)(2,1)S(1)} %copy-done.2), channel_id=1, source_target_pairs={{0,1},{1,0},{2,3},{3,2},{4,5},{5,4},{6,7},{7,6},{8,9},{9,8},{10,11... | collective-permute-start | bytes 3145736 | tf_op jit(solution)/shard_map/ppermute | solution.py:424
  34.3 66.8 %collective-permute-start.5 = (bf16[512,1024]{1,0:T(8,128)(2,1)S(1)}, bf16[512,1024]{1,0:T(8,128)(2,1)}, u32[]{:S(2)}, u32[]{:S(2)}) collective-permute-start(bf16[512,1024]{1,0:T(8,128)(2,1)S(1)} %copy-done.2), channel_id=1, source_target_pairs={{0,2},{1,3},{2,0},{3,1},{4,6},{5,7},{6,4},{7,5},{8,10},{9,11},{10,... | collective-permute-start | bytes 3145736 | tf_op jit(solution)/shard_map/ppermute | solution.py:424
  36.0 323.8 %reduce-scatter.7.cloned.1.call-start = ((), (), s32[]{:S(2)}) async-start(), calls=%async_computation.8 | async-start | bytes 589824 | tf_op jit(solution)/shard_map/reduce_scatter | solution.py:485
  94.2 15.3 %collective-permute-start.2 = (bf16[256,1024]{1,0:T(8,128)(2,1)S(1)}, bf16[256,1024]{1,0:T(8,128)(2,1)S(1)}, u32[]{:S(2)}, u32[]{:S(2)}) collective-permute-start(bf16[256,1024]{1,0:T(8,128)(2,1)S(1)} %slice.144), channel_id=1, source_target_pairs={{0,2},{1,3},{2,0},{3,1},{4,6},{5,7},{6,4},{7,5},{8,10},{9,11},{10,... | collective-permute-start | bytes 1572872 | tf_op jit(solution)/shard_map/ppermute | solution.py:424
  97.3 14.8 %collective-permute-start.3 = (bf16[256,1024]{1,0:T(8,128)(2,1)S(1)}, bf16[256,1024]{1,0:T(8,128)(2,1)S(1)}, u32[]{:S(2)}, u32[]{:S(2)}) collective-permute-start(bf16[256,1024]{1,0:T(8,128)(2,1)S(1)} %slice.145), channel_id=1, source_target_pairs={{0,1},{1,0},{2,3},{3,2},{4,5},{5,4},{6,7},{7,6},{8,9},{9,8},{10,11... | collective-permute-start | bytes 1572872 | tf_op jit(solution)/shard_map/ppermute | solution.py:424
  99.1 20.8 %collective-permute-start.6 = (bf16[256,1024]{1,0:T(8,128)(2,1)S(1)}, bf16[256,1024]{1,0:T(8,128)(2,1)S(1)}, u32[]{:S(2)}, u32[]{:S(2)}) collective-permute-start(bf16[256,1024]{1,0:T(8,128)(2,1)S(1)} %slice.146), channel_id=1, source_target_pairs={{0,2},{1,3},{2,0},{3,1},{4,6},{5,7},{6,4},{7,5},{8,10},{9,11},{10,... | collective-permute-start | bytes 1572872 | tf_op jit(solution)/shard_map/ppermute | solution.py:424
  102.3 20.2 %collective-permute-start.7 = (bf16[256,1024]{1,0:T(8,128)(2,1)S(1)}, bf16[256,1024]{1,0:T(8,128)(2,1)S(1)}, u32[]{:S(2)}, u32[]{:S(2)}) collective-permute-start(bf16[256,1024]{1,0:T(8,128)(2,1)S(1)} %slice.147), channel_id=1, source_target_pairs={{0,1},{1,0},{2,3},{3,2},{4,5},{5,4},{6,7},{7,6},{8,9},{9,8},{10,11... | collective-permute-start | bytes 1572872 | tf_op jit(solution)/shard_map/ppermute | solution.py:424
  205.0 178.0 %reduce-scatter.5.cloned.1.call-start = ((), (), s32[]{:S(2)}) async-start(), calls=%async_computation.7 | async-start | bytes 1769472 | tf_op jit(solution)/shard_map/reduce_scatter | solution.py:485
  280.4 110.4 %reduce-scatter.9.cloned.1.call-start = ((), (), s32[]{:S(2)}) async-start(), calls=%async_computation.9 | async-start | bytes 2359296 | tf_op jit(solution)/shard_map/reduce_scatter | solution.py:485
  281.0 120.0 %reduce-scatter.11.cloned.1.call-start = ((), (), s32[]{:S(2)}) async-start(), calls=%async_computation.10 | async-start | bytes 2359296 | tf_op jit(solution)/shard_map/reduce_scatter | solution.py:485
  284.0 15.2 %collective-permute-start.16 = (bf16[256,1024]{1,0:T(8,128)(2,1)}, bf16[256,1024]{1,0:T(8,128)(2,1)}, u32[]{:S(2)}, u32[]{:S(2)}) collective-permute-start(bf16[256,1024]{1,0:T(8,128)(2,1)} %get-tuple-element.49), channel_id=1, source_target_pairs={{0,2},{1,3},{2,0},{3,1},{4,6},{5,7},{6,4},{7,5},{8,10},{9,11},{10,... | collective-permute-start | bytes 1572872 | tf_op jit(solution)/shard_map/ppermute | solution.py:424
  285.0 15.2 %collective-permute-start.18 = (bf16[256,1024]{1,0:T(8,128)(2,1)}, bf16[256,1024]{1,0:T(8,128)(2,1)}, u32[]{:S(2)}, u32[]{:S(2)}) collective-permute-start(bf16[256,1024]{1,0:T(8,128)(2,1)} %get-tuple-element.48), channel_id=1, source_target_pairs={{0,1},{1,0},{2,3},{3,2},{4,5},{5,4},{6,7},{7,6},{8,9},{9,8},{10,11... | collective-permute-start | bytes 1572872 | tf_op jit(solution)/shard_map/ppermute | solution.py:424
  287.9 22.6 %collective-permute-start.12 = (bf16[256,1024]{1,0:T(8,128)(2,1)}, bf16[256,1024]{1,0:T(8,128)(2,1)}, u32[]{:S(2)}, u32[]{:S(2)}) collective-permute-start(bf16[256,1024]{1,0:T(8,128)(2,1)} %get-tuple-element.55), channel_id=1, source_target_pairs={{0,2},{1,3},{2,0},{3,1},{4,6},{5,7},{6,4},{7,5},{8,10},{9,11},{10,... | collective-permute-start | bytes 1572872 | tf_op jit(solution)/shard_map/ppermute | solution.py:424
  288.2 23.2 %collective-permute-start.14 = (bf16[256,1024]{1,0:T(8,128)(2,1)}, bf16[256,1024]{1,0:T(8,128)(2,1)}, u32[]{:S(2)}, u32[]{:S(2)}) collective-permute-start(bf16[256,1024]{1,0:T(8,128)(2,1)} %get-tuple-element.54), channel_id=1, source_target_pairs={{0,1},{1,0},{2,3},{3,2},{4,5},{5,4},{6,7},{7,6},{8,9},{9,8},{10,11... | collective-permute-start | bytes 1572872 | tf_op jit(solution)/shard_map/ppermute | solution.py:424
  304.2 29.7 %collective-permute-start.17 = (bf16[512,1024]{1,0:T(8,128)(2,1)}, bf16[512,1024]{1,0:T(8,128)(2,1)}, u32[]{:S(2)}, u32[]{:S(2)}) collective-permute-start(bf16[512,1024]{1,0:T(8,128)(2,1)} %pad_maximum_fusion.2), channel_id=1, source_target_pairs={{0,1},{1,0},{2,3},{3,2},{4,5},{5,4},{6,7},{7,6},{8,9},{9,8},{10,11... | collective-permute-start | bytes 3145736 | tf_op jit(solution)/shard_map/ppermute | solution.py:424
  307.0 26.9 %collective-permute-start.19 = (bf16[512,1024]{1,0:T(8,128)(2,1)}, bf16[512,1024]{1,0:T(8,128)(2,1)}, u32[]{:S(2)}, u32[]{:S(2)}) collective-permute-start(bf16[512,1024]{1,0:T(8,128)(2,1)} %pad_maximum_fusion.3), channel_id=1, source_target_pairs={{0,2},{1,3},{2,0},{3,1},{4,6},{5,7},{6,4},{7,5},{8,10},{9,11},{10,... | collective-permute-start | bytes 3145736 | tf_op jit(solution)/shard_map/ppermute | solution.py:424
  314.3 61.7 %collective-permute-start.13 = (bf16[512,1024]{1,0:T(8,128)(2,1)}, bf16[512,1024]{1,0:T(8,128)(2,1)}, u32[]{:S(2)}, u32[]{:S(2)}) collective-permute-start(bf16[512,1024]{1,0:T(8,128)(2,1)} %pad_maximum_fusion), channel_id=1, source_target_pairs={{0,1},{1,0},{2,3},{3,2},{4,5},{5,4},{6,7},{7,6},{8,9},{9,8},{10,11... | collective-permute-start | bytes 3145736 | tf_op jit(solution)/shard_map/ppermute | solution.py:424
  317.1 58.9 %collective-permute-start.15 = (bf16[512,1024]{1,0:T(8,128)(2,1)}, bf16[512,1024]{1,0:T(8,128)(2,1)S(1)}, u32[]{:S(2)}, u32[]{:S(2)}) collective-permute-start(bf16[512,1024]{1,0:T(8,128)(2,1)} %pad_maximum_fusion.1), channel_id=1, source_target_pairs={{0,2},{1,3},{2,0},{3,1},{4,6},{5,7},{6,4},{7,5},{8,10},{9,11},{10,... | collective-permute-start | bytes 3145736 | tf_op jit(solution)/shard_map/ppermute | solution.py:424
  337.6 18.0 %collective-permute-start.20 = (f32[12288]{0:T(1024)S(1)}, f32[12288]{0:T(1024)S(1)}, u32[]{:S(2)}, u32[]{:S(2)}) collective-permute-start(f32[12288]{0:T(1024)S(1)} %constant_dynamic-update-slice_fusion.12), channel_id=1, source_target_pairs={{0,1},{1,0},{2,3},{3,2},{4,5},{5,4},{6,7},{7,6},{8,9},{9,8},{10,11... | collective-permute-start | bytes 147464 | tf_op jit(solution)/shard_map/ppermute | solution.py:467
  (23 other events, 256.9 us)
Sparse Core Ops, SparseCore 0:
  30.5 30.1 all-gather.3
  62.2 31.8 all-gather.7
  96.3 28.4 all-gather.5
  205.2 31.4 reduce-scatter.6
  280.5 34.6 reduce-scatter.4
  317.4 33.5 reduce-scatter.8
  353.5 35.9 reduce-scatter.10

commit v2 on v1

v2 whole, which is shorter than its diff:
```python
import functools

import jax
import jax.numpy as jnp
import numpy as np
from jax import lax
from jax.experimental import pallas as pl
from jax.experimental.pallas import tpu as pltpu
from jax.sharding import PartitionSpec as P

HEADS = 16
HEAD = 64
ROT = 16
BLOCK = 256
EPS = 1e-05
VMEM = 60 * 1024 * 1024
ALL = ("dp", "fsdp")
SHORT = pl.CostEstimate(flops=0, bytes_accessed=0, transcendentals=0)
F32 = jnp.float32
LOW = jnp.bfloat16


def dot(left, right, contract=((1,), (0,))):
    return lax.dot_general(left, right, (contract, ((), ())), preferred_element_type=F32)


NT = ((1,), (1,))
TN = ((0,), (0,))


def normed(x_rows):
    centre = x_rows - jnp.mean(x_rows, axis=-1, keepdims=True)
    spread = jnp.mean(centre * centre, axis=-1, keepdims=True)
    scale = lax.rsqrt(spread + EPS)
    return centre * scale, scale


def turned(z, cosine, sine_a, sine_b, sign):
    groups = []
    for start in range(0, z.shape[1], 128):
        part = z[:, start : start + 128]
        ahead = pltpu.roll(part, 128 - ROT // 2, 1)
        behind = pltpu.roll(part, ROT // 2, 1)
        groups.append(part * cosine + sign * (ahead * sine_a + behind * sine_b))
    return groups[0] if len(groups) == 1 else jnp.concatenate(groups, axis=1)


def head_only(array, head):
    lane = lax.broadcasted_iota(jnp.int32, array.shape, 1)
    keep = (lane >= head * HEAD) & (lane < (head + 1) * HEAD)
    return jnp.where(keep, array, jnp.zeros_like(array))


def params(*order):
    return pltpu.CompilerParams(vmem_limit_bytes=VMEM, dimension_semantics=order)


def whole(shape):
    return pl.BlockSpec(shape, lambda *_: (0,) * len(shape))


HBM = pl.BlockSpec(memory_space=pl.ANY)


def fetch(plan, step, refs, target, sems, begin):
    for at, pieces in enumerate(plan):

        @pl.when(step == at)
        def _():
            for index, (ref, start, put, size) in enumerate(pieces):
                copy = pltpu.make_async_copy(
                    refs[ref].at[pl.ds(start, size)], target.at[pl.ds(put, size)], sems.at[at, index]
                )
                if begin:
                    copy.start()
                else:
                    copy.wait()


def fetch_all(plan, refs, target, sems):
    for at in range(len(plan)):
        fetch(plan, at, refs, target, sems, True)


def plan_of(pieces, span):
    plan, total = [], sum(p.shape[0] for p in pieces)
    for low in range(0, total, span):
        taken, at = [], 0
        for index, piece in enumerate(pieces):
            a, b = max(low, at), min(low + span, at + piece.shape[0])
            if a < b:
                taken.append((index, a - at, a, b - a))
            at += piece.shape[0]
        plan.append(tuple(taken))
    return tuple(plan)


def store(plan, step, source, refs, sems, begin):
    for at, pieces in enumerate(plan):

        @pl.when(step == at)
        def _():
            for index, (ref, start, put, size) in enumerate(pieces):
                copy = pltpu.make_async_copy(
                    source.at[pl.ds(put, size)], refs[ref].at[pl.ds(start, size)], sems.at[at, index]
                )
                if begin:
                    copy.start()
                else:
                    copy.wait()


def pack_kernel(members, member, qkv, up, small, *out):
    width = qkv.shape[1] // 3 // members
    units_dev = 128
    groups = up.shape[1] // units_dev // members
    for bit in range(members):
        to = member[0] ^ bit
        for part in range(3):
            start = pl.multiple_of((part * members + to) * width, 128)
            out[bit][:, part * width : (part + 1) * width] = qkv[:, pl.ds(start, width)]
        out[bit][:, 3 * width : 3 * width + 128] = jnp.zeros((qkv.shape[0], 128), LOW)
        out[bit][0 : small.shape[0], 3 * width : 3 * width + 128] = small[...]
        for group in range(groups):
            start = pl.multiple_of((group * members + to) * units_dev, 128)
            low = 3 * width + 128 + group * units_dev
            out[bit][:, low : low + units_dev] = up[:, pl.ds(start, units_dev)]


def call_pack(member, qkv, up, small, members):
    shard = qkv.shape[0]
    columns = (qkv.shape[1] + up.shape[1]) // members + 128
    return pl.pallas_call(
        functools.partial(pack_kernel, members),
        grid_spec=pltpu.PrefetchScalarGridSpec(
            num_scalar_prefetch=1,
            grid=(1,),
            in_specs=[whole(qkv.shape), whole(up.shape), whole(small.shape)],
            out_specs=[whole((shard, columns))] * members,
        ),
        out_shape=[jax.ShapeDtypeStruct((shard, columns), LOW)] * members,
        compiler_params=params("arbitrary"),
        cost_estimate=SHORT,
        name="pack",
    )(member, qkv, up, small)


def place_kernel(cut, member, *refs):
    *pieces, first, second = refs
    shard = pieces[0].shape[0]
    for bit, piece in enumerate(pieces):
        rows = pl.ds(pl.multiple_of((member[0] ^ bit) * shard, shard), shard)
        first[rows, :] = piece[:, :cut]
        second[rows, :] = piece[:, cut:]


def call_place(member, pieces, cut):
    members, (shard, columns) = len(pieces), pieces[0].shape
    shapes = [(members * shard, cut), (members * shard, columns - cut)]
    return pl.pallas_call(
        functools.partial(place_kernel, cut),
        grid_spec=pltpu.PrefetchScalarGridSpec(
            num_scalar_prefetch=1,
            grid=(1,),
            in_specs=[whole(p.shape) for p in pieces],
            out_specs=[whole(a) for a in shapes],
        ),
        out_shape=[jax.ShapeDtypeStruct(a, LOW) for a in shapes],
        compiler_params=params("arbitrary"),
        cost_estimate=SHORT,
        name="place",
    )(member, *pieces)


def small_block(member, members, vectors, qkv_bias, up_bias):
    size = vectors[0].shape[0]
    wide = 128 // members * (members - 1)
    rows = jnp.pad(jnp.stack(vectors), ((0, 0), (wide, wide)))
    rows = lax.dynamic_slice_in_dim(rows, wide - member * size, 128, 1)
    wide = 3 * wide
    shift = lax.dynamic_slice_in_dim(jnp.pad(qkv_bias, (wide, wide)), wide - member * 3 * size, 384, 0)
    return jnp.concatenate([rows, shift.reshape(3, 128), up_bias[None], jnp.zeros((16 - len(vectors) - 4, 128), LOW)], axis=0)


def vectors_kernel(members, member, gathered, out, wide):
    groups, rows, _ = gathered.shape
    shard = rows // members
    model = groups * 128
    out[...] = jnp.zeros_like(out)
    for group in range(groups):
        blocks = [gathered[group, m * shard : m * shard + 16, :].astype(F32) for m in range(members)]
        block = blocks[0]
        for other in blocks[1:]:
            block = block + other
        lanes = slice(group * 128, (group + 1) * 128)
        for row in range(6):
            out[row : row + 1, lanes] = block[row : row + 1, :]
        for row in range(3):
            low = group * 384 + row * 128
            wide[0:1, low : low + 128] = block[6 + row : 7 + row, :]
        own = jnp.zeros((1, 128), F32)
        for m in range(members):
            own = own + jnp.where(member[0] == m, blocks[m][9:10, :], 0.0)
        out[6:7, lanes] = own
    width = model // members
    for part in range(3):
        start = pl.multiple_of(part * model + member[0] * width, 128)
        out[7 + part : 8 + part, :width] = wide[0:1, pl.ds(start, width)]


def call_vectors(member, gathered, members, cut):
    groups, rows, _ = gathered.shape
    model = groups * 128
    return pl.pallas_call(
        functools.partial(vectors_kernel, members),
        grid_spec=pltpu.PrefetchScalarGridSpec(
            num_scalar_prefetch=1,
            grid=(1,),
            in_specs=[pl.BlockSpec((groups, rows, 128), lambda i, o: (0, 0, cut // 128 - 1))],
            out_specs=whole((16, model)),
            scratch_shapes=[pltpu.VMEM((8, 3 * model), F32)],
        ),
        out_shape=jax.ShapeDtypeStruct((16, model), F32),
        compiler_params=params("arbitrary"),
        cost_estimate=SHORT,
        name="vectors",
    )(member, gathered)


def qkv_kernel(plan, count, order, *refs):
    pieces, rest = refs[:count], refs[count:]
    vectors, weight, cosine, sine_a, sine_b, q, k, v, normal, x, sems = rest
    step = pl.program_id(0)
    width = q.shape[1]
    span = q.shape[0]
    model = x.shape[1]

    @pl.when(step == 0)
    def _():
        fetch_all(plan, pieces, x, sems)

    fetch(plan, step, pieces, x, sems, False)
    n, _ = normed(x[pl.ds(pl.multiple_of(step * span, span), span), :].astype(F32))
    h = (n * vectors[0:1, :] + vectors[1:2, :]).astype(LOW)
    normal[...] = h
    tables = (cosine[...], sine_a[...], sine_b[...])
    rows = dot(h, weight[...].reshape(model, 3 * width))
    q[...] = (turned(rows[:, :width] + vectors[7:8, :width], *tables, 1.0) * 0.125).astype(LOW)
    k[...] = turned(rows[:, width : 2 * width] + vectors[8:9, :width], *tables, 1.0).astype(LOW)
    v[...] = (rows[:, 2 * width :] + vectors[9:10, :width]).astype(LOW)


def call_qkv(order, pieces, vectors, weight, tables, span, width):
    model = pieces[0].shape[1]
    plan = plan_of(pieces, span)
    rows = span * len(plan)
    there = lambda i, o: (o[i], 0)
    return pl.pallas_call(
        functools.partial(qkv_kernel, plan, len(pieces)),
        grid_spec=pltpu.PrefetchScalarGridSpec(
            num_scalar_prefetch=1,
            grid=(rows // span,),
            in_specs=[HBM] * len(pieces)
            + [whole(vectors.shape), whole(weight.shape[:2] + (3 * width,))]
            + [pl.BlockSpec((span, 128), there)] * 3,
            out_specs=[pl.BlockSpec((span, width), there)] * 3 + [pl.BlockSpec((span, model), there)],
            scratch_shapes=[pltpu.VMEM((rows, model), LOW), pltpu.SemaphoreType.DMA((len(plan), 2))],
        ),
        out_shape=[jax.ShapeDtypeStruct((rows, width), LOW)] * 3 + [jax.ShapeDtypeStruct((rows, model), LOW)],
        compiler_params=params("arbitrary"),
        cost_estimate=SHORT,
        name="qkv",
    )(order, *pieces, vectors, weight, *tables)


def masked_rows(target, array):
    for head in range(array.shape[1] // HEAD):
        target[head * BLOCK : (head + 1) * BLOCK, :] = head_only(array, head)


def over_keys(first, step, tiles):
    begin = first[step]
    count = step + 1 - begin

    def pair(i, _):
        tiles(begin + 2 * i, 2)
        return 0

    def single(at, _):
        tiles(at, 1)
        return 0

    lax.fori_loop(0, count // 2, pair, 0)
    lax.fori_loop(step + 1 - count % 2, step + 1, single, 0)


def by_eight(array):
    return array.reshape(BLOCK // 8, 8, BLOCK)


def fwd_kernel(first, q, k, v, mixed, low_mixed, lse, keys, values, scores, top, total, out):
    step = pl.program_id(0)
    width = q.shape[1]
    heads = width // HEAD
    stack = heads * BLOCK
    own = pl.ds(pl.multiple_of(step * BLOCK, BLOCK), BLOCK)
    masked_rows(keys.at[step], k[own, :])
    masked_rows(values.at[step], v[own, :])
    q_t = q[own, :].T
    top[...] = jnp.full_like(top, -1e30)
    total[...] = jnp.zeros_like(total)
    out[...] = jnp.zeros_like(out)

    def score(at, count):
        s = dot(keys[pl.ds(at, count)].reshape(count * stack, width), q_t)
        scores[pl.ds(at, count)] = s.reshape(count, stack, BLOCK)
        for head in range(heads):
            best = top[head]
            for tile in range(count):
                low = tile * stack + head * BLOCK
                best = jnp.maximum(best, jnp.max(by_eight(s[low : low + BLOCK]), axis=0))
            top[head] = best

    over_keys(first, step, score)
    peak = [jnp.max(top[head], axis=0, keepdims=True) for head in range(heads)]

    def mix(at, count):
        grown = []
        for tile in range(count):
            for head in range(heads):
                e = jnp.exp(scores[at + tile, head * BLOCK : (head + 1) * BLOCK] - peak[head])
                total[head] += jnp.sum(by_eight(e), axis=0)
                grown.append(e.astype(LOW))
        out[...] += dot(jnp.concatenate(grown, axis=0), values[pl.ds(at, count)].reshape(count * stack, width), TN)

    over_keys(first, step, mix)
    shares = []
    for head in range(heads):
        sums = jnp.sum(total[head], axis=0, keepdims=True)
        lse[head : head + 1, :] = peak[head] + jnp.log(sums)
        shares.append(jnp.broadcast_to(1.0 / sums, (HEAD, BLOCK)))
    result = out[...] * jnp.concatenate(shares, axis=0).T
    mixed[...] = result
    low_mixed[...] = result.astype(LOW)


def call_fwd(first, q, k, v):
    rows, width = q.shape
    heads = width // HEAD
    blocks = rows // BLOCK
    return pl.pallas_call(
        fwd_kernel,
        grid_spec=pltpu.PrefetchScalarGridSpec(
            num_scalar_prefetch=1,
            grid=(blocks,),
            in_specs=[whole((rows, width))] * 3,
            out_specs=[
                pl.BlockSpec((BLOCK, width), lambda i, o: (i, 0)),
                pl.BlockSpec((BLOCK, width), lambda i, o: (i, 0)),
                pl.BlockSpec((heads, BLOCK), lambda i, o: (0, i)),
            ],
            scratch_shapes=[
                pltpu.VMEM((blocks, heads * BLOCK, width), LOW),
                pltpu.VMEM((blocks, heads * BLOCK, width), LOW),
                pltpu.VMEM((blocks, heads * BLOCK, BLOCK), F32),
                pltpu.VMEM((heads, 8, BLOCK), F32),
                pltpu.VMEM((heads, 8, BLOCK), F32),
                pltpu.VMEM((BLOCK, width), F32),
            ],
        ),
        out_shape=[
            jax.ShapeDtypeStruct((rows, width), F32),
            jax.ShapeDtypeStruct((rows, width), LOW),
            jax.ShapeDtypeStruct((heads, rows), F32),
        ],
        compiler_params=params("arbitrary"),
        cost_estimate=SHORT,
        name="attend",
    )(first, q, k, v)


def bwd_kernel(
    low_head, count_before, first, q, k, v, d_mixed, mixed, lse, cosine, sine_a, sine_b, normal, *rest
):
    before, rest = rest[:count_before], rest[count_before:]
    d_rows, grad, sums, keys, values, sum_q, sum_k, sum_v, queries, seeds, h, sem = rest
    step = pl.program_id(0)
    width = q.shape[1]
    heads = width // HEAD
    stack = heads * BLOCK
    own = pl.ds(pl.multiple_of(step * BLOCK, BLOCK), BLOCK)
    load = pltpu.make_async_copy(normal, h, sem.at[0])

    @pl.when(step == 0)
    def _():
        load.start()

    q_own = q[own, :]
    s_own = d_mixed[own, :]
    masked_rows(keys.at[step], k[own, :])
    masked_rows(values.at[step], v[own, :])
    masked_rows(queries, q_own)
    masked_rows(seeds, s_own)
    q_t = q_own.T
    s_t = s_own.T
    product_t = (s_own.astype(F32) * mixed[own, :]).T
    delta = [jnp.sum(product_t[head * HEAD : (head + 1) * HEAD, :], axis=0, keepdims=True) for head in range(heads)]
    log_total = [lse[low_head + head : low_head + head + 1, :] for head in range(heads)]
    sum_q[...] = jnp.zeros_like(sum_q)
    sum_k[own, :] = jnp.zeros((BLOCK, width), F32)
    sum_v[own, :] = jnp.zeros((BLOCK, width), F32)

    def tiles(at, count):
        key_rows = keys[pl.ds(at, count)].reshape(count * stack, width)
        s = dot(key_rows, q_t)
        d_p = dot(values[pl.ds(at, count)].reshape(count * stack, width), s_t)
        wide_probs, wide_scores, tall_scores = [], [], []
        for tile in range(count):
            low_probs, low_scores = [], []
            for head in range(heads):
                low = tile * stack + head * BLOCK
                probs = jnp.exp(s[low : low + BLOCK] - log_total[head])
                low_scores.append((probs * (d_p[low : low + BLOCK] - delta[head])).astype(LOW))
                low_probs.append(probs.astype(LOW))
            wide_probs.append(jnp.concatenate(low_probs, axis=1))
            wide_scores.append(jnp.concatenate(low_scores, axis=1))
            tall_scores += low_scores
        rows = pl.ds(pl.multiple_of(at * BLOCK, BLOCK), count * BLOCK)
        sum_v[rows, :] += dot(jnp.concatenate(wide_probs, axis=0), seeds[...])
        sum_k[rows, :] += dot(jnp.concatenate(wide_scores, axis=0), queries[...])
        sum_q[...] += dot(jnp.concatenate(tall_scores, axis=0), key_rows, TN)

    over_keys(first, step, tiles)
    d_rows[own, :width] = (turned(sum_q[...], cosine[own, :], sine_a[own, :], sine_b[own, :], -1.0) * 0.125).astype(LOW)

    @pl.when(step == pl.num_programs(0) - 1)
    def _():
        def close(at, _):
            rows = pl.ds(pl.multiple_of(at * BLOCK, BLOCK), BLOCK)
            d_rows[rows, width : 2 * width] = turned(sum_k[rows, :], cosine[rows, :], sine_a[rows, :], sine_b[rows, :], -1.0).astype(LOW)
            d_rows[rows, 2 * width :] = sum_v[rows, :].astype(LOW)
            return 0

        lax.fori_loop(0, q.shape[0] // BLOCK, close, 0)
        low = 0
        for ref in before:
            low = ref.shape[1]
            grad[:, :low] = ref[...]
        load.wait()
        grad[:, low:] = dot(h[...], d_rows[...], TN).astype(LOW)
        sums[0:1, :] = jnp.sum(d_rows[...].astype(F32), axis=0, keepdims=True)


def call_bwd(first, q, k, v, d_mixed, mixed, lse, tables, normal, part, parts, before):
    model = normal.shape[1]
    rows, full = q.shape
    width = full // parts
    heads = width // HEAD
    blocks = rows // BLOCK
    lanes = pl.BlockSpec((rows, width), lambda i, o: (0, part))
    return pl.pallas_call(
        functools.partial(bwd_kernel, part * heads, len(before)),
        grid_spec=pltpu.PrefetchScalarGridSpec(
            num_scalar_prefetch=1,
            grid=(blocks,),
            in_specs=[lanes] * 5
            + [pl.BlockSpec((heads * parts, BLOCK), lambda i, o: (0, i))]
            + [whole((rows, 128))] * 3
            + [HBM]
            + [whole(b.shape) for b in before],
            out_specs=[whole((rows, 3 * width)), whole((model, 3 * width * (part + 1))), whole((8, 3 * width))],
            scratch_shapes=[
                pltpu.VMEM((blocks, heads * BLOCK, width), LOW),
                pltpu.VMEM((blocks, heads * BLOCK, width), LOW),
                pltpu.VMEM((BLOCK, width), F32),
                pltpu.VMEM((rows, width), F32),
                pltpu.VMEM((rows, width), F32),
                pltpu.VMEM((heads * BLOCK, width), LOW),
                pltpu.VMEM((heads * BLOCK, width), LOW),
                pltpu.VMEM((rows, model), LOW),
                pltpu.SemaphoreType.DMA((1,)),
            ],
        ),
        out_shape=[
            jax.ShapeDtypeStruct((rows, 3 * width), LOW),
            jax.ShapeDtypeStruct((model, 3 * width * (part + 1)), LOW),
            jax.ShapeDtypeStruct((8, 3 * width), F32),
        ],
        compiler_params=params("arbitrary"),
        cost_estimate=SHORT,
        name="attend_back",
    )(first, q, k, v, d_mixed, mixed, lse, *tables, normal, *before)


def mlp_kernel(plan, out_plan, count, out_count, joined, chunk, order, *refs):
    x_pieces, cot_pieces, rest = refs[:count], refs[count : 2 * count], refs[2 * count :]
    mixed, vectors, rest = rest[0], rest[1], rest[2:]
    mats, rest = rest[: 1 if joined else 3], rest[1 if joined else 3 :]
    parts, rest = rest[:out_count], rest[out_count:]
    d_mixed, to_norm, rest = rest[0], rest[1], rest[2:]
    grads, rest = rest[: 1 if joined else 3], rest[1 if joined else 3 :]
    sums, normal, cot, active, d_up, own_mixed, g_out, staged, x_sems, cot_sems, out_sems = rest
    step = pl.program_id(0)
    steps = len(plan)
    span, width = own_mixed.shape[0] // steps, own_mixed.shape[1]
    model, units = normal.shape[1], active.shape[1]
    if joined:
        groups = mats[0].shape[0]
        cuts = [0, model // groups, (model + units) // groups, (model + units + width) // groups]
        w_up, w_down, w_out = (mats[0].at[:, pl.ds(cuts[i], cuts[i + 1] - cuts[i]), :] for i in range(3))
    else:
        w_up, w_down, w_out = mats
    as_up = lambda: w_up[...].reshape(model, units)
    as_down = lambda: w_down[...].reshape(units, model)
    as_out = lambda: w_out[...].reshape(width, model)

    @pl.when(step == 0)
    def _():
        fetch_all(plan, x_pieces, normal, x_sems)
        fetch_all(plan, cot_pieces, cot, cot_sems)
        sums[...] = jnp.zeros_like(sums)

    fetch(plan, step, x_pieces, normal, x_sems, False)
    fetch(plan, step, cot_pieces, cot, cot_sems, False)

    @pl.when(step < steps)
    def _():
        here = pl.ds(pl.multiple_of(step * span, span), span)
        n, _ = normed(normal[here, :].astype(F32))
        h = (n * vectors[2:3, :] + vectors[3:4, :]).astype(LOW)
        normal[here, :] = h
        dy = cot[here, :]
        own = mixed[pl.ds(pl.multiple_of(order[step] * span, span), span), :]
        own_mixed[here, :] = own
        d_mixed[...] = dot(dy, as_out(), NT).astype(LOW)
        up, down = as_up(), as_down()
        for low in range(0, units, chunk):
            cols = slice(low, low + chunk)
            u = dot(h, up[:, cols]) + vectors[6:7, cols]
            d_active = dot(dy, down[cols], NT)
            cdf = 0.5 * (1.0 + lax.erf(u * np.float32(np.sqrt(0.5))))
            slope = cdf + u * (jnp.exp(-0.5 * u * u) * np.float32(1.0 / np.sqrt(2.0 * np.pi)))
            active[here, cols] = (u * cdf).astype(LOW)
            back = (d_active * slope).astype(LOW)
            d_up[here, cols] = back
            sums[0:1, cols] += jnp.sum(back.astype(F32), axis=0, keepdims=True)
        staged[here, :] = (dot(active[here, :], down) + dot(own, as_out())).astype(LOW)
        d_h = dot(d_up[here, :], up, NT)
        sums[1:2, :model] += jnp.sum(d_h, axis=0, keepdims=True)
        sums[2:3, :model] += jnp.sum(d_h * n, axis=0, keepdims=True)
        to_norm[...] = d_h * vectors[2:3, :]

        @pl.when(step == 0)
        def _():
            sums[3:4, :model] = jnp.sum(dy.astype(F32), axis=0, keepdims=True)

    store(out_plan, step, staged, parts, out_sems, True)

    @pl.when(step >= steps)
    def _():
        at = step - steps
        many = pl.num_programs(0) - steps

        @pl.when(at == 0)
        def _():
            g_out[...] = dot(own_mixed[...], cot[...], TN).astype(LOW)

        up_cols = pl.ds(pl.multiple_of(at * (model // many), 128), model // many)
        down_cols = pl.ds(pl.multiple_of(at * (units // many), 128), units // many)
        out_rows = pl.ds(pl.multiple_of(at * (width // many), 16), width // many)
        up_grad = dot(normal[:, up_cols], d_up[...], TN).astype(LOW)
        down_grad = dot(active[:, down_cols], cot[...], TN).astype(LOW)
        if joined:
            block = grads[0].shape[0]
            grads[0][:, cuts[0] : cuts[1], :] = up_grad.reshape(block, cuts[1], units)
            grads[0][:, cuts[1] : cuts[2], :] = down_grad.reshape(block, cuts[2] - cuts[1], model)
            grads[0][:, cuts[2] : cuts[3], :] = g_out[out_rows, :].reshape(block, cuts[3] - cuts[2], model)
        else:
            grads[0][...] = up_grad
            grads[1][...] = down_grad
            grads[2][...] = g_out[out_rows, :]

    @pl.when(step == pl.num_programs(0) - 1)
    def _():
        for at in range(steps):
            store(out_plan, at, staged, parts, out_sems, False)


def call_mlp(order, x_pieces, cot_pieces, mixed, vectors, mats, span, units, out_shapes):
    rows, width = mixed.shape
    model = x_pieces[0].shape[1]
    joined = len(mats) == 1
    plan, out_plan = plan_of(x_pieces, span), plan_of(out_shapes, span)
    steps, many = len(plan), 4
    count = len(x_pieces)
    here = lambda i, o: (jnp.minimum(i, steps - 1), 0)
    there = lambda i, o: (o[jnp.minimum(i, steps - 1)], 0)
    later = lambda i, o: (jnp.maximum(i - steps, 0), 0)
    if joined:
        groups = mats[0].shape[0]
        grads = [(groups, (model + units + width) // groups, model)]
        grad_specs = [pl.BlockSpec((groups // many,) + grads[0][1:], lambda i, o: (jnp.maximum(i - steps, 0), 0, 0))]
    else:
        grads = [(model, units), (units, model), (width, model)]
        grad_specs = [pl.BlockSpec((a // many, b), later) for a, b in grads]
    sums = (8, max(model, units))
    return pl.pallas_call(
        functools.partial(mlp_kernel, plan, out_plan, count, len(out_shapes), joined, 256),
        grid_spec=pltpu.PrefetchScalarGridSpec(
            num_scalar_prefetch=1,
            grid=(steps + many,),
            in_specs=[HBM] * (2 * count)
            + [whole((rows, width)), whole(vectors.shape)]
            + [pl.BlockSpec(m.shape, lambda *_: (0, 0, 0), pipeline_mode=pl.Buffered(1)) for m in mats],
            out_specs=[HBM] * len(out_shapes)
            + [pl.BlockSpec((span, width), there), pl.BlockSpec((span, model), here)]
            + grad_specs
            + [whole(sums)],
            scratch_shapes=[
                pltpu.VMEM((rows, model), LOW),
                pltpu.VMEM((rows, model), LOW),
                pltpu.VMEM((rows, units), LOW),
                pltpu.VMEM((rows, units), LOW),
                pltpu.VMEM((rows, width), LOW),
                pltpu.VMEM((width, model), LOW),
                pltpu.VMEM((rows, model), LOW),
                pltpu.SemaphoreType.DMA((steps, 2)),
                pltpu.SemaphoreType.DMA((steps, 2)),
                pltpu.SemaphoreType.DMA((steps, 2)),
            ],
        ),
        out_shape=list(out_shapes)
        + [jax.ShapeDtypeStruct((rows, width), LOW), jax.ShapeDtypeStruct((rows, model), F32)]
        + [jax.ShapeDtypeStruct(g, LOW) for g in grads]
        + [jax.ShapeDtypeStruct(sums, F32)],
        compiler_params=params("arbitrary"),
        cost_estimate=SHORT,
        name="mlp",
    )(order, *x_pieces, *cot_pieces, mixed, vectors, *mats)


def close_kernel(plan, many, parts, order, *refs):
    xs, refs = refs[:many], refs[many:]
    d_rows, (to_norm, vectors, weight), refs = refs[:parts], refs[parts : parts + 3], refs[parts + 3 :]
    outs, (sums, x, e_low) = refs[: len(plan)], refs[len(plan) :]
    step = pl.program_id(0)

    @pl.when(step == 0)
    def _():
        sums[...] = jnp.zeros_like(sums)

    for at, (piece, _, _) in enumerate(plan):

        @pl.when(step == at)
        def _():
            x[...] = xs[piece][...]

    model = x.shape[1]
    n, scale = normed(x[...].astype(F32))
    width = d_rows[0].shape[1] // 3
    rows = jnp.concatenate([d[:, i * width : (i + 1) * width] for i in range(3) for d in d_rows], axis=1)
    d_h = dot(rows, weight[...].reshape(model, 3 * width * parts), NT)
    sums[1:2, :] += jnp.sum(d_h, axis=0, keepdims=True)
    sums[0:1, :] += jnp.sum(d_h * n, axis=0, keepdims=True)
    e = d_h * vectors[0:1, :] + to_norm[...]
    e = e - jnp.mean(e, axis=-1, keepdims=True) - n * jnp.mean(e * n, axis=-1, keepdims=True)
    e_low[...] = (e * scale).astype(LOW)
    for at in range(len(plan)):

        @pl.when(step == at)
        def _():
            outs[at][...] = e_low[...]


def call_close(order, pieces, plan, d_rows, to_norm, vectors, weight, span):
    model = pieces[0].shape[1]
    width3 = sum(d.shape[1] for d in d_rows)
    per = span // BLOCK
    steps = len(plan)

    def pick(values, i):
        value = jnp.int32(values[-1])
        for at in range(len(values) - 1):
            value = jnp.where(i == at, jnp.int32(values[at]), value)
        return value

    def block_of(piece):
        reads = [(at, start // BLOCK) for at, (index, start, _) in enumerate(plan) if index == piece]
        values = [next((b for a, b in reversed(reads) if a <= at), reads[0][1]) for at in range(steps)]
        return lambda i, o: (pick(values, i), 0)

    places = [low // BLOCK for _, _, low in plan]
    here = lambda i, o: (pick(places, i), 0)
    there = lambda i, o: (o[pick(places, i) // per] * per + pick(places, i) % per, 0)
    return pl.pallas_call(
        functools.partial(close_kernel, plan, len(pieces), len(d_rows)),
        grid_spec=pltpu.PrefetchScalarGridSpec(
            num_scalar_prefetch=1,
            grid=(steps,),
            in_specs=[pl.BlockSpec((BLOCK, model), block_of(piece)) for piece in range(len(pieces))]
            + [pl.BlockSpec((BLOCK, d.shape[1]), there) for d in d_rows]
            + [pl.BlockSpec((BLOCK, model), here), whole(vectors.shape), whole(weight.shape[:2] + (width3,))],
            out_specs=[whole((BLOCK, model))] * steps + [whole((8, model))],
            scratch_shapes=[pltpu.VMEM((BLOCK, model), LOW), pltpu.VMEM((BLOCK, model), LOW)],
        ),
        out_shape=[jax.ShapeDtypeStruct((BLOCK, model), LOW)] * steps + [jax.ShapeDtypeStruct((8, model), F32)],
        compiler_params=params("arbitrary"),
        cost_estimate=SHORT,
        name="close",
    )(order, *pieces, *d_rows, to_norm, vectors, weight)


def finish_kernel(halves, base, shift, *refs):
    parts, out = refs[:-1], refs[-1]
    shifts = jnp.sum(shift[...], axis=0, keepdims=True)
    for at in range(2):

        @pl.when(pl.program_id(0) == at)
        def _():
            total = base[...].astype(F32) + shifts
            for part in parts[at::2]:
                total = total + part[...].astype(F32)
            out[...] = total.astype(LOW)


def call_finish(base, shift, low, high):
    rows, model = base.shape
    half = rows // 2
    arrays = [a for pair in zip(low, high) for a in pair]
    return pl.pallas_call(
        functools.partial(finish_kernel, len(low)),
        grid=(2,),
        in_specs=[pl.BlockSpec((half, model), lambda i: (i, 0)), whole(shift.shape)] + [whole((half, model))] * len(arrays),
        out_specs=pl.BlockSpec((half, model), lambda i: (i, 0)),
        out_shape=jax.ShapeDtypeStruct((rows, model), LOW),
        compiler_params=params("arbitrary"),
        cost_estimate=SHORT,
        name="finish",
    )(base, shift, *arrays)


def cut_kernel(count, member, source, *out):
    shard = out[0].shape[0]
    for bit in range(count):
        out[bit][...] = source[pl.ds(pl.multiple_of((member[0] ^ bit) * shard, shard), shard), :]
    low = count * shard
    for ref in out[count:]:
        ref[...] = source[low : low + ref.shape[0], :].astype(ref.dtype)
        low += ref.shape[0]


def call_cut(member, source, count, shard, rest):
    columns = source.shape[1]
    shapes = [jax.ShapeDtypeStruct((shard, columns), LOW)] * count
    shapes += [jax.ShapeDtypeStruct((rows, columns), kind) for rows, kind in rest]
    return pl.pallas_call(
        functools.partial(cut_kernel, count),
        grid_spec=pltpu.PrefetchScalarGridSpec(
            num_scalar_prefetch=1,
            grid=(1,),
            in_specs=[whole(source.shape)],
            out_specs=[whole(a.shape) for a in shapes],
        ),
        out_shape=shapes,
        compiler_params=params("arbitrary"),
        cost_estimate=SHORT,
        name="cut",
    )(member, source)


def join_kernel(places, stride, member, *refs):
    *pieces, out = refs
    for bit, piece in enumerate(pieces):
        for block, place in enumerate(places):
            start = pl.multiple_of(place + (member[0] ^ bit) * stride, 128)
            out[:, pl.ds(start, 128)] = piece[:, block * 128 : (block + 1) * 128].astype(F32)


def call_join(member, pieces, places, stride):
    shard, columns = pieces[0].shape
    shape = (shard, columns * len(pieces))
    return pl.pallas_call(
        functools.partial(join_kernel, tuple(places), stride),
        grid_spec=pltpu.PrefetchScalarGridSpec(
            num_scalar_prefetch=1,
            grid=(1,),
            in_specs=[whole(p.shape) for p in pieces],
            out_specs=whole(shape),
        ),
        out_shape=jax.ShapeDtypeStruct(shape, F32),
        compiler_params=params("arbitrary"),
        cost_estimate=SHORT,
        name="join",
    )(member, *pieces)


def bundle_kernel(members, halves, member, two, *refs):
    *ones, out = refs
    thirds, ones = ones[:halves], ones[halves:]
    out[...] = jnp.zeros_like(out)
    out[0:2, :] = functools.reduce(lambda a, b: a + b, [one[0:2, :] for one in ones])
    out[2:3, :] = two[2:3, :]
    out[3:4, :] = two[1:2, :]
    out[4:5, :] = two[3:4, :]
    model = out.shape[1]
    width = model // members
    size = width // halves
    for half, third in enumerate(thirds):
        lanes = pl.ds(pl.multiple_of(member[0] * width + half * size, 128), size)
        for part in range(3):
            out[5 + part : 6 + part, lanes] = third[0:1, part * size : (part + 1) * size]
    per = model // (128 * members)
    for group in range(two.shape[1] // 128):
        start = pl.multiple_of((group % per * members + member[0]) * 128, 128)
        row = 8 + group // per
        out[row : row + 1, pl.ds(start, 128)] = two[0:1, group * 128 : (group + 1) * 128]


def call_bundle(member, members, two, thirds, ones):
    shape = (16, two.shape[1])
    return pl.pallas_call(
        functools.partial(bundle_kernel, members, len(thirds)),
        grid_spec=pltpu.PrefetchScalarGridSpec(
            num_scalar_prefetch=1,
            grid=(1,),
            in_specs=[whole(a.shape) for a in (two, *thirds, *ones)],
            out_specs=whole(shape),
        ),
        out_shape=jax.ShapeDtypeStruct(shape, F32),
        compiler_params=params("arbitrary"),
        cost_estimate=SHORT,
        name="bundle",
    )(member, two, *thirds, *ones)


def across(array, bit):
    size = lax.axis_size("fsdp")
    return lax.ppermute(array, "fsdp", [(i, i ^ bit) for i in range(size)])


def exchange(pieces):
    size = lax.axis_size("fsdp")
    if size != 4:
        return lax.all_to_all(pieces, "fsdp", split_axis=0, concat_axis=0, tiled=True)
    member = lax.axis_index("fsdp")
    out = pieces
    for bit in range(1, size):
        mine = lax.dynamic_index_in_dim(pieces, member ^ bit, 0, keepdims=False)
        out = lax.dynamic_update_index_in_dim(out, across(mine, bit), member ^ bit, 0)
    return out


def behind(array, *others):
    return lax.optimization_barrier((array, *others))[0]


def behind_all(arrays, *others):
    return tuple(behind(array, *others) for array in arrays)


def gather_rows(rows, near, *others):
    if lax.axis_size("fsdp") != 4:
        return [lax.all_gather(rows, "fsdp", axis=0, tiled=True)]
    half = rows.shape[0] // 2
    one, two = near
    low_half = across(behind(one, *others)[:half], 2)
    high_half = across(behind(two, *others)[half:], 1)
    return [rows, one, two, low_half, high_half]


def reduce_begin(parts):
    if len(parts) == 1:
        return ()
    _, _, one_low, _, _, two_high, three_low, three_high = parts
    return across(three_low, 1), across(three_high, 2), across(one_low, 1), across(two_high, 2)


def reduce_middle(parts, begun):
    if len(parts) == 1:
        return ()
    add = lambda a, b: (a.astype(F32) + b.astype(F32)).astype(LOW)
    return add(parts[3], begun[1]), add(parts[4], begun[0])


def reduce_end(base, shift, parts, begun, middle):
    if len(parts) == 1:
        total = lax.psum_scatter(parts[0], "fsdp", scatter_dimension=0, tiled=True).astype(F32)
        return (base.astype(F32) + total + jnp.sum(shift, axis=0, keepdims=True)).astype(LOW)
    one_high, two_low = across(middle[0], 1), across(middle[1], 2)
    return call_finish(base, shift, (parts[0], begun[2], two_low), (parts[1], one_high, begun[3]))


def total_over_all(vector, between=()):
    count = lax.axis_size("dp") * lax.axis_size("fsdp")
    step = 1
    while step < count:
        radix = 4 if count // step >= 4 else 2
        far = [lax.ppermute(vector, ALL, [(i, i ^ (step * k)) for i in range(count)]) for k in range(1, radix)]
        for other in far:
            vector = vector + other
        if step == 1 and between:
            vector = behind(vector, *between)
        step *= radix
    return vector


def swap_owner(array, back):
    groups, members = lax.axis_size("dp"), lax.axis_size("fsdp")
    pairs = [(m * groups + g, g * members + m) for g in range(groups) for m in range(members)]
    if back:
        pairs = [(b, a) for a, b in pairs]
    return lax.ppermute(array, ALL, pairs)


def gather_dp(array):
    return lax.all_gather(array, "dp", axis=0)


def scatter_dp(array):
    return lax.psum_scatter(array, "dp", scatter_dimension=0, tiled=True)


def rotary_tables(length):
    half = ROT // 2
    frequency = (np.float32(10000.0) ** (-(np.arange(half, dtype=np.float32) * np.float32(2.0)) / np.float32(ROT))).astype(np.float32)
    angles = (np.arange(length, dtype=np.float32)[:, None] * frequency[None, :]).astype(np.float32)
    cosine = np.cos(angles).astype(np.float32)
    sine = np.sin(angles).astype(np.float32)
    cos_row = np.ones((length, 128), np.float32)
    ahead = np.zeros((length, 128), np.float32)
    behind = np.zeros((length, 128), np.float32)
    for start in range(0, 128, HEAD):
        cos_row[:, start : start + half] = cosine
        cos_row[:, start + half : start + ROT] = cosine
        ahead[:, start : start + half] = -sine
        behind[:, start + half : start + ROT] = sine
    return tuple(jnp.asarray(t) for t in (cos_row, ahead, behind))


def local(
    tokens, cotangent, doc_ids, norm1_gain, norm1_bias, norm2_gain, norm2_bias, qkv_weight, qkv_bias,
    out_weight, out_bias, up_weight, up_bias, down_weight, down_bias,
):
    groups, members = lax.axis_size("dp"), lax.axis_size("fsdp")
    group, member = lax.axis_index("dp"), lax.axis_index("fsdp")
    devices = groups * members
    rows, model = tokens.shape
    stream = rows * members
    shard = qkv_weight.shape[0]
    width = model // members
    units_dev = up_bias.shape[0]
    units = groups * units_dev
    paired = members == 4 and units_dev == 128 and units == model
    me = member.astype(jnp.int32).reshape(1)
    vectors_in = [norm1_gain, norm1_bias, norm2_gain, norm2_bias, out_bias, down_bias]

    if paired:
        small = small_block(member, members, vectors_in, qkv_bias, up_bias)
        packed = call_pack(me, qkv_weight, up_weight, small, members)
        arrived = [packed[0]] + [across(packed[bit], bit) for bit in range(1, members)]
        x_in = behind(tokens, *arrived[1:])
        cut = 3 * width + 128
        first_in, up_in = call_place(me, arrived, cut)
        w_first = gather_dp(first_in)
        mats = (gather_dp(jnp.concatenate([up_in, down_weight, swap_owner(out_weight, False)], axis=0)),)
        vectors = call_vectors(me, w_first, members, cut)
    else:
        qkv_cut = qkv_weight.reshape(shard, 3, members, width).transpose(2, 0, 1, 3).reshape(members, shard, 3 * width)
        up_cut = up_weight.reshape(shard, groups, members, units_dev).transpose(2, 0, 1, 3).reshape(members, shard, units)
        arrived = exchange(jnp.concatenate([qkv_cut, up_cut], axis=2)).reshape(members * shard, -1)
        w_first = gather_dp(arrived[:, : 3 * width])
        x_in = tokens
        mats = (gather_dp(arrived[:, 3 * width :]), gather_dp(down_weight), gather_dp(swap_owner(out_weight, False)))
        full = [lax.all_gather(a, ALL, axis=0, tiled=True).astype(F32) for a in vectors_in]
        shift = lax.all_gather(qkv_bias, ALL, axis=0, tiled=True).astype(F32).reshape(3, members, width)
        shift = lax.dynamic_index_in_dim(shift, member, 1, keepdims=False)
        up_all = lax.all_gather(up_bias, "dp", axis=0, tiled=True).astype(F32)
        lines = full + [jnp.pad(a, (0, model - a.shape[0])) for a in (up_all, shift[0], shift[1], shift[2])]
        vectors = jnp.pad(jnp.stack(lines), ((0, 6), (0, 0)))

    x_near = (across(x_in, 1), across(x_in, 2)) if members == 4 else ()
    x_pieces = gather_rows(x_in, x_near)
    sources = jnp.arange(members, dtype=jnp.int32)
    order = sources ^ member if members == 4 else sources
    doc_row = doc_ids[0]
    first = jnp.sum((doc_row[None, :] < doc_row[:, None]).astype(jnp.int32), axis=1)
    tables = rotary_tables(stream)

    q, k, v, normal = call_qkv(order, x_pieces, vectors, w_first, tables, rows, width)
    cot_in = behind(cotangent, *x_pieces[1:])
    cot_near = (across(cot_in, 1), across(cot_in, 2)) if members == 4 else ()
    cot_pieces = gather_rows(cot_in, cot_near, q)
    mixed, low_mixed, lse = call_fwd(first, q, k, v)
    half = rows // 2
    out_sizes = [half] * (2 * members) if members == 4 else [stream]
    out_shapes = [jax.ShapeDtypeStruct((size, model), LOW) for size in out_sizes]
    results = call_mlp(order, x_pieces, cot_pieces, low_mixed, vectors, mats, rows, units, out_shapes)
    count = len(out_shapes)
    parts, (d_mixed, to_norm), grads, sums_two = results[:count], results[count : count + 2], results[count + 2 : -1], results[-1]
    scattered = scatter_dp(grads[0].reshape(-1, model)) if paired else None

    begun = reduce_begin(parts)
    halves = 2 if width % 256 == 0 else 1
    back = [call_bwd(first, q, k, v, d_mixed, mixed, lse, tables, normal, 0, halves, ())]
    middle = reduce_middle(parts, behind_all(begun, back[0][0]))
    output = reduce_end(tokens, vectors[4:6, :], parts, begun, middle)
    for part in range(1, halves):
        q = behind(q, *middle)
        back.append(call_bwd(first, q, k, v, d_mixed, mixed, lse, tables, normal, part, halves, (back[-1][1],)))
    d_qkv = [b[0] for b in back]
    g_qkv = back[-1][1]
    sums_qkv = [b[2] for b in back]
    to_norm = behind(to_norm, output)
    if members == 4:
        plan = [(0, 0, 3 * rows), (1, 0, 3 * rows + half)]
        *three, ones_a = call_close(order, x_pieces[3:], plan, d_qkv, to_norm, vectors, w_first, rows)
        if paired:
            to_norm = behind(to_norm, scattered, *three)
        plan = [(1, 0, rows), (2, half, 2 * rows + half), (1, half, rows + half), (2, 0, 2 * rows), (0, 0, 0), (0, half, half)]
        one_low, two_high, one_high, two_low, own_low, own_high, ones_b = call_close(
            order, x_pieces[:3], plan, d_qkv, to_norm, vectors, w_first, rows
        )
        final = [own_low, own_high, one_low, one_high, two_low, two_high, *three]
        ones = [ones_a, ones_b]
    else:
        plan = [(0, low, low) for low in range(0, stream, BLOCK)]
        *final, ones = call_close(order, x_pieces, plan, d_qkv, to_norm, vectors, w_first, rows)
        final, ones = [jnp.concatenate(final, axis=0)], [ones]
    begun = reduce_begin(final)
    middle = reduce_middle(final, begun)
    grad_tokens = reduce_end(cotangent, jnp.zeros((1, model), F32), final, begun, middle)

    if paired:
        g_qkv = scatter_dp(behind(g_qkv, scattered, *three))
        *g_up, g_down, g_out = call_cut(me, scattered, members, shard, [(down_weight.shape[0], F32), (shard, LOW)])
        places = [b * members * units_dev for b in range(groups)]
        g_up = call_join(me, [g_up[0]] + [across(g_up[bit], bit) for bit in range(1, members)], places, units_dev)
        g_out = swap_owner(g_out, True).astype(F32)
        ready = call_bundle(me, members, sums_two, sums_qkv, [behind(ones[0], g_up, g_out)] + ones[1:])
        g_qkv_pieces = g_qkv = call_cut(me, g_qkv, members, shard, [])
        places = [part * model + half * (width // halves) for half in range(halves) for part in range(3)]
        g_qkv = call_join(me, [g_qkv[0]] + [across(g_qkv[bit], bit) for bit in range(1, members)], places, width)
        summed = total_over_all(ready, g_qkv_pieces).reshape(-1)
    else:
        g_up, g_down, g_out = [scatter_dp(g) for g in grads]
        g_qkv = scatter_dp(g_qkv)
        g_down = g_down.astype(F32)
        g_out = swap_owner(g_out, True).astype(F32)
        g_up = exchange(g_up.reshape(members, shard, units))
        g_up = g_up.reshape(members, shard, groups, units_dev).transpose(1, 2, 0, 3).reshape(shard, -1).astype(F32)
        g_qkv = exchange(g_qkv.reshape(members, shard, 3 * width)).reshape(members, shard, halves, 3, width // halves)
        g_qkv = g_qkv.transpose(1, 3, 0, 2, 4).reshape(shard, -1).astype(F32)
        thirds = jnp.concatenate([a[0].reshape(3, 1, width // halves) for a in sums_qkv], axis=2)
        wide_qkv = lax.dynamic_update_index_in_dim(jnp.zeros((3, members, width), F32), thirds, member, 1)
        wide_up = lax.dynamic_update_index_in_dim(
            jnp.zeros((groups, members, units_dev), F32), sums_two[0, :units].reshape(groups, 1, units_dev), member, 1
        )
        ones = sum(ones)
        summed = total_over_all(jnp.concatenate([
            ones[0], ones[1], sums_two[2], sums_two[1], sums_two[3], wide_qkv.reshape(-1), wide_up.reshape(-1),
        ]))
    place = group * members + member
    mine, start = [], 0
    for size in [model] * 5 + [3 * model, groups * members * units_dev]:
        mine.append(lax.dynamic_slice_in_dim(summed, start + place * (size // devices), size // devices))
        start += size
    gain_1, bias_1, gain_2, bias_2, end_bias, qkv_shift, up_shift = mine
    return (
        output, grad_tokens, gain_1, bias_1, gain_2, bias_2, g_qkv, qkv_shift, g_out, end_bias, g_up, up_shift, g_down, end_bias,
    )


def solution(mesh):
    row, vec = P(ALL, None), P(ALL)
    return jax.shard_map(
        local,
        mesh=mesh,
        in_specs=(row, row, P("dp", None), vec, vec, vec, vec, row, vec, row, vec, row, vec, row, vec),
        out_specs=(row, row, vec, vec, vec, vec, row, vec, row, vec, row, vec, row, vec),
        check_vma=False,
    )
```

time: 417 us -> 317 us (0.76)
  blocking collectives: 54 us -> 0 us
  local copies, waits for them, and re-layouts: 49.3 us -> 14.9 us
  waiting for transfers between devices: 89 us -> 54.9 us
  starting transfers between devices: 38.7 us -> 62.8 us
  other arithmetic: 21 us -> 6.94 us
  Pallas kernels: 152 us -> 164 us
    all_gather x1 -> x0, blocking collectives: 54 us -> none  [gather_dp(): return lax.all_gather(array, 'dp', axis=0, tiled=True)]
    ppermute x5 -> x7, waiting for transfers between devices: 33.6 us -> 8.85 us  [total_over_all(): lax.ppermute(vector, ALL, [(i, i ^ step * k) for i in range(count)])]
    ppermute x25 -> x29, starting transfers between devices: 30.4 us -> 51.5 us  [across(): return lax.ppermute(array, 'fsdp', [(i, i ^ bit) for i in range(size)])]
    pallas_call x4 -> x16, Pallas kernels: 127 us -> 143 us  [the longest x2 50.5 us: call_bwd(): pl.pallas_call(functools.partial(bwd_kernel, part * heads, len(before)),...]
    convert_element_type x6 -> x5, other arithmetic: 10.7 us -> 2.48 us  [the longest x4 1.81 us: reduce_middle(): add = lambda a, b: (a.astype(F32) + b.astype(F32)).astype(LOW)]
    slice x13 -> x5, local copies, waits for them, and re-layouts: 11.7 us -> 3.6 us  [the longest x1 1.35 us: local(): output = reduce_end(tokens, vectors[4:6, :], parts, begun, middle)]
    ppermute x25 -> x29, waiting for transfers between devices: 54 us -> 45.9 us  [across(): return lax.ppermute(array, 'fsdp', [(i, i ^ bit) for i in range(size)])]
    concatenate x4 -> x1, local copies, waits for them, and re-layouts: 6.31 us -> 0.08 us  [small_block(): jnp.concatenate([rows, shift.reshape(3, 128), up_bias[None], jnp.zeros((1...]
  transfers between devices with their start and end apart: 39 -> 42, of which waited for: 18 -> 13; matrix products, arithmetic and copies ran while one was open for 14% -> 3% of each run, Pallas kernels for 26% -> 37%
where the time goes in v2:
time: 317 us; the launch traced here: 318 us
  Pallas kernels  164 us (52%)
  starting transfers between devices  62.8 us (20%)
  waiting for transfers between devices  54.9 us (17%)
  local copies, waits for them, and re-layouts  14.9 us (5%)
  between operations  14.2 us (4%)
  other arithmetic  6.94 us (2%)
    ppermute x29, starting transfers between devices, across(): return lax.ppermute(array, 'fsdp', [(i, i ^ bit) for i in range(size)])  51.5 us
    pallas_call x2, Pallas kernels, call_bwd(): pl.pallas_call(functools.partial(bwd_kernel, part * heads, len(before)),...  50.5 us
    ppermute x29, waiting for transfers between devices, across(): return lax.ppermute(array, 'fsdp', [(i, i ^ bit) for i in range(size)])  45.9 us
    pallas_call x1, Pallas kernels, call_mlp(): pl.pallas_call(functools.partial(mlp_kernel, plan, out_plan, count, len(o...  41.3 us
    pallas_call x1, Pallas kernels, call_fwd(): pl.pallas_call(fwd_kernel, grid_spec=pltpu.PrefetchScalarGridSpec(num_sca...  21.1 us
    pallas_call x2, Pallas kernels, call_close(): pl.pallas_call(functools.partial(close_kernel, plan, len(pieces), len(d_r...  18.3 us
    pallas_call x1, Pallas kernels, call_qkv(): pl.pallas_call(functools.partial(qkv_kernel, plan, len(pieces)), grid_spe...  11.9 us
    ppermute x7, waiting for transfers between devices, total_over_all(): lax.ppermute(vector, ALL, [(i, i ^ step * k) for i in range(count)])  8.85 us
  transfers between devices with their start and end apart: 42, of which 13 were waited for; matrix products, arithmetic and copies ran while one was open for 3% of the time, Pallas kernels for 37%

profile of v2, /device:TPU:0, one launch (start us, length us, event | category | flops | bytes accessed | tf_op | source)
XLA Modules:
  0.0 317.7 jit_solution(10193509713232966758)
XLA Ops:
  12.2 2.9 collective-permute-start
  16.6 2.5 collective-permute-done.refs_1_
  19.2 3.7 %collective-permute-done.1.refs_2_ = bf16[32,1920]{1,0:T(8,128)(2,1)S(1)} collective-permute-done((bf16[32,1920]{1,0:T(8,128)(2,1)}, bf16[32,1920]{1,0:T(8,128)(2,1)S(1)}, u32[]{:S(2)}, u32[]{:S(2)}) %collective-permute-start.1) | collective-permute-done | bytes 122912 | tf_op jit(solution)/shard_map/ppermute | solution.py:838
  29.0 6.9 %collective-permute-start.3 = (bf16[512,1024]{1,0:T(8,128)(2,1)S(1)}, bf16[512,1024]{1,0:T(8,128)(2,1)S(1)}, u32[]{:S(2)}, u32[]{:S(2)}) collective-permute-start(bf16[512,1024]{1,0:T(8,128)(2,1)S(1)} %copy-done), channel_id=1, source_target_pairs={{0,1},{1,0},{2,3},{3,2},{4,5},{5,4},{6,7},{7,6},{8,9},{9,8},{10,11... | collective-permute-start | bytes 3145736 | tf_op jit(solution)/shard_map/ppermute | solution.py:838
  35.9 3.9 %collective-permute-start.4 = (bf16[512,1024]{1,0:T(8,128)(2,1)S(1)}, bf16[512,1024]{1,0:T(8,128)(2,1)S(1)}, u32[]{:S(2)}, u32[]{:S(2)}) collective-permute-start(bf16[512,1024]{1,0:T(8,128)(2,1)S(1)} %copy-done), channel_id=1, source_target_pairs={{0,2},{1,3},{2,0},{3,1},{4,6},{5,7},{6,4},{7,5},{8,10},{9,11},{10,... | collective-permute-start | bytes 3145736 | tf_op jit(solution)/shard_map/ppermute | solution.py:838
  39.8 19.0 %collective-permute-done.3.refs_1_ = bf16[512,1024]{1,0:T(8,128)(2,1)S(1)} collective-permute-done((bf16[512,1024]{1,0:T(8,128)(2,1)S(1)}, bf16[512,1024]{1,0:T(8,128)(2,1)S(1)}, u32[]{:S(2)}, u32[]{:S(2)}) %collective-permute-start.3) | collective-permute-done | bytes 1048608 | tf_op jit(solution)/shard_map/ppermute | solution.py:838
  58.9 2.6 collective-permute-start.5
  63.2 9.1 %collective-permute-done.5.refs_3_.refs_0_ = bf16[256,1024]{1,0:T(8,128)(2,1)} collective-permute-done((bf16[256,1024]{1,0:T(8,128)(2,1)S(1)}, bf16[256,1024]{1,0:T(8,128)(2,1)}, u32[]{:S(2)}, u32[]{:S(2)}) %collective-permute-start.5) | collective-permute-done | bytes 524320 | tf_op jit(solution)/shard_map/ppermute | solution.py:838
  77.1 11.9 %qkv.3 = (bf16[2048,256]{1,0:T(8,128)(2,1)}, bf16[2048,256]{1,0:T(8,128)(2,1)}, bf16[2048,256]{1,0:T(8,128)(2,1)}, bf16[2048,1024]{1,0:T(8,128)(2,1)}) custom-call(s32[4]{0:T(128)} %iota_xor_fusion.order, bf16[512,1024]{1,0:T(8,128)(2,1)} %refs_0_.2, bf16[512,1024]{1,0:T(8,128)(2,1)} %copy-done.1, bf16[512,1024]{1,0:T(8,128)(2,1)} %copy-done.2, ...), custom_call_target="tpu_custom_call" | custom-call | tf_op jit(solution)/shard_map/qkv/pallas_call | solution.py:258
  89.0 6.5 %collective-permute-done.8.refs_7_ = bf16[512,1024]{1,0:T(8,128)(2,1)} collective-permute-done((bf16[512,1024]{1,0:T(8,128)(2,1)}, bf16[512,1024]{1,0:T(8,128)(2,1)}, u32[]{:S(2)}, u32[]{:S(2)}) %collective-permute-start.8) | collective-permute-done | bytes 1048608 | tf_op jit(solution)/shard_map/ppermute | solution.py:838
  100.1 21.1 %attend.1 = (f32[2048,256]{1,0:T(8,128)}, bf16[2048,256]{1,0:T(8,128)(2,1)}, f32[4,2048]{1,0:T(4,128)}) custom-call(s32[8]{0:T(128)} %convert_reduce_fusion.first, bf16[2048,256]{1,0:T(8,128)(2,1)} %get-tuple-element.106.q, bf16[2048,256]{1,0:T(8,128)(2,1)} %get-tuple-element.87.k, bf16[2048,256]{1,0:T(8,128)(2,1)} %get-tuple-element.88.v), custom_call_target="tpu_custom_call" | custom-call | tf_op jit(solution)/shard_map/attend/pallas_call | solution.py:351
  122.1 41.3 %mlp.1 = (bf16[256,1024]{1,0:T(8,128)(2,1)}, bf16[256,1024]{1,0:T(8,128)(2,1)}, bf16[256,1024]{1,0:T(8,128)(2,1)}, bf16[256,1024]{1,0:T(8,128)(2,1)}, bf16[256,1...) custom-call(s32[4]{0:T(128)} %iota_xor_fusion.order, ...), custom_call_target="tpu_custom_call" | custom-call | tf_op jit(solution)/shard_map/mlp/pallas_call | solution.py:607
  168.5 25.1 %attend_back.2 = (bf16[2048,384]{1,0:T(8,128)(2,1)}, bf16[1024,384]{1,0:T(8,128)(2,1)}, f32[8,384]{1,0:T(8,128)}) custom-call(s32[8]{0:T(128)} %convert_reduce_fusion.first, bf16[2048,256]{1,0:T(8,128)(2,1)} %get-tuple-element.106.q, bf16[2048,256]{1,0:T(8,128)(2,1)} %get-tuple-element.87.k, bf16[2048,256]{1,0:T(8,128)(2,1)} %get-tuple-element.88.v, ...), custom_call_target="tpu_custom_call" | custom-call | tf_op jit(solution)/shard_map/attend_back/pallas_call | solution.py:461
  198.4 25.4 %attend_back.3 = (bf16[2048,384]{1,0:T(8,128)(2,1)}, bf16[1024,768]{1,0:T(8,128)(2,1)}, f32[8,384]{1,0:T(8,128)}) custom-call(s32[8]{0:T(128)} %convert_reduce_fusion.first, bf16[2048,256]{1,0:T(8,128)(2,1)} %get-tuple-element.106.q, bf16[2048,256]{1,0:T(8,128)(2,1)} %get-tuple-element.87.k, bf16[2048,256]{1,0:T(8,128)(2,1)} %get-tuple-element.88.v, ...), custom_call_target="tpu_custom_call" | custom-call | tf_op jit(solution)/shard_map/attend_back/pallas_call | solution.py:461
  225.2 3.4 %finish.2 = bf16[512,1024]{1,0:T(8,128)(2,1)} custom-call(bf16[512,1024]{1,0:T(8,128)(2,1)} %refs_0_.2, f32[2,1024]{1,0:T(2,128)} %slice.20.shift, bf16[256,1024]{1,0:T(8,128)(2,1)} %get-tuple-element.91.refs_0_, bf16[256,1024]{1,0:T(8,128)(2,1)} %get-tuple-element.92.refs_1_, bf16[256,1024]{1,0:T(8,128)(2,1)} %copy-done.9, bf16[256,1024]{1,0:T(8,128)(2,1)} %copy-done.15, ...), custom_call_target="tpu_custom_call" | custom-call | tf_op jit(solution)/shard_map/finish/pallas_call | solution.py:730
  228.6 6.0 %close.2 = (bf16[256,1024]{1,0:T(8,128)(2,1)}, bf16[256,1024]{1,0:T(8,128)(2,1)}, f32[8,1024]{1,0:T(8,128)}) custom-call(s32[4]{0:T(128)} %iota_xor_fusion.order, bf16[256,1024]{1,0:T(8,128)(2,1)} %collective-permute-done.5.refs_3_.refs_0_, bf16[256,1024]{1,0:T(8,128)(2,1)} %copy-done.3, bf16[2048,384]{1,0:T(8,128)(2,1)} %get-tuple-element.100.refs_2_.refs_3_, ...), custom_call_target="tpu_custom_call" | custom-call | tf_op jit(solution)/shard_map/close/pallas_call | solution.py:695
  242.6 12.3 %close.3 = (bf16[256,1024]{1,0:T(8,128)(2,1)}, bf16[256,1024]{1,0:T(8,128)(2,1)}, bf16[256,1024]{1,0:T(8,128)(2,1)}, bf16[256,1024]{1,0:T(8,128)(2,1)}, bf16[256...) custom-call(s32[4]{0:T(128)} %iota_xor_fusion.order, bf16[512,1024]{1,0:T(8,128)(2,1)} %refs_0_.2, ...), custom_call_target="tpu_custom_call" | custom-call | tf_op jit(solution)/shard_map/close/pallas_call | solution.py:695
  257.2 9.6 %collective-permute-start.22 = (bf16[256,1024]{1,0:T(8,128)(2,1)S(1)}, bf16[256,1024]{1,0:T(8,128)(2,1)S(1)}, u32[]{:S(2)}, u32[]{:S(2)}) collective-permute-start(bf16[256,1024]{1,0:T(8,128)(2,1)S(1)} %add_convert_fusion), channel_id=1, source_target_pairs={{0,2},{1,3},{2,0},{3,1},{4,6},{5,7},{6,4},{7,5},{8,10},{9,11},{10,... | collective-permute-start | bytes 1572872 | tf_op jit(solution)/shard_map/ppermute | solution.py:838
  282.6 3.0 collective-permute-start.32
  285.6 2.4 collective-permute-done.32
  288.7 3.3 %collective-permute-done.33 = f32[16,1024]{1,0:T(8,128)S(1)} collective-permute-done((f32[16,1024]{1,0:T(8,128)S(1)}, f32[16,1024]{1,0:T(8,128)S(1)}, u32[]{:S(2)}, u32[]{:S(2)}) %collective-permute-start.33) | collective-permute-done | bytes 65568 | tf_op jit(solution)/shard_map/ppermute | solution.py:898
  295.5 3.5 %collective-permute-done.18.refs_2_ = bf16[256,1024]{1,0:T(8,128)(2,1)S(1)} collective-permute-done((bf16[256,1024]{1,0:T(8,128)(2,1)}, bf16[256,1024]{1,0:T(8,128)(2,1)S(1)}, u32[]{:S(2)}, u32[]{:S(2)}) %collective-permute-start.18) | collective-permute-done | bytes 524320 | tf_op jit(solution)/shard_map/ppermute | solution.py:838
  299.0 2.7 collective-permute-start.37
  302.5 3.4 %finish.3 = bf16[512,1024]{1,0:T(8,128)(2,1)} custom-call(bf16[512,1024]{1,0:T(8,128)(2,1)} %base.3, f32[1,1024]{1,0:T(1,128)} %broadcast_in_dim.11.shift, bf16[256,1024]{1,0:T(8,128)(2,1)} %get-tuple-element.115.refs_0_, bf16[256,1024]{1,0:T(8,128)(2,1)} %get-tuple-element.116.refs_1_, bf16[256,1024]{1,0:T(8,128)(2,1)} %copy-done.6, ...), custom_call_target="tpu_custom_call" | custom-call | tf_op jit(solution)/shard_map/finish/pallas_call | solution.py:730
  (177 shorter events, 71.7 us)
Async XLA Ops:
  7.2 68.3 %all-gather.5.cloned.1.call-start = ((), (), s32[]{:S(2)}) async-start(), calls=%async_computation.4 | async-start | bytes 2064384 | tf_op jit(solution)/shard_map/all_gather | solution.py:916
  25.4 95.8 %all-gather.7.cloned.1.call-start = ((), (), s32[]{:S(2)}) async-start(), calls=%async_computation.5 | async-start | bytes 5308416 | tf_op jit(solution)/shard_map/all_gather | solution.py:916
  28.9 205.8 %reduce-scatter.3.cloned.1.call-start = ((), (), s32[]{:S(2)}) async-start(), calls=%async_computation.2 | async-start | bytes 5308416 | tf_op jit(solution)/shard_map/reduce_scatter | solution.py:920
  29.0 29.9 %collective-permute-start.3 = (bf16[512,1024]{1,0:T(8,128)(2,1)S(1)}, bf16[512,1024]{1,0:T(8,128)(2,1)S(1)}, u32[]{:S(2)}, u32[]{:S(2)}) collective-permute-start(bf16[512,1024]{1,0:T(8,128)(2,1)S(1)} %copy-done), channel_id=1, source_target_pairs={{0,1},{1,0},{2,3},{3,2},{4,5},{5,4},{6,7},{7,6},{8,9},{9,8},{10,11... | collective-permute-start | bytes 3145736 | tf_op jit(solution)/shard_map/ppermute | solution.py:838
  35.9 25.6 %collective-permute-start.4 = (bf16[512,1024]{1,0:T(8,128)(2,1)S(1)}, bf16[512,1024]{1,0:T(8,128)(2,1)S(1)}, u32[]{:S(2)}, u32[]{:S(2)}) collective-permute-start(bf16[512,1024]{1,0:T(8,128)(2,1)S(1)} %copy-done), channel_id=1, source_target_pairs={{0,2},{1,3},{2,0},{3,1},{4,6},{5,7},{6,4},{7,5},{8,10},{9,11},{10,... | collective-permute-start | bytes 3145736 | tf_op jit(solution)/shard_map/ppermute | solution.py:838
  72.9 22.7 %collective-permute-start.8 = (bf16[512,1024]{1,0:T(8,128)(2,1)}, bf16[512,1024]{1,0:T(8,128)(2,1)}, u32[]{:S(2)}, u32[]{:S(2)}) collective-permute-start(bf16[512,1024]{1,0:T(8,128)(2,1)} %base.3), channel_id=1, source_target_pairs={{0,2},{1,3},{2,0},{3,1},{4,6},{5,7},{6,4},{7,5},{8,10},{9,11},{10,... | collective-permute-start | bytes 3145736 | tf_op jit(solution)/shard_map/ppermute | solution.py:838
  74.0 23.6 %collective-permute-start.7 = (bf16[512,1024]{1,0:T(8,128)(2,1)}, bf16[512,1024]{1,0:T(8,128)(2,1)}, u32[]{:S(2)}, u32[]{:S(2)}) collective-permute-start(bf16[512,1024]{1,0:T(8,128)(2,1)} %base.3), channel_id=1, source_target_pairs={{0,1},{1,0},{2,3},{3,2},{4,5},{5,4},{6,7},{7,6},{8,9},{9,8},{10,11... | collective-permute-start | bytes 3145736 | tf_op jit(solution)/shard_map/ppermute | solution.py:838
  96.7 24.5 %collective-permute-start.10 = (bf16[256,1024]{1,0:T(8,128)(2,1)S(1)}, bf16[256,1024]{1,0:T(8,128)(2,1)S(1)}, u32[]{:S(2)}, u32[]{:S(2)}) collective-permute-start(bf16[256,1024]{1,0:T(8,128)(2,1)S(1)} %slice.19), channel_id=1, source_target_pairs={{0,1},{1,0},{2,3},{3,2},{4,5},{5,4},{6,7},{7,6},{8,9},{9,8},{10,11... | collective-permute-start | bytes 1572872 | tf_op jit(solution)/shard_map/ppermute | solution.py:838
  98.7 22.5 %collective-permute-start.9 = (bf16[256,1024]{1,0:T(8,128)(2,1)S(1)}, bf16[256,1024]{1,0:T(8,128)(2,1)S(1)}, u32[]{:S(2)}, u32[]{:S(2)}) collective-permute-start(bf16[256,1024]{1,0:T(8,128)(2,1)S(1)} %slice.18), channel_id=1, source_target_pairs={{0,2},{1,3},{2,0},{3,1},{4,6},{5,7},{6,4},{7,5},{8,10},{9,11},{10,... | collective-permute-start | bytes 1572872 | tf_op jit(solution)/shard_map/ppermute | solution.py:838
  163.5 116.2 %reduce-scatter.5.cloned.1.call-start = ((), (), s32[]{:S(2)}) async-start(), calls=%async_computation.3 | async-start | bytes 1769472 | tf_op jit(solution)/shard_map/reduce_scatter | solution.py:920
  164.5 29.2 %collective-permute-start.15 = (bf16[256,1024]{1,0:T(8,128)(2,1)S(1)}, bf16[256,1024]{1,0:T(8,128)(2,1)S(1)}, u32[]{:S(2)}, u32[]{:S(2)}) collective-permute-start(bf16[256,1024]{1,0:T(8,128)(2,1)S(1)} %copy-done.31), channel_id=1, source_target_pairs={{0,1},{1,0},{2,3},{3,2},{4,5},{5,4},{6,7},{7,6},{8,9},{9,8},{10,11... | collective-permute-start | bytes 1572872 | tf_op jit(solution)/shard_map/ppermute | solution.py:838
  166.5 28.7 %collective-permute-start.13 = (bf16[256,1024]{1,0:T(8,128)(2,1)}, bf16[256,1024]{1,0:T(8,128)(2,1)S(1)}, u32[]{:S(2)}, u32[]{:S(2)}) collective-permute-start(bf16[256,1024]{1,0:T(8,128)(2,1)} %get-tuple-element.95), channel_id=1, source_target_pairs={{0,2},{1,3},{2,0},{3,1},{4,6},{5,7},{6,4},{7,5},{8,10},{9,11},{10,... | collective-permute-start | bytes 1572872 | tf_op jit(solution)/shard_map/ppermute | solution.py:838
  167.0 56.9 %collective-permute-start.12 = (bf16[256,1024]{1,0:T(8,128)(2,1)}, bf16[256,1024]{1,0:T(8,128)(2,1)S(1)}, u32[]{:S(2)}, u32[]{:S(2)}) collective-permute-start(bf16[256,1024]{1,0:T(8,128)(2,1)} %get-tuple-element.93), channel_id=1, source_target_pairs={{0,1},{1,0},{2,3},{3,2},{4,5},{5,4},{6,7},{7,6},{8,9},{9,8},{10,11... | collective-permute-start | bytes 1572872 | tf_op jit(solution)/shard_map/ppermute | solution.py:838
  167.9 56.0 %collective-permute-start.17 = (bf16[256,1024]{1,0:T(8,128)(2,1)S(1)}, bf16[256,1024]{1,0:T(8,128)(2,1)S(1)}, u32[]{:S(2)}, u32[]{:S(2)}) collective-permute-start(bf16[256,1024]{1,0:T(8,128)(2,1)S(1)} %copy-done.29), channel_id=1, source_target_pairs={{0,2},{1,3},{2,0},{3,1},{4,6},{5,7},{6,4},{7,5},{8,10},{9,11},{10,... | collective-permute-start | bytes 1572872 | tf_op jit(solution)/shard_map/ppermute | solution.py:838
  193.9 30.0 %collective-permute-start.16 = (bf16[256,1024]{1,0:T(8,128)(2,1)S(1)}, bf16[256,1024]{1,0:T(8,128)(2,1)S(1)}, u32[]{:S(2)}, u32[]{:S(2)}) collective-permute-start(bf16[256,1024]{1,0:T(8,128)(2,1)S(1)} %add_convert_fusion.2), channel_id=1, source_target_pairs={{0,2},{1,3},{2,0},{3,1},{4,6},{5,7},{6,4},{7,5},{8,10},{9,11},{10,... | collective-permute-start | bytes 1572872 | tf_op jit(solution)/shard_map/ppermute | solution.py:838
  195.4 28.5 %collective-permute-start.14 = (bf16[256,1024]{1,0:T(8,128)(2,1)S(1)}, bf16[256,1024]{1,0:T(8,128)(2,1)S(1)}, u32[]{:S(2)}, u32[]{:S(2)}) collective-permute-start(bf16[256,1024]{1,0:T(8,128)(2,1)S(1)} %add_convert_fusion.3), channel_id=1, source_target_pairs={{0,1},{1,0},{2,3},{3,2},{4,5},{5,4},{6,7},{7,6},{8,9},{9,8},{10,11... | collective-permute-start | bytes 1572872 | tf_op jit(solution)/shard_map/ppermute | solution.py:838
  235.7 19.2 %collective-permute-start.21 = (bf16[256,1024]{1,0:T(8,128)(2,1)S(1)}, bf16[256,1024]{1,0:T(8,128)(2,1)S(1)}, u32[]{:S(2)}, u32[]{:S(2)}) collective-permute-start(bf16[256,1024]{1,0:T(8,128)(2,1)S(1)} %copy-done.30), channel_id=1, source_target_pairs={{0,1},{1,0},{2,3},{3,2},{4,5},{5,4},{6,7},{7,6},{8,9},{9,8},{10,11... | collective-permute-start | bytes 1572872 | tf_op jit(solution)/shard_map/ppermute | solution.py:838
  236.2 38.7 %collective-permute-start.19 = (bf16[256,1024]{1,0:T(8,128)(2,1)S(1)}, bf16[256,1024]{1,0:T(8,128)(2,1)S(1)}, u32[]{:S(2)}, u32[]{:S(2)}) collective-permute-start(bf16[256,1024]{1,0:T(8,128)(2,1)S(1)} %copy-done.28), channel_id=1, source_target_pairs={{0,2},{1,3},{2,0},{3,1},{4,6},{5,7},{6,4},{7,5},{8,10},{9,11},{10,... | collective-permute-start | bytes 1572872 | tf_op jit(solution)/shard_map/ppermute | solution.py:838
  239.1 28.3 %collective-permute-start.24 = (bf16[32,1024]{1,0:T(8,128)(2,1)}, bf16[32,1024]{1,0:T(8,128)(2,1)S(1)}, u32[]{:S(2)}, u32[]{:S(2)}) collective-permute-start(bf16[32,1024]{1,0:T(8,128)(2,1)} %get-tuple-element.126), channel_id=1, source_target_pairs={{0,1},{1,0},{2,3},{3,2},{4,5},{5,4},{6,7},{7,6},{8,9},{9,8},{10,11... | collective-permute-start | bytes 196616 | tf_op jit(solution)/shard_map/ppermute | solution.py:838
  241.0 26.5 %collective-permute-start.25 = (bf16[32,1024]{1,0:T(8,128)(2,1)}, bf16[32,1024]{1,0:T(8,128)(2,1)S(1)}, u32[]{:S(2)}, u32[]{:S(2)}) collective-permute-start(bf16[32,1024]{1,0:T(8,128)(2,1)} %get-tuple-element.127), channel_id=1, source_target_pairs={{0,2},{1,3},{2,0},{3,1},{4,6},{5,7},{6,4},{7,5},{8,10},{9,11},{10,... | collective-permute-start | bytes 196616 | tf_op jit(solution)/shard_map/ppermute | solution.py:838
  241.7 25.7 %collective-permute-start.26 = (bf16[32,1024]{1,0:T(8,128)(2,1)}, bf16[32,1024]{1,0:T(8,128)(2,1)S(1)}, u32[]{:S(2)}, u32[]{:S(2)}) collective-permute-start(bf16[32,1024]{1,0:T(8,128)(2,1)} %get-tuple-element.128), channel_id=1, source_target_pairs={{0,3},{1,2},{2,1},{3,0},{4,7},{5,6},{6,5},{7,4},{8,11},{9,10},{10,... | collective-permute-start | bytes 196616 | tf_op jit(solution)/shard_map/ppermute | solution.py:838
  257.2 36.0 %collective-permute-start.22 = (bf16[256,1024]{1,0:T(8,128)(2,1)S(1)}, bf16[256,1024]{1,0:T(8,128)(2,1)S(1)}, u32[]{:S(2)}, u32[]{:S(2)}) collective-permute-start(bf16[256,1024]{1,0:T(8,128)(2,1)S(1)} %add_convert_fusion), channel_id=1, source_target_pairs={{0,2},{1,3},{2,0},{3,1},{4,6},{5,7},{6,4},{7,5},{8,10},{9,11},{10,... | collective-permute-start | bytes 1572872 | tf_op jit(solution)/shard_map/ppermute | solution.py:838
  276.6 22.4 %collective-permute-start.18 = (bf16[256,1024]{1,0:T(8,128)(2,1)}, bf16[256,1024]{1,0:T(8,128)(2,1)S(1)}, u32[]{:S(2)}, u32[]{:S(2)}) collective-permute-start(bf16[256,1024]{1,0:T(8,128)(2,1)} %get-tuple-element.117), channel_id=1, source_target_pairs={{0,1},{1,0},{2,3},{3,2},{4,5},{5,4},{6,7},{7,6},{8,9},{9,8},{10,11... | collective-permute-start | bytes 1572872 | tf_op jit(solution)/shard_map/ppermute | solution.py:838
  277.2 24.5 %collective-permute-start.23 = (bf16[256,1024]{1,0:T(8,128)(2,1)}, bf16[256,1024]{1,0:T(8,128)(2,1)S(1)}, u32[]{:S(2)}, u32[]{:S(2)}) collective-permute-start(bf16[256,1024]{1,0:T(8,128)(2,1)} %get-tuple-element.120), channel_id=1, source_target_pairs={{0,2},{1,3},{2,0},{3,1},{4,6},{5,7},{6,4},{7,5},{8,10},{9,11},{10,... | collective-permute-start | bytes 1572872 | tf_op jit(solution)/shard_map/ppermute | solution.py:838
  (52 other events, 327.3 us)
Sparse Core Ops, SparseCore 0:
  25.6 27.1 all-gather.4
  54.4 51.2 all-gather.6
  163.6 57.3 reduce-scatter.2
  234.8 35.3 reduce-scatter.4

commit v3 on v2

--- a/solution.py
+++ b/solution.py
@@ -15,6 +15,7 @@
 EPS = 1e-05
 VMEM = 60 * 1024 * 1024
 ALL = ("dp", "fsdp")
+LONG = pl.CostEstimate(flops=2 * 10**10, bytes_accessed=10**7, transcendentals=0)
 SHORT = pl.CostEstimate(flops=0, bytes_accessed=0, transcendentals=0)
 F32 = jnp.float32
 LOW = jnp.bfloat16
@@ -229,7 +230,7 @@
 
 def qkv_kernel(plan, count, order, *refs):
     pieces, rest = refs[:count], refs[count:]
-    vectors, weight, cosine, sine_a, sine_b, q, k, v, normal, x, sems = rest
+    vectors, weight, turn, q, k, v, normal, x, sems = rest
     step = pl.program_id(0)
     width = q.shape[1]
     span = q.shape[0]
@@ -243,7 +244,7 @@
     n, _ = normed(x[pl.ds(pl.multiple_of(step * span, span), span), :].astype(F32))
     h = (n * vectors[0:1, :] + vectors[1:2, :]).astype(LOW)
     normal[...] = h
-    tables = (cosine[...], sine_a[...], sine_b[...])
+    tables = (turn[:, :128], turn[:, 128:256], turn[:, 256:])
     rows = dot(h, weight[...].reshape(model, 3 * width))
     q[...] = (turned(rows[:, :width] + vectors[7:8, :width], *tables, 1.0) * 0.125).astype(LOW)
     k[...] = turned(rows[:, width : 2 * width] + vectors[8:9, :width], *tables, 1.0).astype(LOW)
@@ -262,7 +263,7 @@
             grid=(rows // span,),
             in_specs=[HBM] * len(pieces)
             + [whole(vectors.shape), whole(weight.shape[:2] + (3 * width,))]
-            + [pl.BlockSpec((span, 128), there)] * 3,
+            + [pl.BlockSpec((span, 384), there)],
             out_specs=[pl.BlockSpec((span, width), there)] * 3 + [pl.BlockSpec((span, model), there)],
             scratch_shapes=[pltpu.VMEM((rows, model), LOW), pltpu.SemaphoreType.DMA((len(plan), 2))],
         ),
@@ -270,7 +271,7 @@
         compiler_params=params("arbitrary"),
         cost_estimate=SHORT,
         name="qkv",
-    )(order, *pieces, vectors, weight, *tables)
+    )(order, *pieces, vectors, weight, tables)
 
 
 def masked_rows(target, array):
@@ -379,20 +380,22 @@
     )(first, q, k, v)
 
 
-def bwd_kernel(
-    low_head, count_before, first, q, k, v, d_mixed, mixed, lse, cosine, sine_a, sine_b, normal, *rest
-):
+def bwd_kernel(low_head, count_before, last, first, q, k, v, d_mixed, mixed, lse, tables, normal, *rest):
     before, rest = rest[:count_before], rest[count_before:]
-    d_rows, grad, sums, keys, values, sum_q, sum_k, sum_v, queries, seeds, h, sem = rest
+    d_rows, rest = rest[0], rest[1:]
+    grads, rest = rest[: 2 if last else 1], rest[2 if last else 1 :]
+    sums, keys, values, sum_q, sum_k, sum_v, queries, seeds, h, turn, sem = rest
     step = pl.program_id(0)
     width = q.shape[1]
     heads = width // HEAD
     stack = heads * BLOCK
     own = pl.ds(pl.multiple_of(step * BLOCK, BLOCK), BLOCK)
-    load = pltpu.make_async_copy(normal, h, sem.at[0])
+    load_turn = pltpu.make_async_copy(tables, turn, sem.at[0])
+    load = pltpu.make_async_copy(normal, h, sem.at[1])
 
     @pl.when(step == 0)
     def _():
+        load_turn.start()
         load.start()
 
     q_own = q[own, :]
@@ -431,44 +434,69 @@
         sum_q[...] += dot(jnp.concatenate(tall_scores, axis=0), key_rows, TN)
 
     over_keys(first, step, tiles)
-    d_rows[own, :width] = (turned(sum_q[...], cosine[own, :], sine_a[own, :], sine_b[own, :], -1.0) * 0.125).astype(LOW)
+
+    @pl.when(step == 0)
+    def _():
+        load_turn.wait()
+
+    def turned_back(array, rows):
+        return turned(array, turn[rows, :128], turn[rows, 128:256], turn[rows, 256:], -1.0)
+
+    d_rows[own, :width] = (turned_back(sum_q[...], own) * 0.125).astype(LOW)
 
     @pl.when(step == pl.num_programs(0) - 1)
     def _():
         def close(at, _):
             rows = pl.ds(pl.multiple_of(at * BLOCK, BLOCK), BLOCK)
-            d_rows[rows, width : 2 * width] = turned(sum_k[rows, :], cosine[rows, :], sine_a[rows, :], sine_b[rows, :], -1.0).astype(LOW)
+            d_rows[rows, width : 2 * width] = turned_back(sum_k[rows, :], rows).astype(LOW)
             d_rows[rows, 2 * width :] = sum_v[rows, :].astype(LOW)
             return 0
 
         lax.fori_loop(0, q.shape[0] // BLOCK, close, 0)
-        low = 0
-        for ref in before:
-            low = ref.shape[1]
-            grad[:, :low] = ref[...]
         load.wait()
-        grad[:, low:] = dot(h[...], d_rows[...], TN).astype(LOW)
         sums[0:1, :] = jnp.sum(d_rows[...].astype(F32), axis=0, keepdims=True)
-
-
-def call_bwd(first, q, k, v, d_mixed, mixed, lse, tables, normal, part, parts, before):
-    model = normal.shape[1]
+        if not last:
+            grads[0][...] = dot(h[...], d_rows[...], TN).astype(LOW)
+        else:
+            group = first[first.shape[0] - 1]
+            per = grads[0].shape[1]
+            own_low = sum(b.shape[1] for b in before)
+            for place in range(2 * grads[0].shape[0]):
+                to = grads[place % 2].at[place // 2]
+                rows = pl.ds(pl.multiple_of((group ^ place) * per, per), per)
+                low = 0
+                for ref in before:
+                    to[:, low : low + ref.shape[1]] = ref[rows, :]
+                    low += ref.shape[1]
+            grad = dot(h[...], d_rows[...], TN).astype(LOW)
+            h[: grad.shape[0], : 3 * width] = grad
+            for place in range(2 * grads[0].shape[0]):
+                rows = pl.ds(pl.multiple_of((group ^ place) * per, per), per)
+                grads[place % 2][place // 2, :, own_low:] = h[rows, : 3 * width]
+
+
+def call_bwd(first, q, k, v, d_mixed, mixed, lse, tables, normal, part, parts, before, groups):
     rows, full = q.shape
     width = full // parts
     heads = width // HEAD
     blocks = rows // BLOCK
+    model = normal.shape[1]
+    last = part == parts - 1
     lanes = pl.BlockSpec((rows, width), lambda i, o: (0, part))
+    if last:
+        grads = [(groups // 2, model // groups, 3 * width * parts)] * 2
+    else:
+        grads = [(model, 3 * width)]
     return pl.pallas_call(
-        functools.partial(bwd_kernel, part * heads, len(before)),
+        functools.partial(bwd_kernel, part * heads, len(before), last),
         grid_spec=pltpu.PrefetchScalarGridSpec(
             num_scalar_prefetch=1,
             grid=(blocks,),
             in_specs=[lanes] * 5
             + [pl.BlockSpec((heads * parts, BLOCK), lambda i, o: (0, i))]
-            + [whole((rows, 128))] * 3
-            + [HBM]
+            + [HBM] * 2
             + [whole(b.shape) for b in before],
-            out_specs=[whole((rows, 3 * width)), whole((model, 3 * width * (part + 1))), whole((8, 3 * width))],
+            out_specs=[whole((rows, 3 * width))] + [whole(g) for g in grads] + [whole((8, 3 * width))],
             scratch_shapes=[
                 pltpu.VMEM((blocks, heads * BLOCK, width), LOW),
                 pltpu.VMEM((blocks, heads * BLOCK, width), LOW),
@@ -478,18 +506,17 @@
                 pltpu.VMEM((heads * BLOCK, width), LOW),
                 pltpu.VMEM((heads * BLOCK, width), LOW),
                 pltpu.VMEM((rows, model), LOW),
-                pltpu.SemaphoreType.DMA((1,)),
+                pltpu.VMEM((rows, tables.shape[1]), F32),
+                pltpu.SemaphoreType.DMA((2,)),
             ],
         ),
-        out_shape=[
-            jax.ShapeDtypeStruct((rows, 3 * width), LOW),
-            jax.ShapeDtypeStruct((model, 3 * width * (part + 1)), LOW),
-            jax.ShapeDtypeStruct((8, 3 * width), F32),
-        ],
+        out_shape=[jax.ShapeDtypeStruct((rows, 3 * width), LOW)]
+        + [jax.ShapeDtypeStruct(g, LOW) for g in grads]
+        + [jax.ShapeDtypeStruct((8, 3 * width), F32)],
         compiler_params=params("arbitrary"),
         cost_estimate=SHORT,
         name="attend_back",
-    )(first, q, k, v, d_mixed, mixed, lse, *tables, normal, *before)
+    )(first, q, k, v, d_mixed, mixed, lse, tables, normal, *before)
 
 
 def mlp_kernel(plan, out_plan, count, out_count, joined, chunk, order, *refs):
@@ -639,10 +666,11 @@
     )(order, *x_pieces, *cot_pieces, mixed, vectors, *mats)
 
 
-def close_kernel(plan, many, parts, order, *refs):
+def close_kernel(plan, many, parts, summed, order, *refs):
     xs, refs = refs[:many], refs[many:]
     d_rows, (to_norm, vectors, weight), refs = refs[:parts], refs[parts : parts + 3], refs[parts + 3 :]
-    outs, (sums, x, e_low) = refs[: len(plan)], refs[len(plan) :]
+    lows, highs, refs = refs[:summed], refs[summed : 2 * summed], refs[2 * summed :]
+    outs, output, (sums, x, e_low) = refs[: len(plan)], refs[len(plan) : -3], refs[-3:]
     step = pl.program_id(0)
 
     @pl.when(step == 0)
@@ -670,9 +698,14 @@
         @pl.when(step == at)
         def _():
             outs[at][...] = e_low[...]
-
-
-def call_close(order, pieces, plan, d_rows, to_norm, vectors, weight, span):
+            if summed:
+                total = x[...].astype(F32) + vectors[4:5, :] + vectors[5:6, :]
+                for ref in highs if at else lows:
+                    total = total + ref[...].astype(F32)
+                output[0][...] = total.astype(LOW)
+
+
+def call_close(order, pieces, plan, d_rows, to_norm, vectors, weight, span, cost=SHORT, low=(), high=()):
     model = pieces[0].shape[1]
     width3 = sum(d.shape[1] for d in d_rows)
     per = span // BLOCK
@@ -693,21 +726,26 @@
     here = lambda i, o: (pick(places, i), 0)
     there = lambda i, o: (o[pick(places, i) // per] * per + pick(places, i) % per, 0)
     return pl.pallas_call(
-        functools.partial(close_kernel, plan, len(pieces), len(d_rows)),
+        functools.partial(close_kernel, plan, len(pieces), len(d_rows), len(low)),
         grid_spec=pltpu.PrefetchScalarGridSpec(
             num_scalar_prefetch=1,
             grid=(steps,),
             in_specs=[pl.BlockSpec((BLOCK, model), block_of(piece)) for piece in range(len(pieces))]
             + [pl.BlockSpec((BLOCK, d.shape[1]), there) for d in d_rows]
-            + [pl.BlockSpec((BLOCK, model), here), whole(vectors.shape), whole(weight.shape[:2] + (width3,))],
-            out_specs=[whole((BLOCK, model))] * steps + [whole((8, model))],
+            + [pl.BlockSpec((BLOCK, model), here), whole(vectors.shape), whole(weight.shape[:2] + (width3,))]
+            + [whole((BLOCK, model))] * (2 * len(low)),
+            out_specs=[whole((BLOCK, model))] * steps
+            + [pl.BlockSpec((BLOCK, model), lambda i, o: (i, 0))] * bool(low)
+            + [whole((8, model))],
             scratch_shapes=[pltpu.VMEM((BLOCK, model), LOW), pltpu.VMEM((BLOCK, model), LOW)],
         ),
-        out_shape=[jax.ShapeDtypeStruct((BLOCK, model), LOW)] * steps + [jax.ShapeDtypeStruct((8, model), F32)],
+        out_shape=[jax.ShapeDtypeStruct((BLOCK, model), LOW)] * steps
+        + [jax.ShapeDtypeStruct((steps * BLOCK, model), LOW)] * bool(low)
+        + [jax.ShapeDtypeStruct((8, model), F32)],
         compiler_params=params("arbitrary"),
-        cost_estimate=SHORT,
+        cost_estimate=cost,
         name="close",
-    )(order, *pieces, *d_rows, to_norm, vectors, weight)
+    )(order, *pieces, *d_rows, to_norm, vectors, weight, *low, *high)
 
 
 def finish_kernel(halves, base, shift, *refs):
@@ -739,55 +777,59 @@
     )(base, shift, *arrays)
 
 
-def cut_kernel(count, member, source, *out):
-    shard = out[0].shape[0]
-    for bit in range(count):
-        out[bit][...] = source[pl.ds(pl.multiple_of((member[0] ^ bit) * shard, shard), shard), :]
-    low = count * shard
-    for ref in out[count:]:
-        ref[...] = source[low : low + ref.shape[0], :].astype(ref.dtype)
-        low += ref.shape[0]
-
-
-def call_cut(member, source, count, shard, rest):
-    columns = source.shape[1]
-    shapes = [jax.ShapeDtypeStruct((shard, columns), LOW)] * count
-    shapes += [jax.ShapeDtypeStruct((rows, columns), kind) for rows, kind in rest]
+def cut_kernel(members, member, first, second, *out):
+    pieces, (down, last) = out[:members], out[members:]
+    shard = last.shape[0]
+    columns = first.shape[1]
+    for bit, piece in enumerate(pieces):
+        rows = pl.ds(pl.multiple_of((member[0] ^ bit) * shard, shard), shard)
+        piece[:, :columns] = first[rows, :]
+        piece[:, columns:] = second[rows, :]
+    low = members * shard
+    down[...] = first[low : low + down.shape[0], :].astype(F32)
+    last[...] = first[low + down.shape[0] :, :]
+
+
+def call_cut(member, first, second, members, shard):
+    columns = first.shape[1]
+    shapes = [jax.ShapeDtypeStruct((shard, columns + second.shape[1]), LOW)] * members + [
+        jax.ShapeDtypeStruct((first.shape[0] - (members + 1) * shard, columns), F32),
+        jax.ShapeDtypeStruct((shard, columns), LOW),
+    ]
     return pl.pallas_call(
-        functools.partial(cut_kernel, count),
+        functools.partial(cut_kernel, members),
         grid_spec=pltpu.PrefetchScalarGridSpec(
             num_scalar_prefetch=1,
             grid=(1,),
-            in_specs=[whole(source.shape)],
+            in_specs=[whole(first.shape), whole(second.shape)],
             out_specs=[whole(a.shape) for a in shapes],
         ),
         out_shape=shapes,
         compiler_params=params("arbitrary"),
         cost_estimate=SHORT,
         name="cut",
-    )(member, source)
-
-
-def join_kernel(places, stride, member, *refs):
-    *pieces, out = refs
+    )(member, first, second)
+
+
+def join_kernel(places, member, *refs):
+    pieces, outs = refs[:-2], refs[-2:]
     for bit, piece in enumerate(pieces):
-        for block, place in enumerate(places):
-            start = pl.multiple_of(place + (member[0] ^ bit) * stride, 128)
-            out[:, pl.ds(start, 128)] = piece[:, block * 128 : (block + 1) * 128].astype(F32)
-
-
-def call_join(member, pieces, places, stride):
-    shard, columns = pieces[0].shape
-    shape = (shard, columns * len(pieces))
+        for block, (index, column, stride) in enumerate(places):
+            start = pl.multiple_of(column + (member[0] ^ bit) * stride, 128)
+            outs[index][:, pl.ds(start, 128)] = piece[:, block * 128 : (block + 1) * 128].astype(F32)
+
+
+def call_join(member, pieces, places, columns):
+    shard = pieces[0].shape[0]
     return pl.pallas_call(
-        functools.partial(join_kernel, tuple(places), stride),
+        functools.partial(join_kernel, tuple(places)),
         grid_spec=pltpu.PrefetchScalarGridSpec(
             num_scalar_prefetch=1,
             grid=(1,),
             in_specs=[whole(p.shape) for p in pieces],
-            out_specs=whole(shape),
+            out_specs=[whole((shard, c)) for c in columns],
         ),
-        out_shape=jax.ShapeDtypeStruct(shape, F32),
+        out_shape=[jax.ShapeDtypeStruct((shard, c), F32) for c in columns],
         compiler_params=params("arbitrary"),
         cost_estimate=SHORT,
         name="join",
@@ -795,29 +837,33 @@
 
 
 def bundle_kernel(members, halves, member, two, *refs):
-    *ones, out = refs
+    *ones, out, wide = refs
     thirds, ones = ones[:halves], ones[halves:]
+    groups = out.shape[0] // members
     out[...] = jnp.zeros_like(out)
-    out[0:2, :] = functools.reduce(lambda a, b: a + b, [one[0:2, :] for one in ones])
-    out[2:3, :] = two[2:3, :]
-    out[3:4, :] = two[1:2, :]
-    out[4:5, :] = two[3:4, :]
-    model = out.shape[1]
-    width = model // members
-    size = width // halves
-    for half, third in enumerate(thirds):
-        lanes = pl.ds(pl.multiple_of(member[0] * width + half * size, 128), size)
-        for part in range(3):
-            out[5 + part : 6 + part, lanes] = third[0:1, part * size : (part + 1) * size]
-    per = model // (128 * members)
-    for group in range(two.shape[1] // 128):
-        start = pl.multiple_of((group % per * members + member[0]) * 128, 128)
-        row = 8 + group // per
-        out[row : row + 1, pl.ds(start, 128)] = two[0:1, group * 128 : (group + 1) * 128]
-
-
-def call_bundle(member, members, two, thirds, ones):
-    shape = (16, two.shape[1])
+    wide[...] = jnp.zeros_like(wide)
+    one = functools.reduce(lambda a, b: a + b, [one[0:2, :] for one in ones])
+    lines = [one[0:1, :], one[1:2, :], two[2:3, :], two[1:2, :], two[3:4, :]]
+    size = thirds[0].shape[1] // 3
+    per_member = halves * size // 128
+    for part in range(3):
+        for half, third in enumerate(thirds):
+            for at in range(size // 128):
+                row = (part * members + member[0]) * per_member + half * (size // 128) + at
+                low = part * size + at * 128
+                wide[pl.ds(row, 1), :] = third[0:1, low : low + 128]
+    for group in range(groups):
+        lanes = slice(group * 128, (group + 1) * 128)
+        for to in range(members):
+            device = group * members + to
+            for row, line in enumerate(lines):
+                out[device, row : row + 1, :] = line[:, lanes]
+            out[device, 5:8, :] = wide[3 * group : 3 * group + 3, :]
+            out[device, 8:9, :] = jnp.where(member[0] == to, two[0:1, lanes], 0.0)
+
+
+def call_bundle(member, members, groups, two, thirds, ones):
+    shape = (groups * members, 16, 128)
     return pl.pallas_call(
         functools.partial(bundle_kernel, members, len(thirds)),
         grid_spec=pltpu.PrefetchScalarGridSpec(
@@ -825,6 +871,7 @@
             grid=(1,),
             in_specs=[whole(a.shape) for a in (two, *thirds, *ones)],
             out_specs=whole(shape),
+            scratch_shapes=[pltpu.VMEM((3 * groups, 128), F32)],
         ),
         out_shape=jax.ShapeDtypeStruct(shape, F32),
         compiler_params=params("arbitrary"),
@@ -858,14 +905,32 @@
     return tuple(behind(array, *others) for array in arrays)
 
 
-def gather_rows(rows, near, *others):
+def gather_rows(halves, near=None, *others):
     if lax.axis_size("fsdp") != 4:
-        return [lax.all_gather(rows, "fsdp", axis=0, tiled=True)]
-    half = rows.shape[0] // 2
-    one, two = near
-    low_half = across(behind(one, *others)[:half], 2)
-    high_half = across(behind(two, *others)[half:], 1)
-    return [rows, one, two, low_half, high_half]
+        return [lax.all_gather(jnp.concatenate(halves, axis=0), "fsdp", axis=0, tiled=True)]
+    one_low, two_high, one_high, two_low = near
+    return [
+        *halves, one_low, one_high, two_low, two_high,
+        across(behind(one_low, *others), 2), across(behind(two_high, *others), 1),
+    ]
+
+
+def near_rows(halves):
+    low, high = halves
+    return across(low, 1), across(high, 2), across(high, 1), across(low, 2)
+
+
+def hop(array, bit):
+    return lax.ppermute(array, "dp", [(i, i ^ bit) for i in range(lax.axis_size("dp"))])
+
+
+def scatter_relative(even, odd):
+    add = lambda a, b: (a.astype(F32) + b.astype(F32)).astype(LOW)
+    blocks, bit = add(even, hop(odd, 1)), 2
+    while blocks.shape[0] > 1:
+        blocks = add(blocks[0::2], hop(blocks[1::2], bit))
+        bit *= 2
+    return blocks[0]
 
 
 def reduce_begin(parts):
@@ -882,25 +947,21 @@
     return add(parts[3], begun[1]), add(parts[4], begun[0])
 
 
-def reduce_end(base, shift, parts, begun, middle):
+def reduce_last(parts, begun, middle):
     if len(parts) == 1:
-        total = lax.psum_scatter(parts[0], "fsdp", scatter_dimension=0, tiled=True).astype(F32)
-        return (base.astype(F32) + total + jnp.sum(shift, axis=0, keepdims=True)).astype(LOW)
+        total = lax.psum_scatter(parts[0], "fsdp", scatter_dimension=0, tiled=True)
+        half = total.shape[0] // 2
+        return (total[:half],), (total[half:],)
     one_high, two_low = across(middle[0], 1), across(middle[1], 2)
-    return call_finish(base, shift, (parts[0], begun[2], two_low), (parts[1], one_high, begun[3]))
-
-
-def total_over_all(vector, between=()):
+    return (parts[0], begun[2], two_low), (parts[1], one_high, begun[3])
+
+
+def total_over_all(vector):
     count = lax.axis_size("dp") * lax.axis_size("fsdp")
     step = 1
     while step < count:
-        radix = 4 if count // step >= 4 else 2
-        far = [lax.ppermute(vector, ALL, [(i, i ^ (step * k)) for i in range(count)]) for k in range(1, radix)]
-        for other in far:
-            vector = vector + other
-        if step == 1 and between:
-            vector = behind(vector, *between)
-        step *= radix
+        vector = vector + lax.ppermute(vector, ALL, [(i, i ^ step) for i in range(count)])
+        step *= 2
     return vector
 
 
@@ -934,7 +995,7 @@
         cos_row[:, start + half : start + ROT] = cosine
         ahead[:, start : start + half] = -sine
         behind[:, start + half : start + ROT] = sine
-    return tuple(jnp.asarray(t) for t in (cos_row, ahead, behind))
+    return jnp.asarray(np.concatenate([cos_row, ahead, behind], axis=1))
 
 
 def local(
@@ -954,22 +1015,27 @@
     me = member.astype(jnp.int32).reshape(1)
     vectors_in = [norm1_gain, norm1_bias, norm2_gain, norm2_bias, out_bias, down_bias]
 
+    half = rows // 2
+    x_halves = [tokens[:half], tokens[half:]]
+    cot_halves = [cotangent[:half], cotangent[half:]]
     if paired:
         small = small_block(member, members, vectors_in, qkv_bias, up_bias)
         packed = call_pack(me, qkv_weight, up_weight, small, members)
         arrived = [packed[0]] + [across(packed[bit], bit) for bit in range(1, members)]
-        x_in = behind(tokens, *arrived[1:])
+        x_near = near_rows(behind_all(x_halves, *arrived[1:]))
         cut = 3 * width + 128
         first_in, up_in = call_place(me, arrived, cut)
         w_first = gather_dp(first_in)
-        mats = (gather_dp(jnp.concatenate([up_in, down_weight, swap_owner(out_weight, False)], axis=0)),)
+        out_own = swap_owner(behind(out_weight, first_in), False)
+        out_own = behind(out_own, *x_near[:2])
+        mats = (gather_dp(jnp.concatenate([up_in, down_weight, out_own], axis=0)),)
         vectors = call_vectors(me, w_first, members, cut)
     else:
         qkv_cut = qkv_weight.reshape(shard, 3, members, width).transpose(2, 0, 1, 3).reshape(members, shard, 3 * width)
         up_cut = up_weight.reshape(shard, groups, members, units_dev).transpose(2, 0, 1, 3).reshape(members, shard, units)
         arrived = exchange(jnp.concatenate([qkv_cut, up_cut], axis=2)).reshape(members * shard, -1)
         w_first = gather_dp(arrived[:, : 3 * width])
-        x_in = tokens
+        x_near = near_rows(x_halves) if members == 4 else None
         mats = (gather_dp(arrived[:, 3 * width :]), gather_dp(down_weight), gather_dp(swap_owner(out_weight, False)))
         full = [lax.all_gather(a, ALL, axis=0, tiled=True).astype(F32) for a in vectors_in]
         shift = lax.all_gather(qkv_bias, ALL, axis=0, tiled=True).astype(F32).reshape(3, members, width)
@@ -978,72 +1044,76 @@
         lines = full + [jnp.pad(a, (0, model - a.shape[0])) for a in (up_all, shift[0], shift[1], shift[2])]
         vectors = jnp.pad(jnp.stack(lines), ((0, 6), (0, 0)))
 
-    x_near = (across(x_in, 1), across(x_in, 2)) if members == 4 else ()
-    x_pieces = gather_rows(x_in, x_near)
+    x_pieces = gather_rows(x_halves, x_near)
     sources = jnp.arange(members, dtype=jnp.int32)
     order = sources ^ member if members == 4 else sources
     doc_row = doc_ids[0]
     first = jnp.sum((doc_row[None, :] < doc_row[:, None]).astype(jnp.int32), axis=1)
+    first = jnp.concatenate([first, group.astype(jnp.int32).reshape(1)])
     tables = rotary_tables(stream)
 
     q, k, v, normal = call_qkv(order, x_pieces, vectors, w_first, tables, rows, width)
-    cot_in = behind(cotangent, *x_pieces[1:])
-    cot_near = (across(cot_in, 1), across(cot_in, 2)) if members == 4 else ()
-    cot_pieces = gather_rows(cot_in, cot_near, q)
+    cot_near = near_rows(behind_all(cot_halves, *x_pieces[2:])) if members == 4 else None
+    cot_pieces = gather_rows(cot_halves, cot_near, q)
     mixed, low_mixed, lse = call_fwd(first, q, k, v)
-    half = rows // 2
     out_sizes = [half] * (2 * members) if members == 4 else [stream]
     out_shapes = [jax.ShapeDtypeStruct((size, model), LOW) for size in out_sizes]
-    results = call_mlp(order, x_pieces, cot_pieces, low_mixed, vectors, mats, rows, units, out_shapes)
+    results = call_mlp(
+        order, x_pieces, cot_pieces, low_mixed, vectors, mats, rows, units, out_shapes
+    )
     count = len(out_shapes)
     parts, (d_mixed, to_norm), grads, sums_two = results[:count], results[count : count + 2], results[count + 2 : -1], results[-1]
     scattered = scatter_dp(grads[0].reshape(-1, model)) if paired else None
 
     begun = reduce_begin(parts)
     halves = 2 if width % 256 == 0 else 1
-    back = [call_bwd(first, q, k, v, d_mixed, mixed, lse, tables, normal, 0, halves, ())]
+    back = [call_bwd(first, q, k, v, d_mixed, mixed, lse, tables, normal, 0, halves, (), groups)]
     middle = reduce_middle(parts, behind_all(begun, back[0][0]))
-    output = reduce_end(tokens, vectors[4:6, :], parts, begun, middle)
+    summed = reduce_last(parts, begun, middle)
     for part in range(1, halves):
-        q = behind(q, *middle)
-        back.append(call_bwd(first, q, k, v, d_mixed, mixed, lse, tables, normal, part, halves, (back[-1][1],)))
+        q = behind(q, *middle, *begun[2:])
+        back.append(call_bwd(first, q, k, v, d_mixed, mixed, lse, tables, normal, part, halves, (back[-1][1],), groups))
     d_qkv = [b[0] for b in back]
-    g_qkv = back[-1][1]
-    sums_qkv = [b[2] for b in back]
-    to_norm = behind(to_norm, output)
+    even, odd = back[-1][1:3]
+    sums_qkv = [b[-1] for b in back]
+    to_norm = behind(to_norm, *summed[0], *summed[1])
     if members == 4:
-        plan = [(0, 0, 3 * rows), (1, 0, 3 * rows + half)]
-        *three, ones_a = call_close(order, x_pieces[3:], plan, d_qkv, to_norm, vectors, w_first, rows)
-        if paired:
-            to_norm = behind(to_norm, scattered, *three)
-        plan = [(1, 0, rows), (2, half, 2 * rows + half), (1, half, rows + half), (2, 0, 2 * rows), (0, 0, 0), (0, half, half)]
-        one_low, two_high, one_high, two_low, own_low, own_high, ones_b = call_close(
-            order, x_pieces[:3], plan, d_qkv, to_norm, vectors, w_first, rows
+        close = lambda pieces, cost=SHORT, low=(), high=(): call_close(
+            order, [x_pieces[p] for p in pieces], [(i, 0, p * half) for i, p in enumerate(pieces)],
+            d_qkv, to_norm, vectors, w_first, rows, cost, low, high,
         )
+        *three, ones_a = close((6, 7), LONG)
+        to_norm = behind(to_norm, *three, *(() if scattered is None else (scattered,)))
+        one_low, two_high, one_high, two_low, ones_b = close((2, 5, 3, 4))
+        to_norm = behind(to_norm, one_low)
+        own_low, own_high, output, ones_c = close((0, 1), SHORT, *summed)
         final = [own_low, own_high, one_low, one_high, two_low, two_high, *three]
-        ones = [ones_a, ones_b]
+        ones = [ones_a, ones_b, ones_c]
     else:
         plan = [(0, low, low) for low in range(0, stream, BLOCK)]
         *final, ones = call_close(order, x_pieces, plan, d_qkv, to_norm, vectors, w_first, rows)
         final, ones = [jnp.concatenate(final, axis=0)], [ones]
+        output = call_finish(tokens, vectors[4:6, :], *summed)
     begun = reduce_begin(final)
     middle = reduce_middle(final, begun)
-    grad_tokens = reduce_end(cotangent, jnp.zeros((1, model), F32), final, begun, middle)
-
+    grad_tokens = call_finish(cotangent, jnp.zeros((1, model), F32), *reduce_last(final, begun, middle))
+
+    g_qkv = scatter_relative(behind(even, *final[2:4]) if members == 4 else even, odd)
+    place = group * members + member
     if paired:
-        g_qkv = scatter_dp(behind(g_qkv, scattered, *three))
-        *g_up, g_down, g_out = call_cut(me, scattered, members, shard, [(down_weight.shape[0], F32), (shard, LOW)])
-        places = [b * members * units_dev for b in range(groups)]
-        g_up = call_join(me, [g_up[0]] + [across(g_up[bit], bit) for bit in range(1, members)], places, units_dev)
-        g_out = swap_owner(g_out, True).astype(F32)
-        ready = call_bundle(me, members, sums_two, sums_qkv, [behind(ones[0], g_up, g_out)] + ones[1:])
-        g_qkv_pieces = g_qkv = call_cut(me, g_qkv, members, shard, [])
-        places = [part * model + half * (width // halves) for half in range(halves) for part in range(3)]
-        g_qkv = call_join(me, [g_qkv[0]] + [across(g_qkv[bit], bit) for bit in range(1, members)], places, width)
-        summed = total_over_all(ready, g_qkv_pieces).reshape(-1)
+        *mixed_pieces, g_down, g_out = call_cut(me, scattered, g_qkv, members, shard)
+        places = [(0, b * members * units_dev, units_dev) for b in range(groups)]
+        places += [(1, part * model + half * (width // halves), width) for half in range(halves) for part in range(3)]
+        arrived = [mixed_pieces[0]] + [across(mixed_pieces[bit], bit) for bit in range(1, members)]
+        g_up, g_qkv = call_join(me, arrived, places, (up_weight.shape[1], qkv_weight.shape[1]))
+        ready = behind(call_bundle(me, members, groups, sums_two, sums_qkv, ones), *middle, *begun[2:])
+        totals = jnp.sum(lax.all_to_all(ready, ALL, split_axis=0, concat_axis=0), axis=0)
+        g_out = swap_owner(behind(g_out, totals), True).astype(F32)
+        size = model // devices
+        mine = [a[0] for a in jnp.split(lax.dynamic_slice_in_dim(totals[:5], member * size, size, 1), 5)]
+        mine += [lax.dynamic_slice_in_dim(totals[5:8].reshape(-1), member * 3 * size, 3 * size), totals[8]]
     else:
         g_up, g_down, g_out = [scatter_dp(g) for g in grads]
-        g_qkv = scatter_dp(g_qkv)
         g_down = g_down.astype(F32)
         g_out = swap_owner(g_out, True).astype(F32)
         g_up = exchange(g_up.reshape(members, shard, units))
@@ -1059,11 +1129,10 @@
         summed = total_over_all(jnp.concatenate([
             ones[0], ones[1], sums_two[2], sums_two[1], sums_two[3], wide_qkv.reshape(-1), wide_up.reshape(-1),
         ]))
-    place = group * members + member
-    mine, start = [], 0
-    for size in [model] * 5 + [3 * model, groups * members * units_dev]:
-        mine.append(lax.dynamic_slice_in_dim(summed, start + place * (size // devices), size // devices))
-        start += size
+        mine, start = [], 0
+        for size in [model] * 5 + [3 * model, groups * members * units_dev]:
+            mine.append(lax.dynamic_slice_in_dim(summed, start + place * (size // devices), size // devices))
+            start += size
     gain_1, bias_1, gain_2, bias_2, end_bias, qkv_shift, up_shift = mine
     return (
         output, grad_tokens, gain_1, bias_1, gain_2, bias_2, g_qkv, qkv_shift, g_out, end_bias, g_up, up_shift, g_down, end_bias,

time: 317 us -> 292 us (0.921); the launches traced: 318 us -> 287 us
  starting transfers between devices: 62.8 us -> 37.7 us
  local copies, waits for them, and re-layouts: 14.9 us -> 11.5 us
  waiting for transfers between devices: 54.9 us -> 51.7 us
    ppermute x29 -> x30, starting transfers between devices: 51.5 us -> 31.6 us  [across(): return lax.ppermute(array, 'fsdp', [(i, i ^ bit) for i in range(size)])]
    ppermute x7 -> x3, starting transfers between devices: 8.38 us -> 2.08 us  [hop(): lax.ppermute(array, 'dp', [(i, i ^ bit) for i in range(lax.axis_size('dp'...]
    pallas_call x2 -> x3, Pallas kernels: 18.3 us -> 23.3 us  [call_close(): pl.pallas_call(functools.partial(close_kernel, plan, len(pieces), len(d_r...]
    pallas_call x2 -> x1, Pallas kernels: 6.86 us -> 3.46 us  [call_finish(): pl.pallas_call(functools.partial(finish_kernel, len(low)), grid=(2,), in_...]
    pallas_call x6 -> x4, Pallas kernels: 57.6 us -> 54.9 us  [the longest x2 50.7 us: call_bwd(): pl.pallas_call(functools.partial(bwd_kernel, part * heads, len(before), l...]
    unnamed x70 -> x85, local copies, waits for them, and re-layouts: 7.19 us -> 5.05 us
    ppermute x7 -> x3, waiting for transfers between devices: 8.85 us -> 6.72 us  [hop(): lax.ppermute(array, 'dp', [(i, i ^ bit) for i in range(lax.axis_size('dp'...]
    ppermute x29 -> x30, waiting for transfers between devices: 45.9 us -> 44.9 us  [across(): return lax.ppermute(array, 'fsdp', [(i, i ^ bit) for i in range(size)])]
  transfers between devices with their start and end apart: 42 -> 39, of which waited for: 13 -> 11; matrix products, arithmetic and copies ran while one was open for 3% -> 4% of each run, Pallas kernels for 37% -> 41%
where the time goes in v3:
time: 292 us; the launch traced here: 287 us
  Pallas kernels  163 us (56%)
  waiting for transfers between devices  51.7 us (18%)
  starting transfers between devices  37.7 us (13%)
  between operations  14.3 us (5%)
  local copies, waits for them, and re-layouts  11.5 us (4%)
  other arithmetic  8.53 us (3%)
    pallas_call x2, Pallas kernels, call_bwd(): pl.pallas_call(functools.partial(bwd_kernel, part * heads, len(before), l...  50.7 us
    ppermute x30, waiting for transfers between devices, across(): return lax.ppermute(array, 'fsdp', [(i, i ^ bit) for i in range(size)])  44.9 us
    pallas_call x1, Pallas kernels, call_mlp(): pl.pallas_call(functools.partial(mlp_kernel, plan, out_plan, count, len(o...  41.5 us
    ppermute x30, starting transfers between devices, across(): return lax.ppermute(array, 'fsdp', [(i, i ^ bit) for i in range(size)])  31.6 us
    pallas_call x3, Pallas kernels, call_close(): pl.pallas_call(functools.partial(close_kernel, plan, len(pieces), len(d_r...  23.3 us
    pallas_call x1, Pallas kernels, call_fwd(): pl.pallas_call(fwd_kernel, grid_spec=pltpu.PrefetchScalarGridSpec(num_sca...  21.1 us
    pallas_call x1, Pallas kernels, call_qkv(): pl.pallas_call(functools.partial(qkv_kernel, plan, len(pieces)), grid_spe...  11.8 us
    ppermute x3, waiting for transfers between devices, hop(): lax.ppermute(array, 'dp', [(i, i ^ bit) for i in range(lax.axis_size('dp'...  6.72 us
  transfers between devices with their start and end apart: 39, of which 11 were waited for; matrix products, arithmetic and copies ran while one was open for 4% of the time, Pallas kernels for 41%

profile of v3, /device:TPU:0, one launch (start us, length us, event | category | flops | bytes accessed | tf_op | source)
XLA Modules:
  0.0 286.8 jit_solution(14074471734288463198)
XLA Ops:
  12.2 2.9 %collective-permute-start = (bf16[32,1920]{1,0:T(8,128)(2,1)}, bf16[32,1920]{1,0:T(8,128)(2,1)S(1)}, u32[]{:S(2)}, u32[]{:S(2)}) collective-permute-start(bf16[32,1920]{1,0:T(8,128)(2,1)} %get-tuple-element.83), channel_id=1, source_target_pairs={{0,1},{1,0},{2,3},{3,2},{4,5},{5,4},{6,7},{7,6},{8,9},{9,8},{10,11... | collective-permute-start | bytes 368648 | tf_op jit(solution)/shard_map/ppermute | solution.py:885
  16.7 2.5 collective-permute-done.refs_1_
  19.2 3.7 %collective-permute-done.1.refs_2_ = bf16[32,1920]{1,0:T(8,128)(2,1)S(1)} collective-permute-done((bf16[32,1920]{1,0:T(8,128)(2,1)}, bf16[32,1920]{1,0:T(8,128)(2,1)S(1)}, u32[]{:S(2)}, u32[]{:S(2)}) %collective-permute-start.1) | collective-permute-done | bytes 122912 | tf_op jit(solution)/shard_map/ppermute | solution.py:885
  28.4 9.4 %collective-permute-done.6.refs_5_.refs_1_ = bf16[256,1024]{1,0:T(8,128)(2,1)S(1)} collective-permute-done((bf16[256,1024]{1,0:T(8,128)(2,1)S(1)}, bf16[256,1024]{1,0:T(8,128)(2,1)S(1)}, u32[]{:S(2)}, u32[]{:S(2)}) %collective-permute-start.6) | collective-permute-done | bytes 524320 | tf_op jit(solution)/shard_map/ppermute | solution.py:885
  39.9 2.4 collective-permute-start.4
  44.4 2.3 fusion.2
  46.7 8.4 %collective-permute-done.4.refs_3_.refs_2_ = bf16[256,1024]{1,0:T(8,128)(2,1)S(1)} collective-permute-done((bf16[256,1024]{1,0:T(8,128)(2,1)S(1)}, bf16[256,1024]{1,0:T(8,128)(2,1)S(1)}, u32[]{:S(2)}, u32[]{:S(2)}) %collective-permute-start.4) | collective-permute-done | bytes 524320 | tf_op jit(solution)/shard_map/ppermute | solution.py:885
  55.1 2.1 collective-permute-done.5.refs_4_.refs_3_
  57.2 8.8 %collective-permute-done.8.refs_7_.refs_1_ = bf16[256,1024]{1,0:T(8,128)(2,1)S(1)} collective-permute-done((bf16[256,1024]{1,0:T(8,128)(2,1)S(1)}, bf16[256,1024]{1,0:T(8,128)(2,1)S(1)}, u32[]{:S(2)}, u32[]{:S(2)}) %collective-permute-start.8) | collective-permute-done | bytes 524320 | tf_op jit(solution)/shard_map/ppermute | solution.py:885
  73.8 11.8 %qkv.3 = (bf16[2048,256]{1,0:T(8,128)(2,1)}, bf16[2048,256]{1,0:T(8,128)(2,1)}, bf16[2048,256]{1,0:T(8,128)(2,1)}, bf16[2048,1024]{1,0:T(8,128)(2,1)}) custom-call(s32[4]{0:T(128)} %iota_xor_fusion.order, bf16[256,1024]{1,0:T(8,128)(2,1)} %copy-done.1, bf16[256,1024]{1,0:T(8,128)(2,1)} %copy-done, bf16[256,1024]{1,0:T(8,128)(2,1)} %copy-done.3, ...), custom_call_target="tpu_custom_call" | custom-call | tf_op jit(solution)/shard_map/qkv/pallas_call | solution.py:259
  87.8 21.1 %attend.1 = (f32[2048,256]{1,0:T(8,128)}, bf16[2048,256]{1,0:T(8,128)(2,1)}, f32[4,2048]{1,0:T(4,128)}) custom-call(s32[9]{0:T(128)} %pad_add_fusion.first, bf16[2048,256]{1,0:T(8,128)(2,1)} %get-tuple-element.114.q, bf16[2048,256]{1,0:T(8,128)(2,1)} %get-tuple-element.91.k, bf16[2048,256]{1,0:T(8,128)(2,1)} %get-tuple-element.92.v), custom_call_target="tpu_custom_call" | custom-call | tf_op jit(solution)/shard_map/attend/pallas_call | solution.py:352
  110.2 41.5 %mlp.1 = (bf16[256,1024]{1,0:T(8,128)(2,1)}, bf16[256,1024]{1,0:T(8,128)(2,1)}, bf16[256,1024]{1,0:T(8,128)(2,1)}, bf16[256,1024]{1,0:T(8,128)(2,1)}, bf16[256,1...) custom-call(s32[4]{0:T(128)} %iota_xor_fusion.order, ...), custom_call_target="tpu_custom_call" | custom-call | tf_op jit(solution)/shard_map/mlp/pallas_call | solution.py:634
  155.9 25.2 %attend_back.2 = (bf16[2048,384]{1,0:T(8,128)(2,1)}, bf16[1024,384]{1,0:T(8,128)(2,1)}, f32[8,384]{1,0:T(8,128)}) custom-call(s32[9]{0:T(128)} %pad_add_fusion.first, bf16[2048,256]{1,0:T(8,128)(2,1)} %get-tuple-element.114.q, bf16[2048,256]{1,0:T(8,128)(2,1)} %get-tuple-element.91.k, bf16[2048,256]{1,0:T(8,128)(2,1)} %get-tuple-element.92.v, ...), custom_call_target="tpu_custom_call" | custom-call | tf_op jit(solution)/shard_map/attend_back/pallas_call | solution.py:490
  185.2 25.5 %attend_back.3 = (bf16[2048,384]{1,0:T(8,128)(2,1)}, bf16[4,128,768]{2,1,0:T(8,128)(2,1)}, bf16[4,128,768]{2,1,0:T(8,128)(2,1)}, f32[8,384]{1,0:T(8,128)}) custom-call(s32[9]{0:T(128)} %pad_add_fusion.first, bf16[2048,256]{1,0:T(8,128)(2,1)} %get-tuple-element.114.q, bf16[2048,256]{1,0:T(8,128)(2,1)} %get-tuple-element.91.k, ...), custom_call_target="tpu_custom_call" | custom-call | tf_op jit(solution)/shard_map/attend_back/pallas_call | solution.py:490
  210.9 6.1 %close.3 = (bf16[256,1024]{1,0:T(8,128)(2,1)}, bf16[256,1024]{1,0:T(8,128)(2,1)}, f32[8,1024]{1,0:T(8,128)}) custom-call(s32[4]{0:T(128)} %iota_xor_fusion.order, bf16[256,1024]{1,0:T(8,128)(2,1)} %copy-done.7, bf16[256,1024]{1,0:T(8,128)(2,1)} %copy-done.6, bf16[2048,384]{1,0:T(8,128)(2,1)} %get-tuple-element.105.refs_2_.refs_4_, ...), custom_call_target="tpu_custom_call" | custom-call | flops 20000000000 | bytes 10000000 | tf_op jit(solution)/shard_map/close/pallas_call | solution.py:728
  218.0 9.4 %close.4 = (bf16[256,1024]{1,0:T(8,128)(2,1)}, bf16[256,1024]{1,0:T(8,128)(2,1)}, bf16[256,1024]{1,0:T(8,128)(2,1)}, bf16[256,1024]{1,0:T(8,128)(2,1)}, f32[8,1024]{1,0:T(8,128)}) custom-call(s32[4]{0:T(128)} %iota_xor_fusion.order, bf16[256,1024]{1,0:T(8,128)(2,1)} %copy-done.3, bf16[256,1024]{1,0:T(8,128)(2,1)} %copy-done.2, bf16[256,1024]{1,0:T(8,128)(2,1)} %copy-done.4, ...), custom_call_target="tpu_custom_call" | custom-call | tf_op jit(solution)/shard_map/close/pallas_call | solution.py:728
  232.2 6.7 %collective-permute-done.29 = bf16[2,128,768]{2,1,0:T(8,128)(2,1)S(1)} collective-permute-done((bf16[2,128,768]{2,1,0:T(8,128)(2,1)S(1)}, bf16[2,128,768]{2,1,0:T(8,128)(2,1)S(1)}, u32[]{:S(2)}, u32[]{:S(2)}) %collective-permute-start.29) | collective-permute-done | bytes 393248 | tf_op jit(solution)/shard_map/ppermute | solution.py:924
  239.6 4.4 %collective-permute-done.23 = bf16[256,1024]{1,0:T(8,128)(2,1)S(1)} collective-permute-done((bf16[256,1024]{1,0:T(8,128)(2,1)S(1)}, bf16[256,1024]{1,0:T(8,128)(2,1)S(1)}, u32[]{:S(2)}, u32[]{:S(2)}) %collective-permute-start.23) | collective-permute-done | bytes 524320 | tf_op jit(solution)/shard_map/ppermute | solution.py:885
  245.7 7.8 %close.5 = (bf16[256,1024]{1,0:T(8,128)(2,1)}, bf16[256,1024]{1,0:T(8,128)(2,1)}, bf16[512,1024]{1,0:T(8,128)(2,1)}, f32[8,1024]{1,0:T(8,128)}) custom-call(s32[4]{0:T(128)} %iota_xor_fusion.order, bf16[256,1024]{1,0:T(8,128)(2,1)} %copy-done.1, bf16[256,1024]{1,0:T(8,128)(2,1)} %copy-done, bf16[2048,384]{1,0:T(8,128)(2,1)} %get-tuple-element.105.refs_2_.refs_4_, ...), custom_call_target="tpu_custom_call" | custom-call | tf_op jit(solution)/shard_map/close/pallas_call | solution.py:728
  255.2 2.6 all-to-all-start
  259.5 2.1 cut.1
  265.1 4.3 %collective-permute-done.26.refs_4_ = bf16[256,1024]{1,0:T(8,128)(2,1)S(1)} collective-permute-done((bf16[256,1024]{1,0:T(8,128)(2,1)S(1)}, bf16[256,1024]{1,0:T(8,128)(2,1)S(1)}, u32[]{:S(2)}, u32[]{:S(2)}) %collective-permute-start.26) | collective-permute-done | bytes 524320 | tf_op jit(solution)/shard_map/ppermute | solution.py:885
  270.4 3.5 %finish.1 = bf16[512,1024]{1,0:T(8,128)(2,1)} custom-call(bf16[512,1024]{1,0:T(8,128)(2,1)} %base.1, f32[1,1024]{1,0:T(1,128)} %broadcast_in_dim.11.shift, bf16[256,1024]{1,0:T(8,128)(2,1)} %get-tuple-element.128.refs_0_, bf16[256,1024]{1,0:T(8,128)(2,1)} %get-tuple-element.129.refs_1_, bf16[256,1024]{1,0:T(8,128)(2,1)} %copy-done.13, ...), custom_call_target="tpu_custom_call" | custom-call | tf_op jit(solution)/shard_map/finish/pallas_call | solution.py:768
  274.6 2.1 join.1
  (187 shorter events, 55.9 us)
Async XLA Ops:
  7.2 65.0 %all-gather.5.cloned.1.call-start = ((), (), s32[]{:S(2)}) async-start(), calls=%async_computation.3 | async-start | bytes 2064384 | tf_op jit(solution)/shard_map/all_gather | solution.py:977
  25.5 83.5 %all-gather.7.cloned.1.call-start = ((), (), s32[]{:S(2)}) async-start(), calls=%async_computation.4 | async-start | bytes 5308416 | tf_op jit(solution)/shard_map/all_gather | solution.py:977
  39.9 178.1 %reduce-scatter.2.cloned.1.call-start = ((), (), s32[]{:S(2)}) async-start(), calls=%async_computation.2 | async-start | bytes 5308416 | tf_op jit(solution)/shard_map/reduce_scatter | solution.py:981
  42.6 23.4 %collective-permute-start.8 = (bf16[256,1024]{1,0:T(8,128)(2,1)S(1)}, bf16[256,1024]{1,0:T(8,128)(2,1)S(1)}, u32[]{:S(2)}, u32[]{:S(2)}) collective-permute-start(bf16[256,1024]{1,0:T(8,128)(2,1)S(1)} %collective-permute-done.6.refs_5_.refs_1_), channel_id=1, source_target_pairs={{0,1},{1,0},{2,3},{3,2},{4,5},{5,4},{6,7},{7,6},{8,9},{9,8},{10,11... | collective-permute-start | bytes 1572872 | tf_op jit(solution)/shard_map/ppermute | solution.py:885
  43.0 23.1 %collective-permute-start.7 = (bf16[256,1024]{1,0:T(8,128)(2,1)S(1)}, bf16[256,1024]{1,0:T(8,128)(2,1)S(1)}, u32[]{:S(2)}, u32[]{:S(2)}) collective-permute-start(bf16[256,1024]{1,0:T(8,128)(2,1)S(1)} %collective-permute-done.3.refs_2_.refs_0_), channel_id=1, source_target_pairs={{0,2},{1,3},{2,0},{3,1},{4,6},{5,7},{6,4},{7,5},{8,10},{9,11},{10,... | collective-permute-start | bytes 1572872 | tf_op jit(solution)/shard_map/ppermute | solution.py:885
  67.6 18.1 %collective-permute-start.12 = (bf16[256,1024]{1,0:T(8,128)(2,1)}, bf16[256,1024]{1,0:T(8,128)(2,1)S(1)}, u32[]{:S(2)}, u32[]{:S(2)}) collective-permute-start(bf16[256,1024]{1,0:T(8,128)(2,1)} %get-tuple-element.94.refs_9_), channel_id=1, source_target_pairs={{0,2},{1,3},{2,0},{3,1},{4,6},{5,7},{6,4},{7,5},{8,10},{9,11},{10,... | collective-permute-start | bytes 1572872 | tf_op jit(solution)/shard_map/ppermute | solution.py:885
  67.7 19.1 %collective-permute-start.9 = (bf16[256,1024]{1,0:T(8,128)(2,1)}, bf16[256,1024]{1,0:T(8,128)(2,1)S(1)}, u32[]{:S(2)}, u32[]{:S(2)}) collective-permute-start(bf16[256,1024]{1,0:T(8,128)(2,1)} %get-tuple-element.93.refs_8_), channel_id=1, source_target_pairs={{0,1},{1,0},{2,3},{3,2},{4,5},{5,4},{6,7},{7,6},{8,9},{9,8},{10,11... | collective-permute-start | bytes 1572872 | tf_op jit(solution)/shard_map/ppermute | solution.py:885
  69.4 39.5 %collective-permute-start.10 = (bf16[256,1024]{1,0:T(8,128)(2,1)}, bf16[256,1024]{1,0:T(8,128)(2,1)S(1)}, u32[]{:S(2)}, u32[]{:S(2)}) collective-permute-start(bf16[256,1024]{1,0:T(8,128)(2,1)} %get-tuple-element.94.refs_9_), channel_id=1, source_target_pairs={{0,1},{1,0},{2,3},{3,2},{4,5},{5,4},{6,7},{7,6},{8,9},{9,8},{10,11... | collective-permute-start | bytes 1572872 | tf_op jit(solution)/shard_map/ppermute | solution.py:885
  70.2 38.7 %collective-permute-start.11 = (bf16[256,1024]{1,0:T(8,128)(2,1)}, bf16[256,1024]{1,0:T(8,128)(2,1)S(1)}, u32[]{:S(2)}, u32[]{:S(2)}) collective-permute-start(bf16[256,1024]{1,0:T(8,128)(2,1)} %get-tuple-element.93.refs_8_), channel_id=1, source_target_pairs={{0,2},{1,3},{2,0},{3,1},{4,6},{5,7},{6,4},{7,5},{8,10},{9,11},{10,... | collective-permute-start | bytes 1572872 | tf_op jit(solution)/shard_map/ppermute | solution.py:885
  85.7 23.2 %collective-permute-start.14 = (bf16[256,1024]{1,0:T(8,128)(2,1)S(1)}, bf16[256,1024]{1,0:T(8,128)(2,1)S(1)}, u32[]{:S(2)}, u32[]{:S(2)}) collective-permute-start(bf16[256,1024]{1,0:T(8,128)(2,1)S(1)} %collective-permute-done.12.refs_13_), channel_id=1, source_target_pairs={{0,1},{1,0},{2,3},{3,2},{4,5},{5,4},{6,7},{7,6},{8,9},{9,8},{10,11... | collective-permute-start | bytes 1572872 | tf_op jit(solution)/shard_map/ppermute | solution.py:885
  86.8 22.2 %collective-permute-start.13 = (bf16[256,1024]{1,0:T(8,128)(2,1)S(1)}, bf16[256,1024]{1,0:T(8,128)(2,1)S(1)}, u32[]{:S(2)}, u32[]{:S(2)}) collective-permute-start(bf16[256,1024]{1,0:T(8,128)(2,1)S(1)} %collective-permute-done.9.refs_10_), channel_id=1, source_target_pairs={{0,2},{1,3},{2,0},{3,1},{4,6},{5,7},{6,4},{7,5},{8,10},{9,11},{10,... | collective-permute-start | bytes 1572872 | tf_op jit(solution)/shard_map/ppermute | solution.py:885
  151.7 29.3 %collective-permute-start.17 = (bf16[256,1024]{1,0:T(8,128)(2,1)}, bf16[256,1024]{1,0:T(8,128)(2,1)S(1)}, u32[]{:S(2)}, u32[]{:S(2)}) collective-permute-start(bf16[256,1024]{1,0:T(8,128)(2,1)} %get-tuple-element.110), channel_id=1, source_target_pairs={{0,1},{1,0},{2,3},{3,2},{4,5},{5,4},{6,7},{7,6},{8,9},{9,8},{10,11... | collective-permute-start | bytes 1572872 | tf_op jit(solution)/shard_map/ppermute | solution.py:885
  152.5 31.4 %collective-permute-start.16 = (bf16[256,1024]{1,0:T(8,128)(2,1)}, bf16[256,1024]{1,0:T(8,128)(2,1)S(1)}, u32[]{:S(2)}, u32[]{:S(2)}) collective-permute-start(bf16[256,1024]{1,0:T(8,128)(2,1)} %get-tuple-element.107), channel_id=1, source_target_pairs={{0,2},{1,3},{2,0},{3,1},{4,6},{5,7},{6,4},{7,5},{8,10},{9,11},{10,... | collective-permute-start | bytes 1572872 | tf_op jit(solution)/shard_map/ppermute | solution.py:885
  154.5 30.7 %collective-permute-start.18 = (bf16[256,1024]{1,0:T(8,128)(2,1)}, bf16[256,1024]{1,0:T(8,128)(2,1)S(1)}, u32[]{:S(2)}, u32[]{:S(2)}) collective-permute-start(bf16[256,1024]{1,0:T(8,128)(2,1)} %get-tuple-element.112), channel_id=1, source_target_pairs={{0,1},{1,0},{2,3},{3,2},{4,5},{5,4},{6,7},{7,6},{8,9},{9,8},{10,11... | collective-permute-start | bytes 1572872 | tf_op jit(solution)/shard_map/ppermute | solution.py:885
  155.5 29.7 %collective-permute-start.19 = (bf16[256,1024]{1,0:T(8,128)(2,1)S(1)}, bf16[256,1024]{1,0:T(8,128)(2,1)S(1)}, u32[]{:S(2)}, u32[]{:S(2)}) collective-permute-start(bf16[256,1024]{1,0:T(8,128)(2,1)S(1)} %copy-done.37), channel_id=1, source_target_pairs={{0,2},{1,3},{2,0},{3,1},{4,6},{5,7},{6,4},{7,5},{8,10},{9,11},{10,... | collective-permute-start | bytes 1572872 | tf_op jit(solution)/shard_map/ppermute | solution.py:885
  182.1 28.8 %collective-permute-start.20 = (bf16[256,1024]{1,0:T(8,128)(2,1)}, bf16[256,1024]{1,0:T(8,128)(2,1)S(1)}, u32[]{:S(2)}, u32[]{:S(2)}) collective-permute-start(bf16[256,1024]{1,0:T(8,128)(2,1)} %add_convert_fusion.3), channel_id=1, source_target_pairs={{0,2},{1,3},{2,0},{3,1},{4,6},{5,7},{6,4},{7,5},{8,10},{9,11},{10,... | collective-permute-start | bytes 1572872 | tf_op jit(solution)/shard_map/ppermute | solution.py:885
  184.1 26.8 %collective-permute-start.21 = (bf16[256,1024]{1,0:T(8,128)(2,1)S(1)}, bf16[256,1024]{1,0:T(8,128)(2,1)S(1)}, u32[]{:S(2)}, u32[]{:S(2)}) collective-permute-start(bf16[256,1024]{1,0:T(8,128)(2,1)S(1)} %add_convert_fusion.4), channel_id=1, source_target_pairs={{0,1},{1,0},{2,3},{3,2},{4,5},{5,4},{6,7},{7,6},{8,9},{9,8},{10,11... | collective-permute-start | bytes 1572872 | tf_op jit(solution)/shard_map/ppermute | solution.py:885
  210.8 16.7 %collective-permute-start.28 = (bf16[4,128,768]{2,1,0:T(8,128)(2,1)}, bf16[4,128,768]{2,1,0:T(8,128)(2,1)S(1)}, u32[]{:S(2)}, u32[]{:S(2)}) collective-permute-start(bf16[4,128,768]{2,1,0:T(8,128)(2,1)} %get-tuple-element.142), channel_id=1, source_target_pairs={{0,4},{4,0},{8,12},{12,8},{16,20},{20,16},{24,28},{28,24},{1,5},{5... | collective-permute-start | bytes 2359304 | tf_op jit(solution)/shard_map/ppermute | solution.py:924
  229.2 26.0 %collective-permute-start.22 = (bf16[256,1024]{1,0:T(8,128)(2,1)}, bf16[256,1024]{1,0:T(8,128)(2,1)S(1)}, u32[]{:S(2)}, u32[]{:S(2)}) collective-permute-start(bf16[256,1024]{1,0:T(8,128)(2,1)} %get-tuple-element.125), channel_id=1, source_target_pairs={{0,1},{1,0},{2,3},{3,2},{4,5},{5,4},{6,7},{7,6},{8,9},{9,8},{10,11... | collective-permute-start | bytes 1572872 | tf_op jit(solution)/shard_map/ppermute | solution.py:885
  229.9 25.3 %collective-permute-start.27 = (bf16[256,1024]{1,0:T(8,128)(2,1)}, bf16[256,1024]{1,0:T(8,128)(2,1)S(1)}, u32[]{:S(2)}, u32[]{:S(2)}) collective-permute-start(bf16[256,1024]{1,0:T(8,128)(2,1)} %get-tuple-element.132), channel_id=1, source_target_pairs={{0,2},{1,3},{2,0},{3,1},{4,6},{5,7},{6,4},{7,5},{8,10},{9,11},{10,... | collective-permute-start | bytes 1572872 | tf_op jit(solution)/shard_map/ppermute | solution.py:885
  232.2 37.2 %collective-permute-start.26 = (bf16[256,1024]{1,0:T(8,128)(2,1)S(1)}, bf16[256,1024]{1,0:T(8,128)(2,1)S(1)}, u32[]{:S(2)}, u32[]{:S(2)}) collective-permute-start(bf16[256,1024]{1,0:T(8,128)(2,1)S(1)} %add_convert_fusion.1), channel_id=1, source_target_pairs={{0,2},{1,3},{2,0},{3,1},{4,6},{5,7},{6,4},{7,5},{8,10},{9,11},{10,... | collective-permute-start | bytes 1572872 | tf_op jit(solution)/shard_map/ppermute | solution.py:885
  239.1 18.7 %collective-permute-start.30 = (bf16[1,128,768]{2,1,0:T(8,128)(2,1)S(1)}, bf16[1,128,768]{2,1,0:T(8,128)(2,1)}, u32[]{:S(2)}, u32[]{:S(2)}) collective-permute-start(bf16[1,128,768]{2,1,0:T(8,128)(2,1)S(1)} %slice.48), channel_id=1, source_target_pairs={{0,16},{4,20},{8,24},{12,28},{16,0},{20,4},{24,8},{28,12},{1,17},{... | collective-permute-start | bytes 589832 | tf_op jit(solution)/shard_map/ppermute | solution.py:924
  245.0 24.4 %collective-permute-start.24 = (bf16[256,1024]{1,0:T(8,128)(2,1)}, bf16[256,1024]{1,0:T(8,128)(2,1)S(1)}, u32[]{:S(2)}, u32[]{:S(2)}) collective-permute-start(bf16[256,1024]{1,0:T(8,128)(2,1)} %add_convert_fusion.2), channel_id=1, source_target_pairs={{0,1},{1,0},{2,3},{3,2},{4,5},{5,4},{6,7},{7,6},{8,9},{9,8},{10,11... | collective-permute-start | bytes 1572872 | tf_op jit(solution)/shard_map/ppermute | solution.py:885
  255.2 21.5 %all-to-all-start = ((f32[32,16,128]{2,1,0:T(8,128)}), f32[32,16,128]{2,1,0:T(8,128)S(1)}, u32[]{:S(2)}, u32[]{:S(2)}) async-start(f32[32,16,128]{2,1,0:T(8,128)} %bundle.1), calls=%async_computation.1 | async-start | bytes 524288 | tf_op jit(solution)/shard_map/all_to_all | solution.py:1110
  (57 other events, 557.5 us)
Sparse Core Ops, SparseCore 0:
  25.6 27.2 all-gather.4
  54.6 51.0 all-gather.6
  151.8 54.4 reduce-scatter.1

commit v4 on v3

--- a/solution.py
+++ b/solution.py
@@ -13,7 +13,6 @@
 ROT = 16
 BLOCK = 256
 EPS = 1e-05
-VMEM = 60 * 1024 * 1024
 ALL = ("dp", "fsdp")
 LONG = pl.CostEstimate(flops=2 * 10**10, bytes_accessed=10**7, transcendentals=0)
 SHORT = pl.CostEstimate(flops=0, bytes_accessed=0, transcendentals=0)
@@ -36,13 +35,14 @@
     return centre * scale, scale
 
 
-def turned(z, cosine, sine_a, sine_b, sign):
+def turned(z, cosine, sine, sign):
     groups = []
     for start in range(0, z.shape[1], 128):
         part = z[:, start : start + 128]
         ahead = pltpu.roll(part, 128 - ROT // 2, 1)
         behind = pltpu.roll(part, ROT // 2, 1)
-        groups.append(part * cosine + sign * (ahead * sine_a + behind * sine_b))
+        lane = lax.broadcasted_iota(jnp.int32, part.shape, 1) & (HEAD - 1)
+        groups.append(part * cosine + sign * (jnp.where(lane < ROT // 2, ahead, behind) * sine))
     return groups[0] if len(groups) == 1 else jnp.concatenate(groups, axis=1)
 
 
@@ -53,7 +53,7 @@
 
 
 def params(*order):
-    return pltpu.CompilerParams(vmem_limit_bytes=VMEM, dimension_semantics=order)
+    return pltpu.CompilerParams(vmem_limit_bytes=60 * 1024 * 1024, dimension_semantics=order)
 
 
 def whole(shape):
@@ -244,7 +244,7 @@
     n, _ = normed(x[pl.ds(pl.multiple_of(step * span, span), span), :].astype(F32))
     h = (n * vectors[0:1, :] + vectors[1:2, :]).astype(LOW)
     normal[...] = h
-    tables = (turn[:, :128], turn[:, 128:256], turn[:, 256:])
+    tables = (turn[:, :128], turn[:, 128:])
     rows = dot(h, weight[...].reshape(model, 3 * width))
     q[...] = (turned(rows[:, :width] + vectors[7:8, :width], *tables, 1.0) * 0.125).astype(LOW)
     k[...] = turned(rows[:, width : 2 * width] + vectors[8:9, :width], *tables, 1.0).astype(LOW)
@@ -263,7 +263,7 @@
             grid=(rows // span,),
             in_specs=[HBM] * len(pieces)
             + [whole(vectors.shape), whole(weight.shape[:2] + (3 * width,))]
-            + [pl.BlockSpec((span, 384), there)],
+            + [pl.BlockSpec((span, 256), there)],
             out_specs=[pl.BlockSpec((span, width), there)] * 3 + [pl.BlockSpec((span, model), there)],
             scratch_shapes=[pltpu.VMEM((rows, model), LOW), pltpu.SemaphoreType.DMA((len(plan), 2))],
         ),
@@ -279,9 +279,9 @@
         target[head * BLOCK : (head + 1) * BLOCK, :] = head_only(array, head)
 
 
-def over_keys(first, step, tiles):
-    begin = first[step]
-    count = step + 1 - begin
+def over_keys(first, block, tiles):
+    begin = first[block]
+    count = block + 1 - begin
 
     def pair(i, _):
         tiles(begin + 2 * i, 2)
@@ -292,7 +292,7 @@
         return 0
 
     lax.fori_loop(0, count // 2, pair, 0)
-    lax.fori_loop(step + 1 - count % 2, step + 1, single, 0)
+    lax.fori_loop(block + 1 - count % 2, block + 1, single, 0)
 
 
 def by_eight(array):
@@ -304,10 +304,9 @@
     width = q.shape[1]
     heads = width // HEAD
     stack = heads * BLOCK
-    own = pl.ds(pl.multiple_of(step * BLOCK, BLOCK), BLOCK)
-    masked_rows(keys.at[step], k[own, :])
-    masked_rows(values.at[step], v[own, :])
-    q_t = q[own, :].T
+    masked_rows(keys.at[step], k[...])
+    masked_rows(values.at[step], v[...])
+    q_t = q[...].T
     top[...] = jnp.full_like(top, -1e30)
     total[...] = jnp.zeros_like(total)
     out[...] = jnp.zeros_like(out)
@@ -354,7 +353,7 @@
         grid_spec=pltpu.PrefetchScalarGridSpec(
             num_scalar_prefetch=1,
             grid=(blocks,),
-            in_specs=[whole((rows, width))] * 3,
+            in_specs=[pl.BlockSpec((BLOCK, width), lambda i, o: (i, 0))] * 3,
             out_specs=[
                 pl.BlockSpec((BLOCK, width), lambda i, o: (i, 0)),
                 pl.BlockSpec((BLOCK, width), lambda i, o: (i, 0)),
@@ -380,38 +379,67 @@
     )(first, q, k, v)
 
 
-def bwd_kernel(low_head, count_before, last, first, q, k, v, d_mixed, mixed, lse, tables, normal, *rest):
-    before, rest = rest[:count_before], rest[count_before:]
-    d_rows, rest = rest[0], rest[1:]
-    grads, rest = rest[: 2 if last else 1], rest[2 if last else 1 :]
-    sums, keys, values, sum_q, sum_k, sum_v, queries, seeds, h, turn, sem = rest
+def closed_rows(x, rows, to_norm, vectors, weight):
+    n, scale = normed(x.astype(F32))
+    d_h = dot(rows, weight, NT)
+    bias = jnp.sum(d_h, axis=0, keepdims=True)
+    gain = jnp.sum(d_h * n, axis=0, keepdims=True)
+    e = d_h * vectors[0:1, :] + to_norm
+    e = e - jnp.mean(e, axis=-1, keepdims=True) - n * jnp.mean(e * n, axis=-1, keepdims=True)
+    return e * scale, gain, bias
+
+
+def bwd_kernel(groups, closing, first, q, k, v, d_mixed, mixed, lse, turn, normal, *rest):
+    if closing:
+        (x_low, x_high, to_norm, vectors, weight), rest = rest[:5], rest[5:]
+    (d_out, even, odd, sums), rest = rest[:4], rest[4:]
+    if closing:
+        (three_low, three_high, ones), rest = rest[:3], rest[3:]
+    keys, values, sum_q, sum_k, sum_v, queries, seeds, h, d_rows, sem = rest[:10]
     step = pl.program_id(0)
-    width = q.shape[1]
+    blocks = pl.num_programs(0)
+    block = blocks - 1 - step
+    rows, width = k.shape
     heads = width // HEAD
     stack = heads * BLOCK
-    own = pl.ds(pl.multiple_of(step * BLOCK, BLOCK), BLOCK)
-    load_turn = pltpu.make_async_copy(tables, turn, sem.at[0])
-    load = pltpu.make_async_copy(normal, h, sem.at[1])
+    own = pl.ds(pl.multiple_of(block * BLOCK, BLOCK), BLOCK)
+    loads = [pltpu.make_async_copy(normal, h, sem.at[0])]
+    if closing:
+        x, carried, mat = rest[10:]
+        half = x_low.shape[0]
+        loads += [
+            pltpu.make_async_copy(x_low, x.at[pl.ds(0, half)], sem.at[1]),
+            pltpu.make_async_copy(x_high, x.at[pl.ds(half, half)], sem.at[2]),
+            pltpu.make_async_copy(to_norm.at[pl.ds(rows - 2 * half, 2 * half)], carried, sem.at[3]),
+            pltpu.make_async_copy(weight.at[:, :, pl.ds(0, 3 * width)], mat, sem.at[4]),
+        ]
 
     @pl.when(step == 0)
     def _():
-        load_turn.start()
-        load.start()
-
-    q_own = q[own, :]
-    s_own = d_mixed[own, :]
-    masked_rows(keys.at[step], k[own, :])
-    masked_rows(values.at[step], v[own, :])
+        for load in loads:
+            load.start()
+
+        def prepare(at, _):
+            here = pl.ds(pl.multiple_of(at * BLOCK, BLOCK), BLOCK)
+            masked_rows(keys.at[at], k[here, :])
+            masked_rows(values.at[at], v[here, :])
+            sum_k[here, :] = jnp.zeros((BLOCK, width), F32)
+            sum_v[here, :] = jnp.zeros((BLOCK, width), F32)
+            return 0
+
+        lax.fori_loop(0, blocks, prepare, 0)
+        sums[...] = jnp.zeros_like(sums)
+
+    q_own = q[...]
+    s_own = d_mixed[...]
     masked_rows(queries, q_own)
     masked_rows(seeds, s_own)
     q_t = q_own.T
     s_t = s_own.T
-    product_t = (s_own.astype(F32) * mixed[own, :]).T
+    product_t = (s_own.astype(F32) * mixed[...]).T
     delta = [jnp.sum(product_t[head * HEAD : (head + 1) * HEAD, :], axis=0, keepdims=True) for head in range(heads)]
-    log_total = [lse[low_head + head : low_head + head + 1, :] for head in range(heads)]
+    log_total = [lse[head : head + 1, :] for head in range(heads)]
     sum_q[...] = jnp.zeros_like(sum_q)
-    sum_k[own, :] = jnp.zeros((BLOCK, width), F32)
-    sum_v[own, :] = jnp.zeros((BLOCK, width), F32)
 
     def tiles(at, count):
         key_rows = keys[pl.ds(at, count)].reshape(count * stack, width)
@@ -428,95 +456,99 @@
             wide_probs.append(jnp.concatenate(low_probs, axis=1))
             wide_scores.append(jnp.concatenate(low_scores, axis=1))
             tall_scores += low_scores
-        rows = pl.ds(pl.multiple_of(at * BLOCK, BLOCK), count * BLOCK)
-        sum_v[rows, :] += dot(jnp.concatenate(wide_probs, axis=0), seeds[...])
-        sum_k[rows, :] += dot(jnp.concatenate(wide_scores, axis=0), queries[...])
+        here = pl.ds(pl.multiple_of(at * BLOCK, BLOCK), count * BLOCK)
+        sum_v[here, :] += dot(jnp.concatenate(wide_probs, axis=0), seeds[...])
+        sum_k[here, :] += dot(jnp.concatenate(wide_scores, axis=0), queries[...])
         sum_q[...] += dot(jnp.concatenate(tall_scores, axis=0), key_rows, TN)
 
-    over_keys(first, step, tiles)
-
-    @pl.when(step == 0)
+    over_keys(first, block, tiles)
+    turns = (turn[:, :128], turn[:, 128:])
+    done = jnp.concatenate(
+        [
+            (turned(sum_q[...], *turns, -1.0) * 0.125).astype(LOW),
+            turned(sum_k[own, :], *turns, -1.0).astype(LOW),
+            sum_v[own, :].astype(LOW),
+        ],
+        axis=1,
+    )
+    d_rows[own, :] = done
+    d_out[...] = done
+    sums[0:1, :] += jnp.sum(done.astype(F32), axis=0, keepdims=True)
+
+    @pl.when(step == blocks - 1)
     def _():
-        load_turn.wait()
-
-    def turned_back(array, rows):
-        return turned(array, turn[rows, :128], turn[rows, 128:256], turn[rows, 256:], -1.0)
-
-    d_rows[own, :width] = (turned_back(sum_q[...], own) * 0.125).astype(LOW)
-
-    @pl.when(step == pl.num_programs(0) - 1)
-    def _():
-        def close(at, _):
-            rows = pl.ds(pl.multiple_of(at * BLOCK, BLOCK), BLOCK)
-            d_rows[rows, width : 2 * width] = turned_back(sum_k[rows, :], rows).astype(LOW)
-            d_rows[rows, 2 * width :] = sum_v[rows, :].astype(LOW)
-            return 0
-
-        lax.fori_loop(0, q.shape[0] // BLOCK, close, 0)
-        load.wait()
-        sums[0:1, :] = jnp.sum(d_rows[...].astype(F32), axis=0, keepdims=True)
-        if not last:
-            grads[0][...] = dot(h[...], d_rows[...], TN).astype(LOW)
-        else:
-            group = first[first.shape[0] - 1]
-            per = grads[0].shape[1]
-            own_low = sum(b.shape[1] for b in before)
-            for place in range(2 * grads[0].shape[0]):
-                to = grads[place % 2].at[place // 2]
-                rows = pl.ds(pl.multiple_of((group ^ place) * per, per), per)
-                low = 0
-                for ref in before:
-                    to[:, low : low + ref.shape[1]] = ref[rows, :]
-                    low += ref.shape[1]
-            grad = dot(h[...], d_rows[...], TN).astype(LOW)
-            h[: grad.shape[0], : 3 * width] = grad
-            for place in range(2 * grads[0].shape[0]):
-                rows = pl.ds(pl.multiple_of((group ^ place) * per, per), per)
-                grads[place % 2][place // 2, :, own_low:] = h[rows, : 3 * width]
-
-
-def call_bwd(first, q, k, v, d_mixed, mixed, lse, tables, normal, part, parts, before, groups):
-    rows, full = q.shape
-    width = full // parts
+        for load in loads:
+            load.wait()
+        if closing:
+            start = pl.multiple_of(first[first.shape[0] - 1] * 2 * half, 2 * half)
+            gain = bias = 0.0
+            for low, out in ((0, three_low), (half, three_high)):
+                e, a, b = closed_rows(
+                    x[low : low + half, :], d_rows[pl.ds(start + low, half), :], carried[low : low + half, :], vectors,
+                    mat[...].reshape(h.shape[1], 3 * width),
+                )
+                out[...] = e.astype(LOW)
+                gain, bias = gain + a, bias + b
+            ones[0:1, :] = gain
+            ones[1:2, :] = bias
+        group = first[first.shape[0] - 2]
+        model = h.shape[1]
+        grad = dot(h[...], d_rows[...], TN).astype(LOW)
+        h[:model, : 3 * width] = grad
+        per = model // groups
+        for place in range(groups):
+            to = odd if place % 2 else even
+            here = pl.ds(pl.multiple_of((group ^ place) * per, per), per)
+            to[place // 2] = h[here, : 3 * width]
+
+
+def call_bwd(first, q, k, v, d_mixed, mixed, lse, tables, normal, groups, closing=()):
+    rows, width = q.shape
     heads = width // HEAD
     blocks = rows // BLOCK
     model = normal.shape[1]
-    last = part == parts - 1
-    lanes = pl.BlockSpec((rows, width), lambda i, o: (0, part))
-    if last:
-        grads = [(groups // 2, model // groups, 3 * width * parts)] * 2
-    else:
-        grads = [(model, 3 * width)]
+    grad = (groups // 2, model // groups, 3 * width)
+    back = lambda i, o: (blocks - 1 - i, 0)
+    blocked = pl.BlockSpec((BLOCK, width), back)
+    outs = [((rows, 3 * width), LOW), (grad, LOW), (grad, LOW), ((8, 3 * width), F32)]
+    scratch = [
+        pltpu.VMEM((blocks, heads * BLOCK, width), LOW),
+        pltpu.VMEM((blocks, heads * BLOCK, width), LOW),
+        pltpu.VMEM((BLOCK, width), F32),
+        pltpu.VMEM((rows, width), F32),
+        pltpu.VMEM((rows, width), F32),
+        pltpu.VMEM((heads * BLOCK, width), LOW),
+        pltpu.VMEM((heads * BLOCK, width), LOW),
+        pltpu.VMEM((rows, model), LOW),
+        pltpu.VMEM((rows, 3 * width), LOW),
+        pltpu.SemaphoreType.DMA((5,)),
+    ]
+    specs = []
+    if closing:
+        half = closing[0].shape[0]
+        outs += [((half, model), LOW)] * 2 + [((8, model), F32)]
+        scratch += [
+            pltpu.VMEM((2 * half, model), LOW),
+            pltpu.VMEM((2 * half, model), F32),
+            pltpu.VMEM(closing[4].shape[:2] + (3 * width,), LOW),
+        ]
+        specs = [HBM] * 3 + [whole(closing[3].shape), HBM]
     return pl.pallas_call(
-        functools.partial(bwd_kernel, part * heads, len(before), last),
+        functools.partial(bwd_kernel, groups, bool(closing)),
         grid_spec=pltpu.PrefetchScalarGridSpec(
             num_scalar_prefetch=1,
             grid=(blocks,),
-            in_specs=[lanes] * 5
-            + [pl.BlockSpec((heads * parts, BLOCK), lambda i, o: (0, i))]
-            + [HBM] * 2
-            + [whole(b.shape) for b in before],
-            out_specs=[whole((rows, 3 * width))] + [whole(g) for g in grads] + [whole((8, 3 * width))],
-            scratch_shapes=[
-                pltpu.VMEM((blocks, heads * BLOCK, width), LOW),
-                pltpu.VMEM((blocks, heads * BLOCK, width), LOW),
-                pltpu.VMEM((BLOCK, width), F32),
-                pltpu.VMEM((rows, width), F32),
-                pltpu.VMEM((rows, width), F32),
-                pltpu.VMEM((heads * BLOCK, width), LOW),
-                pltpu.VMEM((heads * BLOCK, width), LOW),
-                pltpu.VMEM((rows, model), LOW),
-                pltpu.VMEM((rows, tables.shape[1]), F32),
-                pltpu.SemaphoreType.DMA((2,)),
-            ],
+            in_specs=[blocked, whole((rows, width)), whole((rows, width)), blocked, blocked]
+            + [pl.BlockSpec((heads, BLOCK), lambda i, o: (0, blocks - 1 - i)), pl.BlockSpec((BLOCK, 256), back), HBM]
+            + specs,
+            out_specs=[pl.BlockSpec((BLOCK, 3 * width), back)] + [whole(a) for a, _ in outs[1:]],
+            scratch_shapes=scratch,
         ),
-        out_shape=[jax.ShapeDtypeStruct((rows, 3 * width), LOW)]
-        + [jax.ShapeDtypeStruct(g, LOW) for g in grads]
-        + [jax.ShapeDtypeStruct((8, 3 * width), F32)],
+        out_shape=[jax.ShapeDtypeStruct(a, kind) for a, kind in outs],
         compiler_params=params("arbitrary"),
         cost_estimate=SHORT,
         name="attend_back",
-    )(first, q, k, v, d_mixed, mixed, lse, tables, normal, *before)
+    )(first, q, k, v, d_mixed, mixed, lse, tables, normal, *closing)
 
 
 def mlp_kernel(plan, out_plan, count, out_count, joined, chunk, order, *refs):
@@ -525,8 +557,8 @@
     mats, rest = rest[: 1 if joined else 3], rest[1 if joined else 3 :]
     parts, rest = rest[:out_count], rest[out_count:]
     d_mixed, to_norm, rest = rest[0], rest[1], rest[2:]
-    grads, rest = rest[: 1 if joined else 3], rest[1 if joined else 3 :]
-    sums, normal, cot, active, d_up, own_mixed, g_out, staged, x_sems, cot_sems, out_sems = rest
+    grads, rest = rest[: 1 if joined else 2], rest[1 if joined else 2 :]
+    g_out, sums, normal, cot, active, d_up, own_mixed, staged, x_sems, cot_sems, out_sems = rest
     step = pl.program_id(0)
     steps = len(plan)
     span, width = own_mixed.shape[0] // steps, own_mixed.shape[1]
@@ -594,18 +626,15 @@
 
         up_cols = pl.ds(pl.multiple_of(at * (model // many), 128), model // many)
         down_cols = pl.ds(pl.multiple_of(at * (units // many), 128), units // many)
-        out_rows = pl.ds(pl.multiple_of(at * (width // many), 16), width // many)
         up_grad = dot(normal[:, up_cols], d_up[...], TN).astype(LOW)
         down_grad = dot(active[:, down_cols], cot[...], TN).astype(LOW)
         if joined:
             block = grads[0].shape[0]
             grads[0][:, cuts[0] : cuts[1], :] = up_grad.reshape(block, cuts[1], units)
             grads[0][:, cuts[1] : cuts[2], :] = down_grad.reshape(block, cuts[2] - cuts[1], model)
-            grads[0][:, cuts[2] : cuts[3], :] = g_out[out_rows, :].reshape(block, cuts[3] - cuts[2], model)
         else:
             grads[0][...] = up_grad
             grads[1][...] = down_grad
-            grads[2][...] = g_out[out_rows, :]
 
     @pl.when(step == pl.num_programs(0) - 1)
     def _():
@@ -625,10 +654,10 @@
     later = lambda i, o: (jnp.maximum(i - steps, 0), 0)
     if joined:
         groups = mats[0].shape[0]
-        grads = [(groups, (model + units + width) // groups, model)]
+        grads = [(groups, (model + units) // groups, model)]
         grad_specs = [pl.BlockSpec((groups // many,) + grads[0][1:], lambda i, o: (jnp.maximum(i - steps, 0), 0, 0))]
     else:
-        grads = [(model, units), (units, model), (width, model)]
+        grads = [(model, units), (units, model)]
         grad_specs = [pl.BlockSpec((a // many, b), later) for a, b in grads]
     sums = (8, max(model, units))
     return pl.pallas_call(
@@ -642,14 +671,13 @@
             out_specs=[HBM] * len(out_shapes)
             + [pl.BlockSpec((span, width), there), pl.BlockSpec((span, model), here)]
             + grad_specs
-            + [whole(sums)],
+            + [whole((width, model)), whole(sums)],
             scratch_shapes=[
                 pltpu.VMEM((rows, model), LOW),
                 pltpu.VMEM((rows, model), LOW),
                 pltpu.VMEM((rows, units), LOW),
                 pltpu.VMEM((rows, units), LOW),
                 pltpu.VMEM((rows, width), LOW),
-                pltpu.VMEM((width, model), LOW),
                 pltpu.VMEM((rows, model), LOW),
                 pltpu.SemaphoreType.DMA((steps, 2)),
                 pltpu.SemaphoreType.DMA((steps, 2)),
@@ -658,7 +686,7 @@
         ),
         out_shape=list(out_shapes)
         + [jax.ShapeDtypeStruct((rows, width), LOW), jax.ShapeDtypeStruct((rows, model), F32)]
-        + [jax.ShapeDtypeStruct(g, LOW) for g in grads]
+        + [jax.ShapeDtypeStruct(g, LOW) for g in grads + [(width, model)]]
         + [jax.ShapeDtypeStruct(sums, F32)],
         compiler_params=params("arbitrary"),
         cost_estimate=SHORT,
@@ -666,11 +694,13 @@
     )(order, *x_pieces, *cot_pieces, mixed, vectors, *mats)
 
 
-def close_kernel(plan, many, parts, summed, order, *refs):
+def close_kernel(plan, many, parts, summed, joined, merges, order, *refs):
     xs, refs = refs[:many], refs[many:]
     d_rows, (to_norm, vectors, weight), refs = refs[:parts], refs[parts : parts + 3], refs[parts + 3 :]
-    lows, highs, refs = refs[:summed], refs[summed : 2 * summed], refs[2 * summed :]
-    outs, output, (sums, x, e_low) = refs[: len(plan)], refs[len(plan) : -3], refs[-3:]
+    added, refs = refs[:summed], refs[summed:]
+    come, refs = refs[: len(merges)], refs[len(merges) :]
+    count = len(plan) // joined
+    outs, output, (sums, x, e_low) = refs[:count], refs[count:-3], refs[-3:]
     step = pl.program_id(0)
 
     @pl.when(step == 0)
@@ -684,28 +714,28 @@
             x[...] = xs[piece][...]
 
     model = x.shape[1]
-    n, scale = normed(x[...].astype(F32))
-    width = d_rows[0].shape[1] // 3
-    rows = jnp.concatenate([d[:, i * width : (i + 1) * width] for i in range(3) for d in d_rows], axis=1)
-    d_h = dot(rows, weight[...].reshape(model, 3 * width * parts), NT)
-    sums[1:2, :] += jnp.sum(d_h, axis=0, keepdims=True)
-    sums[0:1, :] += jnp.sum(d_h * n, axis=0, keepdims=True)
-    e = d_h * vectors[0:1, :] + to_norm[...]
-    e = e - jnp.mean(e, axis=-1, keepdims=True) - n * jnp.mean(e * n, axis=-1, keepdims=True)
-    e_low[...] = (e * scale).astype(LOW)
+    rows = d_rows[0][...]
+    e, gain, bias = closed_rows(x[...], rows, to_norm[...], vectors, weight[...].reshape(model, rows.shape[1]))
+    sums[0:1, :] += gain
+    sums[1:2, :] += bias
+    e_low[...] = e
     for at in range(len(plan)):
 
         @pl.when(step == at)
         def _():
-            outs[at][...] = e_low[...]
-            if summed:
+            e = e_low[...]
+            if at in merges:
+                e = e + come[merges.index(at)][...].astype(F32)
+            low = at % joined * BLOCK
+            outs[at // joined][low : low + BLOCK, :] = e.astype(LOW)
+            if summed and at >= len(plan) - 2:
                 total = x[...].astype(F32) + vectors[4:5, :] + vectors[5:6, :]
-                for ref in highs if at else lows:
+                for ref in added:
                     total = total + ref[...].astype(F32)
                 output[0][...] = total.astype(LOW)
 
 
-def call_close(order, pieces, plan, d_rows, to_norm, vectors, weight, span, cost=SHORT, low=(), high=()):
+def call_close(order, pieces, plan, d_rows, to_norm, vectors, weight, span, cost=SHORT, added=(), joined=2, merges=(), come=()):
     model = pieces[0].shape[1]
     width3 = sum(d.shape[1] for d in d_rows)
     per = span // BLOCK
@@ -726,89 +756,86 @@
     here = lambda i, o: (pick(places, i), 0)
     there = lambda i, o: (o[pick(places, i) // per] * per + pick(places, i) % per, 0)
     return pl.pallas_call(
-        functools.partial(close_kernel, plan, len(pieces), len(d_rows), len(low)),
+        functools.partial(close_kernel, plan, len(pieces), len(d_rows), len(added), joined, merges),
         grid_spec=pltpu.PrefetchScalarGridSpec(
             num_scalar_prefetch=1,
             grid=(steps,),
             in_specs=[pl.BlockSpec((BLOCK, model), block_of(piece)) for piece in range(len(pieces))]
             + [pl.BlockSpec((BLOCK, d.shape[1]), there) for d in d_rows]
             + [pl.BlockSpec((BLOCK, model), here), whole(vectors.shape), whole(weight.shape[:2] + (width3,))]
-            + [whole((BLOCK, model))] * (2 * len(low)),
-            out_specs=[whole((BLOCK, model))] * steps
-            + [pl.BlockSpec((BLOCK, model), lambda i, o: (i, 0))] * bool(low)
+            + [pl.BlockSpec((BLOCK, model), lambda i, o: (jnp.maximum(i - (steps - 2), 0), 0))] * len(added)
+            + [whole((BLOCK, model))] * len(come),
+            out_specs=[whole((joined * BLOCK, model))] * (steps // joined)
+            + [pl.BlockSpec((BLOCK, model), lambda i, o: (jnp.maximum(i - (steps - 2), 0), 0))] * bool(added)
             + [whole((8, model))],
-            scratch_shapes=[pltpu.VMEM((BLOCK, model), LOW), pltpu.VMEM((BLOCK, model), LOW)],
+            scratch_shapes=[pltpu.VMEM((BLOCK, model), LOW), pltpu.VMEM((BLOCK, model), F32)],
         ),
-        out_shape=[jax.ShapeDtypeStruct((BLOCK, model), LOW)] * steps
-        + [jax.ShapeDtypeStruct((steps * BLOCK, model), LOW)] * bool(low)
+        out_shape=[jax.ShapeDtypeStruct((joined * BLOCK, model), LOW)] * (steps // joined)
+        + [jax.ShapeDtypeStruct((2 * BLOCK, model), LOW)] * bool(added)
         + [jax.ShapeDtypeStruct((8, model), F32)],
         compiler_params=params("arbitrary"),
         cost_estimate=cost,
         name="close",
-    )(order, *pieces, *d_rows, to_norm, vectors, weight, *low, *high)
-
-
-def finish_kernel(halves, base, shift, *refs):
-    parts, out = refs[:-1], refs[-1]
-    shifts = jnp.sum(shift[...], axis=0, keepdims=True)
+    )(order, *pieces, *d_rows, to_norm, vectors, weight, *added, *come)
+
+
+def finish_kernel(base, *refs):
+    *parts, out = refs
     for at in range(2):
 
         @pl.when(pl.program_id(0) == at)
         def _():
-            total = base[...].astype(F32) + shifts
+            total = base[...].astype(F32)
             for part in parts[at::2]:
                 total = total + part[...].astype(F32)
             out[...] = total.astype(LOW)
 
 
-def call_finish(base, shift, low, high):
+def call_finish(base, parts):
     rows, model = base.shape
-    half = rows // 2
-    arrays = [a for pair in zip(low, high) for a in pair]
+    block = pl.BlockSpec((rows // 2, model), lambda i: (i, 0))
     return pl.pallas_call(
-        functools.partial(finish_kernel, len(low)),
+        finish_kernel,
         grid=(2,),
-        in_specs=[pl.BlockSpec((half, model), lambda i: (i, 0)), whole(shift.shape)] + [whole((half, model))] * len(arrays),
-        out_specs=pl.BlockSpec((half, model), lambda i: (i, 0)),
+        in_specs=[block] + [whole((rows // 2, model))] * len(parts),
+        out_specs=block,
         out_shape=jax.ShapeDtypeStruct((rows, model), LOW),
         compiler_params=params("arbitrary"),
         cost_estimate=SHORT,
         name="finish",
-    )(base, shift, *arrays)
-
-
-def cut_kernel(members, member, first, second, *out):
-    pieces, (down, last) = out[:members], out[members:]
-    shard = last.shape[0]
+    )(base, *parts)
+
+
+def cut_kernel(members, member, first, second, third, *out):
+    pieces, down = out[:members], out[members]
+    shard = pieces[0].shape[0]
     columns = first.shape[1]
     for bit, piece in enumerate(pieces):
         rows = pl.ds(pl.multiple_of((member[0] ^ bit) * shard, shard), shard)
         piece[:, :columns] = first[rows, :]
-        piece[:, columns:] = second[rows, :]
+        piece[:, columns:] = (second[rows, :].astype(F32) + third[rows, :].astype(F32)).astype(LOW)
     low = members * shard
     down[...] = first[low : low + down.shape[0], :].astype(F32)
-    last[...] = first[low + down.shape[0] :, :]
-
-
-def call_cut(member, first, second, members, shard):
+
+
+def call_cut(member, first, second, third, members, shard):
     columns = first.shape[1]
     shapes = [jax.ShapeDtypeStruct((shard, columns + second.shape[1]), LOW)] * members + [
-        jax.ShapeDtypeStruct((first.shape[0] - (members + 1) * shard, columns), F32),
-        jax.ShapeDtypeStruct((shard, columns), LOW),
+        jax.ShapeDtypeStruct((first.shape[0] - members * shard, columns), F32),
     ]
     return pl.pallas_call(
         functools.partial(cut_kernel, members),
         grid_spec=pltpu.PrefetchScalarGridSpec(
             num_scalar_prefetch=1,
             grid=(1,),
-            in_specs=[whole(first.shape), whole(second.shape)],
+            in_specs=[whole(first.shape), whole(second.shape), whole(third.shape)],
             out_specs=[whole(a.shape) for a in shapes],
         ),
         out_shape=shapes,
         compiler_params=params("arbitrary"),
         cost_estimate=SHORT,
         name="cut",
-    )(member, first, second)
+    )(member, first, second, third)
 
 
 def join_kernel(places, member, *refs):
@@ -924,36 +951,17 @@
     return lax.ppermute(array, "dp", [(i, i ^ bit) for i in range(lax.axis_size("dp"))])
 
 
-def scatter_relative(even, odd):
-    add = lambda a, b: (a.astype(F32) + b.astype(F32)).astype(LOW)
-    blocks, bit = add(even, hop(odd, 1)), 2
-    while blocks.shape[0] > 1:
-        blocks = add(blocks[0::2], hop(blocks[1::2], bit))
-        bit *= 2
-    return blocks[0]
-
-
-def reduce_begin(parts):
+def scatter_step(blocks, far, bit):
+    blocks = (blocks.astype(F32) + far.astype(F32)).astype(LOW)
+    send = blocks[1::2]
+    return blocks[0::2], hop(send, bit), send
+
+
+def reduce_direct(parts):
     if len(parts) == 1:
-        return ()
-    _, _, one_low, _, _, two_high, three_low, three_high = parts
-    return across(three_low, 1), across(three_high, 2), across(one_low, 1), across(two_high, 2)
-
-
-def reduce_middle(parts, begun):
-    if len(parts) == 1:
-        return ()
-    add = lambda a, b: (a.astype(F32) + b.astype(F32)).astype(LOW)
-    return add(parts[3], begun[1]), add(parts[4], begun[0])
-
-
-def reduce_last(parts, begun, middle):
-    if len(parts) == 1:
-        total = lax.psum_scatter(parts[0], "fsdp", scatter_dimension=0, tiled=True)
-        half = total.shape[0] // 2
-        return (total[:half],), (total[half:],)
-    one_high, two_low = across(middle[0], 1), across(middle[1], 2)
-    return (parts[0], begun[2], two_low), (parts[1], one_high, begun[3])
+        return (lax.psum_scatter(parts[0], "fsdp", scatter_dimension=0, tiled=True),)
+    three = across(parts[3], 3)
+    return parts[0], across(parts[1], 1), across(parts[2], 2), three
 
 
 def total_over_all(vector):
@@ -988,14 +996,13 @@
     cosine = np.cos(angles).astype(np.float32)
     sine = np.sin(angles).astype(np.float32)
     cos_row = np.ones((length, 128), np.float32)
-    ahead = np.zeros((length, 128), np.float32)
-    behind = np.zeros((length, 128), np.float32)
+    sine_row = np.zeros((length, 128), np.float32)
     for start in range(0, 128, HEAD):
         cos_row[:, start : start + half] = cosine
         cos_row[:, start + half : start + ROT] = cosine
-        ahead[:, start : start + half] = -sine
-        behind[:, start + half : start + ROT] = sine
-    return jnp.asarray(np.concatenate([cos_row, ahead, behind], axis=1))
+        sine_row[:, start : start + half] = -sine
+        sine_row[:, start + half : start + ROT] = sine
+    return jnp.asarray(np.concatenate([cos_row, sine_row], axis=1))
 
 
 def local(
@@ -1019,15 +1026,14 @@
     x_halves = [tokens[:half], tokens[half:]]
     cot_halves = [cotangent[:half], cotangent[half:]]
     if paired:
+        out_own = swap_owner(out_weight, False)
         small = small_block(member, members, vectors_in, qkv_bias, up_bias)
         packed = call_pack(me, qkv_weight, up_weight, small, members)
         arrived = [packed[0]] + [across(packed[bit], bit) for bit in range(1, members)]
         x_near = near_rows(behind_all(x_halves, *arrived[1:]))
         cut = 3 * width + 128
-        first_in, up_in = call_place(me, arrived, cut)
+        first_in, up_in = call_place(me, behind_all(arrived, out_own), cut)
         w_first = gather_dp(first_in)
-        out_own = swap_owner(behind(out_weight, first_in), False)
-        out_own = behind(out_own, *x_near[:2])
         mats = (gather_dp(jnp.concatenate([up_in, down_weight, out_own], axis=0)),)
         vectors = call_vectors(me, w_first, members, cut)
     else:
@@ -1049,75 +1055,88 @@
     order = sources ^ member if members == 4 else sources
     doc_row = doc_ids[0]
     first = jnp.sum((doc_row[None, :] < doc_row[:, None]).astype(jnp.int32), axis=1)
-    first = jnp.concatenate([first, group.astype(jnp.int32).reshape(1)])
+    marks = [group, member ^ 3] if members == 4 else [group, member]
+    first = jnp.concatenate([first] + [a.astype(jnp.int32).reshape(1) for a in marks])
     tables = rotary_tables(stream)
 
     q, k, v, normal = call_qkv(order, x_pieces, vectors, w_first, tables, rows, width)
     cot_near = near_rows(behind_all(cot_halves, *x_pieces[2:])) if members == 4 else None
     cot_pieces = gather_rows(cot_halves, cot_near, q)
     mixed, low_mixed, lse = call_fwd(first, q, k, v)
-    out_sizes = [half] * (2 * members) if members == 4 else [stream]
+    out_sizes = [rows] * members if members == 4 else [stream]
     out_shapes = [jax.ShapeDtypeStruct((size, model), LOW) for size in out_sizes]
     results = call_mlp(
         order, x_pieces, cot_pieces, low_mixed, vectors, mats, rows, units, out_shapes
     )
     count = len(out_shapes)
     parts, (d_mixed, to_norm), grads, sums_two = results[:count], results[count : count + 2], results[count + 2 : -1], results[-1]
+    *grads, g_out = grads
     scattered = scatter_dp(grads[0].reshape(-1, model)) if paired else None
-
-    begun = reduce_begin(parts)
-    halves = 2 if width % 256 == 0 else 1
-    back = [call_bwd(first, q, k, v, d_mixed, mixed, lse, tables, normal, 0, halves, (), groups)]
-    middle = reduce_middle(parts, behind_all(begun, back[0][0]))
-    summed = reduce_last(parts, begun, middle)
-    for part in range(1, halves):
-        q = behind(q, *middle, *begun[2:])
-        back.append(call_bwd(first, q, k, v, d_mixed, mixed, lse, tables, normal, part, halves, (back[-1][1],), groups))
-    d_qkv = [b[0] for b in back]
-    even, odd = back[-1][1:3]
-    sums_qkv = [b[-1] for b in back]
-    to_norm = behind(to_norm, *summed[0], *summed[1])
+    g_out = scatter_dp(g_out)
+
+    summed = reduce_direct(parts)
+    closing = (x_pieces[6], x_pieces[7], to_norm, vectors, w_first) if members == 4 else ()
+    d_qkv, even, odd, sums_qkv, *three = call_bwd(first, q, k, v, d_mixed, mixed, lse, tables, normal, groups, closing)
+    d_qkv, sums_qkv, halves = [d_qkv], [sums_qkv], 1
+    blocks, far, bit = even, hop(odd, 1), 2
     if members == 4:
-        close = lambda pieces, cost=SHORT, low=(), high=(): call_close(
+        close = lambda pieces, *more: call_close(
             order, [x_pieces[p] for p in pieces], [(i, 0, p * half) for i, p in enumerate(pieces)],
-            d_qkv, to_norm, vectors, w_first, rows, cost, low, high,
+            d_qkv, to_norm, vectors, w_first, rows, *more,
         )
-        *three, ones_a = close((6, 7), LONG)
-        to_norm = behind(to_norm, *three, *(() if scattered is None else (scattered,)))
-        one_low, two_high, one_high, two_low, ones_b = close((2, 5, 3, 4))
-        to_norm = behind(to_norm, one_low)
-        own_low, own_high, output, ones_c = close((0, 1), SHORT, *summed)
-        final = [own_low, own_high, one_low, one_high, two_low, two_high, *three]
-        ones = [ones_a, ones_b, ones_c]
+        three_low, three_high, ones_a = three
+        come = across(three_high, 2), across(three_low, 1)
+        to_norm = behind(to_norm, *summed[1:])
+        one_low, two_high, ones_b = close((2, 5), LONG, (), 1)
+        near = across(one_low, 1), across(two_high, 2)
+        blocks, far, send = scatter_step(blocks, behind(far, one_low), bit)
+        to_norm = behind(to_norm, send, one_low, *(() if scattered is None else (scattered,)))
+        one_high, two_low, ones_c = close((3, 4), SHORT, (), 1, (0, 1), come)
+        if groups > 4:
+            blocks, far, send = scatter_step(blocks, behind(far, one_high), 2 * bit)
+        near += across(behind(one_high, send), 1), across(behind(two_low, send), 2)
+        to_norm = behind(to_norm, send, one_high)
+        own_low, own_high, output, ones_d = close((0, 1), SHORT, summed, 1)
+        ones = [ones_a, ones_b, ones_c, ones_d]
+        g_out = swap_owner(behind(g_out, own_low), True)
+        bit = 8 if groups > 4 else 4
     else:
         plan = [(0, low, low) for low in range(0, stream, BLOCK)]
         *final, ones = call_close(order, x_pieces, plan, d_qkv, to_norm, vectors, w_first, rows)
-        final, ones = [jnp.concatenate(final, axis=0)], [ones]
-        output = call_finish(tokens, vectors[4:6, :], *summed)
-    begun = reduce_begin(final)
-    middle = reduce_middle(final, begun)
-    grad_tokens = call_finish(cotangent, jnp.zeros((1, model), F32), *reduce_last(final, begun, middle))
-
-    g_qkv = scatter_relative(behind(even, *final[2:4]) if members == 4 else even, odd)
+        ones = [ones]
+        own = reduce_direct([jnp.concatenate(final, axis=0)])[0]
+        own_low, own_high, near = own[:half], own[half:], None
+        output = (tokens.astype(F32) + summed[0].astype(F32) + vectors[4:5, :] + vectors[5:6, :]).astype(LOW)
+
+    while blocks.shape[0] > 1:
+        (blocks, far, _), bit = scatter_step(blocks, far, bit), 2 * bit
+    if near is not None:
+        far = behind(far, *near[:2])
+    g_qkv = blocks[0], far[0]
+    if near is None:
+        parts = own_low, own_high
+    else:
+        parts = own_low, own_high, near[0], near[2], near[3], near[1]
     place = group * members + member
     if paired:
-        *mixed_pieces, g_down, g_out = call_cut(me, scattered, g_qkv, members, shard)
+        *mixed_pieces, g_down = call_cut(me, scattered, *g_qkv, members, shard)
         places = [(0, b * members * units_dev, units_dev) for b in range(groups)]
-        places += [(1, part * model + half * (width // halves), width) for half in range(halves) for part in range(3)]
+        places += [(1, part * model + low, width) for part in range(3) for low in range(0, width, 128)]
         arrived = [mixed_pieces[0]] + [across(mixed_pieces[bit], bit) for bit in range(1, members)]
         g_up, g_qkv = call_join(me, arrived, places, (up_weight.shape[1], qkv_weight.shape[1]))
-        ready = behind(call_bundle(me, members, groups, sums_two, sums_qkv, ones), *middle, *begun[2:])
+        grad_tokens = call_finish(behind(cotangent, g_up), parts)
+        ready = behind(call_bundle(me, members, groups, sums_two, sums_qkv, ones), far, *parts)
         totals = jnp.sum(lax.all_to_all(ready, ALL, split_axis=0, concat_axis=0), axis=0)
-        g_out = swap_owner(behind(g_out, totals), True).astype(F32)
         size = model // devices
         mine = [a[0] for a in jnp.split(lax.dynamic_slice_in_dim(totals[:5], member * size, size, 1), 5)]
         mine += [lax.dynamic_slice_in_dim(totals[5:8].reshape(-1), member * 3 * size, 3 * size), totals[8]]
     else:
-        g_up, g_down, g_out = [scatter_dp(g) for g in grads]
+        g_up, g_down = [scatter_dp(g) for g in grads]
+        grad_tokens = call_finish(cotangent, parts)
         g_down = g_down.astype(F32)
-        g_out = swap_owner(g_out, True).astype(F32)
         g_up = exchange(g_up.reshape(members, shard, units))
         g_up = g_up.reshape(members, shard, groups, units_dev).transpose(1, 2, 0, 3).reshape(shard, -1).astype(F32)
+        g_qkv = (g_qkv[0].astype(F32) + g_qkv[1].astype(F32)).astype(LOW)
         g_qkv = exchange(g_qkv.reshape(members, shard, 3 * width)).reshape(members, shard, halves, 3, width // halves)
         g_qkv = g_qkv.transpose(1, 3, 0, 2, 4).reshape(shard, -1).astype(F32)
         thirds = jnp.concatenate([a[0].reshape(3, 1, width // halves) for a in sums_qkv], axis=2)
@@ -1134,6 +1153,7 @@
             mine.append(lax.dynamic_slice_in_dim(summed, start + place * (size // devices), size // devices))
             start += size
     gain_1, bias_1, gain_2, bias_2, end_bias, qkv_shift, up_shift = mine
+    g_out = (g_out if members == 4 else swap_owner(g_out, True)).astype(F32)
     return (
         output, grad_tokens, gain_1, bias_1, gain_2, bias_2, g_qkv, qkv_shift, g_out, end_bias, g_up, up_shift, g_down, end_bias,
     )

time: 292 us -> 268 us (0.918)
  Pallas kernels: 163 us -> 148 us
  waiting for transfers between devices: 51.7 us -> 38.7 us
  starting transfers between devices: 37.7 us -> 48 us
    pallas_call x3 -> x2, Pallas kernels: 54.1 us -> 42.1 us  [the longest x1 38.7 us: call_bwd(): pl.pallas_call(functools.partial(bwd_kernel, groups, bool(closing)), grid...]
    ppermute x30 -> x27, starting transfers between devices: 31.6 us -> 39.5 us  [across(): return lax.ppermute(array, 'fsdp', [(i, i ^ bit) for i in range(size)])]
    ppermute x30 -> x27, waiting for transfers between devices: 44.9 us -> 37.1 us  [across(): return lax.ppermute(array, 'fsdp', [(i, i ^ bit) for i in range(size)])]
    ppermute x3, waiting for transfers between devices: 6.72 us -> 1.16 us  [hop(): lax.ppermute(array, 'dp', [(i, i ^ bit) for i in range(lax.axis_size('dp'...]
  transfers between devices with their start and end apart: 39 -> 37, of which waited for: 11 -> 13; matrix products, arithmetic and copies ran while one was open for 4% -> 3% of each run, Pallas kernels for 41% -> 39%
where the time goes in v4:
time: 268 us; the launch traced here: 265 us
  Pallas kernels  148 us (55%)
  starting transfers between devices  48 us (18%)
  waiting for transfers between devices  38.7 us (14%)
  between operations  14.1 us (5%)
  local copies, waits for them, and re-layouts  9.67 us (4%)
  other arithmetic  6.59 us (2%)
    pallas_call x1, Pallas kernels, call_mlp(): pl.pallas_call(functools.partial(mlp_kernel, plan, out_plan, count, len(o...  41.4 us
    ppermute x27, starting transfers between devices, across(): return lax.ppermute(array, 'fsdp', [(i, i ^ bit) for i in range(size)])  39.5 us
    pallas_call x1, Pallas kernels, call_bwd(): pl.pallas_call(functools.partial(bwd_kernel, groups, bool(closing)), grid...  38.7 us
    ppermute x27, waiting for transfers between devices, across(): return lax.ppermute(array, 'fsdp', [(i, i ^ bit) for i in range(size)])  37.1 us
    pallas_call x3, Pallas kernels, call_close(): pl.pallas_call(functools.partial(close_kernel, plan, len(pieces), len(d_r...  20.8 us
    pallas_call x1, Pallas kernels, call_fwd(): pl.pallas_call(fwd_kernel, grid_spec=pltpu.PrefetchScalarGridSpec(num_sca...  20.4 us
    pallas_call x1, Pallas kernels, call_qkv(): pl.pallas_call(functools.partial(qkv_kernel, plan, len(pieces)), grid_spe...  11.6 us
  transfers between devices with their start and end apart: 37, of which 13 were waited for; matrix products, arithmetic and copies ran while one was open for 3% of the time, Pallas kernels for 39%

profile of v4, /device:TPU:0, one launch (start us, length us, event | category | flops | bytes accessed | tf_op | source)
XLA Modules:
  0.0 264.7 jit_solution(8871180769752613255)
XLA Ops:
  12.2 2.9 %collective-permute-start = (bf16[32,1920]{1,0:T(8,128)(2,1)}, bf16[32,1920]{1,0:T(8,128)(2,1)S(1)}, u32[]{:S(2)}, u32[]{:S(2)}) collective-permute-start(bf16[32,1920]{1,0:T(8,128)(2,1)} %get-tuple-element.81), channel_id=1, source_target_pairs={{0,1},{1,0},{2,3},{3,2},{4,5},{5,4},{6,7},{7,6},{8,9},{9,8},{10,11... | collective-permute-start | bytes 368648 | tf_op jit(solution)/shard_map/ppermute | solution.py:912
  19.2 3.7 %collective-permute-done.1.refs_2_ = bf16[32,1920]{1,0:T(8,128)(2,1)S(1)} collective-permute-done((bf16[32,1920]{1,0:T(8,128)(2,1)}, bf16[32,1920]{1,0:T(8,128)(2,1)S(1)}, u32[]{:S(2)}, u32[]{:S(2)}) %collective-permute-start.1) | collective-permute-done | bytes 122912 | tf_op jit(solution)/shard_map/ppermute | solution.py:912
  28.2 3.1 %collective-permute-start.3 = (bf16[256,1024]{1,0:T(8,128)(2,1)S(1)}, bf16[256,1024]{1,0:T(8,128)(2,1)S(1)}, u32[]{:S(2)}, u32[]{:S(2)}) collective-permute-start(bf16[256,1024]{1,0:T(8,128)(2,1)S(1)} %get-tuple-element.84.refs_0_), channel_id=1, source_target_pairs={{0,1},{1,0},{2,3},{3,2},{4,5},{5,4},{6,7},{7,6},{8,9},{9,8},{10,11... | collective-permute-start | bytes 1572872 | tf_op jit(solution)/shard_map/ppermute | solution.py:912
  31.3 4.6 %collective-permute-start.6 = (bf16[256,1024]{1,0:T(8,128)(2,1)S(1)}, bf16[256,1024]{1,0:T(8,128)(2,1)S(1)}, u32[]{:S(2)}, u32[]{:S(2)}) collective-permute-start(bf16[256,1024]{1,0:T(8,128)(2,1)S(1)} %get-tuple-element.85.refs_1_), channel_id=1, source_target_pairs={{0,2},{1,3},{2,0},{3,1},{4,6},{5,7},{6,4},{7,5},{8,10},{9,11},{10,... | collective-permute-start | bytes 1572872 | tf_op jit(solution)/shard_map/ppermute | solution.py:912
  36.0 8.1 %collective-permute-done.3.refs_2_.refs_0_ = bf16[256,1024]{1,0:T(8,128)(2,1)S(1)} collective-permute-done((bf16[256,1024]{1,0:T(8,128)(2,1)S(1)}, bf16[256,1024]{1,0:T(8,128)(2,1)S(1)}, u32[]{:S(2)}, u32[]{:S(2)}) %collective-permute-start.3) | collective-permute-done | bytes 524320 | tf_op jit(solution)/shard_map/ppermute | solution.py:912
  44.1 4.6 %collective-permute-start.7 = (bf16[256,1024]{1,0:T(8,128)(2,1)S(1)}, bf16[256,1024]{1,0:T(8,128)(2,1)S(1)}, u32[]{:S(2)}, u32[]{:S(2)}) collective-permute-start(bf16[256,1024]{1,0:T(8,128)(2,1)S(1)} %collective-permute-done.3.refs_2_.refs_0_), channel_id=1, source_target_pairs={{0,2},{1,3},{2,0},{3,1},{4,6},{5,7},{6,4},{7,5},{8,10},{9,11},{10,... | collective-permute-start | bytes 1572872 | tf_op jit(solution)/shard_map/ppermute | solution.py:912
  48.7 2.0 collective-permute-start.8
  50.7 2.2 fusion.1
  53.0 7.0 %collective-permute-done.5.refs_4_.refs_1_ = bf16[256,1024]{1,0:T(8,128)(2,1)S(1)} collective-permute-done((bf16[256,1024]{1,0:T(8,128)(2,1)S(1)}, bf16[256,1024]{1,0:T(8,128)(2,1)S(1)}, u32[]{:S(2)}, u32[]{:S(2)}) %collective-permute-start.5) | collective-permute-done | bytes 524320 | tf_op jit(solution)/shard_map/ppermute | solution.py:912
  60.0 8.2 %collective-permute-done.7.refs_6_.rest_0_ = bf16[256,1024]{1,0:T(8,128)(2,1)S(1)} collective-permute-done((bf16[256,1024]{1,0:T(8,128)(2,1)S(1)}, bf16[256,1024]{1,0:T(8,128)(2,1)S(1)}, u32[]{:S(2)}, u32[]{:S(2)}) %collective-permute-start.7) | collective-permute-done | bytes 524320 | tf_op jit(solution)/shard_map/ppermute | solution.py:912
  68.1 2.1 collective-permute-start.13
  74.5 11.6 %qkv.3 = (bf16[2048,256]{1,0:T(8,128)(2,1)}, bf16[2048,256]{1,0:T(8,128)(2,1)}, bf16[2048,256]{1,0:T(8,128)(2,1)}, bf16[2048,1024]{1,0:T(8,128)(2,1)}) custom-call(s32[4]{0:T(128)} %iota_xor_fusion.order, bf16[256,1024]{1,0:T(8,128)(2,1)} %copy-done.1, bf16[256,1024]{1,0:T(8,128)(2,1)} %copy-done, bf16[256,1024]{1,0:T(8,128)(2,1)} %copy-done.6, ...), custom_call_target="tpu_custom_call" | custom-call | tf_op jit(solution)/shard_map/qkv/pallas_call | solution.py:259
  89.1 20.4 %attend.1 = (f32[2048,256]{1,0:T(8,128)}, bf16[2048,256]{1,0:T(8,128)(2,1)}, f32[4,2048]{1,0:T(4,128)}) custom-call(s32[10]{0:T(128)} %pad_add_fusion.first, bf16[2048,256]{1,0:T(8,128)(2,1)} %get-tuple-element.92.q, bf16[2048,256]{1,0:T(8,128)(2,1)} %get-tuple-element.93.k, bf16[2048,256]{1,0:T(8,128)(2,1)} %get-tuple-element.94.v), custom_call_target="tpu_custom_call" | custom-call | tf_op jit(solution)/shard_map/attend/pallas_call | solution.py:351
  110.5 41.4 %mlp.1 = (bf16[512,1024]{1,0:T(8,128)(2,1)}, bf16[512,1024]{1,0:T(8,128)(2,1)}, bf16[512,1024]{1,0:T(8,128)(2,1)}, bf16[512,1024]{1,0:T(8,128)(2,1)}, bf16[2048,...) custom-call(s32[4]{0:T(128)} %iota_xor_fusion.order, ...), custom_call_target="tpu_custom_call" | custom-call | tf_op jit(solution)/shard_map/mlp/pallas_call | solution.py:663
  155.5 38.7 %attend_back.1 = (bf16[2048,768]{1,0:T(8,128)(2,1)}, bf16[4,128,768]{2,1,0:T(8,128)(2,1)}, bf16[4,128,768]{2,1,0:T(8,128)(2,1)}, f32[8,768]{1,0:T(8,128)}, bf16[...) custom-call(s32[10]{0:T(128)} %pad_add_fusion.first, bf16[2048,256]{1,0:T(8,128)(2,1)} %get-tuple-element.92.q, ...), custom_call_target="tpu_custom_call" | custom-call | tf_op jit(solution)/shard_map/attend_back/pallas_call | solution.py:536
  196.6 3.9 %collective-permute-done.17.refs_8_ = bf16[512,1024]{1,0:T(8,128)(2,1)S(1)} collective-permute-done((bf16[512,1024]{1,0:T(8,128)(2,1)}, bf16[512,1024]{1,0:T(8,128)(2,1)S(1)}, u32[]{:S(2)}, u32[]{:S(2)}) %collective-permute-start.17) | collective-permute-done | bytes 1048608 | tf_op jit(solution)/shard_map/ppermute | solution.py:912
  201.0 6.2 %close.3 = (bf16[256,1024]{1,0:T(8,128)(2,1)}, bf16[256,1024]{1,0:T(8,128)(2,1)}, f32[8,1024]{1,0:T(8,128)}) custom-call(s32[4]{0:T(128)} %iota_xor_fusion.order, bf16[256,1024]{1,0:T(8,128)(2,1)} %copy-done.6, bf16[256,1024]{1,0:T(8,128)(2,1)} %copy-done.7, bf16[2048,768]{1,0:T(8,128)(2,1)} %get-tuple-element.106.refs_2_, ...), custom_call_target="tpu_custom_call" | custom-call | flops 20000000000 | bytes 10000000 | tf_op jit(solution)/shard_map/close/pallas_call | solution.py:758
  211.9 6.4 %close.4 = (bf16[256,1024]{1,0:T(8,128)(2,1)}, bf16[256,1024]{1,0:T(8,128)(2,1)}, f32[8,1024]{1,0:T(8,128)}) custom-call(s32[4]{0:T(128)} %iota_xor_fusion.order, bf16[256,1024]{1,0:T(8,128)(2,1)} %copy-done.3, bf16[256,1024]{1,0:T(8,128)(2,1)} %copy-done.2, bf16[2048,768]{1,0:T(8,128)(2,1)} %get-tuple-element.106.refs_2_, ...), custom_call_target="tpu_custom_call" | custom-call | tf_op jit(solution)/shard_map/close/pallas_call | solution.py:758
  223.9 8.3 %close.5 = (bf16[256,1024]{1,0:T(8,128)(2,1)}, bf16[256,1024]{1,0:T(8,128)(2,1)}, bf16[512,1024]{1,0:T(8,128)(2,1)}, f32[8,1024]{1,0:T(8,128)}) custom-call(s32[4]{0:T(128)} %iota_xor_fusion.order, bf16[256,1024]{1,0:T(8,128)(2,1)} %copy-done.1, bf16[256,1024]{1,0:T(8,128)(2,1)} %copy-done, bf16[2048,768]{1,0:T(8,128)(2,1)} %get-tuple-element.106.refs_2_, ...), custom_call_target="tpu_custom_call" | custom-call | tf_op jit(solution)/shard_map/close/pallas_call | solution.py:758
  234.3 2.9 %all-to-all-start = ((f32[32,16,128]{2,1,0:T(8,128)}), f32[32,16,128]{2,1,0:T(8,128)S(1)}, u32[]{:S(2)}, u32[]{:S(2)}) async-start(f32[32,16,128]{2,1,0:T(8,128)} %bundle.1), calls=%async_computation.1 | async-start | bytes 524288 | tf_op jit(solution)/shard_map/all_to_all | solution.py:1129
  237.2 2.2 cut.1
  246.6 2.1 collective-permute-done.27.refs_2_
  250.4 2.1 join.1
  252.5 3.4 %finish.1 = bf16[512,1024]{1,0:T(8,128)(2,1)} custom-call(bf16[512,1024]{1,0:T(8,128)(2,1)} %base, bf16[256,1024]{1,0:T(8,128)(2,1)} %get-tuple-element.132.refs_0_, bf16[256,1024]{1,0:T(8,128)(2,1)} %get-tuple-element.133.refs_1_, bf16[256,1024]{1,0:T(8,128)(2,1)} %copy-done.13, bf16[256,1024]{1,0:T(8,128)(2,1)} %copy-done.15, ...), custom_call_target="tpu_custom_call" | custom-call | tf_op jit(solution)/shard_map/finish/pallas_call | solution.py:797
  (153 shorter events, 52.6 us)
Async XLA Ops:
  7.2 65.7 %all-gather.5.cloned.1.call-start = ((), (), s32[]{:S(2)}) async-start(), calls=%async_computation.5 | async-start | bytes 2064384 | tf_op jit(solution)/shard_map/all_gather | solution.py:985
  26.1 83.8 %all-gather.7.cloned.1.call-start = ((), (), s32[]{:S(2)}) async-start(), calls=%async_computation.6 | async-start | bytes 5308416 | tf_op jit(solution)/shard_map/all_gather | solution.py:985
  28.0 183.9 %reduce-scatter.3.cloned.1.call-start = ((), (), s32[]{:S(2)}) async-start(), calls=%async_computation.3 | async-start | bytes 4718592 | tf_op jit(solution)/shard_map/reduce_scatter | solution.py:989
  28.2 16.0 %collective-permute-start.3 = (bf16[256,1024]{1,0:T(8,128)(2,1)S(1)}, bf16[256,1024]{1,0:T(8,128)(2,1)S(1)}, u32[]{:S(2)}, u32[]{:S(2)}) collective-permute-start(bf16[256,1024]{1,0:T(8,128)(2,1)S(1)} %get-tuple-element.84.refs_0_), channel_id=1, source_target_pairs={{0,1},{1,0},{2,3},{3,2},{4,5},{5,4},{6,7},{7,6},{8,9},{9,8},{10,11... | collective-permute-start | bytes 1572872 | tf_op jit(solution)/shard_map/ppermute | solution.py:912
  31.3 17.4 %collective-permute-start.6 = (bf16[256,1024]{1,0:T(8,128)(2,1)S(1)}, bf16[256,1024]{1,0:T(8,128)(2,1)S(1)}, u32[]{:S(2)}, u32[]{:S(2)}) collective-permute-start(bf16[256,1024]{1,0:T(8,128)(2,1)S(1)} %get-tuple-element.85.refs_1_), channel_id=1, source_target_pairs={{0,2},{1,3},{2,0},{3,1},{4,6},{5,7},{6,4},{7,5},{8,10},{9,11},{10,... | collective-permute-start | bytes 1572872 | tf_op jit(solution)/shard_map/ppermute | solution.py:912
  35.9 24.1 %collective-permute-start.5 = (bf16[256,1024]{1,0:T(8,128)(2,1)S(1)}, bf16[256,1024]{1,0:T(8,128)(2,1)S(1)}, u32[]{:S(2)}, u32[]{:S(2)}) collective-permute-start(bf16[256,1024]{1,0:T(8,128)(2,1)S(1)} %get-tuple-element.84.refs_0_), channel_id=1, source_target_pairs={{0,2},{1,3},{2,0},{3,1},{4,6},{5,7},{6,4},{7,5},{8,10},{9,11},{10,... | collective-permute-start | bytes 1572872 | tf_op jit(solution)/shard_map/ppermute | solution.py:912
  35.9 24.0 %collective-permute-start.4 = (bf16[256,1024]{1,0:T(8,128)(2,1)S(1)}, bf16[256,1024]{1,0:T(8,128)(2,1)S(1)}, u32[]{:S(2)}, u32[]{:S(2)}) collective-permute-start(bf16[256,1024]{1,0:T(8,128)(2,1)S(1)} %get-tuple-element.85.refs_1_), channel_id=1, source_target_pairs={{0,1},{1,0},{2,3},{3,2},{4,5},{5,4},{6,7},{7,6},{8,9},{9,8},{10,11... | collective-permute-start | bytes 1572872 | tf_op jit(solution)/shard_map/ppermute | solution.py:912
  44.1 24.0 %collective-permute-start.7 = (bf16[256,1024]{1,0:T(8,128)(2,1)S(1)}, bf16[256,1024]{1,0:T(8,128)(2,1)S(1)}, u32[]{:S(2)}, u32[]{:S(2)}) collective-permute-start(bf16[256,1024]{1,0:T(8,128)(2,1)S(1)} %collective-permute-done.3.refs_2_.refs_0_), channel_id=1, source_target_pairs={{0,2},{1,3},{2,0},{3,1},{4,6},{5,7},{6,4},{7,5},{8,10},{9,11},{10,... | collective-permute-start | bytes 1572872 | tf_op jit(solution)/shard_map/ppermute | solution.py:912
  48.7 19.4 %collective-permute-start.8 = (bf16[256,1024]{1,0:T(8,128)(2,1)S(1)}, bf16[256,1024]{1,0:T(8,128)(2,1)S(1)}, u32[]{:S(2)}, u32[]{:S(2)}) collective-permute-start(bf16[256,1024]{1,0:T(8,128)(2,1)S(1)} %collective-permute-done.6.refs_5_.refs_1_), channel_id=1, source_target_pairs={{0,1},{1,0},{2,3},{3,2},{4,5},{5,4},{6,7},{7,6},{8,9},{9,8},{10,11... | collective-permute-start | bytes 1572872 | tf_op jit(solution)/shard_map/ppermute | solution.py:912
  68.1 18.0 %collective-permute-start.13 = (bf16[256,1024]{1,0:T(8,128)(2,1)}, bf16[256,1024]{1,0:T(8,128)(2,1)}, u32[]{:S(2)}, u32[]{:S(2)}) collective-permute-start(bf16[256,1024]{1,0:T(8,128)(2,1)} %get-tuple-element.96.refs_9_), channel_id=1, source_target_pairs={{0,2},{1,3},{2,0},{3,1},{4,6},{5,7},{6,4},{7,5},{8,10},{9,11},{10,... | collective-permute-start | bytes 1572872 | tf_op jit(solution)/shard_map/ppermute | solution.py:912
  70.2 16.0 %collective-permute-start.10 = (bf16[256,1024]{1,0:T(8,128)(2,1)}, bf16[256,1024]{1,0:T(8,128)(2,1)}, u32[]{:S(2)}, u32[]{:S(2)}) collective-permute-start(bf16[256,1024]{1,0:T(8,128)(2,1)} %get-tuple-element.95.refs_8_), channel_id=1, source_target_pairs={{0,1},{1,0},{2,3},{3,2},{4,5},{5,4},{6,7},{7,6},{8,9},{9,8},{10,11... | collective-permute-start | bytes 1572872 | tf_op jit(solution)/shard_map/ppermute | solution.py:912
  70.8 38.7 %collective-permute-start.12 = (bf16[256,1024]{1,0:T(8,128)(2,1)}, bf16[256,1024]{1,0:T(8,128)(2,1)}, u32[]{:S(2)}, u32[]{:S(2)}) collective-permute-start(bf16[256,1024]{1,0:T(8,128)(2,1)} %get-tuple-element.95.refs_8_), channel_id=1, source_target_pairs={{0,2},{1,3},{2,0},{3,1},{4,6},{5,7},{6,4},{7,5},{8,10},{9,11},{10,... | collective-permute-start | bytes 1572872 | tf_op jit(solution)/shard_map/ppermute | solution.py:912
  71.0 38.5 %collective-permute-start.11 = (bf16[256,1024]{1,0:T(8,128)(2,1)}, bf16[256,1024]{1,0:T(8,128)(2,1)}, u32[]{:S(2)}, u32[]{:S(2)}) collective-permute-start(bf16[256,1024]{1,0:T(8,128)(2,1)} %get-tuple-element.96.refs_9_), channel_id=1, source_target_pairs={{0,1},{1,0},{2,3},{3,2},{4,5},{5,4},{6,7},{7,6},{8,9},{9,8},{10,11... | collective-permute-start | bytes 1572872 | tf_op jit(solution)/shard_map/ppermute | solution.py:912
  86.2 23.3 %collective-permute-start.14 = (bf16[256,1024]{1,0:T(8,128)(2,1)}, bf16[256,1024]{1,0:T(8,128)(2,1)S(1)}, u32[]{:S(2)}, u32[]{:S(2)}) collective-permute-start(bf16[256,1024]{1,0:T(8,128)(2,1)} %collective-permute-done.10.refs_10_), channel_id=1, source_target_pairs={{0,2},{1,3},{2,0},{3,1},{4,6},{5,7},{6,4},{7,5},{8,10},{9,11},{10,... | collective-permute-start | bytes 1572872 | tf_op jit(solution)/shard_map/ppermute | solution.py:912
  88.2 21.4 %collective-permute-start.15 = (bf16[256,1024]{1,0:T(8,128)(2,1)}, bf16[256,1024]{1,0:T(8,128)(2,1)S(1)}, u32[]{:S(2)}, u32[]{:S(2)}) collective-permute-start(bf16[256,1024]{1,0:T(8,128)(2,1)} %collective-permute-done.13.refs_13_), channel_id=1, source_target_pairs={{0,1},{1,0},{2,3},{3,2},{4,5},{5,4},{6,7},{7,6},{8,9},{9,8},{10,11... | collective-permute-start | bytes 1572872 | tf_op jit(solution)/shard_map/ppermute | solution.py:912
  151.9 91.0 %reduce-scatter.5.cloned.1.call-start = ((), (), s32[]{:S(2)}) async-start(), calls=%async_computation.4 | async-start | bytes 589824 | tf_op jit(solution)/shard_map/reduce_scatter | solution.py:989
  152.0 44.6 %collective-permute-start.16 = (bf16[512,1024]{1,0:T(8,128)(2,1)}, bf16[512,1024]{1,0:T(8,128)(2,1)S(1)}, u32[]{:S(2)}, u32[]{:S(2)}) collective-permute-start(bf16[512,1024]{1,0:T(8,128)(2,1)} %get-tuple-element.107), channel_id=1, source_target_pairs={{0,1},{1,0},{2,3},{3,2},{4,5},{5,4},{6,7},{7,6},{8,9},{9,8},{10,11... | collective-permute-start | bytes 3145736 | tf_op jit(solution)/shard_map/ppermute | solution.py:912
  153.9 46.6 %collective-permute-start.17 = (bf16[512,1024]{1,0:T(8,128)(2,1)}, bf16[512,1024]{1,0:T(8,128)(2,1)S(1)}, u32[]{:S(2)}, u32[]{:S(2)}) collective-permute-start(bf16[512,1024]{1,0:T(8,128)(2,1)} %get-tuple-element.108), channel_id=1, source_target_pairs={{0,2},{1,3},{2,0},{3,1},{4,6},{5,7},{6,4},{7,5},{8,10},{9,11},{10,... | collective-permute-start | bytes 3145736 | tf_op jit(solution)/shard_map/ppermute | solution.py:912
  154.3 46.7 %collective-permute-start.18 = (bf16[512,1024]{1,0:T(8,128)(2,1)}, bf16[512,1024]{1,0:T(8,128)(2,1)S(1)}, u32[]{:S(2)}, u32[]{:S(2)}) collective-permute-start(bf16[512,1024]{1,0:T(8,128)(2,1)} %get-tuple-element.109), channel_id=1, source_target_pairs={{0,3},{1,2},{2,1},{3,0},{4,7},{5,6},{6,5},{7,4},{8,11},{9,10},{10,... | collective-permute-start | bytes 3145736 | tf_op jit(solution)/shard_map/ppermute | solution.py:912
  194.2 17.7 %collective-permute-start.21 = (bf16[256,1024]{1,0:T(8,128)(2,1)}, bf16[256,1024]{1,0:T(8,128)(2,1)}, u32[]{:S(2)}, u32[]{:S(2)}) collective-permute-start(bf16[256,1024]{1,0:T(8,128)(2,1)} %get-tuple-element.117), channel_id=1, source_target_pairs={{0,2},{1,3},{2,0},{3,1},{4,6},{5,7},{6,4},{7,5},{8,10},{9,11},{10,... | collective-permute-start | bytes 1572872 | tf_op jit(solution)/shard_map/ppermute | solution.py:912
  195.1 16.8 %collective-permute-start.22 = (bf16[256,1024]{1,0:T(8,128)(2,1)}, bf16[256,1024]{1,0:T(8,128)(2,1)}, u32[]{:S(2)}, u32[]{:S(2)}) collective-permute-start(bf16[256,1024]{1,0:T(8,128)(2,1)} %get-tuple-element.118), channel_id=1, source_target_pairs={{0,1},{1,0},{2,3},{3,2},{4,5},{5,4},{6,7},{7,6},{8,9},{9,8},{10,11... | collective-permute-start | bytes 1572872 | tf_op jit(solution)/shard_map/ppermute | solution.py:912
  209.3 24.5 %collective-permute-start.24 = (bf16[256,1024]{1,0:T(8,128)(2,1)}, bf16[256,1024]{1,0:T(8,128)(2,1)S(1)}, u32[]{:S(2)}, u32[]{:S(2)}) collective-permute-start(bf16[256,1024]{1,0:T(8,128)(2,1)} %get-tuple-element.113), channel_id=1, source_target_pairs={{0,1},{1,0},{2,3},{3,2},{4,5},{5,4},{6,7},{7,6},{8,9},{9,8},{10,11... | collective-permute-start | bytes 1572872 | tf_op jit(solution)/shard_map/ppermute | solution.py:912
  210.2 23.6 %collective-permute-start.25 = (bf16[256,1024]{1,0:T(8,128)(2,1)}, bf16[256,1024]{1,0:T(8,128)(2,1)S(1)}, u32[]{:S(2)}, u32[]{:S(2)}) collective-permute-start(bf16[256,1024]{1,0:T(8,128)(2,1)} %get-tuple-element.124), channel_id=1, source_target_pairs={{0,2},{1,3},{2,0},{3,1},{4,6},{5,7},{6,4},{7,5},{8,10},{9,11},{10,... | collective-permute-start | bytes 1572872 | tf_op jit(solution)/shard_map/ppermute | solution.py:912
  234.3 21.5 %all-to-all-start = ((f32[32,16,128]{2,1,0:T(8,128)}), f32[32,16,128]{2,1,0:T(8,128)S(1)}, u32[]{:S(2)}, u32[]{:S(2)}) async-start(f32[32,16,128]{2,1,0:T(8,128)} %bundle.1), calls=%async_computation.1 | async-start | bytes 524288 | tf_op jit(solution)/shard_map/all_to_all | solution.py:1129
  (43 other events, 442.6 us)
Sparse Core Ops, SparseCore 0:
  26.2 30.6 all-gather.4
  58.5 51.2 all-gather.6
  152.0 49.0 reduce-scatter.2
  209.4 30.8 reduce-scatter.4

commit v5 on v4

--- a/solution.py
+++ b/solution.py
@@ -61,6 +61,7 @@
 
 
 HBM = pl.BlockSpec(memory_space=pl.ANY)
+EXTRA = 16
 
 
 def fetch(plan, step, refs, target, sems, begin):
@@ -389,38 +390,35 @@
     return e * scale, gain, bias
 
 
-def bwd_kernel(groups, closing, first, q, k, v, d_mixed, mixed, lse, turn, normal, *rest):
-    if closing:
-        (x_low, x_high, to_norm, vectors, weight), rest = rest[:5], rest[5:]
-    (d_out, even, odd, sums), rest = rest[:4], rest[4:]
-    if closing:
-        (three_low, three_high, ones), rest = rest[:3], rest[3:]
-    keys, values, sum_q, sum_k, sum_v, queries, seeds, h, d_rows, sem = rest[:10]
+def bwd_kernel(plan, per, groups, extra, first, q, k, v, d_mixed, mixed, lse, turn, to_norm, vectors, normal, weight, *rest):
+    many = 1 + max(piece for piece, _ in plan)
+    pieces, outs, (even, odd, sums, ones), rest = rest[:many], rest[many : 2 * many], rest[2 * many : 2 * many + 4], rest[2 * many + 4 :]
+    keys, values, sum_q, sum_k, sum_v, queries, seeds, h, d_rows, x, mat, wide, sem, x_sems, out_sems = rest
     step = pl.program_id(0)
     blocks = pl.num_programs(0)
     block = blocks - 1 - step
-    rows, width = k.shape
+    width = k.shape[1]
     heads = width // HEAD
     stack = heads * BLOCK
-    own = pl.ds(pl.multiple_of(block * BLOCK, BLOCK), BLOCK)
-    loads = [pltpu.make_async_copy(normal, h, sem.at[0])]
-    if closing:
-        x, carried, mat = rest[10:]
-        half = x_low.shape[0]
-        loads += [
-            pltpu.make_async_copy(x_low, x.at[pl.ds(0, half)], sem.at[1]),
-            pltpu.make_async_copy(x_high, x.at[pl.ds(half, half)], sem.at[2]),
-            pltpu.make_async_copy(to_norm.at[pl.ds(rows - 2 * half, 2 * half)], carried, sem.at[3]),
-            pltpu.make_async_copy(weight.at[:, :, pl.ds(0, 3 * width)], mat, sem.at[4]),
-        ]
+    base = first.shape[0] - 1 - len(plan) // per
+    group, order = first[base], lambda at: first[base + 1 + at]
+    rows_of = lambda at: pl.ds(pl.multiple_of(at * BLOCK, BLOCK), BLOCK)
+    own = rows_of(block)
+    loads = [
+        pltpu.make_async_copy(normal, h, sem.at[0]),
+        pltpu.make_async_copy(weight.at[:, :, pl.ds(0, 3 * width)], mat, sem.at[1]),
+    ]
 
     @pl.when(step == 0)
     def _():
-        for load in loads:
-            load.start()
+        loads[1].start()
+        for at, (piece, start) in reversed(list(enumerate(plan))):
+            place = order(at // per) * per + at % per
+            pltpu.make_async_copy(pieces[piece].at[pl.ds(start, BLOCK)], x.at[rows_of(place)], x_sems.at[place]).start()
+        loads[0].start()
 
         def prepare(at, _):
-            here = pl.ds(pl.multiple_of(at * BLOCK, BLOCK), BLOCK)
+            here = rows_of(at)
             masked_rows(keys.at[at], k[here, :])
             masked_rows(values.at[at], v[here, :])
             sum_k[here, :] = jnp.zeros((BLOCK, width), F32)
@@ -429,6 +427,7 @@
 
         lax.fori_loop(0, blocks, prepare, 0)
         sums[...] = jnp.zeros_like(sums)
+        ones[...] = jnp.zeros_like(ones)
 
     q_own = q[...]
     s_own = d_mixed[...]
@@ -462,6 +461,12 @@
         sum_q[...] += dot(jnp.concatenate(tall_scores, axis=0), key_rows, TN)
 
     over_keys(first, block, tiles)
+
+    @pl.when(step == 0)
+    def _():
+        loads[1].wait()
+
+    pltpu.make_async_copy(x.at[own], x.at[own], x_sems.at[block]).wait()
     turns = (turn[:, :128], turn[:, 128:])
     done = jnp.concatenate(
         [
@@ -472,83 +477,98 @@
         axis=1,
     )
     d_rows[own, :] = done
-    d_out[...] = done
     sums[0:1, :] += jnp.sum(done.astype(F32), axis=0, keepdims=True)
+    n, scale = normed(x[own, :].astype(F32))
+    d_h = dot(done, mat[...].reshape(h.shape[1], 3 * width), NT)
+    ones[0:1, :] += jnp.sum(d_h * n, axis=0, keepdims=True)
+    ones[1:2, :] += jnp.sum(d_h, axis=0, keepdims=True)
+    e = d_h * vectors[0:1, :] + to_norm[...].astype(F32)
+    e = e - jnp.mean(e, axis=-1, keepdims=True) - n * jnp.mean(e * n, axis=-1, keepdims=True)
+    x[own, :] = (e * scale).astype(LOW)
+    place = order(block // per) * per + block % per
+    for at, (piece, start) in enumerate(plan):
+
+        @pl.when(place == at)
+        def _():
+            pltpu.make_async_copy(x.at[own], outs[piece].at[pl.ds(start, BLOCK)], out_sems.at[block]).start()
 
     @pl.when(step == blocks - 1)
     def _():
-        for load in loads:
-            load.wait()
-        if closing:
-            start = pl.multiple_of(first[first.shape[0] - 1] * 2 * half, 2 * half)
-            gain = bias = 0.0
-            for low, out in ((0, three_low), (half, three_high)):
-                e, a, b = closed_rows(
-                    x[low : low + half, :], d_rows[pl.ds(start + low, half), :], carried[low : low + half, :], vectors,
-                    mat[...].reshape(h.shape[1], 3 * width),
-                )
-                out[...] = e.astype(LOW)
-                gain, bias = gain + a, bias + b
-            ones[0:1, :] = gain
-            ones[1:2, :] = bias
-        group = first[first.shape[0] - 2]
+        loads[0].wait()
         model = h.shape[1]
         grad = dot(h[...], d_rows[...], TN).astype(LOW)
         h[:model, : 3 * width] = grad
-        per = model // groups
+        size = model // groups
         for place in range(groups):
             to = odd if place % 2 else even
-            here = pl.ds(pl.multiple_of((group ^ place) * per, per), per)
-            to[place // 2] = h[here, : 3 * width]
-
-
-def call_bwd(first, q, k, v, d_mixed, mixed, lse, tables, normal, groups, closing=()):
+            to[place // 2, :size, :] = h[pl.ds(pl.multiple_of((group ^ place) * size, size), size), : 3 * width]
+        if extra:
+            members = len(plan) // per
+            wide[...] = jnp.zeros_like(wide)
+            for part in range(3):
+                for at in range(width // 128):
+                    row = (part * members + order(0)) * (width // 128) + at
+                    low = part * width + at * 128
+                    wide[pl.ds(row, 1), :] = sums[0:1, low : low + 128]
+            for place in range(groups):
+                to, near = odd if place % 2 else even, group ^ place
+                lanes = pl.ds(pl.multiple_of(near * 128, 128), 128)
+                lines = [ones[0:1, lanes], ones[1:2, lanes]] + [wide[pl.ds(3 * near + row, 1), :] for row in range(3)]
+                to[place // 2, size:, :] = jnp.zeros((EXTRA, 3 * width), LOW)
+                to[place // 2, size:, :128] = extra_rows(lines)
+        for at in range(len(plan)):
+            here = pl.ds(at * BLOCK, BLOCK)
+            pltpu.make_async_copy(x.at[here], x.at[here], out_sems.at[at]).wait()
+
+
+def call_bwd(first, q, k, v, d_mixed, mixed, lse, tables, to_norm, vectors, normal, weight, pieces, out_shapes, groups, span, extra):
     rows, width = q.shape
     heads = width // HEAD
     blocks = rows // BLOCK
     model = normal.shape[1]
-    grad = (groups // 2, model // groups, 3 * width)
+    grad = (groups // 2, model // groups + EXTRA * extra, 3 * width)
     back = lambda i, o: (blocks - 1 - i, 0)
     blocked = pl.BlockSpec((BLOCK, width), back)
-    outs = [((rows, 3 * width), LOW), (grad, LOW), (grad, LOW), ((8, 3 * width), F32)]
-    scratch = [
-        pltpu.VMEM((blocks, heads * BLOCK, width), LOW),
-        pltpu.VMEM((blocks, heads * BLOCK, width), LOW),
-        pltpu.VMEM((BLOCK, width), F32),
-        pltpu.VMEM((rows, width), F32),
-        pltpu.VMEM((rows, width), F32),
-        pltpu.VMEM((heads * BLOCK, width), LOW),
-        pltpu.VMEM((heads * BLOCK, width), LOW),
-        pltpu.VMEM((rows, model), LOW),
-        pltpu.VMEM((rows, 3 * width), LOW),
-        pltpu.SemaphoreType.DMA((5,)),
-    ]
-    specs = []
-    if closing:
-        half = closing[0].shape[0]
-        outs += [((half, model), LOW)] * 2 + [((8, model), F32)]
-        scratch += [
-            pltpu.VMEM((2 * half, model), LOW),
-            pltpu.VMEM((2 * half, model), F32),
-            pltpu.VMEM(closing[4].shape[:2] + (3 * width,), LOW),
-        ]
-        specs = [HBM] * 3 + [whole(closing[3].shape), HBM]
+    once = lambda shape: pl.BlockSpec(shape, lambda *_: (0,) * len(shape), pipeline_mode=pl.Buffered(1))
+    plan = tuple((p, start) for block in plan_of(pieces, BLOCK) for p, start, _, _ in block)
+    outs = [(grad, LOW), (grad, LOW), ((8, 3 * width), F32), ((8, model), F32)]
     return pl.pallas_call(
-        functools.partial(bwd_kernel, groups, bool(closing)),
+        functools.partial(bwd_kernel, plan, span // BLOCK, groups, extra),
         grid_spec=pltpu.PrefetchScalarGridSpec(
             num_scalar_prefetch=1,
             grid=(blocks,),
-            in_specs=[blocked, whole((rows, width)), whole((rows, width)), blocked, blocked]
-            + [pl.BlockSpec((heads, BLOCK), lambda i, o: (0, blocks - 1 - i)), pl.BlockSpec((BLOCK, 256), back), HBM]
-            + specs,
-            out_specs=[pl.BlockSpec((BLOCK, 3 * width), back)] + [whole(a) for a, _ in outs[1:]],
-            scratch_shapes=scratch,
+            in_specs=[blocked, once((rows, width)), once((rows, width)), blocked, blocked]
+            + [pl.BlockSpec((heads, BLOCK), lambda i, o: (0, blocks - 1 - i)), pl.BlockSpec((BLOCK, 256), back)]
+            + [pl.BlockSpec((BLOCK, model), back), whole(vectors.shape), HBM, HBM]
+            + [HBM] * len(pieces),
+            out_specs=[HBM] * len(out_shapes) + [whole(a) for a, _ in outs],
+            scratch_shapes=[
+                pltpu.VMEM((blocks, heads * BLOCK, width), LOW),
+                pltpu.VMEM((blocks, heads * BLOCK, width), LOW),
+                pltpu.VMEM((BLOCK, width), F32),
+                pltpu.VMEM((rows, width), F32),
+                pltpu.VMEM((rows, width), F32),
+                pltpu.VMEM((heads * BLOCK, width), LOW),
+                pltpu.VMEM((heads * BLOCK, width), LOW),
+                pltpu.VMEM((rows, model), LOW),
+                pltpu.VMEM((rows, 3 * width), LOW),
+                pltpu.VMEM((rows, model), LOW),
+                pltpu.VMEM(weight.shape[:2] + (3 * width,), LOW),
+                pltpu.VMEM((3 * groups, 128), F32),
+                pltpu.SemaphoreType.DMA((2,)),
+                pltpu.SemaphoreType.DMA((blocks,)),
+                pltpu.SemaphoreType.DMA((blocks,)),
+            ],
         ),
-        out_shape=[jax.ShapeDtypeStruct(a, kind) for a, kind in outs],
+        out_shape=list(out_shapes) + [jax.ShapeDtypeStruct(a, kind) for a, kind in outs],
         compiler_params=params("arbitrary"),
         cost_estimate=SHORT,
         name="attend_back",
-    )(first, q, k, v, d_mixed, mixed, lse, tables, normal, *closing)
+    )(first, q, k, v, d_mixed, mixed, lse, tables, to_norm, vectors, normal, weight, *pieces)
+
+
+def extra_rows(lines):
+    return jnp.concatenate(lines + [jnp.zeros((EXTRA - len(lines), 128), F32)], axis=0).astype(LOW)
 
 
 def mlp_kernel(plan, out_plan, count, out_count, joined, chunk, order, *refs):
@@ -557,8 +577,8 @@
     mats, rest = rest[: 1 if joined else 3], rest[1 if joined else 3 :]
     parts, rest = rest[:out_count], rest[out_count:]
     d_mixed, to_norm, rest = rest[0], rest[1], rest[2:]
-    grads, rest = rest[: 1 if joined else 2], rest[1 if joined else 2 :]
-    g_out, sums, normal, cot, active, d_up, own_mixed, staged, x_sems, cot_sems, out_sems = rest
+    grads, rest = rest[: 1 if joined else 3], rest[1 if joined else 3 :]
+    sums, normal, cot, active, d_up, own_mixed, g_out, staged, x_sems, cot_sems, out_sems = rest
     step = pl.program_id(0)
     steps = len(plan)
     span, width = own_mixed.shape[0] // steps, own_mixed.shape[1]
@@ -607,7 +627,7 @@
         d_h = dot(d_up[here, :], up, NT)
         sums[1:2, :model] += jnp.sum(d_h, axis=0, keepdims=True)
         sums[2:3, :model] += jnp.sum(d_h * n, axis=0, keepdims=True)
-        to_norm[...] = d_h * vectors[2:3, :]
+        to_norm[...] = (d_h * vectors[2:3, :]).astype(LOW)
 
         @pl.when(step == 0)
         def _():
@@ -626,15 +646,23 @@
 
         up_cols = pl.ds(pl.multiple_of(at * (model // many), 128), model // many)
         down_cols = pl.ds(pl.multiple_of(at * (units // many), 128), units // many)
+        out_rows = pl.ds(pl.multiple_of(at * (width // many), 16), width // many)
         up_grad = dot(normal[:, up_cols], d_up[...], TN).astype(LOW)
         down_grad = dot(active[:, down_cols], cot[...], TN).astype(LOW)
         if joined:
             block = grads[0].shape[0]
             grads[0][:, cuts[0] : cuts[1], :] = up_grad.reshape(block, cuts[1], units)
             grads[0][:, cuts[1] : cuts[2], :] = down_grad.reshape(block, cuts[2] - cuts[1], model)
+            grads[0][:, cuts[2] : cuts[3], :] = g_out[out_rows, :].reshape(block, cuts[3] - cuts[2], model)
+            grads[0][:, cuts[3] :, :] = jnp.zeros((block, EXTRA, model), LOW)
+            for place in range(block):
+                lanes = pl.ds(pl.multiple_of((at * block + place) * 128, 128), 128)
+                lines = [sums[row : row + 1, lanes] for row in (2, 1, 3, 0)]
+                grads[0][place, cuts[3] :, :128] = extra_rows(lines)
         else:
             grads[0][...] = up_grad
             grads[1][...] = down_grad
+            grads[2][...] = g_out[out_rows, :]
 
     @pl.when(step == pl.num_programs(0) - 1)
     def _():
@@ -649,15 +677,14 @@
     plan, out_plan = plan_of(x_pieces, span), plan_of(out_shapes, span)
     steps, many = len(plan), 4
     count = len(x_pieces)
-    here = lambda i, o: (jnp.minimum(i, steps - 1), 0)
     there = lambda i, o: (o[jnp.minimum(i, steps - 1)], 0)
     later = lambda i, o: (jnp.maximum(i - steps, 0), 0)
     if joined:
         groups = mats[0].shape[0]
-        grads = [(groups, (model + units) // groups, model)]
+        grads = [(groups, (model + units + width) // groups + EXTRA, model)]
         grad_specs = [pl.BlockSpec((groups // many,) + grads[0][1:], lambda i, o: (jnp.maximum(i - steps, 0), 0, 0))]
     else:
-        grads = [(model, units), (units, model)]
+        grads = [(model, units), (units, model), (width, model)]
         grad_specs = [pl.BlockSpec((a // many, b), later) for a, b in grads]
     sums = (8, max(model, units))
     return pl.pallas_call(
@@ -669,15 +696,16 @@
             + [whole((rows, width)), whole(vectors.shape)]
             + [pl.BlockSpec(m.shape, lambda *_: (0, 0, 0), pipeline_mode=pl.Buffered(1)) for m in mats],
             out_specs=[HBM] * len(out_shapes)
-            + [pl.BlockSpec((span, width), there), pl.BlockSpec((span, model), here)]
+            + [pl.BlockSpec((span, width), there), pl.BlockSpec((span, model), there)]
             + grad_specs
-            + [whole((width, model)), whole(sums)],
+            + [whole(sums)],
             scratch_shapes=[
                 pltpu.VMEM((rows, model), LOW),
                 pltpu.VMEM((rows, model), LOW),
                 pltpu.VMEM((rows, units), LOW),
                 pltpu.VMEM((rows, units), LOW),
                 pltpu.VMEM((rows, width), LOW),
+                pltpu.VMEM((width, model), LOW),
                 pltpu.VMEM((rows, model), LOW),
                 pltpu.SemaphoreType.DMA((steps, 2)),
                 pltpu.SemaphoreType.DMA((steps, 2)),
@@ -685,8 +713,8 @@
             ],
         ),
         out_shape=list(out_shapes)
-        + [jax.ShapeDtypeStruct((rows, width), LOW), jax.ShapeDtypeStruct((rows, model), F32)]
-        + [jax.ShapeDtypeStruct(g, LOW) for g in grads + [(width, model)]]
+        + [jax.ShapeDtypeStruct((rows, width), LOW), jax.ShapeDtypeStruct((rows, model), LOW)]
+        + [jax.ShapeDtypeStruct(g, LOW) for g in grads]
         + [jax.ShapeDtypeStruct(sums, F32)],
         compiler_params=params("arbitrary"),
         cost_estimate=SHORT,
@@ -694,134 +722,62 @@
     )(order, *x_pieces, *cot_pieces, mixed, vectors, *mats)
 
 
-def close_kernel(plan, many, parts, summed, joined, merges, order, *refs):
-    xs, refs = refs[:many], refs[many:]
-    d_rows, (to_norm, vectors, weight), refs = refs[:parts], refs[parts : parts + 3], refs[parts + 3 :]
-    added, refs = refs[:summed], refs[summed:]
-    come, refs = refs[: len(merges)], refs[len(merges) :]
-    count = len(plan) // joined
-    outs, output, (sums, x, e_low) = refs[:count], refs[count:-3], refs[-3:]
-    step = pl.program_id(0)
-
-    @pl.when(step == 0)
-    def _():
-        sums[...] = jnp.zeros_like(sums)
-
-    for at, (piece, _, _) in enumerate(plan):
-
-        @pl.when(step == at)
-        def _():
-            x[...] = xs[piece][...]
-
-    model = x.shape[1]
-    rows = d_rows[0][...]
-    e, gain, bias = closed_rows(x[...], rows, to_norm[...], vectors, weight[...].reshape(model, rows.shape[1]))
-    sums[0:1, :] += gain
-    sums[1:2, :] += bias
-    e_low[...] = e
-    for at in range(len(plan)):
-
-        @pl.when(step == at)
-        def _():
-            e = e_low[...]
-            if at in merges:
-                e = e + come[merges.index(at)][...].astype(F32)
-            low = at % joined * BLOCK
-            outs[at // joined][low : low + BLOCK, :] = e.astype(LOW)
-            if summed and at >= len(plan) - 2:
-                total = x[...].astype(F32) + vectors[4:5, :] + vectors[5:6, :]
-                for ref in added:
-                    total = total + ref[...].astype(F32)
-                output[0][...] = total.astype(LOW)
-
-
-def call_close(order, pieces, plan, d_rows, to_norm, vectors, weight, span, cost=SHORT, added=(), joined=2, merges=(), come=()):
-    model = pieces[0].shape[1]
-    width3 = sum(d.shape[1] for d in d_rows)
-    per = span // BLOCK
-    steps = len(plan)
-
-    def pick(values, i):
-        value = jnp.int32(values[-1])
-        for at in range(len(values) - 1):
-            value = jnp.where(i == at, jnp.int32(values[at]), value)
-        return value
-
-    def block_of(piece):
-        reads = [(at, start // BLOCK) for at, (index, start, _) in enumerate(plan) if index == piece]
-        values = [next((b for a, b in reversed(reads) if a <= at), reads[0][1]) for at in range(steps)]
-        return lambda i, o: (pick(values, i), 0)
-
-    places = [low // BLOCK for _, _, low in plan]
-    here = lambda i, o: (pick(places, i), 0)
-    there = lambda i, o: (o[pick(places, i) // per] * per + pick(places, i) % per, 0)
-    return pl.pallas_call(
-        functools.partial(close_kernel, plan, len(pieces), len(d_rows), len(added), joined, merges),
-        grid_spec=pltpu.PrefetchScalarGridSpec(
-            num_scalar_prefetch=1,
-            grid=(steps,),
-            in_specs=[pl.BlockSpec((BLOCK, model), block_of(piece)) for piece in range(len(pieces))]
-            + [pl.BlockSpec((BLOCK, d.shape[1]), there) for d in d_rows]
-            + [pl.BlockSpec((BLOCK, model), here), whole(vectors.shape), whole(weight.shape[:2] + (width3,))]
-            + [pl.BlockSpec((BLOCK, model), lambda i, o: (jnp.maximum(i - (steps - 2), 0), 0))] * len(added)
-            + [whole((BLOCK, model))] * len(come),
-            out_specs=[whole((joined * BLOCK, model))] * (steps // joined)
-            + [pl.BlockSpec((BLOCK, model), lambda i, o: (jnp.maximum(i - (steps - 2), 0), 0))] * bool(added)
-            + [whole((8, model))],
-            scratch_shapes=[pltpu.VMEM((BLOCK, model), LOW), pltpu.VMEM((BLOCK, model), F32)],
-        ),
-        out_shape=[jax.ShapeDtypeStruct((joined * BLOCK, model), LOW)] * (steps // joined)
-        + [jax.ShapeDtypeStruct((2 * BLOCK, model), LOW)] * bool(added)
-        + [jax.ShapeDtypeStruct((8, model), F32)],
-        compiler_params=params("arbitrary"),
-        cost_estimate=cost,
-        name="close",
-    )(order, *pieces, *d_rows, to_norm, vectors, weight, *added, *come)
-
-
-def finish_kernel(base, *refs):
-    *parts, out = refs
-    for at in range(2):
+def finish_kernel(shifts, wholes, base, *refs):
+    refs, out = refs[:-1], refs[-1]
+    shift, refs = refs[:shifts], refs[shifts:]
+    common, parts = refs[:wholes], refs[wholes:]
+    total = base[...].astype(F32)
+    for ref in shift:
+        total = total + ref[4:5, :] + ref[5:6, :]
+    for ref in common:
+        total = total + ref[...].astype(F32)
+    if not parts:
+        out[...] = total.astype(LOW)
+    for at in range(2 if parts else 0):
 
         @pl.when(pl.program_id(0) == at)
         def _():
-            total = base[...].astype(F32)
-            for part in parts[at::2]:
-                total = total + part[...].astype(F32)
-            out[...] = total.astype(LOW)
-
-
-def call_finish(base, parts):
+            more = total
+            for ref in parts[at::2]:
+                more = more + ref[...].astype(F32)
+            out[...] = more.astype(LOW)
+
+
+def call_finish(base, common, parts, vectors=(), cost=SHORT):
     rows, model = base.shape
     block = pl.BlockSpec((rows // 2, model), lambda i: (i, 0))
     return pl.pallas_call(
-        finish_kernel,
+        functools.partial(finish_kernel, len(vectors), len(common)),
         grid=(2,),
-        in_specs=[block] + [whole((rows // 2, model))] * len(parts),
+        in_specs=[block] + [whole(v.shape) for v in vectors] + [block] * len(common) + [whole((rows // 2, model))] * len(parts),
         out_specs=block,
         out_shape=jax.ShapeDtypeStruct((rows, model), LOW),
         compiler_params=params("arbitrary"),
-        cost_estimate=SHORT,
+        cost_estimate=cost,
         name="finish",
-    )(base, *parts)
+    )(base, *vectors, *common, *parts)
 
 
 def cut_kernel(members, member, first, second, third, *out):
-    pieces, down = out[:members], out[members]
-    shard = pieces[0].shape[0]
+    pieces, (down, line) = out[:members], out[members:]
     columns = first.shape[1]
+    shard = pieces[0].shape[0] - EXTRA
+    low = members * shard
     for bit, piece in enumerate(pieces):
         rows = pl.ds(pl.multiple_of((member[0] ^ bit) * shard, shard), shard)
-        piece[:, :columns] = first[rows, :]
-        piece[:, columns:] = (second[rows, :].astype(F32) + third[rows, :].astype(F32)).astype(LOW)
-    low = members * shard
+        piece[:shard, :columns] = first[rows, :]
+        piece[:shard, columns:] = (second[rows, :].astype(F32) + third[rows, :].astype(F32)).astype(LOW)
+        piece[shard:, :columns] = first[first.shape[0] - EXTRA :, :]
+        piece[shard:, columns:] = (second[low:, :].astype(F32) + third[low:, :].astype(F32)).astype(LOW)
     down[...] = first[low : low + down.shape[0], :].astype(F32)
+    line[...] = first[first.shape[0] - EXTRA :, :128].astype(F32)[3:4, :]
 
 
 def call_cut(member, first, second, third, members, shard):
     columns = first.shape[1]
-    shapes = [jax.ShapeDtypeStruct((shard, columns + second.shape[1]), LOW)] * members + [
-        jax.ShapeDtypeStruct((first.shape[0] - members * shard, columns), F32),
+    shapes = [jax.ShapeDtypeStruct((shard + EXTRA, columns + second.shape[1]), LOW)] * members + [
+        jax.ShapeDtypeStruct((first.shape[0] - (members + 1) * shard - EXTRA, columns), F32),
+        jax.ShapeDtypeStruct((1, 128), F32),
     ]
     return pl.pallas_call(
         functools.partial(cut_kernel, members),
@@ -838,73 +794,33 @@
     )(member, first, second, third)
 
 
-def join_kernel(places, member, *refs):
-    pieces, outs = refs[:-2], refs[-2:]
+def join_kernel(places, second, member, *refs):
+    pieces, outs, total = refs[:-3], refs[-3:-1], refs[-1]
+    shard = outs[0].shape[0]
     for bit, piece in enumerate(pieces):
         for block, (index, column, stride) in enumerate(places):
             start = pl.multiple_of(column + (member[0] ^ bit) * stride, 128)
-            outs[index][:, pl.ds(start, 128)] = piece[:, block * 128 : (block + 1) * 128].astype(F32)
-
-
-def call_join(member, pieces, places, columns):
-    shard = pieces[0].shape[0]
+            outs[index][:, pl.ds(start, 128)] = piece[:shard, block * 128 : (block + 1) * 128].astype(F32)
+    for row, low in ((0, 0), (8, second)):
+        total[row : row + 8, :] = sum(piece[shard:, low : low + 128].astype(F32) for piece in pieces)[:8, :]
+
+
+def call_join(member, pieces, places, second, columns):
+    shard = pieces[0].shape[0] - EXTRA
+    shapes = [(shard, c) for c in columns] + [(16, 128)]
     return pl.pallas_call(
-        functools.partial(join_kernel, tuple(places)),
+        functools.partial(join_kernel, tuple(places), second),
         grid_spec=pltpu.PrefetchScalarGridSpec(
             num_scalar_prefetch=1,
             grid=(1,),
             in_specs=[whole(p.shape) for p in pieces],
-            out_specs=[whole((shard, c)) for c in columns],
+            out_specs=[whole(a) for a in shapes],
         ),
-        out_shape=[jax.ShapeDtypeStruct((shard, c), F32) for c in columns],
+        out_shape=[jax.ShapeDtypeStruct(a, F32) for a in shapes],
         compiler_params=params("arbitrary"),
         cost_estimate=SHORT,
         name="join",
     )(member, *pieces)
-
-
-def bundle_kernel(members, halves, member, two, *refs):
-    *ones, out, wide = refs
-    thirds, ones = ones[:halves], ones[halves:]
-    groups = out.shape[0] // members
-    out[...] = jnp.zeros_like(out)
-    wide[...] = jnp.zeros_like(wide)
-    one = functools.reduce(lambda a, b: a + b, [one[0:2, :] for one in ones])
-    lines = [one[0:1, :], one[1:2, :], two[2:3, :], two[1:2, :], two[3:4, :]]
-    size = thirds[0].shape[1] // 3
-    per_member = halves * size // 128
-    for part in range(3):
-        for half, third in enumerate(thirds):
-            for at in range(size // 128):
-                row = (part * members + member[0]) * per_member + half * (size // 128) + at
-                low = part * size + at * 128
-                wide[pl.ds(row, 1), :] = third[0:1, low : low + 128]
-    for group in range(groups):
-        lanes = slice(group * 128, (group + 1) * 128)
-        for to in range(members):
-            device = group * members + to
-            for row, line in enumerate(lines):
-                out[device, row : row + 1, :] = line[:, lanes]
-            out[device, 5:8, :] = wide[3 * group : 3 * group + 3, :]
-            out[device, 8:9, :] = jnp.where(member[0] == to, two[0:1, lanes], 0.0)
-
-
-def call_bundle(member, members, groups, two, thirds, ones):
-    shape = (groups * members, 16, 128)
-    return pl.pallas_call(
-        functools.partial(bundle_kernel, members, len(thirds)),
-        grid_spec=pltpu.PrefetchScalarGridSpec(
-            num_scalar_prefetch=1,
-            grid=(1,),
-            in_specs=[whole(a.shape) for a in (two, *thirds, *ones)],
-            out_specs=whole(shape),
-            scratch_shapes=[pltpu.VMEM((3 * groups, 128), F32)],
-        ),
-        out_shape=jax.ShapeDtypeStruct(shape, F32),
-        compiler_params=params("arbitrary"),
-        cost_estimate=SHORT,
-        name="bundle",
-    )(member, two, *thirds, *ones)
 
 
 def across(array, bit):
@@ -1055,8 +971,7 @@
     order = sources ^ member if members == 4 else sources
     doc_row = doc_ids[0]
     first = jnp.sum((doc_row[None, :] < doc_row[:, None]).astype(jnp.int32), axis=1)
-    marks = [group, member ^ 3] if members == 4 else [group, member]
-    first = jnp.concatenate([first] + [a.astype(jnp.int32).reshape(1) for a in marks])
+    first = jnp.concatenate([first, group.astype(jnp.int32).reshape(1), order])
     tables = rotary_tables(stream)
 
     q, k, v, normal = call_qkv(order, x_pieces, vectors, w_first, tables, rows, width)
@@ -1070,81 +985,65 @@
     )
     count = len(out_shapes)
     parts, (d_mixed, to_norm), grads, sums_two = results[:count], results[count : count + 2], results[count + 2 : -1], results[-1]
-    *grads, g_out = grads
     scattered = scatter_dp(grads[0].reshape(-1, model)) if paired else None
-    g_out = scatter_dp(g_out)
 
     summed = reduce_direct(parts)
-    closing = (x_pieces[6], x_pieces[7], to_norm, vectors, w_first) if members == 4 else ()
-    d_qkv, even, odd, sums_qkv, *three = call_bwd(first, q, k, v, d_mixed, mixed, lse, tables, normal, groups, closing)
-    d_qkv, sums_qkv, halves = [d_qkv], [sums_qkv], 1
-    blocks, far, bit = even, hop(odd, 1), 2
+    sizes = [half] * (2 * members) if members == 4 else [stream]
+    *pieces, even, odd, sums_qkv, ones = call_bwd(
+        first, q, k, v, d_mixed, mixed, lse, tables, to_norm, vectors, normal, w_first, x_pieces,
+        [jax.ShapeDtypeStruct((size, model), LOW) for size in sizes], groups, rows, paired,
+    )
+    far, bit = hop(odd, 1), 2
     if members == 4:
-        close = lambda pieces, *more: call_close(
-            order, [x_pieces[p] for p in pieces], [(i, 0, p * half) for i, p in enumerate(pieces)],
-            d_qkv, to_norm, vectors, w_first, rows, *more,
-        )
-        three_low, three_high, ones_a = three
+        add = lambda a, b: (a.astype(F32) + b.astype(F32)).astype(LOW)
+        own_low, own_high, one_low, one_high, two_low, two_high, three_low, three_high = pieces
         come = across(three_high, 2), across(three_low, 1)
-        to_norm = behind(to_norm, *summed[1:])
-        one_low, two_high, ones_b = close((2, 5), LONG, (), 1)
         near = across(one_low, 1), across(two_high, 2)
-        blocks, far, send = scatter_step(blocks, behind(far, one_low), bit)
-        to_norm = behind(to_norm, send, one_low, *(() if scattered is None else (scattered,)))
-        one_high, two_low, ones_c = close((3, 4), SHORT, (), 1, (0, 1), come)
-        if groups > 4:
-            blocks, far, send = scatter_step(blocks, behind(far, one_high), 2 * bit)
-        near += across(behind(one_high, send), 1), across(behind(two_low, send), 2)
-        to_norm = behind(to_norm, send, one_high)
-        own_low, own_high, output, ones_d = close((0, 1), SHORT, summed, 1)
-        ones = [ones_a, ones_b, ones_c, ones_d]
-        g_out = swap_owner(behind(g_out, own_low), True)
-        bit = 8 if groups > 4 else 4
-    else:
-        plan = [(0, low, low) for low in range(0, stream, BLOCK)]
-        *final, ones = call_close(order, x_pieces, plan, d_qkv, to_norm, vectors, w_first, rows)
-        ones = [ones]
-        own = reduce_direct([jnp.concatenate(final, axis=0)])[0]
-        own_low, own_high, near = own[:half], own[half:], None
-        output = (tokens.astype(F32) + summed[0].astype(F32) + vectors[4:5, :] + vectors[5:6, :]).astype(LOW)
-
+        output = call_finish(tokens, summed, (), (vectors,), LONG)
+        blocks, far, send = scatter_step(even, behind(far, output), bit)
+        come = behind_all(come, send)
+        one_high, two_low = add(one_high, come[0]), add(two_low, come[1])
+        near += across(one_high, 1), across(two_low, 2)
+        parts = own_low, own_high, near[0], near[2], near[3], near[1]
+        blocks, far, send = scatter_step(blocks, behind(far, one_high, two_low), 2 * bit)
+        bit = 8
+    if members != 4:
+        blocks, far, _ = scatter_step(even, far, bit)
+        bit = 4
+        output = call_finish(tokens, summed, (), (vectors,))
+        total = reduce_direct(pieces)[0]
+        parts = total[:half], total[half:]
     while blocks.shape[0] > 1:
         (blocks, far, _), bit = scatter_step(blocks, far, bit), 2 * bit
-    if near is not None:
-        far = behind(far, *near[:2])
     g_qkv = blocks[0], far[0]
-    if near is None:
-        parts = own_low, own_high
-    else:
-        parts = own_low, own_high, near[0], near[2], near[3], near[1]
     place = group * members + member
     if paired:
-        *mixed_pieces, g_down = call_cut(me, scattered, *g_qkv, members, shard)
+        *mixed_pieces, g_down, up_shift = call_cut(me, scattered, *g_qkv, members, shard)
+        g_out = scattered[scattered.shape[0] - shard - EXTRA : scattered.shape[0] - EXTRA]
+        g_out = swap_owner(behind(g_out, g_down), True)
+        grad_tokens = call_finish(behind(cotangent, g_down), (), parts)
         places = [(0, b * members * units_dev, units_dev) for b in range(groups)]
         places += [(1, part * model + low, width) for part in range(3) for low in range(0, width, 128)]
         arrived = [mixed_pieces[0]] + [across(mixed_pieces[bit], bit) for bit in range(1, members)]
-        g_up, g_qkv = call_join(me, arrived, places, (up_weight.shape[1], qkv_weight.shape[1]))
-        grad_tokens = call_finish(behind(cotangent, g_up), parts)
-        ready = behind(call_bundle(me, members, groups, sums_two, sums_qkv, ones), far, *parts)
-        totals = jnp.sum(lax.all_to_all(ready, ALL, split_axis=0, concat_axis=0), axis=0)
+        g_up, g_qkv, totals = call_join(me, arrived, places, model, (up_weight.shape[1], qkv_weight.shape[1]))
         size = model // devices
-        mine = [a[0] for a in jnp.split(lax.dynamic_slice_in_dim(totals[:5], member * size, size, 1), 5)]
-        mine += [lax.dynamic_slice_in_dim(totals[5:8].reshape(-1), member * 3 * size, 3 * size), totals[8]]
+        lines = lax.dynamic_slice_in_dim(totals, member * size, size, 1)
+        mine = [lines[row] for row in (8, 9, 0, 1, 2)]
+        mine += [lax.dynamic_slice_in_dim(totals[10:13].reshape(-1), member * 3 * size, 3 * size), up_shift[0]]
     else:
-        g_up, g_down = [scatter_dp(g) for g in grads]
-        grad_tokens = call_finish(cotangent, parts)
+        grad_tokens = call_finish(cotangent, (), parts)
+        g_up, g_down, g_out = [scatter_dp(g) for g in grads]
         g_down = g_down.astype(F32)
         g_up = exchange(g_up.reshape(members, shard, units))
         g_up = g_up.reshape(members, shard, groups, units_dev).transpose(1, 2, 0, 3).reshape(shard, -1).astype(F32)
         g_qkv = (g_qkv[0].astype(F32) + g_qkv[1].astype(F32)).astype(LOW)
-        g_qkv = exchange(g_qkv.reshape(members, shard, 3 * width)).reshape(members, shard, halves, 3, width // halves)
+        g_qkv = exchange(g_qkv.reshape(members, shard, 3 * width)).reshape(members, shard, 1, 3, width)
         g_qkv = g_qkv.transpose(1, 3, 0, 2, 4).reshape(shard, -1).astype(F32)
-        thirds = jnp.concatenate([a[0].reshape(3, 1, width // halves) for a in sums_qkv], axis=2)
+        thirds = jnp.concatenate([a[0].reshape(3, 1, width) for a in [sums_qkv]], axis=2)
         wide_qkv = lax.dynamic_update_index_in_dim(jnp.zeros((3, members, width), F32), thirds, member, 1)
         wide_up = lax.dynamic_update_index_in_dim(
             jnp.zeros((groups, members, units_dev), F32), sums_two[0, :units].reshape(groups, 1, units_dev), member, 1
         )
-        ones = sum(ones)
         summed = total_over_all(jnp.concatenate([
             ones[0], ones[1], sums_two[2], sums_two[1], sums_two[3], wide_qkv.reshape(-1), wide_up.reshape(-1),
         ]))
@@ -1153,7 +1052,7 @@
             mine.append(lax.dynamic_slice_in_dim(summed, start + place * (size // devices), size // devices))
             start += size
     gain_1, bias_1, gain_2, bias_2, end_bias, qkv_shift, up_shift = mine
-    g_out = (g_out if members == 4 else swap_owner(g_out, True)).astype(F32)
+    g_out = (g_out if paired else swap_owner(g_out, True)).astype(F32)
     return (
         output, grad_tokens, gain_1, bias_1, gain_2, bias_2, g_qkv, qkv_shift, g_out, end_bias, g_up, up_shift, g_down, end_bias,
     )

time: 268 us -> 261 us (0.974)
  Pallas kernels: 148 us -> 134 us
  waiting for transfers between devices: 38.7 us -> 46.2 us
  local copies, waits for them, and re-layouts: 9.67 us -> 15.6 us
  starting transfers between devices: 48 us -> 42.2 us
    pallas_call x7 -> x4, Pallas kernels: 66.6 us -> 53.4 us  [the longest x1 44 us: call_bwd(): pl.pallas_call(functools.partial(bwd_kernel, plan, span // BLOCK, groups,...]
    ppermute x3, waiting for transfers between devices: 1.16 us -> 9.03 us  [hop(): lax.ppermute(array, 'dp', [(i, i ^ bit) for i in range(lax.axis_size('dp'...]
    unnamed x61 -> x59, local copies, waits for them, and re-layouts: 3.19 us -> 7.29 us
    all_to_all x1 -> x0, starting transfers between devices: 2.87 us -> none  [local(): lax.all_to_all(ready, ALL, split_axis=0, concat_axis=0)]
  transfers between devices with their start and end apart: 37 -> 35, of which waited for: 13 -> 9; matrix products, arithmetic and copies ran while one was open for 3% -> 3% of each run, Pallas kernels for 39% -> 34%
where the time goes in v5:
time: 261 us; the launch traced here: 258 us
  Pallas kernels  134 us (51%)
  waiting for transfers between devices  46.2 us (18%)
  starting transfers between devices  42.2 us (16%)
  local copies, waits for them, and re-layouts  15.6 us (6%)
  between operations  14.1 us (5%)
  other arithmetic  5.89 us (2%)
    pallas_call x1, Pallas kernels, call_bwd(): pl.pallas_call(functools.partial(bwd_kernel, plan, span // BLOCK, groups,...  44 us
    pallas_call x1, Pallas kernels, call_mlp(): pl.pallas_call(functools.partial(mlp_kernel, plan, out_plan, count, len(o...  41 us
    ppermute x27, starting transfers between devices, across(): return lax.ppermute(array, 'fsdp', [(i, i ^ bit) for i in range(size)])  37.2 us
    ppermute x27, waiting for transfers between devices, across(): return lax.ppermute(array, 'fsdp', [(i, i ^ bit) for i in range(size)])  37.1 us
    pallas_call x1, Pallas kernels, call_fwd(): pl.pallas_call(fwd_kernel, grid_spec=pltpu.PrefetchScalarGridSpec(num_sca...  20.4 us
    pallas_call x1, Pallas kernels, call_qkv(): pl.pallas_call(functools.partial(qkv_kernel, plan, len(pieces)), grid_spe...  11.7 us
    ppermute x3, waiting for transfers between devices, hop(): lax.ppermute(array, 'dp', [(i, i ^ bit) for i in range(lax.axis_size('dp'...  9.03 us
    unnamed x59, local copies, waits for them, and re-layouts  7.29 us
  transfers between devices with their start and end apart: 35, of which 9 were waited for; matrix products, arithmetic and copies ran while one was open for 3% of the time, Pallas kernels for 34%

profile of v5, /device:TPU:0, one launch (start us, length us, event | category | flops | bytes accessed | tf_op | source)
XLA Modules:
  0.0 258.2 jit_solution(4160602493858445267)
XLA Ops:
  10.3 1.9 pack.1
  12.2 2.9 %collective-permute-start.1 = (bf16[32,1920]{1,0:T(8,128)(2,1)}, bf16[32,1920]{1,0:T(8,128)(2,1)S(1)}, u32[]{:S(2)}, u32[]{:S(2)}) collective-permute-start(bf16[32,1920]{1,0:T(8,128)(2,1)} %get-tuple-element.71), channel_id=1, source_target_pairs={{0,1},{1,0},{2,3},{3,2},{4,5},{5,4},{6,7},{7,6},{8,9},{9,8},{10,11... | collective-permute-start | bytes 368648 | tf_op jit(solution)/shard_map/ppermute | solution.py:828
  19.2 3.7 %collective-permute-done.2.refs_2_ = bf16[32,1920]{1,0:T(8,128)(2,1)S(1)} collective-permute-done((bf16[32,1920]{1,0:T(8,128)(2,1)}, bf16[32,1920]{1,0:T(8,128)(2,1)S(1)}, u32[]{:S(2)}, u32[]{:S(2)}) %collective-permute-start.2) | collective-permute-done | bytes 122912 | tf_op jit(solution)/shard_map/ppermute | solution.py:828
  24.1 1.9 place.1
  26.1 1.9 pad_maximum_fusion
  28.2 4.4 %collective-permute-start.7 = (bf16[256,1024]{1,0:T(8,128)(2,1)S(1)}, bf16[256,1024]{1,0:T(8,128)(2,1)S(1)}, u32[]{:S(2)}, u32[]{:S(2)}) collective-permute-start(bf16[256,1024]{1,0:T(8,128)(2,1)S(1)} %get-tuple-element.79.refs_1_.rest_1_), channel_id=1, source_target_pairs={{0,2},{1,3},{2,0},{3,1},{4,6},{5,7},{6,4},{7,5},{8,10},{9,11},{10,... | collective-permute-start | bytes 1572872 | tf_op jit(solution)/shard_map/ppermute | solution.py:828
  32.6 3.3 %collective-permute-start.4 = (bf16[256,1024]{1,0:T(8,128)(2,1)S(1)}, bf16[256,1024]{1,0:T(8,128)(2,1)S(1)}, u32[]{:S(2)}, u32[]{:S(2)}) collective-permute-start(bf16[256,1024]{1,0:T(8,128)(2,1)S(1)} %get-tuple-element.78.refs_0_.rest_0_), channel_id=1, source_target_pairs={{0,1},{1,0},{2,3},{3,2},{4,5},{5,4},{6,7},{7,6},{8,9},{9,8},{10,11... | collective-permute-start | bytes 1572872 | tf_op jit(solution)/shard_map/ppermute | solution.py:828
  36.1 9.4 %collective-permute-done.7.refs_5_.rest_5_ = bf16[256,1024]{1,0:T(8,128)(2,1)S(1)} collective-permute-done((bf16[256,1024]{1,0:T(8,128)(2,1)S(1)}, bf16[256,1024]{1,0:T(8,128)(2,1)S(1)}, u32[]{:S(2)}, u32[]{:S(2)}) %collective-permute-start.7) | collective-permute-done | bytes 524320 | tf_op jit(solution)/shard_map/ppermute | solution.py:828
  45.4 3.3 %collective-permute-start.9 = (bf16[256,1024]{1,0:T(8,128)(2,1)S(1)}, bf16[256,1024]{1,0:T(8,128)(2,1)S(1)}, u32[]{:S(2)}, u32[]{:S(2)}) collective-permute-start(bf16[256,1024]{1,0:T(8,128)(2,1)S(1)} %collective-permute-done.7.refs_5_.rest_5_), channel_id=1, source_target_pairs={{0,1},{1,0},{2,3},{3,2},{4,5},{5,4},{6,7},{7,6},{8,9},{9,8},{10,11... | collective-permute-start | bytes 1572872 | tf_op jit(solution)/shard_map/ppermute | solution.py:828
  48.8 2.0 collective-permute-start.8
  50.8 2.3 fusion.1
  53.1 6.9 %collective-permute-done.5.refs_3_.rest_3_ = bf16[256,1024]{1,0:T(8,128)(2,1)S(1)} collective-permute-done((bf16[256,1024]{1,0:T(8,128)(2,1)S(1)}, bf16[256,1024]{1,0:T(8,128)(2,1)S(1)}, u32[]{:S(2)}, u32[]{:S(2)}) %collective-permute-start.5) | collective-permute-done | bytes 524320 | tf_op jit(solution)/shard_map/ppermute | solution.py:828
  60.0 8.1 %collective-permute-done.9.refs_7_.rest_7_ = bf16[256,1024]{1,0:T(8,128)(2,1)S(1)} collective-permute-done((bf16[256,1024]{1,0:T(8,128)(2,1)S(1)}, bf16[256,1024]{1,0:T(8,128)(2,1)S(1)}, u32[]{:S(2)}, u32[]{:S(2)}) %collective-permute-start.9) | collective-permute-done | bytes 524320 | tf_op jit(solution)/shard_map/ppermute | solution.py:828
  76.0 11.7 %qkv.3 = (bf16[2048,256]{1,0:T(8,128)(2,1)}, bf16[2048,256]{1,0:T(8,128)(2,1)}, bf16[2048,256]{1,0:T(8,128)(2,1)}, bf16[2048,1024]{1,0:T(8,128)(2,1)}) custom-call(s32[4]{0:T(128)} %iota_xor_fusion.order, bf16[256,1024]{1,0:T(8,128)(2,1)} %copy-done.1, bf16[256,1024]{1,0:T(8,128)(2,1)} %copy-done, bf16[256,1024]{1,0:T(8,128)(2,1)} %copy-done.3, ...), custom_call_target="tpu_custom_call" | custom-call | tf_op jit(solution)/shard_map/qkv/pallas_call | solution.py:260
  90.3 20.4 %attend.1 = (f32[2048,256]{1,0:T(8,128)}, bf16[2048,256]{1,0:T(8,128)(2,1)}, f32[4,2048]{1,0:T(4,128)}) custom-call(s32[13]{0:T(128)} %pad_add_fusion.first, bf16[2048,256]{1,0:T(8,128)(2,1)} %get-tuple-element.82.q, bf16[2048,256]{1,0:T(8,128)(2,1)} %get-tuple-element.85.k, bf16[2048,256]{1,0:T(8,128)(2,1)} %get-tuple-element.86.v), custom_call_target="tpu_custom_call" | custom-call | tf_op jit(solution)/shard_map/attend/pallas_call | solution.py:352
  111.8 41.0 %mlp.1 = (bf16[512,1024]{1,0:T(8,128)(2,1)}, bf16[512,1024]{1,0:T(8,128)(2,1)}, bf16[512,1024]{1,0:T(8,128)(2,1)}, bf16[512,1024]{1,0:T(8,128)(2,1)}, bf16[2048,...) custom-call(s32[4]{0:T(128)} %iota_xor_fusion.order, ...), custom_call_target="tpu_custom_call" | custom-call | tf_op jit(solution)/shard_map/mlp/pallas_call | solution.py:690
  156.3 44.0 %attend_back.1 = (bf16[256,1024]{1,0:T(8,128)(2,1)}, bf16[256,1024]{1,0:T(8,128)(2,1)}, bf16[256,1024]{1,0:T(8,128)(2,1)}, bf16[256,1024]{1,0:T(8,128)(2,1)}, bf...) custom-call(s32[13]{0:T(128)} %pad_add_fusion.first, ...), custom_call_target="tpu_custom_call" | custom-call | tf_op jit(solution)/shard_map/attend_back/pallas_call | solution.py:535
  204.6 3.8 %finish.2 = bf16[512,1024]{1,0:T(8,128)(2,1)} custom-call(bf16[512,1024]{1,0:T(8,128)(2,1)} %base.1, f32[16,1024]{1,0:T(8,128)} %vectors.1.refs_8_.refs_17_.refs_0_, bf16[512,1024]{1,0:T(8,128)(2,1)} %get-tuple-element.89.refs_1_, bf16[512,1024]{1,0:T(8,128)(2,1)} %collective-permute-done.16.refs_2_, bf16[512,1024]{1,0:T(8,128)(2,1)} %collective-permute-done.17.refs_3_, ...), custom_call_target="tpu_custom_call" | custom-call | flops 20000000000 | bytes 10000000 | tf_op jit(solution)/shard_map/finish/pallas_call | solution.py:749
  209.3 6.1 %collective-permute-done.22 = bf16[256,1024]{1,0:T(8,128)(2,1)S(1)} collective-permute-done((bf16[256,1024]{1,0:T(8,128)(2,1)}, bf16[256,1024]{1,0:T(8,128)(2,1)S(1)}, u32[]{:S(2)}, u32[]{:S(2)}) %collective-permute-start.22) | collective-permute-done | bytes 524320 | tf_op jit(solution)/shard_map/ppermute | solution.py:828
  221.3 2.1 collective-permute-start.23
  223.3 9.0 %collective-permute-done.23 = bf16[1,144,768]{2,1,0:T(8,128)(2,1)S(1)} collective-permute-done((bf16[1,144,768]{2,1,0:T(8,128)(2,1)S(1)}, bf16[1,144,768]{2,1,0:T(8,128)(2,1)S(1)}, u32[]{:S(2)}, u32[]{:S(2)}) %collective-permute-start.23) | collective-permute-done | bytes 221216 | tf_op jit(solution)/shard_map/ppermute | solution.py:867
  233.1 2.3 cut.1
  241.2 3.4 %finish.3 = bf16[512,1024]{1,0:T(8,128)(2,1)} custom-call(bf16[512,1024]{1,0:T(8,128)(2,1)} %base.2, bf16[256,1024]{1,0:T(8,128)(2,1)} %get-tuple-element.111.refs_0_, bf16[256,1024]{1,0:T(8,128)(2,1)} %get-tuple-element.112.refs_1_, bf16[256,1024]{1,0:T(8,128)(2,1)} %copy-done.10, bf16[256,1024]{1,0:T(8,128)(2,1)} %copy-done.13, ...), custom_call_target="tpu_custom_call" | custom-call | tf_op jit(solution)/shard_map/finish/pallas_call | solution.py:749
  246.3 2.2 join.1
  (142 shorter events, 46.0 us)
Async XLA Ops:
  7.2 67.1 %all-gather.5.cloned.1.call-start = ((), (), s32[]{:S(2)}) async-start(), calls=%async_computation.2 | async-start | bytes 2064384 | tf_op jit(solution)/shard_map/all_gather | solution.py:901
  26.1 84.7 %all-gather.7.cloned.1.call-start = ((), (), s32[]{:S(2)}) async-start(), calls=%async_computation.3 | async-start | bytes 5308416 | tf_op jit(solution)/shard_map/all_gather | solution.py:901
  28.0 204.3 %reduce-scatter.2.cloned.1.call-start = ((), (), s32[]{:S(2)}) async-start(), calls=%async_computation.1 | async-start | bytes 5603328 | tf_op jit(solution)/shard_map/reduce_scatter | solution.py:905
  28.2 17.2 %collective-permute-start.7 = (bf16[256,1024]{1,0:T(8,128)(2,1)S(1)}, bf16[256,1024]{1,0:T(8,128)(2,1)S(1)}, u32[]{:S(2)}, u32[]{:S(2)}) collective-permute-start(bf16[256,1024]{1,0:T(8,128)(2,1)S(1)} %get-tuple-element.79.refs_1_.rest_1_), channel_id=1, source_target_pairs={{0,2},{1,3},{2,0},{3,1},{4,6},{5,7},{6,4},{7,5},{8,10},{9,11},{10,... | collective-permute-start | bytes 1572872 | tf_op jit(solution)/shard_map/ppermute | solution.py:828
  32.6 16.1 %collective-permute-start.4 = (bf16[256,1024]{1,0:T(8,128)(2,1)S(1)}, bf16[256,1024]{1,0:T(8,128)(2,1)S(1)}, u32[]{:S(2)}, u32[]{:S(2)}) collective-permute-start(bf16[256,1024]{1,0:T(8,128)(2,1)S(1)} %get-tuple-element.78.refs_0_.rest_0_), channel_id=1, source_target_pairs={{0,1},{1,0},{2,3},{3,2},{4,5},{5,4},{6,7},{7,6},{8,9},{9,8},{10,11... | collective-permute-start | bytes 1572872 | tf_op jit(solution)/shard_map/ppermute | solution.py:828
  35.9 24.1 %collective-permute-start.5 = (bf16[256,1024]{1,0:T(8,128)(2,1)S(1)}, bf16[256,1024]{1,0:T(8,128)(2,1)S(1)}, u32[]{:S(2)}, u32[]{:S(2)}) collective-permute-start(bf16[256,1024]{1,0:T(8,128)(2,1)S(1)} %get-tuple-element.79.refs_1_.rest_1_), channel_id=1, source_target_pairs={{0,1},{1,0},{2,3},{3,2},{4,5},{5,4},{6,7},{7,6},{8,9},{9,8},{10,11... | collective-permute-start | bytes 1572872 | tf_op jit(solution)/shard_map/ppermute | solution.py:828
  35.9 24.0 %collective-permute-start.6 = (bf16[256,1024]{1,0:T(8,128)(2,1)S(1)}, bf16[256,1024]{1,0:T(8,128)(2,1)S(1)}, u32[]{:S(2)}, u32[]{:S(2)}) collective-permute-start(bf16[256,1024]{1,0:T(8,128)(2,1)S(1)} %get-tuple-element.78.refs_0_.rest_0_), channel_id=1, source_target_pairs={{0,2},{1,3},{2,0},{3,1},{4,6},{5,7},{6,4},{7,5},{8,10},{9,11},{10,... | collective-permute-start | bytes 1572872 | tf_op jit(solution)/shard_map/ppermute | solution.py:828
  45.4 22.7 %collective-permute-start.9 = (bf16[256,1024]{1,0:T(8,128)(2,1)S(1)}, bf16[256,1024]{1,0:T(8,128)(2,1)S(1)}, u32[]{:S(2)}, u32[]{:S(2)}) collective-permute-start(bf16[256,1024]{1,0:T(8,128)(2,1)S(1)} %collective-permute-done.7.refs_5_.rest_5_), channel_id=1, source_target_pairs={{0,1},{1,0},{2,3},{3,2},{4,5},{5,4},{6,7},{7,6},{8,9},{9,8},{10,11... | collective-permute-start | bytes 1572872 | tf_op jit(solution)/shard_map/ppermute | solution.py:828
  48.8 19.4 %collective-permute-start.8 = (bf16[256,1024]{1,0:T(8,128)(2,1)S(1)}, bf16[256,1024]{1,0:T(8,128)(2,1)S(1)}, u32[]{:S(2)}, u32[]{:S(2)}) collective-permute-start(bf16[256,1024]{1,0:T(8,128)(2,1)S(1)} %collective-permute-done.4.refs_2_.rest_2_), channel_id=1, source_target_pairs={{0,2},{1,3},{2,0},{3,1},{4,6},{5,7},{6,4},{7,5},{8,10},{9,11},{10,... | collective-permute-start | bytes 1572872 | tf_op jit(solution)/shard_map/ppermute | solution.py:828
  69.8 18.0 %collective-permute-start.13 = (bf16[256,1024]{1,0:T(8,128)(2,1)}, bf16[256,1024]{1,0:T(8,128)(2,1)}, u32[]{:S(2)}, u32[]{:S(2)}) collective-permute-start(bf16[256,1024]{1,0:T(8,128)(2,1)} %get-tuple-element.81.refs_9_), channel_id=1, source_target_pairs={{0,2},{1,3},{2,0},{3,1},{4,6},{5,7},{6,4},{7,5},{8,10},{9,11},{10,... | collective-permute-start | bytes 1572872 | tf_op jit(solution)/shard_map/ppermute | solution.py:828
  70.1 19.0 %collective-permute-start.10 = (bf16[256,1024]{1,0:T(8,128)(2,1)}, bf16[256,1024]{1,0:T(8,128)(2,1)}, u32[]{:S(2)}, u32[]{:S(2)}) collective-permute-start(bf16[256,1024]{1,0:T(8,128)(2,1)} %get-tuple-element.80.refs_8_), channel_id=1, source_target_pairs={{0,1},{1,0},{2,3},{3,2},{4,5},{5,4},{6,7},{7,6},{8,9},{9,8},{10,11... | collective-permute-start | bytes 1572872 | tf_op jit(solution)/shard_map/ppermute | solution.py:828
  72.0 38.7 %collective-permute-start.11 = (bf16[256,1024]{1,0:T(8,128)(2,1)}, bf16[256,1024]{1,0:T(8,128)(2,1)}, u32[]{:S(2)}, u32[]{:S(2)}) collective-permute-start(bf16[256,1024]{1,0:T(8,128)(2,1)} %get-tuple-element.81.refs_9_), channel_id=1, source_target_pairs={{0,1},{1,0},{2,3},{3,2},{4,5},{5,4},{6,7},{7,6},{8,9},{9,8},{10,11... | collective-permute-start | bytes 1572872 | tf_op jit(solution)/shard_map/ppermute | solution.py:828
  72.7 38.0 %collective-permute-start.12 = (bf16[256,1024]{1,0:T(8,128)(2,1)}, bf16[256,1024]{1,0:T(8,128)(2,1)}, u32[]{:S(2)}, u32[]{:S(2)}) collective-permute-start(bf16[256,1024]{1,0:T(8,128)(2,1)} %get-tuple-element.80.refs_8_), channel_id=1, source_target_pairs={{0,2},{1,3},{2,0},{3,1},{4,6},{5,7},{6,4},{7,5},{8,10},{9,11},{10,... | collective-permute-start | bytes 1572872 | tf_op jit(solution)/shard_map/ppermute | solution.py:828
  87.8 23.0 %collective-permute-start.15 = (bf16[256,1024]{1,0:T(8,128)(2,1)}, bf16[256,1024]{1,0:T(8,128)(2,1)S(1)}, u32[]{:S(2)}, u32[]{:S(2)}) collective-permute-start(bf16[256,1024]{1,0:T(8,128)(2,1)} %collective-permute-done.13.refs_13_), channel_id=1, source_target_pairs={{0,1},{1,0},{2,3},{3,2},{4,5},{5,4},{6,7},{7,6},{8,9},{9,8},{10,11... | collective-permute-start | bytes 1572872 | tf_op jit(solution)/shard_map/ppermute | solution.py:828
  89.2 21.6 %collective-permute-start.14 = (bf16[256,1024]{1,0:T(8,128)(2,1)}, bf16[256,1024]{1,0:T(8,128)(2,1)S(1)}, u32[]{:S(2)}, u32[]{:S(2)}) collective-permute-start(bf16[256,1024]{1,0:T(8,128)(2,1)} %collective-permute-done.10.refs_10_), channel_id=1, source_target_pairs={{0,2},{1,3},{2,0},{3,1},{4,6},{5,7},{6,4},{7,5},{8,10},{9,11},{10,... | collective-permute-start | bytes 1572872 | tf_op jit(solution)/shard_map/ppermute | solution.py:828
  152.8 48.5 %collective-permute-start.16 = (bf16[512,1024]{1,0:T(8,128)(2,1)}, bf16[512,1024]{1,0:T(8,128)(2,1)}, u32[]{:S(2)}, u32[]{:S(2)}) collective-permute-start(bf16[512,1024]{1,0:T(8,128)(2,1)} %get-tuple-element.90), channel_id=1, source_target_pairs={{0,1},{1,0},{2,3},{3,2},{4,5},{5,4},{6,7},{7,6},{8,9},{9,8},{10,11... | collective-permute-start | bytes 3145736 | tf_op jit(solution)/shard_map/ppermute | solution.py:828
  154.0 49.1 %collective-permute-start.17 = (bf16[512,1024]{1,0:T(8,128)(2,1)S(1)}, bf16[512,1024]{1,0:T(8,128)(2,1)}, u32[]{:S(2)}, u32[]{:S(2)}) collective-permute-start(bf16[512,1024]{1,0:T(8,128)(2,1)S(1)} %copy-done.27), channel_id=1, source_target_pairs={{0,2},{1,3},{2,0},{3,1},{4,6},{5,7},{6,4},{7,5},{8,10},{9,11},{10,... | collective-permute-start | bytes 3145736 | tf_op jit(solution)/shard_map/ppermute | solution.py:828
  155.6 48.5 %collective-permute-start.18 = (bf16[512,1024]{1,0:T(8,128)(2,1)}, bf16[512,1024]{1,0:T(8,128)(2,1)}, u32[]{:S(2)}, u32[]{:S(2)}) collective-permute-start(bf16[512,1024]{1,0:T(8,128)(2,1)} %get-tuple-element.92), channel_id=1, source_target_pairs={{0,3},{1,2},{2,1},{3,0},{4,7},{5,6},{6,5},{7,4},{8,11},{9,10},{10,... | collective-permute-start | bytes 3145736 | tf_op jit(solution)/shard_map/ppermute | solution.py:828
  200.4 15.0 %collective-permute-start.22 = (bf16[256,1024]{1,0:T(8,128)(2,1)}, bf16[256,1024]{1,0:T(8,128)(2,1)S(1)}, u32[]{:S(2)}, u32[]{:S(2)}) collective-permute-start(bf16[256,1024]{1,0:T(8,128)(2,1)} %get-tuple-element.106), channel_id=1, source_target_pairs={{0,1},{1,0},{2,3},{3,2},{4,5},{5,4},{6,7},{7,6},{8,9},{9,8},{10,11... | collective-permute-start | bytes 1572872 | tf_op jit(solution)/shard_map/ppermute | solution.py:828
  201.2 15.0 %collective-permute-start.21 = (bf16[256,1024]{1,0:T(8,128)(2,1)}, bf16[256,1024]{1,0:T(8,128)(2,1)S(1)}, u32[]{:S(2)}, u32[]{:S(2)}) collective-permute-start(bf16[256,1024]{1,0:T(8,128)(2,1)} %get-tuple-element.103), channel_id=1, source_target_pairs={{0,2},{1,3},{2,0},{3,1},{4,6},{5,7},{6,4},{7,5},{8,10},{9,11},{10,... | collective-permute-start | bytes 1572872 | tf_op jit(solution)/shard_map/ppermute | solution.py:828
  203.0 33.3 %collective-permute-start.24 = (bf16[256,1024]{1,0:T(8,128)(2,1)}, bf16[256,1024]{1,0:T(8,128)(2,1)S(1)}, u32[]{:S(2)}, u32[]{:S(2)}) collective-permute-start(bf16[256,1024]{1,0:T(8,128)(2,1)} %get-tuple-element.113), channel_id=1, source_target_pairs={{0,1},{1,0},{2,3},{3,2},{4,5},{5,4},{6,7},{7,6},{8,9},{9,8},{10,11... | collective-permute-start | bytes 1572872 | tf_op jit(solution)/shard_map/ppermute | solution.py:828
  204.1 33.8 %collective-permute-start.27 = (bf16[256,1024]{1,0:T(8,128)(2,1)}, bf16[256,1024]{1,0:T(8,128)(2,1)S(1)}, u32[]{:S(2)}, u32[]{:S(2)}) collective-permute-start(bf16[256,1024]{1,0:T(8,128)(2,1)} %get-tuple-element.114), channel_id=1, source_target_pairs={{0,2},{1,3},{2,0},{3,1},{4,6},{5,7},{6,4},{7,5},{8,10},{9,11},{10,... | collective-permute-start | bytes 1572872 | tf_op jit(solution)/shard_map/ppermute | solution.py:828
  217.2 22.5 %collective-permute-start.26 = (bf16[256,1024]{1,0:T(8,128)(2,1)S(1)}, bf16[256,1024]{1,0:T(8,128)(2,1)S(1)}, u32[]{:S(2)}, u32[]{:S(2)}) collective-permute-start(bf16[256,1024]{1,0:T(8,128)(2,1)S(1)} %add_convert_fusion.1), channel_id=1, source_target_pairs={{0,2},{1,3},{2,0},{3,1},{4,6},{5,7},{6,4},{7,5},{8,10},{9,11},{10,... | collective-permute-start | bytes 1572872 | tf_op jit(solution)/shard_map/ppermute | solution.py:828
  219.2 21.1 %collective-permute-start.25 = (bf16[256,1024]{1,0:T(8,128)(2,1)S(1)}, bf16[256,1024]{1,0:T(8,128)(2,1)S(1)}, u32[]{:S(2)}, u32[]{:S(2)}) collective-permute-start(bf16[256,1024]{1,0:T(8,128)(2,1)S(1)} %add_convert_fusion.2), channel_id=1, source_target_pairs={{0,1},{1,0},{2,3},{3,2},{4,5},{5,4},{6,7},{7,6},{8,9},{9,8},{10,11... | collective-permute-start | bytes 1572872 | tf_op jit(solution)/shard_map/ppermute | solution.py:828
  (40 other events, 365.5 us)
Sparse Core Ops, SparseCore 0:
  26.2 30.6 all-gather.4
  58.5 51.2 all-gather.6
  152.9 57.0 reduce-scatter.1

commit v6 on v5

--- a/solution.py
+++ b/solution.py
@@ -231,7 +231,7 @@
 
 def qkv_kernel(plan, count, order, *refs):
     pieces, rest = refs[:count], refs[count:]
-    vectors, weight, turn, q, k, v, normal, x, sems = rest
+    vectors, weight, turn, q, k, v, x, sems = rest
     step = pl.program_id(0)
     width = q.shape[1]
     span = q.shape[0]
@@ -244,7 +244,6 @@
     fetch(plan, step, pieces, x, sems, False)
     n, _ = normed(x[pl.ds(pl.multiple_of(step * span, span), span), :].astype(F32))
     h = (n * vectors[0:1, :] + vectors[1:2, :]).astype(LOW)
-    normal[...] = h
     tables = (turn[:, :128], turn[:, 128:])
     rows = dot(h, weight[...].reshape(model, 3 * width))
     q[...] = (turned(rows[:, :width] + vectors[7:8, :width], *tables, 1.0) * 0.125).astype(LOW)
@@ -265,10 +264,10 @@
             in_specs=[HBM] * len(pieces)
             + [whole(vectors.shape), whole(weight.shape[:2] + (3 * width,))]
             + [pl.BlockSpec((span, 256), there)],
-            out_specs=[pl.BlockSpec((span, width), there)] * 3 + [pl.BlockSpec((span, model), there)],
+            out_specs=[pl.BlockSpec((span, width), there)] * 3,
             scratch_shapes=[pltpu.VMEM((rows, model), LOW), pltpu.SemaphoreType.DMA((len(plan), 2))],
         ),
-        out_shape=[jax.ShapeDtypeStruct((rows, width), LOW)] * 3 + [jax.ShapeDtypeStruct((rows, model), LOW)],
+        out_shape=[jax.ShapeDtypeStruct((rows, width), LOW)] * 3,
         compiler_params=params("arbitrary"),
         cost_estimate=SHORT,
         name="qkv",
@@ -390,7 +389,7 @@
     return e * scale, gain, bias
 
 
-def bwd_kernel(plan, per, groups, extra, first, q, k, v, d_mixed, mixed, lse, turn, to_norm, vectors, normal, weight, *rest):
+def bwd_kernel(plan, per, groups, extra, first, q, k, v, d_mixed, mixed, lse, turn, to_norm, vectors, weight, *rest):
     many = 1 + max(piece for piece, _ in plan)
     pieces, outs, (even, odd, sums, ones), rest = rest[:many], rest[many : 2 * many], rest[2 * many : 2 * many + 4], rest[2 * many + 4 :]
     keys, values, sum_q, sum_k, sum_v, queries, seeds, h, d_rows, x, mat, wide, sem, x_sems, out_sems = rest
@@ -404,18 +403,14 @@
     group, order = first[base], lambda at: first[base + 1 + at]
     rows_of = lambda at: pl.ds(pl.multiple_of(at * BLOCK, BLOCK), BLOCK)
     own = rows_of(block)
-    loads = [
-        pltpu.make_async_copy(normal, h, sem.at[0]),
-        pltpu.make_async_copy(weight.at[:, :, pl.ds(0, 3 * width)], mat, sem.at[1]),
-    ]
+    load = pltpu.make_async_copy(weight.at[:, :, pl.ds(0, 3 * width)], mat, sem.at[0])
 
     @pl.when(step == 0)
     def _():
-        loads[1].start()
+        load.start()
         for at, (piece, start) in reversed(list(enumerate(plan))):
             place = order(at // per) * per + at % per
             pltpu.make_async_copy(pieces[piece].at[pl.ds(start, BLOCK)], x.at[rows_of(place)], x_sems.at[place]).start()
-        loads[0].start()
 
         def prepare(at, _):
             here = rows_of(at)
@@ -464,7 +459,7 @@
 
     @pl.when(step == 0)
     def _():
-        loads[1].wait()
+        load.wait()
 
     pltpu.make_async_copy(x.at[own], x.at[own], x_sems.at[block]).wait()
     turns = (turn[:, :128], turn[:, 128:])
@@ -479,6 +474,7 @@
     d_rows[own, :] = done
     sums[0:1, :] += jnp.sum(done.astype(F32), axis=0, keepdims=True)
     n, scale = normed(x[own, :].astype(F32))
+    h[own, :] = (n * vectors[0:1, :] + vectors[1:2, :]).astype(LOW)
     d_h = dot(done, mat[...].reshape(h.shape[1], 3 * width), NT)
     ones[0:1, :] += jnp.sum(d_h * n, axis=0, keepdims=True)
     ones[1:2, :] += jnp.sum(d_h, axis=0, keepdims=True)
@@ -494,7 +490,6 @@
 
     @pl.when(step == blocks - 1)
     def _():
-        loads[0].wait()
         model = h.shape[1]
         grad = dot(h[...], d_rows[...], TN).astype(LOW)
         h[:model, : 3 * width] = grad
@@ -521,11 +516,11 @@
             pltpu.make_async_copy(x.at[here], x.at[here], out_sems.at[at]).wait()
 
 
-def call_bwd(first, q, k, v, d_mixed, mixed, lse, tables, to_norm, vectors, normal, weight, pieces, out_shapes, groups, span, extra):
+def call_bwd(first, q, k, v, d_mixed, mixed, lse, tables, to_norm, vectors, weight, pieces, out_shapes, groups, span, extra):
     rows, width = q.shape
     heads = width // HEAD
     blocks = rows // BLOCK
-    model = normal.shape[1]
+    model = to_norm.shape[1]
     grad = (groups // 2, model // groups + EXTRA * extra, 3 * width)
     back = lambda i, o: (blocks - 1 - i, 0)
     blocked = pl.BlockSpec((BLOCK, width), back)
@@ -539,7 +534,7 @@
             grid=(blocks,),
             in_specs=[blocked, once((rows, width)), once((rows, width)), blocked, blocked]
             + [pl.BlockSpec((heads, BLOCK), lambda i, o: (0, blocks - 1 - i)), pl.BlockSpec((BLOCK, 256), back)]
-            + [pl.BlockSpec((BLOCK, model), back), whole(vectors.shape), HBM, HBM]
+            + [pl.BlockSpec((BLOCK, model), back), whole(vectors.shape), HBM]
             + [HBM] * len(pieces),
             out_specs=[HBM] * len(out_shapes) + [whole(a) for a, _ in outs],
             scratch_shapes=[
@@ -555,7 +550,7 @@
                 pltpu.VMEM((rows, model), LOW),
                 pltpu.VMEM(weight.shape[:2] + (3 * width,), LOW),
                 pltpu.VMEM((3 * groups, 128), F32),
-                pltpu.SemaphoreType.DMA((2,)),
+                pltpu.SemaphoreType.DMA((1,)),
                 pltpu.SemaphoreType.DMA((blocks,)),
                 pltpu.SemaphoreType.DMA((blocks,)),
             ],
@@ -564,7 +559,7 @@
         compiler_params=params("arbitrary"),
         cost_estimate=SHORT,
         name="attend_back",
-    )(first, q, k, v, d_mixed, mixed, lse, tables, to_norm, vectors, normal, weight, *pieces)
+    )(first, q, k, v, d_mixed, mixed, lse, tables, to_norm, vectors, weight, *pieces)
 
 
 def extra_rows(lines):
@@ -942,14 +937,14 @@
     x_halves = [tokens[:half], tokens[half:]]
     cot_halves = [cotangent[:half], cotangent[half:]]
     if paired:
-        out_own = swap_owner(out_weight, False)
         small = small_block(member, members, vectors_in, qkv_bias, up_bias)
         packed = call_pack(me, qkv_weight, up_weight, small, members)
         arrived = [packed[0]] + [across(packed[bit], bit) for bit in range(1, members)]
         x_near = near_rows(behind_all(x_halves, *arrived[1:]))
         cut = 3 * width + 128
-        first_in, up_in = call_place(me, behind_all(arrived, out_own), cut)
+        first_in, up_in = call_place(me, arrived, cut)
         w_first = gather_dp(first_in)
+        out_own = behind(swap_owner(behind(out_weight, first_in), False), *x_near[:2])
         mats = (gather_dp(jnp.concatenate([up_in, down_weight, out_own], axis=0)),)
         vectors = call_vectors(me, w_first, members, cut)
     else:
@@ -974,8 +969,8 @@
     first = jnp.concatenate([first, group.astype(jnp.int32).reshape(1), order])
     tables = rotary_tables(stream)
 
-    q, k, v, normal = call_qkv(order, x_pieces, vectors, w_first, tables, rows, width)
-    cot_near = near_rows(behind_all(cot_halves, *x_pieces[2:])) if members == 4 else None
+    q, k, v = call_qkv(order, x_pieces, vectors, w_first, tables, rows, width)
+    cot_near = near_rows(behind_all(cot_halves, *x_near)) if members == 4 else None
     cot_pieces = gather_rows(cot_halves, cot_near, q)
     mixed, low_mixed, lse = call_fwd(first, q, k, v)
     out_sizes = [rows] * members if members == 4 else [stream]
@@ -990,7 +985,7 @@
     summed = reduce_direct(parts)
     sizes = [half] * (2 * members) if members == 4 else [stream]
     *pieces, even, odd, sums_qkv, ones = call_bwd(
-        first, q, k, v, d_mixed, mixed, lse, tables, to_norm, vectors, normal, w_first, x_pieces,
+        first, q, k, v, d_mixed, mixed, lse, tables, to_norm, vectors, w_first, x_pieces,
         [jax.ShapeDtypeStruct((size, model), LOW) for size in sizes], groups, rows, paired,
     )
     far, bit = hop(odd, 1), 2

time: 261 us -> 256 us (0.981)
  waiting for transfers between devices: 46.2 us -> 54.5 us
  starting transfers between devices: 42.2 us -> 34 us
  local copies, waits for them, and re-layouts: 15.6 us -> 12 us
    ppermute x27, starting transfers between devices: 37.2 us -> 30.4 us  [across(): return lax.ppermute(array, 'fsdp', [(i, i ^ bit) for i in range(size)])]
    ppermute x27, waiting for transfers between devices: 37.1 us -> 41.8 us  [across(): return lax.ppermute(array, 'fsdp', [(i, i ^ bit) for i in range(size)])]
    unnamed x59 -> x67, local copies, waits for them, and re-layouts: 7.29 us -> 3.57 us
    all_gather x2, waiting for transfers between devices: 0.02 us -> 2.7 us  [gather_dp(): return lax.all_gather(array, 'dp', axis=0)]
  transfers between devices with their start and end apart: 35 -> 35, of which waited for: 9 -> 13; matrix products, arithmetic and copies ran while one was open for 3% -> 3% of each run, Pallas kernels for 34% -> 34%
where the time goes in v6:
time: 256 us; the launch traced here: 253 us
  Pallas kernels  134 us (52%)
  waiting for transfers between devices  54.5 us (21%)
  starting transfers between devices  34 us (13%)
  between operations  14.1 us (6%)
  local copies, waits for them, and re-layouts  12 us (5%)
  other arithmetic  4.9 us (2%)
    pallas_call x1, Pallas kernels, call_bwd(): pl.pallas_call(functools.partial(bwd_kernel, plan, span // BLOCK, groups,...  44 us
    ppermute x27, waiting for transfers between devices, across(): return lax.ppermute(array, 'fsdp', [(i, i ^ bit) for i in range(size)])  41.8 us
    pallas_call x1, Pallas kernels, call_mlp(): pl.pallas_call(functools.partial(mlp_kernel, plan, out_plan, count, len(o...  41 us
    ppermute x27, starting transfers between devices, across(): return lax.ppermute(array, 'fsdp', [(i, i ^ bit) for i in range(size)])  30.4 us
    pallas_call x1, Pallas kernels, call_fwd(): pl.pallas_call(fwd_kernel, grid_spec=pltpu.PrefetchScalarGridSpec(num_sca...  20.4 us
    pallas_call x1, Pallas kernels, call_qkv(): pl.pallas_call(functools.partial(qkv_kernel, plan, len(pieces)), grid_spe...  11.2 us
    ppermute x3, waiting for transfers between devices, hop(): lax.ppermute(array, 'dp', [(i, i ^ bit) for i in range(lax.axis_size('dp'...  9.98 us
    pallas_call x2, Pallas kernels, call_finish(): pl.pallas_call(functools.partial(finish_kernel, len(vectors), len(common)...  7.24 us
  transfers between devices with their start and end apart: 35, of which 13 were waited for; matrix products, arithmetic and copies ran while one was open for 3% of the time, Pallas kernels for 34%

profile of v6, /device:TPU:0, one launch (start us, length us, event | category | flops | bytes accessed | tf_op | source)
XLA Modules:
  0.0 253.1 jit_solution(7215540315163866543)
XLA Ops:
  10.3 1.9 pack.1
  12.2 2.9 %collective-permute-start = (bf16[32,1920]{1,0:T(8,128)(2,1)}, bf16[32,1920]{1,0:T(8,128)(2,1)S(1)}, u32[]{:S(2)}, u32[]{:S(2)}) collective-permute-start(bf16[32,1920]{1,0:T(8,128)(2,1)} %get-tuple-element.67), channel_id=1, source_target_pairs={{0,1},{1,0},{2,3},{3,2},{4,5},{5,4},{6,7},{7,6},{8,9},{9,8},{10,11... | collective-permute-start | bytes 368648 | tf_op jit(solution)/shard_map/ppermute | solution.py:823
  16.7 2.5 collective-permute-done.refs_1_
  19.2 3.7 %collective-permute-done.1.refs_2_ = bf16[32,1920]{1,0:T(8,128)(2,1)S(1)} collective-permute-done((bf16[32,1920]{1,0:T(8,128)(2,1)}, bf16[32,1920]{1,0:T(8,128)(2,1)S(1)}, u32[]{:S(2)}, u32[]{:S(2)}) %collective-permute-start.1) | collective-permute-done | bytes 122912 | tf_op jit(solution)/shard_map/ppermute | solution.py:823
  23.6 1.9 place.1
  28.3 9.4 %collective-permute-done.6.refs_5_.rest_5_ = bf16[256,1024]{1,0:T(8,128)(2,1)S(1)} collective-permute-done((bf16[256,1024]{1,0:T(8,128)(2,1)S(1)}, bf16[256,1024]{1,0:T(8,128)(2,1)S(1)}, u32[]{:S(2)}, u32[]{:S(2)}) %collective-permute-start.6) | collective-permute-done | bytes 524320 | tf_op jit(solution)/shard_map/ppermute | solution.py:823
  39.9 2.4 collective-permute-start.4
  42.6 2.3 fusion.1
  46.8 8.3 %collective-permute-done.4.refs_3_.rest_3_ = bf16[256,1024]{1,0:T(8,128)(2,1)S(1)} collective-permute-done((bf16[256,1024]{1,0:T(8,128)(2,1)S(1)}, bf16[256,1024]{1,0:T(8,128)(2,1)S(1)}, u32[]{:S(2)}, u32[]{:S(2)}) %collective-permute-start.4) | collective-permute-done | bytes 524320 | tf_op jit(solution)/shard_map/ppermute | solution.py:823
  55.1 2.1 collective-permute-done.5.refs_4_.rest_4_
  58.3 1.7 collective-permute-start.10
  61.7 4.8 %collective-permute-done.8.refs_7_.rest_7_ = bf16[256,1024]{1,0:T(8,128)(2,1)} collective-permute-done((bf16[256,1024]{1,0:T(8,128)(2,1)S(1)}, bf16[256,1024]{1,0:T(8,128)(2,1)}, u32[]{:S(2)}, u32[]{:S(2)}) %collective-permute-start.8) | collective-permute-done | bytes 524320 | tf_op jit(solution)/shard_map/ppermute | solution.py:823
  68.5 11.2 %qkv.3 = (bf16[2048,256]{1,0:T(8,128)(2,1)}, bf16[2048,256]{1,0:T(8,128)(2,1)}, bf16[2048,256]{1,0:T(8,128)(2,1)}) custom-call(s32[4]{0:T(128)} %iota_xor_fusion.order, bf16[256,1024]{1,0:T(8,128)(2,1)} %copy-done.1, bf16[256,1024]{1,0:T(8,128)(2,1)} %copy-done, bf16[256,1024]{1,0:T(8,128)(2,1)} %copy-done.3, bf16[256,1024]{1,0:T(8,128)(2,1)} %copy-done.4, ...), custom_call_target="tpu_custom_call" | custom-call | tf_op jit(solution)/shard_map/qkv/pallas_call | solution.py:259
  80.1 1.7 collective-permute-start.13
  82.6 20.4 %attend.1 = (f32[2048,256]{1,0:T(8,128)}, bf16[2048,256]{1,0:T(8,128)(2,1)}, f32[4,2048]{1,0:T(4,128)}) custom-call(s32[13]{0:T(128)} %pad_add_fusion.first, bf16[2048,256]{1,0:T(8,128)(2,1)} %get-tuple-element.75.q, bf16[2048,256]{1,0:T(8,128)(2,1)} %get-tuple-element.78.k, bf16[2048,256]{1,0:T(8,128)(2,1)} %get-tuple-element.79.v), custom_call_target="tpu_custom_call" | custom-call | tf_op jit(solution)/shard_map/attend/pallas_call | solution.py:351
  103.0 2.7 %all-gather.7.cloned.1.call-done = bf16[2304,1024]{1,0:T(8,128)(2,1)} async-done(((bf16[288,1024]{1,0:T(8,128)(2,1)}), bf16[2304,1024]{1,0:T(8,128)(2,1)}) %all-gather.7.cloned.1.call-update) | async-done | bytes 4718608 | tf_op jit(solution)/shard_map/all_gather | solution.py:896
  105.7 41.0 %mlp.1 = (bf16[512,1024]{1,0:T(8,128)(2,1)}, bf16[512,1024]{1,0:T(8,128)(2,1)}, bf16[512,1024]{1,0:T(8,128)(2,1)}, bf16[512,1024]{1,0:T(8,128)(2,1)}, bf16[2048,...) custom-call(s32[4]{0:T(128)} %iota_xor_fusion.order, ...), custom_call_target="tpu_custom_call" | custom-call | tf_op jit(solution)/shard_map/mlp/pallas_call | solution.py:685
  150.9 44.0 %attend_back.1 = (bf16[256,1024]{1,0:T(8,128)(2,1)}, bf16[256,1024]{1,0:T(8,128)(2,1)}, bf16[256,1024]{1,0:T(8,128)(2,1)}, bf16[256,1024]{1,0:T(8,128)(2,1)}, bf...) custom-call(s32[13]{0:T(128)} %pad_add_fusion.first, ...), custom_call_target="tpu_custom_call" | custom-call | tf_op jit(solution)/shard_map/attend_back/pallas_call | solution.py:530
  199.1 3.8 %finish.2 = bf16[512,1024]{1,0:T(8,128)(2,1)} custom-call(bf16[512,1024]{1,0:T(8,128)(2,1)} %base.1, f32[16,1024]{1,0:T(8,128)} %vectors.1.refs_8_.refs_17_.refs_0_, bf16[512,1024]{1,0:T(8,128)(2,1)} %get-tuple-element.84.refs_1_, bf16[512,1024]{1,0:T(8,128)(2,1)} %collective-permute-done.16.refs_2_, bf16[512,1024]{1,0:T(8,128)(2,1)} %collective-permute-done.17.refs_3_, ...), custom_call_target="tpu_custom_call" | custom-call | flops 20000000000 | bytes 10000000 | tf_op jit(solution)/shard_map/finish/pallas_call | solution.py:744
  204.1 5.9 %collective-permute-done.22 = bf16[256,1024]{1,0:T(8,128)(2,1)S(1)} collective-permute-done((bf16[256,1024]{1,0:T(8,128)(2,1)}, bf16[256,1024]{1,0:T(8,128)(2,1)S(1)}, u32[]{:S(2)}, u32[]{:S(2)}) %collective-permute-start.22) | collective-permute-done | bytes 524320 | tf_op jit(solution)/shard_map/ppermute | solution.py:823
  216.9 10.0 %collective-permute-done.23 = bf16[1,144,768]{2,1,0:T(8,128)(2,1)S(1)} collective-permute-done((bf16[1,144,768]{2,1,0:T(8,128)(2,1)S(1)}, bf16[1,144,768]{2,1,0:T(8,128)(2,1)S(1)}, u32[]{:S(2)}, u32[]{:S(2)}) %collective-permute-start.23) | collective-permute-done | bytes 221216 | tf_op jit(solution)/shard_map/ppermute | solution.py:862
  227.6 2.3 cut.1
  235.7 3.4 %finish.3 = bf16[512,1024]{1,0:T(8,128)(2,1)} custom-call(bf16[512,1024]{1,0:T(8,128)(2,1)} %base.2, bf16[256,1024]{1,0:T(8,128)(2,1)} %get-tuple-element.105.refs_0_, bf16[256,1024]{1,0:T(8,128)(2,1)} %get-tuple-element.106.refs_1_, bf16[256,1024]{1,0:T(8,128)(2,1)} %copy-done.8, bf16[256,1024]{1,0:T(8,128)(2,1)} %copy-done.11, ...), custom_call_target="tpu_custom_call" | custom-call | tf_op jit(solution)/shard_map/finish/pallas_call | solution.py:744
  241.2 2.2 join.1
  (150 shorter events, 46.7 us)
Async XLA Ops:
  7.2 52.8 %all-gather.5.cloned.1.call-start = ((), (), s32[]{:S(2)}) async-start(), calls=%async_computation.2 | async-start | bytes 2064384 | tf_op jit(solution)/shard_map/all_gather | solution.py:896
  25.5 80.2 %all-gather.7.cloned.1.call-start = ((), (), s32[]{:S(2)}) async-start(), calls=%async_computation.3 | async-start | bytes 5308416 | tf_op jit(solution)/shard_map/all_gather | solution.py:896
  25.6 12.1 %collective-permute-start.6 = (bf16[256,1024]{1,0:T(8,128)(2,1)S(1)}, bf16[256,1024]{1,0:T(8,128)(2,1)S(1)}, u32[]{:S(2)}, u32[]{:S(2)}) collective-permute-start(bf16[256,1024]{1,0:T(8,128)(2,1)S(1)} %get-tuple-element.72.refs_1_.rest_1_), channel_id=1, source_target_pairs={{0,2},{1,3},{2,0},{3,1},{4,6},{5,7},{6,4},{7,5},{8,10},{9,11},{10,... | collective-permute-start | bytes 1572872 | tf_op jit(solution)/shard_map/ppermute | solution.py:823
  27.1 11.8 %collective-permute-start.3 = (bf16[256,1024]{1,0:T(8,128)(2,1)S(1)}, bf16[256,1024]{1,0:T(8,128)(2,1)S(1)}, u32[]{:S(2)}, u32[]{:S(2)}) collective-permute-start(bf16[256,1024]{1,0:T(8,128)(2,1)S(1)} %get-tuple-element.71.refs_0_.rest_0_), channel_id=1, source_target_pairs={{0,1},{1,0},{2,3},{3,2},{4,5},{5,4},{6,7},{7,6},{8,9},{9,8},{10,11... | collective-permute-start | bytes 1572872 | tf_op jit(solution)/shard_map/ppermute | solution.py:823
  39.9 187.0 %reduce-scatter.2.cloned.1.call-start = ((), (), s32[]{:S(2)}) async-start(), calls=%async_computation.1 | async-start | bytes 5603328 | tf_op jit(solution)/shard_map/reduce_scatter | solution.py:900
  39.9 15.2 %collective-permute-start.4 = (bf16[256,1024]{1,0:T(8,128)(2,1)S(1)}, bf16[256,1024]{1,0:T(8,128)(2,1)S(1)}, u32[]{:S(2)}, u32[]{:S(2)}) collective-permute-start(bf16[256,1024]{1,0:T(8,128)(2,1)S(1)} %get-tuple-element.72.refs_1_.rest_1_), channel_id=1, source_target_pairs={{0,1},{1,0},{2,3},{3,2},{4,5},{5,4},{6,7},{7,6},{8,9},{9,8},{10,11... | collective-permute-start | bytes 1572872 | tf_op jit(solution)/shard_map/ppermute | solution.py:823
  42.3 14.9 %collective-permute-start.5 = (bf16[256,1024]{1,0:T(8,128)(2,1)S(1)}, bf16[256,1024]{1,0:T(8,128)(2,1)S(1)}, u32[]{:S(2)}, u32[]{:S(2)}) collective-permute-start(bf16[256,1024]{1,0:T(8,128)(2,1)S(1)} %get-tuple-element.71.refs_0_.rest_0_), channel_id=1, source_target_pairs={{0,2},{1,3},{2,0},{3,1},{4,6},{5,7},{6,4},{7,5},{8,10},{9,11},{10,... | collective-permute-start | bytes 1572872 | tf_op jit(solution)/shard_map/ppermute | solution.py:823
  44.9 21.5 %collective-permute-start.8 = (bf16[256,1024]{1,0:T(8,128)(2,1)S(1)}, bf16[256,1024]{1,0:T(8,128)(2,1)}, u32[]{:S(2)}, u32[]{:S(2)}) collective-permute-start(bf16[256,1024]{1,0:T(8,128)(2,1)S(1)} %collective-permute-done.6.refs_5_.rest_5_), channel_id=1, source_target_pairs={{0,1},{1,0},{2,3},{3,2},{4,5},{5,4},{6,7},{7,6},{8,9},{9,8},{10,11... | collective-permute-start | bytes 1572872 | tf_op jit(solution)/shard_map/ppermute | solution.py:823
  45.4 23.1 %collective-permute-start.7 = (bf16[256,1024]{1,0:T(8,128)(2,1)S(1)}, bf16[256,1024]{1,0:T(8,128)(2,1)}, u32[]{:S(2)}, u32[]{:S(2)}) collective-permute-start(bf16[256,1024]{1,0:T(8,128)(2,1)S(1)} %collective-permute-done.3.refs_2_.rest_2_), channel_id=1, source_target_pairs={{0,2},{1,3},{2,0},{3,1},{4,6},{5,7},{6,4},{7,5},{8,10},{9,11},{10,... | collective-permute-start | bytes 1572872 | tf_op jit(solution)/shard_map/ppermute | solution.py:823
  57.2 22.5 %collective-permute-start.12 = (bf16[256,1024]{1,0:T(8,128)(2,1)}, bf16[256,1024]{1,0:T(8,128)(2,1)S(1)}, u32[]{:S(2)}, u32[]{:S(2)}) collective-permute-start(bf16[256,1024]{1,0:T(8,128)(2,1)} %get-tuple-element.74.refs_9_), channel_id=1, source_target_pairs={{0,2},{1,3},{2,0},{3,1},{4,6},{5,7},{6,4},{7,5},{8,10},{9,11},{10,... | collective-permute-start | bytes 1572872 | tf_op jit(solution)/shard_map/ppermute | solution.py:823
  57.5 22.6 %collective-permute-start.9 = (bf16[256,1024]{1,0:T(8,128)(2,1)}, bf16[256,1024]{1,0:T(8,128)(2,1)S(1)}, u32[]{:S(2)}, u32[]{:S(2)}) collective-permute-start(bf16[256,1024]{1,0:T(8,128)(2,1)} %get-tuple-element.73.refs_8_), channel_id=1, source_target_pairs={{0,1},{1,0},{2,3},{3,2},{4,5},{5,4},{6,7},{7,6},{8,9},{9,8},{10,11... | collective-permute-start | bytes 1572872 | tf_op jit(solution)/shard_map/ppermute | solution.py:823
  58.3 44.7 %collective-permute-start.10 = (bf16[256,1024]{1,0:T(8,128)(2,1)}, bf16[256,1024]{1,0:T(8,128)(2,1)}, u32[]{:S(2)}, u32[]{:S(2)}) collective-permute-start(bf16[256,1024]{1,0:T(8,128)(2,1)} %get-tuple-element.74.refs_9_), channel_id=1, source_target_pairs={{0,1},{1,0},{2,3},{3,2},{4,5},{5,4},{6,7},{7,6},{8,9},{9,8},{10,11... | collective-permute-start | bytes 1572872 | tf_op jit(solution)/shard_map/ppermute | solution.py:823
  66.4 36.5 %collective-permute-start.11 = (bf16[256,1024]{1,0:T(8,128)(2,1)}, bf16[256,1024]{1,0:T(8,128)(2,1)S(1)}, u32[]{:S(2)}, u32[]{:S(2)}) collective-permute-start(bf16[256,1024]{1,0:T(8,128)(2,1)} %get-tuple-element.73.refs_8_), channel_id=1, source_target_pairs={{0,2},{1,3},{2,0},{3,1},{4,6},{5,7},{6,4},{7,5},{8,10},{9,11},{10,... | collective-permute-start | bytes 1572872 | tf_op jit(solution)/shard_map/ppermute | solution.py:823
  79.7 23.3 %collective-permute-start.14 = (bf16[256,1024]{1,0:T(8,128)(2,1)S(1)}, bf16[256,1024]{1,0:T(8,128)(2,1)S(1)}, u32[]{:S(2)}, u32[]{:S(2)}) collective-permute-start(bf16[256,1024]{1,0:T(8,128)(2,1)S(1)} %collective-permute-done.12.refs_13_), channel_id=1, source_target_pairs={{0,1},{1,0},{2,3},{3,2},{4,5},{5,4},{6,7},{7,6},{8,9},{9,8},{10,11... | collective-permute-start | bytes 1572872 | tf_op jit(solution)/shard_map/ppermute | solution.py:823
  80.1 22.9 %collective-permute-start.13 = (bf16[256,1024]{1,0:T(8,128)(2,1)S(1)}, bf16[256,1024]{1,0:T(8,128)(2,1)S(1)}, u32[]{:S(2)}, u32[]{:S(2)}) collective-permute-start(bf16[256,1024]{1,0:T(8,128)(2,1)S(1)} %collective-permute-done.9.refs_10_), channel_id=1, source_target_pairs={{0,2},{1,3},{2,0},{3,1},{4,6},{5,7},{6,4},{7,5},{8,10},{9,11},{10,... | collective-permute-start | bytes 1572872 | tf_op jit(solution)/shard_map/ppermute | solution.py:823
  146.8 49.5 %collective-permute-start.16 = (bf16[512,1024]{1,0:T(8,128)(2,1)}, bf16[512,1024]{1,0:T(8,128)(2,1)}, u32[]{:S(2)}, u32[]{:S(2)}) collective-permute-start(bf16[512,1024]{1,0:T(8,128)(2,1)} %get-tuple-element.85), channel_id=1, source_target_pairs={{0,1},{1,0},{2,3},{3,2},{4,5},{5,4},{6,7},{7,6},{8,9},{9,8},{10,11... | collective-permute-start | bytes 3145736 | tf_op jit(solution)/shard_map/ppermute | solution.py:823
  148.3 49.4 %collective-permute-start.17 = (bf16[512,1024]{1,0:T(8,128)(2,1)S(1)}, bf16[512,1024]{1,0:T(8,128)(2,1)}, u32[]{:S(2)}, u32[]{:S(2)}) collective-permute-start(bf16[512,1024]{1,0:T(8,128)(2,1)S(1)} %copy-done.30), channel_id=1, source_target_pairs={{0,2},{1,3},{2,0},{3,1},{4,6},{5,7},{6,4},{7,5},{8,10},{9,11},{10,... | collective-permute-start | bytes 3145736 | tf_op jit(solution)/shard_map/ppermute | solution.py:823
  149.8 48.8 %collective-permute-start.18 = (bf16[512,1024]{1,0:T(8,128)(2,1)}, bf16[512,1024]{1,0:T(8,128)(2,1)}, u32[]{:S(2)}, u32[]{:S(2)}) collective-permute-start(bf16[512,1024]{1,0:T(8,128)(2,1)} %get-tuple-element.87), channel_id=1, source_target_pairs={{0,3},{1,2},{2,1},{3,0},{4,7},{5,6},{6,5},{7,4},{8,11},{9,10},{10,... | collective-permute-start | bytes 3145736 | tf_op jit(solution)/shard_map/ppermute | solution.py:823
  194.9 15.0 %collective-permute-start.22 = (bf16[256,1024]{1,0:T(8,128)(2,1)}, bf16[256,1024]{1,0:T(8,128)(2,1)S(1)}, u32[]{:S(2)}, u32[]{:S(2)}) collective-permute-start(bf16[256,1024]{1,0:T(8,128)(2,1)} %get-tuple-element.100), channel_id=1, source_target_pairs={{0,1},{1,0},{2,3},{3,2},{4,5},{5,4},{6,7},{7,6},{8,9},{9,8},{10,11... | collective-permute-start | bytes 1572872 | tf_op jit(solution)/shard_map/ppermute | solution.py:823
  196.3 15.0 %collective-permute-start.21 = (bf16[256,1024]{1,0:T(8,128)(2,1)}, bf16[256,1024]{1,0:T(8,128)(2,1)S(1)}, u32[]{:S(2)}, u32[]{:S(2)}) collective-permute-start(bf16[256,1024]{1,0:T(8,128)(2,1)} %get-tuple-element.97), channel_id=1, source_target_pairs={{0,2},{1,3},{2,0},{3,1},{4,6},{5,7},{6,4},{7,5},{8,10},{9,11},{10,... | collective-permute-start | bytes 1572872 | tf_op jit(solution)/shard_map/ppermute | solution.py:823
  197.7 33.4 %collective-permute-start.24 = (bf16[256,1024]{1,0:T(8,128)(2,1)}, bf16[256,1024]{1,0:T(8,128)(2,1)S(1)}, u32[]{:S(2)}, u32[]{:S(2)}) collective-permute-start(bf16[256,1024]{1,0:T(8,128)(2,1)} %get-tuple-element.107), channel_id=1, source_target_pairs={{0,1},{1,0},{2,3},{3,2},{4,5},{5,4},{6,7},{7,6},{8,9},{9,8},{10,11... | collective-permute-start | bytes 1572872 | tf_op jit(solution)/shard_map/ppermute | solution.py:823
  198.6 34.0 %collective-permute-start.27 = (bf16[256,1024]{1,0:T(8,128)(2,1)}, bf16[256,1024]{1,0:T(8,128)(2,1)S(1)}, u32[]{:S(2)}, u32[]{:S(2)}) collective-permute-start(bf16[256,1024]{1,0:T(8,128)(2,1)} %get-tuple-element.108), channel_id=1, source_target_pairs={{0,2},{1,3},{2,0},{3,1},{4,6},{5,7},{6,4},{7,5},{8,10},{9,11},{10,... | collective-permute-start | bytes 1572872 | tf_op jit(solution)/shard_map/ppermute | solution.py:823
  212.3 22.0 %collective-permute-start.26 = (bf16[256,1024]{1,0:T(8,128)(2,1)S(1)}, bf16[256,1024]{1,0:T(8,128)(2,1)S(1)}, u32[]{:S(2)}, u32[]{:S(2)}) collective-permute-start(bf16[256,1024]{1,0:T(8,128)(2,1)S(1)} %add_convert_fusion.1), channel_id=1, source_target_pairs={{0,2},{1,3},{2,0},{3,1},{4,6},{5,7},{6,4},{7,5},{8,10},{9,11},{10,... | collective-permute-start | bytes 1572872 | tf_op jit(solution)/shard_map/ppermute | solution.py:823
  214.0 20.9 %collective-permute-start.25 = (bf16[256,1024]{1,0:T(8,128)(2,1)S(1)}, bf16[256,1024]{1,0:T(8,128)(2,1)S(1)}, u32[]{:S(2)}, u32[]{:S(2)}) collective-permute-start(bf16[256,1024]{1,0:T(8,128)(2,1)S(1)} %add_convert_fusion.2), channel_id=1, source_target_pairs={{0,1},{1,0},{2,3},{3,2},{4,5},{5,4},{6,7},{7,6},{8,9},{9,8},{10,11... | collective-permute-start | bytes 1572872 | tf_op jit(solution)/shard_map/ppermute | solution.py:823
  (44 other events, 390.8 us)
Sparse Core Ops, SparseCore 0:
  25.6 27.2 all-gather.4
  54.6 51.0 all-gather.6
  146.9 56.2 reduce-scatter.1

commit v7 on v6

--- a/solution.py
+++ b/solution.py
@@ -112,24 +112,40 @@
                     copy.wait()
 
 
-def pack_kernel(members, member, qkv, up, small, *out):
+def pack_kernel(members, member, qkv, up, *refs):
+    vectors, (qkv_bias, up_bias), out, (small, wide) = refs[:6], refs[6:8], refs[8:-2], refs[-2:]
     width = qkv.shape[1] // 3 // members
-    units_dev = 128
+    units_dev = up_bias.shape[0]
     groups = up.shape[1] // units_dev // members
+    size = 128 // members
+    small[...] = jnp.zeros_like(small)
+    wide[...] = jnp.zeros_like(wide)
+    for at in range(members):
+
+        @pl.when(member[0] == at)
+        def _():
+            for row, vector in enumerate(vectors):
+                small[row, at * size : (at + 1) * size] = vector[...].astype(F32)
+            wide[0, 3 * at * size : 3 * (at + 1) * size] = qkv_bias[...].astype(F32)
+
+    for row in range(3):
+        small[6 + row : 7 + row, :] = wide[0:1, row * 128 : (row + 1) * 128]
+    small[9, :] = up_bias[...].astype(F32)
+    block = small[...].astype(LOW)
     for bit in range(members):
         to = member[0] ^ bit
         for part in range(3):
             start = pl.multiple_of((part * members + to) * width, 128)
             out[bit][:, part * width : (part + 1) * width] = qkv[:, pl.ds(start, width)]
         out[bit][:, 3 * width : 3 * width + 128] = jnp.zeros((qkv.shape[0], 128), LOW)
-        out[bit][0 : small.shape[0], 3 * width : 3 * width + 128] = small[...]
+        out[bit][0:16, 3 * width : 3 * width + 128] = block
         for group in range(groups):
             start = pl.multiple_of((group * members + to) * units_dev, 128)
             low = 3 * width + 128 + group * units_dev
             out[bit][:, low : low + units_dev] = up[:, pl.ds(start, units_dev)]
 
 
-def call_pack(member, qkv, up, small, members):
+def call_pack(member, qkv, up, vectors, members):
     shard = qkv.shape[0]
     columns = (qkv.shape[1] + up.shape[1]) // members + 128
     return pl.pallas_call(
@@ -137,14 +153,15 @@
         grid_spec=pltpu.PrefetchScalarGridSpec(
             num_scalar_prefetch=1,
             grid=(1,),
-            in_specs=[whole(qkv.shape), whole(up.shape), whole(small.shape)],
+            in_specs=[whole(a.shape) for a in (qkv, up, *vectors)],
             out_specs=[whole((shard, columns))] * members,
+            scratch_shapes=[pltpu.VMEM((16, 128), F32), pltpu.VMEM((8, 384), F32)],
         ),
         out_shape=[jax.ShapeDtypeStruct((shard, columns), LOW)] * members,
         compiler_params=params("arbitrary"),
         cost_estimate=SHORT,
         name="pack",
-    )(member, qkv, up, small)
+    )(member, qkv, up, *vectors)
 
 
 def place_kernel(cut, member, *refs):
@@ -172,16 +189,6 @@
         cost_estimate=SHORT,
         name="place",
     )(member, *pieces)
-
-
-def small_block(member, members, vectors, qkv_bias, up_bias):
-    size = vectors[0].shape[0]
-    wide = 128 // members * (members - 1)
-    rows = jnp.pad(jnp.stack(vectors), ((0, 0), (wide, wide)))
-    rows = lax.dynamic_slice_in_dim(rows, wide - member * size, 128, 1)
-    wide = 3 * wide
-    shift = lax.dynamic_slice_in_dim(jnp.pad(qkv_bias, (wide, wide)), wide - member * 3 * size, 384, 0)
-    return jnp.concatenate([rows, shift.reshape(3, 128), up_bias[None], jnp.zeros((16 - len(vectors) - 4, 128), LOW)], axis=0)
 
 
 def vectors_kernel(members, member, gathered, out, wide):
@@ -765,14 +772,14 @@
         piece[shard:, :columns] = first[first.shape[0] - EXTRA :, :]
         piece[shard:, columns:] = (second[low:, :].astype(F32) + third[low:, :].astype(F32)).astype(LOW)
     down[...] = first[low : low + down.shape[0], :].astype(F32)
-    line[...] = first[first.shape[0] - EXTRA :, :128].astype(F32)[3:4, :]
+    line[...] = first[first.shape[0] - EXTRA :, :128].astype(F32)[3, :]
 
 
 def call_cut(member, first, second, third, members, shard):
     columns = first.shape[1]
     shapes = [jax.ShapeDtypeStruct((shard + EXTRA, columns + second.shape[1]), LOW)] * members + [
         jax.ShapeDtypeStruct((first.shape[0] - (members + 1) * shard - EXTRA, columns), F32),
-        jax.ShapeDtypeStruct((1, 128), F32),
+        jax.ShapeDtypeStruct((128,), F32),
     ]
     return pl.pallas_call(
         functools.partial(cut_kernel, members),
@@ -789,33 +796,55 @@
     )(member, first, second, third)
 
 
-def join_kernel(places, second, member, *refs):
-    pieces, outs, total = refs[:-3], refs[-3:-1], refs[-1]
-    shard = outs[0].shape[0]
+def join_kernel(places, second, count, member, *refs):
+    base, parts, refs, total = refs[0], refs[1 : 1 + count], refs[1 + count : -1], refs[-1]
+    finish_kernel(0, 0, base, *parts, total)
+
+    @pl.when(pl.program_id(0) == 0)
+    def _():
+        join_pieces(places, second, member, *refs)
+
+
+def join_pieces(places, second, member, *refs):
+    *pieces, last, up, qkv, out, gain_1, bias_1, gain_2, bias_2, end_bias, end_bias_2, shift = refs
+    outs = up, qkv
+    shard = up.shape[0]
     for bit, piece in enumerate(pieces):
         for block, (index, column, stride) in enumerate(places):
             start = pl.multiple_of(column + (member[0] ^ bit) * stride, 128)
             outs[index][:, pl.ds(start, 128)] = piece[:shard, block * 128 : (block + 1) * 128].astype(F32)
-    for row, low in ((0, 0), (8, second)):
-        total[row : row + 8, :] = sum(piece[shard:, low : low + 128].astype(F32) for piece in pieces)[:8, :]
-
-
-def call_join(member, pieces, places, second, columns):
+    out[...] = last[...].astype(F32)
+    size = gain_1.shape[0]
+    two, one = (sum(piece[shard:, low : low + 128].astype(F32) for piece in pieces) for low in (0, second))
+    wide = jnp.concatenate([one[2:3, :], one[3:4, :], one[4:5, :]], axis=1)
+    for at in range(len(pieces)):
+
+        @pl.when(member[0] == at)
+        def _():
+            lanes = slice(at * size, (at + 1) * size)
+            for ref, rows, row in ((gain_1, one, 0), (bias_1, one, 1), (gain_2, two, 0), (bias_2, two, 1), (end_bias, two, 2), (end_bias_2, two, 2)):
+                ref[...] = rows[row, lanes]
+            shift[...] = wide[0, 3 * at * size : 3 * (at + 1) * size]
+
+
+def call_join(member, base, parts, pieces, last, places, second, columns):
     shard = pieces[0].shape[0] - EXTRA
-    shapes = [(shard, c) for c in columns] + [(16, 128)]
+    size = 128 // len(pieces)
+    shapes = [(shard, c) for c in columns] + [last.shape] + [(size,)] * 6 + [(3 * size,)]
+    block = pl.BlockSpec((base.shape[0] // 2, base.shape[1]), lambda i, o: (i, 0))
     return pl.pallas_call(
-        functools.partial(join_kernel, tuple(places), second),
+        functools.partial(join_kernel, tuple(places), second, len(parts)),
         grid_spec=pltpu.PrefetchScalarGridSpec(
             num_scalar_prefetch=1,
-            grid=(1,),
-            in_specs=[whole(p.shape) for p in pieces],
-            out_specs=[whole(a) for a in shapes],
+            grid=(2,),
+            in_specs=[block] + [whole(p.shape) for p in (*parts, *pieces, last)],
+            out_specs=[whole(a) for a in shapes] + [block],
         ),
-        out_shape=[jax.ShapeDtypeStruct(a, F32) for a in shapes],
+        out_shape=[jax.ShapeDtypeStruct(a, F32) for a in shapes] + [jax.ShapeDtypeStruct(base.shape, LOW)],
         compiler_params=params("arbitrary"),
         cost_estimate=SHORT,
         name="join",
-    )(member, *pieces)
+    )(member, base, *parts, *pieces, last)
 
 
 def across(array, bit):
@@ -937,8 +966,7 @@
     x_halves = [tokens[:half], tokens[half:]]
     cot_halves = [cotangent[:half], cotangent[half:]]
     if paired:
-        small = small_block(member, members, vectors_in, qkv_bias, up_bias)
-        packed = call_pack(me, qkv_weight, up_weight, small, members)
+        packed = call_pack(me, qkv_weight, up_weight, (*vectors_in, qkv_bias, up_bias), members)
         arrived = [packed[0]] + [across(packed[bit], bit) for bit in range(1, members)]
         x_near = near_rows(behind_all(x_halves, *arrived[1:]))
         cut = 3 * width + 128
@@ -993,8 +1021,9 @@
         add = lambda a, b: (a.astype(F32) + b.astype(F32)).astype(LOW)
         own_low, own_high, one_low, one_high, two_low, two_high, three_low, three_high = pieces
         come = across(three_high, 2), across(three_low, 1)
+        output = call_finish(tokens, summed, (), (vectors,), LONG)
+        one_low, two_high = behind_all((one_low, two_high), output)
         near = across(one_low, 1), across(two_high, 2)
-        output = call_finish(tokens, summed, (), (vectors,), LONG)
         blocks, far, send = scatter_step(even, behind(far, output), bit)
         come = behind_all(come, send)
         one_high, two_low = add(one_high, come[0]), add(two_low, come[1])
@@ -1016,15 +1045,13 @@
         *mixed_pieces, g_down, up_shift = call_cut(me, scattered, *g_qkv, members, shard)
         g_out = scattered[scattered.shape[0] - shard - EXTRA : scattered.shape[0] - EXTRA]
         g_out = swap_owner(behind(g_out, g_down), True)
-        grad_tokens = call_finish(behind(cotangent, g_down), (), parts)
         places = [(0, b * members * units_dev, units_dev) for b in range(groups)]
         places += [(1, part * model + low, width) for part in range(3) for low in range(0, width, 128)]
         arrived = [mixed_pieces[0]] + [across(mixed_pieces[bit], bit) for bit in range(1, members)]
-        g_up, g_qkv, totals = call_join(me, arrived, places, model, (up_weight.shape[1], qkv_weight.shape[1]))
-        size = model // devices
-        lines = lax.dynamic_slice_in_dim(totals, member * size, size, 1)
-        mine = [lines[row] for row in (8, 9, 0, 1, 2)]
-        mine += [lax.dynamic_slice_in_dim(totals[10:13].reshape(-1), member * 3 * size, 3 * size), up_shift[0]]
+        g_up, g_qkv, g_out, *mine, grad_tokens = call_join(
+            me, cotangent, parts, arrived, g_out, places, model, (up_weight.shape[1], qkv_weight.shape[1])
+        )
+        mine.append(up_shift)
     else:
         grad_tokens = call_finish(cotangent, (), parts)
         g_up, g_down, g_out = [scatter_dp(g) for g in grads]
@@ -1046,10 +1073,12 @@
         for size in [model] * 5 + [3 * model, groups * members * units_dev]:
             mine.append(lax.dynamic_slice_in_dim(summed, start + place * (size // devices), size // devices))
             start += size
-    gain_1, bias_1, gain_2, bias_2, end_bias, qkv_shift, up_shift = mine
-    g_out = (g_out if paired else swap_owner(g_out, True)).astype(F32)
+        mine.insert(5, mine[4])
+    gain_1, bias_1, gain_2, bias_2, end_bias, end_bias_2, qkv_shift, up_shift = mine
+    if not paired:
+        g_out = swap_owner(g_out, True).astype(F32)
     return (
-        output, grad_tokens, gain_1, bias_1, gain_2, bias_2, g_qkv, qkv_shift, g_out, end_bias, g_up, up_shift, g_down, end_bias,
+        output, grad_tokens, gain_1, bias_1, gain_2, bias_2, g_qkv, qkv_shift, g_out, end_bias, g_up, up_shift, g_down, end_bias_2,
     )
 
 

time: 256 us -> 253 us (0.988)
  Pallas kernels: 134 us -> 125 us
  starting transfers between devices: 34 us -> 41.4 us
  waiting for transfers between devices: 54.5 us -> 60 us
  local copies, waits for them, and re-layouts: 12 us -> 7.26 us
    ppermute x3, starting transfers between devices: 2.11 us -> 8.05 us  [hop(): lax.ppermute(array, 'dp', [(i, i ^ bit) for i in range(lax.axis_size('dp'...]
    pallas_call x1, Pallas kernels: 44 us -> 39.2 us  [call_bwd(): pl.pallas_call(functools.partial(bwd_kernel, plan, span // BLOCK, groups,...]
    pallas_call x2 -> x1, Pallas kernels: 7.24 us -> 3.88 us  [call_finish(): pl.pallas_call(functools.partial(finish_kernel, len(vectors), len(common)...]
    pallas_call x1, Pallas kernels: 20.4 us -> 17.4 us  [call_fwd(): pl.pallas_call(fwd_kernel, grid_spec=pltpu.PrefetchScalarGridSpec(num_sca...]
    all_gather x2, waiting for transfers between devices: 2.7 us -> 5.67 us  [gather_dp(): return lax.all_gather(array, 'dp', axis=0)]
  transfers between devices with their start and end apart: 35 -> 35, of which waited for: 13 -> 16; matrix products, arithmetic and copies ran while one was open for 3% -> 3% of each run, Pallas kernels for 34% -> 30%
where the time goes in v7:
time: 253 us; the launch traced here: 250 us
  Pallas kernels  125 us (49%)
  waiting for transfers between devices  60 us (24%)
  starting transfers between devices  41.4 us (16%)
  between operations  14.2 us (6%)
  local copies, waits for them, and re-layouts  7.26 us (3%)
  other arithmetic  2.91 us (1%)
    ppermute x27, waiting for transfers between devices, across(): return lax.ppermute(array, 'fsdp', [(i, i ^ bit) for i in range(size)])  41.9 us
    pallas_call x1, Pallas kernels, call_mlp(): pl.pallas_call(functools.partial(mlp_kernel, plan, out_plan, count, len(o...  41.1 us
    pallas_call x1, Pallas kernels, call_bwd(): pl.pallas_call(functools.partial(bwd_kernel, plan, span // BLOCK, groups,...  39.2 us
    ppermute x27, starting transfers between devices, across(): return lax.ppermute(array, 'fsdp', [(i, i ^ bit) for i in range(size)])  31.9 us
    pallas_call x1, Pallas kernels, call_fwd(): pl.pallas_call(fwd_kernel, grid_spec=pltpu.PrefetchScalarGridSpec(num_sca...  17.4 us
    ppermute x3, waiting for transfers between devices, hop(): lax.ppermute(array, 'dp', [(i, i ^ bit) for i in range(lax.axis_size('dp'...  12.4 us
    pallas_call x1, Pallas kernels, call_qkv(): pl.pallas_call(functools.partial(qkv_kernel, plan, len(pieces)), grid_spe...  11.2 us
    ppermute x3, starting transfers between devices, hop(): lax.ppermute(array, 'dp', [(i, i ^ bit) for i in range(lax.axis_size('dp'...  8.05 us
  transfers between devices with their start and end apart: 35, of which 16 were waited for; matrix products, arithmetic and copies ran while one was open for 3% of the time, Pallas kernels for 30%

profile of v7, /device:TPU:0, one launch (start us, length us, event | category | flops | bytes accessed | tf_op | source)
XLA Modules:
  0.0 250.5 jit_solution(1183391378075475103)
XLA Ops:
  7.3 2.0 pack.1
  9.3 3.0 %collective-permute-start = (bf16[32,1920]{1,0:T(8,128)(2,1)}, bf16[32,1920]{1,0:T(8,128)(2,1)S(1)}, u32[]{:S(2)}, u32[]{:S(2)}) collective-permute-start(bf16[32,1920]{1,0:T(8,128)(2,1)} %get-tuple-element.76), channel_id=1, source_target_pairs={{0,1},{1,0},{2,3},{3,2},{4,5},{5,4},{6,7},{7,6},{8,9},{9,8},{10,11... | collective-permute-start | bytes 368648 | tf_op jit(solution)/shard_map/ppermute | solution.py:852
  13.8 2.5 %collective-permute-done.refs_1_ = bf16[32,1920]{1,0:T(8,128)(2,1)S(1)} collective-permute-done((bf16[32,1920]{1,0:T(8,128)(2,1)}, bf16[32,1920]{1,0:T(8,128)(2,1)S(1)}, u32[]{:S(2)}, u32[]{:S(2)}) %collective-permute-start) | collective-permute-done | bytes 122912 | tf_op jit(solution)/shard_map/ppermute | solution.py:852
  16.3 3.7 %collective-permute-done.1.refs_2_ = bf16[32,1920]{1,0:T(8,128)(2,1)S(1)} collective-permute-done((bf16[32,1920]{1,0:T(8,128)(2,1)}, bf16[32,1920]{1,0:T(8,128)(2,1)S(1)}, u32[]{:S(2)}, u32[]{:S(2)}) %collective-permute-start.1) | collective-permute-done | bytes 122912 | tf_op jit(solution)/shard_map/ppermute | solution.py:852
  25.5 10.2 %collective-permute-done.3.refs_2_.rest_2_ = bf16[256,1024]{1,0:T(8,128)(2,1)S(1)} collective-permute-done((bf16[256,1024]{1,0:T(8,128)(2,1)S(1)}, bf16[256,1024]{1,0:T(8,128)(2,1)S(1)}, u32[]{:S(2)}, u32[]{:S(2)}) %collective-permute-start.3) | collective-permute-done | bytes 524320 | tf_op jit(solution)/shard_map/ppermute | solution.py:852
  39.8 2.3 fusion
  44.0 8.3 %collective-permute-done.5.refs_4_.rest_4_ = bf16[256,1024]{1,0:T(8,128)(2,1)S(1)} collective-permute-done((bf16[256,1024]{1,0:T(8,128)(2,1)S(1)}, bf16[256,1024]{1,0:T(8,128)(2,1)S(1)}, u32[]{:S(2)}, u32[]{:S(2)}) %collective-permute-start.5) | collective-permute-done | bytes 524320 | tf_op jit(solution)/shard_map/ppermute | solution.py:852
  52.3 2.0 collective-permute-done.4.refs_3_.rest_3_
  58.9 4.8 %collective-permute-done.7.refs_6_.rest_6_ = bf16[256,1024]{1,0:T(8,128)(2,1)} collective-permute-done((bf16[256,1024]{1,0:T(8,128)(2,1)S(1)}, bf16[256,1024]{1,0:T(8,128)(2,1)}, u32[]{:S(2)}, u32[]{:S(2)}) %collective-permute-start.7) | collective-permute-done | bytes 524320 | tf_op jit(solution)/shard_map/ppermute | solution.py:852
  65.6 11.2 %qkv.3 = (bf16[2048,256]{1,0:T(8,128)(2,1)}, bf16[2048,256]{1,0:T(8,128)(2,1)}, bf16[2048,256]{1,0:T(8,128)(2,1)}) custom-call(s32[4]{0:T(128)} %iota_xor_fusion.order, bf16[256,1024]{1,0:T(8,128)(2,1)} %copy-done.1, bf16[256,1024]{1,0:T(8,128)(2,1)} %copy-done, bf16[256,1024]{1,0:T(8,128)(2,1)} %copy-done.2, bf16[256,1024]{1,0:T(8,128)(2,1)} %copy-done.5, ...), custom_call_target="tpu_custom_call" | custom-call | tf_op jit(solution)/shard_map/qkv/pallas_call | solution.py:266
  79.7 17.4 %attend.1 = (f32[2048,256]{1,0:T(8,128)}, bf16[2048,256]{1,0:T(8,128)(2,1)}, f32[4,2048]{1,0:T(4,128)}) custom-call(s32[13]{0:T(128)} %pad_add_fusion.first, bf16[2048,256]{1,0:T(8,128)(2,1)} %get-tuple-element.84.q, bf16[2048,256]{1,0:T(8,128)(2,1)} %get-tuple-element.87.k, bf16[2048,256]{1,0:T(8,128)(2,1)} %get-tuple-element.88.v), custom_call_target="tpu_custom_call" | custom-call | tf_op jit(solution)/shard_map/attend/pallas_call | solution.py:358
  97.2 5.7 %all-gather.7.cloned.1.call-done = bf16[2304,1024]{1,0:T(8,128)(2,1)} async-done(((bf16[288,1024]{1,0:T(8,128)(2,1)}), bf16[2304,1024]{1,0:T(8,128)(2,1)}) %all-gather.7.cloned.1.call-update) | async-done | bytes 4718608 | tf_op jit(solution)/shard_map/all_gather | solution.py:925
  102.9 41.1 %mlp.1 = (bf16[512,1024]{1,0:T(8,128)(2,1)}, bf16[512,1024]{1,0:T(8,128)(2,1)}, bf16[512,1024]{1,0:T(8,128)(2,1)}, bf16[512,1024]{1,0:T(8,128)(2,1)}, bf16[2048,...) custom-call(s32[4]{0:T(128)} %iota_xor_fusion.order, ...), custom_call_target="tpu_custom_call" | custom-call | tf_op jit(solution)/shard_map/mlp/pallas_call | solution.py:692
  148.7 39.2 %attend_back.1 = (bf16[256,1024]{1,0:T(8,128)(2,1)}, bf16[256,1024]{1,0:T(8,128)(2,1)}, bf16[256,1024]{1,0:T(8,128)(2,1)}, bf16[256,1024]{1,0:T(8,128)(2,1)}, bf...) custom-call(s32[13]{0:T(128)} %pad_add_fusion.first, ...), custom_call_target="tpu_custom_call" | custom-call | tf_op jit(solution)/shard_map/attend_back/pallas_call | solution.py:537
  191.6 3.2 %collective-permute-start.21 = (bf16[4,144,768]{2,1,0:T(8,128)(2,1)}, bf16[4,144,768]{2,1,0:T(8,128)(2,1)S(1)}, u32[]{:S(2)}, u32[]{:S(2)}) collective-permute-start(bf16[4,144,768]{2,1,0:T(8,128)(2,1)} %get-tuple-element.108), channel_id=1, source_target_pairs={{0,4},{4,0},{8,12},{12,8},{16,20},{20,16},{24,28},{28,24},{1,5},{5... | collective-permute-start | bytes 2654216 | tf_op jit(solution)/shard_map/ppermute | solution.py:891
  194.8 3.9 %finish.1 = bf16[512,1024]{1,0:T(8,128)(2,1)} custom-call(bf16[512,1024]{1,0:T(8,128)(2,1)} %base.1, f32[16,1024]{1,0:T(8,128)} %vectors.1.refs_8_.refs_17_.refs_0_, bf16[512,1024]{1,0:T(8,128)(2,1)} %get-tuple-element.93.refs_1_, bf16[512,1024]{1,0:T(8,128)(2,1)} %collective-permute-done.16.refs_2_, bf16[512,1024]{1,0:T(8,128)(2,1)} %collective-permute-done.17.refs_3_, ...), custom_call_target="tpu_custom_call" | custom-call | flops 20000000000 | bytes 10000000 | tf_op jit(solution)/shard_map/finish/pallas_call | solution.py:751
  202.0 2.5 %collective-permute-done.20 = bf16[256,1024]{1,0:T(8,128)(2,1)S(1)} collective-permute-done((bf16[256,1024]{1,0:T(8,128)(2,1)}, bf16[256,1024]{1,0:T(8,128)(2,1)S(1)}, u32[]{:S(2)}, u32[]{:S(2)}) %collective-permute-start.20) | collective-permute-done | bytes 524320 | tf_op jit(solution)/shard_map/ppermute | solution.py:852
  209.1 2.4 collective-permute-done.26
  212.3 3.1 %collective-permute-start.27 = (bf16[1,144,768]{2,1,0:T(8,128)(2,1)S(1)}, bf16[1,144,768]{2,1,0:T(8,128)(2,1)S(1)}, u32[]{:S(2)}, u32[]{:S(2)}) collective-permute-start(bf16[1,144,768]{2,1,0:T(8,128)(2,1)S(1)} %get-tuple-element.140), channel_id=1, source_target_pairs={{0,16},{4,20},{8,24},{12,28},{16,0},{20,4},{24,8},{28,12},{1,17},{... | collective-permute-start | bytes 663560 | tf_op jit(solution)/shard_map/ppermute | solution.py:891
  215.5 10.0 %collective-permute-done.27 = bf16[1,144,768]{2,1,0:T(8,128)(2,1)S(1)} collective-permute-done((bf16[1,144,768]{2,1,0:T(8,128)(2,1)S(1)}, bf16[1,144,768]{2,1,0:T(8,128)(2,1)S(1)}, u32[]{:S(2)}, u32[]{:S(2)}) %collective-permute-start.27) | collective-permute-done | bytes 221216 | tf_op jit(solution)/shard_map/ppermute | solution.py:891
  226.2 2.3 cut.1
  229.3 2.7 %collective-permute-start.30 = (bf16[48,1792]{1,0:T(8,128)(2,1)}, bf16[48,1792]{1,0:T(8,128)(2,1)S(1)}, u32[]{:S(2)}, u32[]{:S(2)}) collective-permute-start(bf16[48,1792]{1,0:T(8,128)(2,1)} %get-tuple-element.121), channel_id=1, source_target_pairs={{0,3},{1,2},{2,1},{3,0},{4,7},{5,6},{6,5},{7,4},{8,11},{9,10},{10,... | collective-permute-start | bytes 516104 | tf_op jit(solution)/shard_map/ppermute | solution.py:852
  233.5 2.5 collective-permute-done.28.refs_8_
  239.8 4.2 %join.1 = (f32[32,4096]{1,0:T(8,128)}, f32[32,3072]{1,0:T(8,128)}, f32[32,1024]{1,0:T(8,128)}, f32[32]{0:T(128)}, f32[32]{0:T(128)}, /*index=5*/f32[32]{0:T(128)...) custom-call(s32[1]{0:T(128)} %bitcast.member, ...), custom_call_target="tpu_custom_call" | custom-call | tf_op jit(solution)/shard_map/join/pallas_call | solution.py:835
  (140 shorter events, 46.2 us)
Async XLA Ops:
  7.2 50.0 %all-gather.5.cloned.1.call-start = ((), (), s32[]{:S(2)}) async-start(), calls=%async_computation.2 | async-start | bytes 2064384 | tf_op jit(solution)/shard_map/all_gather | solution.py:925
  22.6 80.2 %all-gather.7.cloned.1.call-start = ((), (), s32[]{:S(2)}) async-start(), calls=%async_computation.3 | async-start | bytes 5308416 | tf_op jit(solution)/shard_map/all_gather | solution.py:925
  22.8 12.9 %collective-permute-start.3 = (bf16[256,1024]{1,0:T(8,128)(2,1)S(1)}, bf16[256,1024]{1,0:T(8,128)(2,1)S(1)}, u32[]{:S(2)}, u32[]{:S(2)}) collective-permute-start(bf16[256,1024]{1,0:T(8,128)(2,1)S(1)} %get-tuple-element.80.refs_0_.rest_0_), channel_id=1, source_target_pairs={{0,1},{1,0},{2,3},{3,2},{4,5},{5,4},{6,7},{7,6},{8,9},{9,8},{10,11... | collective-permute-start | bytes 1572872 | tf_op jit(solution)/shard_map/ppermute | solution.py:852
  23.9 12.5 %collective-permute-start.6 = (bf16[256,1024]{1,0:T(8,128)(2,1)S(1)}, bf16[256,1024]{1,0:T(8,128)(2,1)S(1)}, u32[]{:S(2)}, u32[]{:S(2)}) collective-permute-start(bf16[256,1024]{1,0:T(8,128)(2,1)S(1)} %get-tuple-element.81.refs_1_.rest_1_), channel_id=1, source_target_pairs={{0,2},{1,3},{2,0},{3,1},{4,6},{5,7},{6,4},{7,5},{8,10},{9,11},{10,... | collective-permute-start | bytes 1572872 | tf_op jit(solution)/shard_map/ppermute | solution.py:852
  37.4 188.1 %reduce-scatter.2.cloned.1.call-start = ((), (), s32[]{:S(2)}) async-start(), calls=%async_computation.1 | async-start | bytes 5603328 | tf_op jit(solution)/shard_map/reduce_scatter | solution.py:929
  37.4 14.8 %collective-permute-start.5 = (bf16[256,1024]{1,0:T(8,128)(2,1)S(1)}, bf16[256,1024]{1,0:T(8,128)(2,1)S(1)}, u32[]{:S(2)}, u32[]{:S(2)}) collective-permute-start(bf16[256,1024]{1,0:T(8,128)(2,1)S(1)} %get-tuple-element.80.refs_0_.rest_0_), channel_id=1, source_target_pairs={{0,2},{1,3},{2,0},{3,1},{4,6},{5,7},{6,4},{7,5},{8,10},{9,11},{10,... | collective-permute-start | bytes 1572872 | tf_op jit(solution)/shard_map/ppermute | solution.py:852
  39.4 14.9 %collective-permute-start.4 = (bf16[256,1024]{1,0:T(8,128)(2,1)S(1)}, bf16[256,1024]{1,0:T(8,128)(2,1)S(1)}, u32[]{:S(2)}, u32[]{:S(2)}) collective-permute-start(bf16[256,1024]{1,0:T(8,128)(2,1)S(1)} %get-tuple-element.81.refs_1_.rest_1_), channel_id=1, source_target_pairs={{0,1},{1,0},{2,3},{3,2},{4,5},{5,4},{6,7},{7,6},{8,9},{9,8},{10,11... | collective-permute-start | bytes 1572872 | tf_op jit(solution)/shard_map/ppermute | solution.py:852
  42.1 21.5 %collective-permute-start.7 = (bf16[256,1024]{1,0:T(8,128)(2,1)S(1)}, bf16[256,1024]{1,0:T(8,128)(2,1)}, u32[]{:S(2)}, u32[]{:S(2)}) collective-permute-start(bf16[256,1024]{1,0:T(8,128)(2,1)S(1)} %collective-permute-done.3.refs_2_.rest_2_), channel_id=1, source_target_pairs={{0,2},{1,3},{2,0},{3,1},{4,6},{5,7},{6,4},{7,5},{8,10},{9,11},{10,... | collective-permute-start | bytes 1572872 | tf_op jit(solution)/shard_map/ppermute | solution.py:852
  43.7 22.0 %collective-permute-start.8 = (bf16[256,1024]{1,0:T(8,128)(2,1)S(1)}, bf16[256,1024]{1,0:T(8,128)(2,1)}, u32[]{:S(2)}, u32[]{:S(2)}) collective-permute-start(bf16[256,1024]{1,0:T(8,128)(2,1)S(1)} %collective-permute-done.6.refs_5_.rest_5_), channel_id=1, source_target_pairs={{0,1},{1,0},{2,3},{3,2},{4,5},{5,4},{6,7},{7,6},{8,9},{9,8},{10,11... | collective-permute-start | bytes 1572872 | tf_op jit(solution)/shard_map/ppermute | solution.py:852
  54.3 22.5 %collective-permute-start.12 = (bf16[256,1024]{1,0:T(8,128)(2,1)}, bf16[256,1024]{1,0:T(8,128)(2,1)S(1)}, u32[]{:S(2)}, u32[]{:S(2)}) collective-permute-start(bf16[256,1024]{1,0:T(8,128)(2,1)} %get-tuple-element.83.refs_9_), channel_id=1, source_target_pairs={{0,2},{1,3},{2,0},{3,1},{4,6},{5,7},{6,4},{7,5},{8,10},{9,11},{10,... | collective-permute-start | bytes 1572872 | tf_op jit(solution)/shard_map/ppermute | solution.py:852
  54.4 22.5 %collective-permute-start.9 = (bf16[256,1024]{1,0:T(8,128)(2,1)}, bf16[256,1024]{1,0:T(8,128)(2,1)S(1)}, u32[]{:S(2)}, u32[]{:S(2)}) collective-permute-start(bf16[256,1024]{1,0:T(8,128)(2,1)} %get-tuple-element.82.refs_8_), channel_id=1, source_target_pairs={{0,1},{1,0},{2,3},{3,2},{4,5},{5,4},{6,7},{7,6},{8,9},{9,8},{10,11... | collective-permute-start | bytes 1572872 | tf_op jit(solution)/shard_map/ppermute | solution.py:852
  56.6 40.5 %collective-permute-start.11 = (bf16[256,1024]{1,0:T(8,128)(2,1)}, bf16[256,1024]{1,0:T(8,128)(2,1)}, u32[]{:S(2)}, u32[]{:S(2)}) collective-permute-start(bf16[256,1024]{1,0:T(8,128)(2,1)} %get-tuple-element.82.refs_8_), channel_id=1, source_target_pairs={{0,2},{1,3},{2,0},{3,1},{4,6},{5,7},{6,4},{7,5},{8,10},{9,11},{10,... | collective-permute-start | bytes 1572872 | tf_op jit(solution)/shard_map/ppermute | solution.py:852
  63.6 33.5 %collective-permute-start.10 = (bf16[256,1024]{1,0:T(8,128)(2,1)}, bf16[256,1024]{1,0:T(8,128)(2,1)S(1)}, u32[]{:S(2)}, u32[]{:S(2)}) collective-permute-start(bf16[256,1024]{1,0:T(8,128)(2,1)} %get-tuple-element.83.refs_9_), channel_id=1, source_target_pairs={{0,1},{1,0},{2,3},{3,2},{4,5},{5,4},{6,7},{7,6},{8,9},{9,8},{10,11... | collective-permute-start | bytes 1572872 | tf_op jit(solution)/shard_map/ppermute | solution.py:852
  76.8 20.3 %collective-permute-start.13 = (bf16[256,1024]{1,0:T(8,128)(2,1)S(1)}, bf16[256,1024]{1,0:T(8,128)(2,1)S(1)}, u32[]{:S(2)}, u32[]{:S(2)}) collective-permute-start(bf16[256,1024]{1,0:T(8,128)(2,1)S(1)} %collective-permute-done.9.refs_10_), channel_id=1, source_target_pairs={{0,2},{1,3},{2,0},{3,1},{4,6},{5,7},{6,4},{7,5},{8,10},{9,11},{10,... | collective-permute-start | bytes 1572872 | tf_op jit(solution)/shard_map/ppermute | solution.py:852
  77.3 19.9 %collective-permute-start.14 = (bf16[256,1024]{1,0:T(8,128)(2,1)S(1)}, bf16[256,1024]{1,0:T(8,128)(2,1)S(1)}, u32[]{:S(2)}, u32[]{:S(2)}) collective-permute-start(bf16[256,1024]{1,0:T(8,128)(2,1)S(1)} %collective-permute-done.12.refs_13_), channel_id=1, source_target_pairs={{0,1},{1,0},{2,3},{3,2},{4,5},{5,4},{6,7},{7,6},{8,9},{9,8},{10,11... | collective-permute-start | bytes 1572872 | tf_op jit(solution)/shard_map/ppermute | solution.py:852
  145.2 46.4 %collective-permute-start.16 = (bf16[512,1024]{1,0:T(8,128)(2,1)S(1)}, bf16[512,1024]{1,0:T(8,128)(2,1)}, u32[]{:S(2)}, u32[]{:S(2)}) collective-permute-start(bf16[512,1024]{1,0:T(8,128)(2,1)S(1)} %copy-done.31), channel_id=1, source_target_pairs={{0,1},{1,0},{2,3},{3,2},{4,5},{5,4},{6,7},{7,6},{8,9},{9,8},{10,11... | collective-permute-start | bytes 3145736 | tf_op jit(solution)/shard_map/ppermute | solution.py:852
  146.5 48.3 %collective-permute-start.17 = (bf16[512,1024]{1,0:T(8,128)(2,1)}, bf16[512,1024]{1,0:T(8,128)(2,1)}, u32[]{:S(2)}, u32[]{:S(2)}) collective-permute-start(bf16[512,1024]{1,0:T(8,128)(2,1)} %get-tuple-element.95), channel_id=1, source_target_pairs={{0,2},{1,3},{2,0},{3,1},{4,6},{5,7},{6,4},{7,5},{8,10},{9,11},{10,... | collective-permute-start | bytes 3145736 | tf_op jit(solution)/shard_map/ppermute | solution.py:852
  148.1 46.8 %collective-permute-start.18 = (bf16[512,1024]{1,0:T(8,128)(2,1)S(1)}, bf16[512,1024]{1,0:T(8,128)(2,1)}, u32[]{:S(2)}, u32[]{:S(2)}) collective-permute-start(bf16[512,1024]{1,0:T(8,128)(2,1)S(1)} %copy-done.30), channel_id=1, source_target_pairs={{0,3},{1,2},{2,1},{3,0},{4,7},{5,6},{6,5},{7,4},{8,11},{9,10},{10,... | collective-permute-start | bytes 3145736 | tf_op jit(solution)/shard_map/ppermute | solution.py:852
  187.9 16.6 %collective-permute-start.20 = (bf16[256,1024]{1,0:T(8,128)(2,1)}, bf16[256,1024]{1,0:T(8,128)(2,1)S(1)}, u32[]{:S(2)}, u32[]{:S(2)}) collective-permute-start(bf16[256,1024]{1,0:T(8,128)(2,1)} %get-tuple-element.106), channel_id=1, source_target_pairs={{0,2},{1,3},{2,0},{3,1},{4,6},{5,7},{6,4},{7,5},{8,10},{9,11},{10,... | collective-permute-start | bytes 1572872 | tf_op jit(solution)/shard_map/ppermute | solution.py:852
  204.7 24.2 %collective-permute-start.22 = (bf16[256,1024]{1,0:T(8,128)(2,1)S(1)}, bf16[256,1024]{1,0:T(8,128)(2,1)S(1)}, u32[]{:S(2)}, u32[]{:S(2)}) collective-permute-start(bf16[256,1024]{1,0:T(8,128)(2,1)S(1)} %add_convert_fusion.2), channel_id=1, source_target_pairs={{0,1},{1,0},{2,3},{3,2},{4,5},{5,4},{6,7},{7,6},{8,9},{9,8},{10,11... | collective-permute-start | bytes 1572872 | tf_op jit(solution)/shard_map/ppermute | solution.py:852
  205.6 23.7 %collective-permute-start.24 = (bf16[256,1024]{1,0:T(8,128)(2,1)S(1)}, bf16[256,1024]{1,0:T(8,128)(2,1)S(1)}, u32[]{:S(2)}, u32[]{:S(2)}) collective-permute-start(bf16[256,1024]{1,0:T(8,128)(2,1)S(1)} %add_convert_fusion.1), channel_id=1, source_target_pairs={{0,2},{1,3},{2,0},{3,1},{4,6},{5,7},{6,4},{7,5},{8,10},{9,11},{10,... | collective-permute-start | bytes 1572872 | tf_op jit(solution)/shard_map/ppermute | solution.py:852
  206.6 26.2 %collective-permute-start.19 = (bf16[256,1024]{1,0:T(8,128)(2,1)}, bf16[256,1024]{1,0:T(8,128)(2,1)S(1)}, u32[]{:S(2)}, u32[]{:S(2)}) collective-permute-start(bf16[256,1024]{1,0:T(8,128)(2,1)} %get-tuple-element.104), channel_id=1, source_target_pairs={{0,1},{1,0},{2,3},{3,2},{4,5},{5,4},{6,7},{7,6},{8,9},{9,8},{10,11... | collective-permute-start | bytes 1572872 | tf_op jit(solution)/shard_map/ppermute | solution.py:852
  208.6 24.9 %collective-permute-start.25 = (bf16[256,1024]{1,0:T(8,128)(2,1)}, bf16[256,1024]{1,0:T(8,128)(2,1)S(1)}, u32[]{:S(2)}, u32[]{:S(2)}) collective-permute-start(bf16[256,1024]{1,0:T(8,128)(2,1)} %get-tuple-element.115), channel_id=1, source_target_pairs={{0,2},{1,3},{2,0},{3,1},{4,6},{5,7},{6,4},{7,5},{8,10},{9,11},{10,... | collective-permute-start | bytes 1572872 | tf_op jit(solution)/shard_map/ppermute | solution.py:852
  212.3 13.1 %collective-permute-start.27 = (bf16[1,144,768]{2,1,0:T(8,128)(2,1)S(1)}, bf16[1,144,768]{2,1,0:T(8,128)(2,1)S(1)}, u32[]{:S(2)}, u32[]{:S(2)}) collective-permute-start(bf16[1,144,768]{2,1,0:T(8,128)(2,1)S(1)} %get-tuple-element.140), channel_id=1, source_target_pairs={{0,16},{4,20},{8,24},{12,28},{16,0},{20,4},{24,8},{28,12},{1,17},{... | collective-permute-start | bytes 663560 | tf_op jit(solution)/shard_map/ppermute | solution.py:891
  (45 other events, 413.2 us)
Sparse Core Ops, SparseCore 0:
  22.7 27.2 all-gather.4
  51.7 51.0 all-gather.6
  144.1 56.7 reduce-scatter.1

commit v8 on v7

--- a/solution.py
+++ b/solution.py
@@ -760,64 +760,63 @@
     )(base, *vectors, *common, *parts)
 
 
-def cut_kernel(members, member, first, second, third, *out):
-    pieces, (down, line) = out[:members], out[members:]
+def cut_kernel(first, second, third, pieces, down, line):
     columns = first.shape[1]
-    shard = pieces[0].shape[0] - EXTRA
+    members, shard, _ = pieces.shape
     low = members * shard
-    for bit, piece in enumerate(pieces):
-        rows = pl.ds(pl.multiple_of((member[0] ^ bit) * shard, shard), shard)
-        piece[:shard, :columns] = first[rows, :]
-        piece[:shard, columns:] = (second[rows, :].astype(F32) + third[rows, :].astype(F32)).astype(LOW)
-        piece[shard:, :columns] = first[first.shape[0] - EXTRA :, :]
-        piece[shard:, columns:] = (second[low:, :].astype(F32) + third[low:, :].astype(F32)).astype(LOW)
+    both = columns + second.shape[1]
+    for at in range(members):
+        rows = slice(at * shard, (at + 1) * shard)
+        pieces[at, :, :columns] = first[rows, :]
+        pieces[at, :, columns:both] = (second[rows, :].astype(F32) + third[rows, :].astype(F32)).astype(LOW)
+        pieces[at, :EXTRA, both:] = first[first.shape[0] - EXTRA :, :128]
+        pieces[at, EXTRA:, both:] = (second[low:, :128].astype(F32) + third[low:, :128].astype(F32)).astype(LOW)
     down[...] = first[low : low + down.shape[0], :].astype(F32)
     line[...] = first[first.shape[0] - EXTRA :, :128].astype(F32)[3, :]
 
 
-def call_cut(member, first, second, third, members, shard):
+def call_cut(first, second, third, members, shard):
     columns = first.shape[1]
-    shapes = [jax.ShapeDtypeStruct((shard + EXTRA, columns + second.shape[1]), LOW)] * members + [
+    shapes = [
+        jax.ShapeDtypeStruct((members, shard, columns + second.shape[1] + 128), LOW),
         jax.ShapeDtypeStruct((first.shape[0] - (members + 1) * shard - EXTRA, columns), F32),
         jax.ShapeDtypeStruct((128,), F32),
     ]
     return pl.pallas_call(
-        functools.partial(cut_kernel, members),
-        grid_spec=pltpu.PrefetchScalarGridSpec(
-            num_scalar_prefetch=1,
-            grid=(1,),
-            in_specs=[whole(first.shape), whole(second.shape), whole(third.shape)],
-            out_specs=[whole(a.shape) for a in shapes],
-        ),
+        cut_kernel,
+        grid=(1,),
+        in_specs=[whole(first.shape), whole(second.shape), whole(third.shape)],
+        out_specs=[whole(a.shape) for a in shapes],
         out_shape=shapes,
         compiler_params=params("arbitrary"),
         cost_estimate=SHORT,
         name="cut",
-    )(member, first, second, third)
-
-
-def join_kernel(places, second, count, member, *refs):
+    )(first, second, third)
+
+
+def join_kernel(places, count, member, *refs):
     base, parts, refs, total = refs[0], refs[1 : 1 + count], refs[1 + count : -1], refs[-1]
     finish_kernel(0, 0, base, *parts, total)
 
     @pl.when(pl.program_id(0) == 0)
     def _():
-        join_pieces(places, second, member, *refs)
-
-
-def join_pieces(places, second, member, *refs):
-    *pieces, last, up, qkv, out, gain_1, bias_1, gain_2, bias_2, end_bias, end_bias_2, shift = refs
+        join_pieces(places, member, *refs)
+
+
+def join_pieces(places, member, *refs):
+    pieces, last, up, qkv, out, gain_1, bias_1, gain_2, bias_2, end_bias, end_bias_2, shift = refs
     outs = up, qkv
-    shard = up.shape[0]
-    for bit, piece in enumerate(pieces):
+    members = pieces.shape[0]
+    for at in range(members):
         for block, (index, column, stride) in enumerate(places):
-            start = pl.multiple_of(column + (member[0] ^ bit) * stride, 128)
-            outs[index][:, pl.ds(start, 128)] = piece[:shard, block * 128 : (block + 1) * 128].astype(F32)
+            start = column + at * stride
+            outs[index][:, start : start + 128] = pieces[at, :, block * 128 : (block + 1) * 128].astype(F32)
     out[...] = last[...].astype(F32)
     size = gain_1.shape[0]
-    two, one = (sum(piece[shard:, low : low + 128].astype(F32) for piece in pieces) for low in (0, second))
+    low = len(places) * 128
+    two, one = (sum(pieces[at, row : row + EXTRA, low:].astype(F32) for at in range(members)) for row in (0, EXTRA))
     wide = jnp.concatenate([one[2:3, :], one[3:4, :], one[4:5, :]], axis=1)
-    for at in range(len(pieces)):
+    for at in range(members):
 
         @pl.when(member[0] == at)
         def _():
@@ -827,24 +826,24 @@
             shift[...] = wide[0, 3 * at * size : 3 * (at + 1) * size]
 
 
-def call_join(member, base, parts, pieces, last, places, second, columns):
-    shard = pieces[0].shape[0] - EXTRA
-    size = 128 // len(pieces)
+def call_join(member, base, parts, pieces, last, places, columns):
+    members, shard, _ = pieces.shape
+    size = 128 // members
     shapes = [(shard, c) for c in columns] + [last.shape] + [(size,)] * 6 + [(3 * size,)]
     block = pl.BlockSpec((base.shape[0] // 2, base.shape[1]), lambda i, o: (i, 0))
     return pl.pallas_call(
-        functools.partial(join_kernel, tuple(places), second, len(parts)),
+        functools.partial(join_kernel, tuple(places), len(parts)),
         grid_spec=pltpu.PrefetchScalarGridSpec(
             num_scalar_prefetch=1,
             grid=(2,),
-            in_specs=[block] + [whole(p.shape) for p in (*parts, *pieces, last)],
+            in_specs=[block] + [whole(p.shape) for p in (*parts, pieces, last)],
             out_specs=[whole(a) for a in shapes] + [block],
         ),
         out_shape=[jax.ShapeDtypeStruct(a, F32) for a in shapes] + [jax.ShapeDtypeStruct(base.shape, LOW)],
         compiler_params=params("arbitrary"),
         cost_estimate=SHORT,
         name="join",
-    )(member, base, *parts, *pieces, last)
+    )(member, base, *parts, pieces, last)
 
 
 def across(array, bit):
@@ -958,7 +957,7 @@
     width = model // members
     units_dev = up_bias.shape[0]
     units = groups * units_dev
-    paired = members == 4 and units_dev == 128 and units == model
+    paired = members == 4 and units_dev == 128 and units == model and shard == 2 * EXTRA
     me = member.astype(jnp.int32).reshape(1)
     vectors_in = [norm1_gain, norm1_bias, norm2_gain, norm2_bias, out_bias, down_bias]
 
@@ -1039,17 +1038,19 @@
         parts = total[:half], total[half:]
     while blocks.shape[0] > 1:
         (blocks, far, _), bit = scatter_step(blocks, far, bit), 2 * bit
+    if members == 4:
+        far = behind(far, *near[2:])
     g_qkv = blocks[0], far[0]
     place = group * members + member
     if paired:
-        *mixed_pieces, g_down, up_shift = call_cut(me, scattered, *g_qkv, members, shard)
+        mixed_pieces, g_down, up_shift = call_cut(scattered, *g_qkv, members, shard)
         g_out = scattered[scattered.shape[0] - shard - EXTRA : scattered.shape[0] - EXTRA]
         g_out = swap_owner(behind(g_out, g_down), True)
         places = [(0, b * members * units_dev, units_dev) for b in range(groups)]
         places += [(1, part * model + low, width) for part in range(3) for low in range(0, width, 128)]
-        arrived = [mixed_pieces[0]] + [across(mixed_pieces[bit], bit) for bit in range(1, members)]
+        arrived = lax.all_to_all(mixed_pieces, "fsdp", split_axis=0, concat_axis=0)
         g_up, g_qkv, g_out, *mine, grad_tokens = call_join(
-            me, cotangent, parts, arrived, g_out, places, model, (up_weight.shape[1], qkv_weight.shape[1])
+            me, cotangent, parts, arrived, g_out, places, (up_weight.shape[1], qkv_weight.shape[1])
         )
         mine.append(up_shift)
     else:

time: 253 us -> 252 us (level)
  starting transfers between devices: 41.4 us -> 34 us
  Pallas kernels: 125 us -> 132 us
    ppermute x3, starting transfers between devices: 8.05 us -> 0.39 us  [hop(): lax.ppermute(array, 'dp', [(i, i ^ bit) for i in range(lax.axis_size('dp'...]
    all_to_all x0 -> x1, waiting for transfers between devices: none -> 6.52 us  [local(): arrived = lax.all_to_all(mixed_pieces, 'fsdp', split_axis=0, concat_axis=0)]
    pallas_call x1, Pallas kernels: 39.2 us -> 44.1 us  [call_bwd(): pl.pallas_call(functools.partial(bwd_kernel, plan, span // BLOCK, groups,...]
    all_to_all x0 -> x1, starting transfers between devices: none -> 3.47 us  [local(): arrived = lax.all_to_all(mixed_pieces, 'fsdp', split_axis=0, concat_axis=0)]
    ppermute x27 -> x24, starting transfers between devices: 31.9 us -> 28.7 us  [across(): return lax.ppermute(array, 'fsdp', [(i, i ^ bit) for i in range(size)])]
    pallas_call x1, Pallas kernels: 17.4 us -> 20.4 us  [call_fwd(): pl.pallas_call(fwd_kernel, grid_spec=pltpu.PrefetchScalarGridSpec(num_sca...]
    all_gather x2, waiting for transfers between devices: 5.67 us -> 2.71 us  [gather_dp(): return lax.all_gather(array, 'dp', axis=0)]
    ppermute x27 -> x24, waiting for transfers between devices: 41.9 us -> 41.5 us  [across(): return lax.ppermute(array, 'fsdp', [(i, i ^ bit) for i in range(size)])]
  transfers between devices with their start and end apart: 35 -> 33, of which waited for: 16 -> 16; matrix products, arithmetic and copies ran while one was open for 3% -> 3% of each run, Pallas kernels for 30% -> 33%
where the time goes in v8:
time: 252 us; the launch traced here: 251 us
  Pallas kernels  132 us (52%)
  waiting for transfers between devices  61.2 us (24%)
  starting transfers between devices  34 us (13%)
  between operations  14.2 us (6%)
  local copies, waits for them, and re-layouts  6.24 us (2%)
  other arithmetic  2.9 us (1%)
    pallas_call x1, Pallas kernels, call_bwd(): pl.pallas_call(functools.partial(bwd_kernel, plan, span // BLOCK, groups,...  44.1 us
    ppermute x24, waiting for transfers between devices, across(): return lax.ppermute(array, 'fsdp', [(i, i ^ bit) for i in range(size)])  41.5 us
    pallas_call x1, Pallas kernels, call_mlp(): pl.pallas_call(functools.partial(mlp_kernel, plan, out_plan, count, len(o...  41 us
    ppermute x24, starting transfers between devices, across(): return lax.ppermute(array, 'fsdp', [(i, i ^ bit) for i in range(size)])  28.7 us
    pallas_call x1, Pallas kernels, call_fwd(): pl.pallas_call(fwd_kernel, grid_spec=pltpu.PrefetchScalarGridSpec(num_sca...  20.4 us
    pallas_call x1, Pallas kernels, call_qkv(): pl.pallas_call(functools.partial(qkv_kernel, plan, len(pieces)), grid_spe...  11.2 us
    ppermute x3, waiting for transfers between devices, hop(): lax.ppermute(array, 'dp', [(i, i ^ bit) for i in range(lax.axis_size('dp'...  10.4 us
    all_to_all x1, waiting for transfers between devices, local(): arrived = lax.all_to_all(mixed_pieces, 'fsdp', split_axis=0, concat_axis=0)  6.52 us
  transfers between devices with their start and end apart: 33, of which 16 were waited for; matrix products, arithmetic and copies ran while one was open for 3% of the time, Pallas kernels for 33%

profile of v8, /device:TPU:0, one launch (start us, length us, event | category | flops | bytes accessed | tf_op | source)
XLA Modules:
  0.0 251.0 jit_solution(2532535314549407118)
XLA Ops:
  7.3 2.0 pack.1
  9.3 3.0 %collective-permute-start = (bf16[32,1920]{1,0:T(8,128)(2,1)}, bf16[32,1920]{1,0:T(8,128)(2,1)S(1)}, u32[]{:S(2)}, u32[]{:S(2)}) collective-permute-start(bf16[32,1920]{1,0:T(8,128)(2,1)} %get-tuple-element.74), channel_id=1, source_target_pairs={{0,1},{1,0},{2,3},{3,2},{4,5},{5,4},{6,7},{7,6},{8,9},{9,8},{10,11... | collective-permute-start | bytes 368648 | tf_op jit(solution)/shard_map/ppermute | solution.py:851
  13.8 2.5 %collective-permute-done.refs_1_ = bf16[32,1920]{1,0:T(8,128)(2,1)S(1)} collective-permute-done((bf16[32,1920]{1,0:T(8,128)(2,1)}, bf16[32,1920]{1,0:T(8,128)(2,1)S(1)}, u32[]{:S(2)}, u32[]{:S(2)}) %collective-permute-start) | collective-permute-done | bytes 122912 | tf_op jit(solution)/shard_map/ppermute | solution.py:851
  16.3 3.7 %collective-permute-done.1.refs_2_ = bf16[32,1920]{1,0:T(8,128)(2,1)S(1)} collective-permute-done((bf16[32,1920]{1,0:T(8,128)(2,1)}, bf16[32,1920]{1,0:T(8,128)(2,1)S(1)}, u32[]{:S(2)}, u32[]{:S(2)}) %collective-permute-start.1) | collective-permute-done | bytes 122912 | tf_op jit(solution)/shard_map/ppermute | solution.py:851
  25.5 10.2 %collective-permute-done.3.refs_2_.rest_2_ = bf16[256,1024]{1,0:T(8,128)(2,1)S(1)} collective-permute-done((bf16[256,1024]{1,0:T(8,128)(2,1)S(1)}, bf16[256,1024]{1,0:T(8,128)(2,1)S(1)}, u32[]{:S(2)}, u32[]{:S(2)}) %collective-permute-start.3) | collective-permute-done | bytes 524320 | tf_op jit(solution)/shard_map/ppermute | solution.py:851
  37.4 2.0 collective-permute-start.5
  39.8 2.3 fusion
  44.0 8.3 %collective-permute-done.5.refs_4_.rest_4_ = bf16[256,1024]{1,0:T(8,128)(2,1)S(1)} collective-permute-done((bf16[256,1024]{1,0:T(8,128)(2,1)S(1)}, bf16[256,1024]{1,0:T(8,128)(2,1)S(1)}, u32[]{:S(2)}, u32[]{:S(2)}) %collective-permute-start.5) | collective-permute-done | bytes 524320 | tf_op jit(solution)/shard_map/ppermute | solution.py:851
  52.3 2.0 collective-permute-done.4.refs_3_.rest_3_
  58.8 4.8 %collective-permute-done.7.refs_6_.rest_6_ = bf16[256,1024]{1,0:T(8,128)(2,1)} collective-permute-done((bf16[256,1024]{1,0:T(8,128)(2,1)S(1)}, bf16[256,1024]{1,0:T(8,128)(2,1)}, u32[]{:S(2)}, u32[]{:S(2)}) %collective-permute-start.7) | collective-permute-done | bytes 524320 | tf_op jit(solution)/shard_map/ppermute | solution.py:851
  65.6 11.2 %qkv.3 = (bf16[2048,256]{1,0:T(8,128)(2,1)}, bf16[2048,256]{1,0:T(8,128)(2,1)}, bf16[2048,256]{1,0:T(8,128)(2,1)}) custom-call(s32[4]{0:T(128)} %iota_xor_fusion.order, bf16[256,1024]{1,0:T(8,128)(2,1)} %copy-done.1, bf16[256,1024]{1,0:T(8,128)(2,1)} %copy-done, bf16[256,1024]{1,0:T(8,128)(2,1)} %copy-done.2, bf16[256,1024]{1,0:T(8,128)(2,1)} %copy-done.5, ...), custom_call_target="tpu_custom_call" | custom-call | tf_op jit(solution)/shard_map/qkv/pallas_call | solution.py:266
  79.7 20.4 %attend.1 = (f32[2048,256]{1,0:T(8,128)}, bf16[2048,256]{1,0:T(8,128)(2,1)}, f32[4,2048]{1,0:T(4,128)}) custom-call(s32[13]{0:T(128)} %pad_add_fusion.first, bf16[2048,256]{1,0:T(8,128)(2,1)} %get-tuple-element.82.q, bf16[2048,256]{1,0:T(8,128)(2,1)} %get-tuple-element.85.k, bf16[2048,256]{1,0:T(8,128)(2,1)} %get-tuple-element.86.v), custom_call_target="tpu_custom_call" | custom-call | tf_op jit(solution)/shard_map/attend/pallas_call | solution.py:358
  100.1 2.7 %all-gather.7.cloned.1.call-done = bf16[2304,1024]{1,0:T(8,128)(2,1)} async-done(((bf16[288,1024]{1,0:T(8,128)(2,1)}), bf16[2304,1024]{1,0:T(8,128)(2,1)}) %all-gather.7.cloned.1.call-update) | async-done | bytes 4718608 | tf_op jit(solution)/shard_map/all_gather | solution.py:924
  102.9 41.0 %mlp.1 = (bf16[512,1024]{1,0:T(8,128)(2,1)}, bf16[512,1024]{1,0:T(8,128)(2,1)}, bf16[512,1024]{1,0:T(8,128)(2,1)}, bf16[512,1024]{1,0:T(8,128)(2,1)}, bf16[2048,...) custom-call(s32[4]{0:T(128)} %iota_xor_fusion.order, ...), custom_call_target="tpu_custom_call" | custom-call | tf_op jit(solution)/shard_map/mlp/pallas_call | solution.py:692
  148.0 44.1 %attend_back.1 = (bf16[256,1024]{1,0:T(8,128)(2,1)}, bf16[256,1024]{1,0:T(8,128)(2,1)}, bf16[256,1024]{1,0:T(8,128)(2,1)}, bf16[256,1024]{1,0:T(8,128)(2,1)}, bf...) custom-call(s32[13]{0:T(128)} %pad_add_fusion.first, ...), custom_call_target="tpu_custom_call" | custom-call | tf_op jit(solution)/shard_map/attend_back/pallas_call | solution.py:537
  194.8 3.9 %finish.1 = bf16[512,1024]{1,0:T(8,128)(2,1)} custom-call(bf16[512,1024]{1,0:T(8,128)(2,1)} %base.1, f32[16,1024]{1,0:T(8,128)} %vectors.1.refs_8_.refs_17_.refs_0_, bf16[512,1024]{1,0:T(8,128)(2,1)} %get-tuple-element.91.refs_1_, bf16[512,1024]{1,0:T(8,128)(2,1)} %collective-permute-done.16.refs_2_, bf16[512,1024]{1,0:T(8,128)(2,1)} %collective-permute-done.17.refs_3_, ...), custom_call_target="tpu_custom_call" | custom-call | flops 20000000000 | bytes 10000000 | tf_op jit(solution)/shard_map/finish/pallas_call | solution.py:751
  199.0 4.2 %collective-permute-done.23 = bf16[256,1024]{1,0:T(8,128)(2,1)S(1)} collective-permute-done((bf16[256,1024]{1,0:T(8,128)(2,1)}, bf16[256,1024]{1,0:T(8,128)(2,1)S(1)}, u32[]{:S(2)}, u32[]{:S(2)}) %collective-permute-start.23) | collective-permute-done | bytes 524320 | tf_op jit(solution)/shard_map/ppermute | solution.py:851
  207.6 4.0 %collective-permute-done.26 = bf16[2,144,768]{2,1,0:T(8,128)(2,1)S(1)} collective-permute-done((bf16[2,144,768]{2,1,0:T(8,128)(2,1)S(1)}, bf16[2,144,768]{2,1,0:T(8,128)(2,1)S(1)}, u32[]{:S(2)}, u32[]{:S(2)}) %collective-permute-start.26) | collective-permute-done | bytes 442400 | tf_op jit(solution)/shard_map/ppermute | solution.py:890
  215.6 3.0 %collective-permute-done.24.refs_5_ = bf16[256,1024]{1,0:T(8,128)(2,1)S(1)} collective-permute-done((bf16[256,1024]{1,0:T(8,128)(2,1)S(1)}, bf16[256,1024]{1,0:T(8,128)(2,1)S(1)}, u32[]{:S(2)}, u32[]{:S(2)}) %collective-permute-start.24) | collective-permute-done | bytes 524320 | tf_op jit(solution)/shard_map/ppermute | solution.py:851
  218.6 6.4 %collective-permute-done.27 = bf16[1,144,768]{2,1,0:T(8,128)(2,1)S(1)} collective-permute-done((bf16[1,144,768]{2,1,0:T(8,128)(2,1)S(1)}, bf16[1,144,768]{2,1,0:T(8,128)(2,1)S(1)}, u32[]{:S(2)}, u32[]{:S(2)}) %collective-permute-start.27) | collective-permute-done | bytes 221216 | tf_op jit(solution)/shard_map/ppermute | solution.py:890
  225.7 2.2 cut.1
  227.9 3.5 %all-to-all-start = ((bf16[4,32,1920]{2,1,0:T(8,128)(2,1)}), bf16[4,32,1920]{2,1,0:T(8,128)(2,1)S(1)}, u32[]{:S(2)}, u32[]{:S(2)}) async-start(bf16[4,32,1920]{2,1,0:T(8,128)(2,1)} %get-tuple-element.117), calls=%async_computation.1 | async-start | bytes 983040 | tf_op jit(solution)/shard_map/all_to_all | solution.py:1051
  233.0 6.5 %all-to-all-done.refs_7_ = bf16[4,32,1920]{2,1,0:T(8,128)(2,1)S(1)} async-done(((bf16[4,32,1920]{2,1,0:T(8,128)(2,1)}), bf16[4,32,1920]{2,1,0:T(8,128)(2,1)S(1)}, u32[]{:S(2)}, u32[]{:S(2)}) %all-to-all-start) | async-done | bytes 491552 | tf_op jit(solution)/shard_map/all_to_all | solution.py:1051
  240.3 4.1 %join.1 = (f32[32,4096]{1,0:T(8,128)}, f32[32,3072]{1,0:T(8,128)}, f32[32,1024]{1,0:T(8,128)}, f32[32]{0:T(128)}, f32[32]{0:T(128)}, /*index=5*/f32[32]{0:T(128)...) custom-call(s32[1]{0:T(128)} %bitcast.member, ...), custom_call_target="tpu_custom_call" | custom-call | tf_op jit(solution)/shard_map/join/pallas_call | solution.py:834
  (134 shorter events, 38.7 us)
Async XLA Ops:
  7.2 50.0 %all-gather.5.cloned.1.call-start = ((), (), s32[]{:S(2)}) async-start(), calls=%async_computation.3 | async-start | bytes 2064384 | tf_op jit(solution)/shard_map/all_gather | solution.py:924
  22.6 80.2 %all-gather.7.cloned.1.call-start = ((), (), s32[]{:S(2)}) async-start(), calls=%async_computation.4 | async-start | bytes 5308416 | tf_op jit(solution)/shard_map/all_gather | solution.py:924
  22.8 12.9 %collective-permute-start.3 = (bf16[256,1024]{1,0:T(8,128)(2,1)S(1)}, bf16[256,1024]{1,0:T(8,128)(2,1)S(1)}, u32[]{:S(2)}, u32[]{:S(2)}) collective-permute-start(bf16[256,1024]{1,0:T(8,128)(2,1)S(1)} %get-tuple-element.78.refs_0_.rest_0_), channel_id=1, source_target_pairs={{0,1},{1,0},{2,3},{3,2},{4,5},{5,4},{6,7},{7,6},{8,9},{9,8},{10,11... | collective-permute-start | bytes 1572872 | tf_op jit(solution)/shard_map/ppermute | solution.py:851
  23.9 12.5 %collective-permute-start.6 = (bf16[256,1024]{1,0:T(8,128)(2,1)S(1)}, bf16[256,1024]{1,0:T(8,128)(2,1)S(1)}, u32[]{:S(2)}, u32[]{:S(2)}) collective-permute-start(bf16[256,1024]{1,0:T(8,128)(2,1)S(1)} %get-tuple-element.79.refs_1_.rest_1_), channel_id=1, source_target_pairs={{0,2},{1,3},{2,0},{3,1},{4,6},{5,7},{6,4},{7,5},{8,10},{9,11},{10,... | collective-permute-start | bytes 1572872 | tf_op jit(solution)/shard_map/ppermute | solution.py:851
  37.4 187.6 %reduce-scatter.2.cloned.1.call-start = ((), (), s32[]{:S(2)}) async-start(), calls=%async_computation.2 | async-start | bytes 5603328 | tf_op jit(solution)/shard_map/reduce_scatter | solution.py:928
  37.4 14.8 %collective-permute-start.5 = (bf16[256,1024]{1,0:T(8,128)(2,1)S(1)}, bf16[256,1024]{1,0:T(8,128)(2,1)S(1)}, u32[]{:S(2)}, u32[]{:S(2)}) collective-permute-start(bf16[256,1024]{1,0:T(8,128)(2,1)S(1)} %get-tuple-element.78.refs_0_.rest_0_), channel_id=1, source_target_pairs={{0,2},{1,3},{2,0},{3,1},{4,6},{5,7},{6,4},{7,5},{8,10},{9,11},{10,... | collective-permute-start | bytes 1572872 | tf_op jit(solution)/shard_map/ppermute | solution.py:851
  39.4 14.9 %collective-permute-start.4 = (bf16[256,1024]{1,0:T(8,128)(2,1)S(1)}, bf16[256,1024]{1,0:T(8,128)(2,1)S(1)}, u32[]{:S(2)}, u32[]{:S(2)}) collective-permute-start(bf16[256,1024]{1,0:T(8,128)(2,1)S(1)} %get-tuple-element.79.refs_1_.rest_1_), channel_id=1, source_target_pairs={{0,1},{1,0},{2,3},{3,2},{4,5},{5,4},{6,7},{7,6},{8,9},{9,8},{10,11... | collective-permute-start | bytes 1572872 | tf_op jit(solution)/shard_map/ppermute | solution.py:851
  42.1 21.5 %collective-permute-start.7 = (bf16[256,1024]{1,0:T(8,128)(2,1)S(1)}, bf16[256,1024]{1,0:T(8,128)(2,1)}, u32[]{:S(2)}, u32[]{:S(2)}) collective-permute-start(bf16[256,1024]{1,0:T(8,128)(2,1)S(1)} %collective-permute-done.3.refs_2_.rest_2_), channel_id=1, source_target_pairs={{0,2},{1,3},{2,0},{3,1},{4,6},{5,7},{6,4},{7,5},{8,10},{9,11},{10,... | collective-permute-start | bytes 1572872 | tf_op jit(solution)/shard_map/ppermute | solution.py:851
  43.7 21.9 %collective-permute-start.8 = (bf16[256,1024]{1,0:T(8,128)(2,1)S(1)}, bf16[256,1024]{1,0:T(8,128)(2,1)}, u32[]{:S(2)}, u32[]{:S(2)}) collective-permute-start(bf16[256,1024]{1,0:T(8,128)(2,1)S(1)} %collective-permute-done.6.refs_5_.rest_5_), channel_id=1, source_target_pairs={{0,1},{1,0},{2,3},{3,2},{4,5},{5,4},{6,7},{7,6},{8,9},{9,8},{10,11... | collective-permute-start | bytes 1572872 | tf_op jit(solution)/shard_map/ppermute | solution.py:851
  54.3 22.5 %collective-permute-start.12 = (bf16[256,1024]{1,0:T(8,128)(2,1)}, bf16[256,1024]{1,0:T(8,128)(2,1)S(1)}, u32[]{:S(2)}, u32[]{:S(2)}) collective-permute-start(bf16[256,1024]{1,0:T(8,128)(2,1)} %get-tuple-element.81.refs_9_), channel_id=1, source_target_pairs={{0,2},{1,3},{2,0},{3,1},{4,6},{5,7},{6,4},{7,5},{8,10},{9,11},{10,... | collective-permute-start | bytes 1572872 | tf_op jit(solution)/shard_map/ppermute | solution.py:851
  54.4 22.5 %collective-permute-start.9 = (bf16[256,1024]{1,0:T(8,128)(2,1)}, bf16[256,1024]{1,0:T(8,128)(2,1)S(1)}, u32[]{:S(2)}, u32[]{:S(2)}) collective-permute-start(bf16[256,1024]{1,0:T(8,128)(2,1)} %get-tuple-element.80.refs_8_), channel_id=1, source_target_pairs={{0,1},{1,0},{2,3},{3,2},{4,5},{5,4},{6,7},{7,6},{8,9},{9,8},{10,11... | collective-permute-start | bytes 1572872 | tf_op jit(solution)/shard_map/ppermute | solution.py:851
  56.6 43.4 %collective-permute-start.11 = (bf16[256,1024]{1,0:T(8,128)(2,1)}, bf16[256,1024]{1,0:T(8,128)(2,1)}, u32[]{:S(2)}, u32[]{:S(2)}) collective-permute-start(bf16[256,1024]{1,0:T(8,128)(2,1)} %get-tuple-element.80.refs_8_), channel_id=1, source_target_pairs={{0,2},{1,3},{2,0},{3,1},{4,6},{5,7},{6,4},{7,5},{8,10},{9,11},{10,... | collective-permute-start | bytes 1572872 | tf_op jit(solution)/shard_map/ppermute | solution.py:851
  63.6 36.5 %collective-permute-start.10 = (bf16[256,1024]{1,0:T(8,128)(2,1)}, bf16[256,1024]{1,0:T(8,128)(2,1)S(1)}, u32[]{:S(2)}, u32[]{:S(2)}) collective-permute-start(bf16[256,1024]{1,0:T(8,128)(2,1)} %get-tuple-element.81.refs_9_), channel_id=1, source_target_pairs={{0,1},{1,0},{2,3},{3,2},{4,5},{5,4},{6,7},{7,6},{8,9},{9,8},{10,11... | collective-permute-start | bytes 1572872 | tf_op jit(solution)/shard_map/ppermute | solution.py:851
  76.8 23.3 %collective-permute-start.13 = (bf16[256,1024]{1,0:T(8,128)(2,1)S(1)}, bf16[256,1024]{1,0:T(8,128)(2,1)S(1)}, u32[]{:S(2)}, u32[]{:S(2)}) collective-permute-start(bf16[256,1024]{1,0:T(8,128)(2,1)S(1)} %collective-permute-done.9.refs_10_), channel_id=1, source_target_pairs={{0,2},{1,3},{2,0},{3,1},{4,6},{5,7},{6,4},{7,5},{8,10},{9,11},{10,... | collective-permute-start | bytes 1572872 | tf_op jit(solution)/shard_map/ppermute | solution.py:851
  77.3 22.8 %collective-permute-start.14 = (bf16[256,1024]{1,0:T(8,128)(2,1)S(1)}, bf16[256,1024]{1,0:T(8,128)(2,1)S(1)}, u32[]{:S(2)}, u32[]{:S(2)}) collective-permute-start(bf16[256,1024]{1,0:T(8,128)(2,1)S(1)} %collective-permute-done.12.refs_13_), channel_id=1, source_target_pairs={{0,1},{1,0},{2,3},{3,2},{4,5},{5,4},{6,7},{7,6},{8,9},{9,8},{10,11... | collective-permute-start | bytes 1572872 | tf_op jit(solution)/shard_map/ppermute | solution.py:851
  143.9 50.9 %collective-permute-start.16 = (bf16[512,1024]{1,0:T(8,128)(2,1)}, bf16[512,1024]{1,0:T(8,128)(2,1)}, u32[]{:S(2)}, u32[]{:S(2)}) collective-permute-start(bf16[512,1024]{1,0:T(8,128)(2,1)} %get-tuple-element.92), channel_id=1, source_target_pairs={{0,1},{1,0},{2,3},{3,2},{4,5},{5,4},{6,7},{7,6},{8,9},{9,8},{10,11... | collective-permute-start | bytes 3145736 | tf_op jit(solution)/shard_map/ppermute | solution.py:851
  145.4 49.4 %collective-permute-start.17 = (bf16[512,1024]{1,0:T(8,128)(2,1)S(1)}, bf16[512,1024]{1,0:T(8,128)(2,1)}, u32[]{:S(2)}, u32[]{:S(2)}) collective-permute-start(bf16[512,1024]{1,0:T(8,128)(2,1)S(1)} %copy-done.29), channel_id=1, source_target_pairs={{0,2},{1,3},{2,0},{3,1},{4,6},{5,7},{6,4},{7,5},{8,10},{9,11},{10,... | collective-permute-start | bytes 3145736 | tf_op jit(solution)/shard_map/ppermute | solution.py:851
  146.9 47.9 %collective-permute-start.18 = (bf16[512,1024]{1,0:T(8,128)(2,1)S(1)}, bf16[512,1024]{1,0:T(8,128)(2,1)}, u32[]{:S(2)}, u32[]{:S(2)}) collective-permute-start(bf16[512,1024]{1,0:T(8,128)(2,1)S(1)} %copy-done.28), channel_id=1, source_target_pairs={{0,3},{1,2},{2,1},{3,0},{4,7},{5,6},{6,5},{7,4},{8,11},{9,10},{10,... | collective-permute-start | bytes 3145736 | tf_op jit(solution)/shard_map/ppermute | solution.py:851
  192.1 12.0 %collective-permute-start.20 = (bf16[256,1024]{1,0:T(8,128)(2,1)}, bf16[256,1024]{1,0:T(8,128)(2,1)S(1)}, u32[]{:S(2)}, u32[]{:S(2)}) collective-permute-start(bf16[256,1024]{1,0:T(8,128)(2,1)} %get-tuple-element.104), channel_id=1, source_target_pairs={{0,2},{1,3},{2,0},{3,1},{4,6},{5,7},{6,4},{7,5},{8,10},{9,11},{10,... | collective-permute-start | bytes 1572872 | tf_op jit(solution)/shard_map/ppermute | solution.py:851
  199.0 12.6 %collective-permute-start.26 = (bf16[2,144,768]{2,1,0:T(8,128)(2,1)S(1)}, bf16[2,144,768]{2,1,0:T(8,128)(2,1)S(1)}, u32[]{:S(2)}, u32[]{:S(2)}) collective-permute-start(bf16[2,144,768]{2,1,0:T(8,128)(2,1)S(1)} %slice.33), channel_id=1, source_target_pairs={{0,8},{4,12},{8,0},{12,4},{16,24},{20,28},{24,16},{28,20},{1,9},{5... | collective-permute-start | bytes 1327112 | tf_op jit(solution)/shard_map/ppermute | solution.py:890
  206.1 12.5 %collective-permute-start.24 = (bf16[256,1024]{1,0:T(8,128)(2,1)S(1)}, bf16[256,1024]{1,0:T(8,128)(2,1)S(1)}, u32[]{:S(2)}, u32[]{:S(2)}) collective-permute-start(bf16[256,1024]{1,0:T(8,128)(2,1)S(1)} %add_convert_fusion.1), channel_id=1, source_target_pairs={{0,2},{1,3},{2,0},{3,1},{4,6},{5,7},{6,4},{7,5},{8,10},{9,11},{10,... | collective-permute-start | bytes 1572872 | tf_op jit(solution)/shard_map/ppermute | solution.py:851
  212.4 12.6 %collective-permute-start.27 = (bf16[1,144,768]{2,1,0:T(8,128)(2,1)S(1)}, bf16[1,144,768]{2,1,0:T(8,128)(2,1)S(1)}, u32[]{:S(2)}, u32[]{:S(2)}) collective-permute-start(bf16[1,144,768]{2,1,0:T(8,128)(2,1)S(1)} %get-tuple-element.136), channel_id=1, source_target_pairs={{0,16},{4,20},{8,24},{12,28},{16,0},{20,4},{24,8},{28,12},{1,17},{... | collective-permute-start | bytes 663560 | tf_op jit(solution)/shard_map/ppermute | solution.py:890
  212.7 20.2 %collective-permute-start.19 = (bf16[256,1024]{1,0:T(8,128)(2,1)}, bf16[256,1024]{1,0:T(8,128)(2,1)S(1)}, u32[]{:S(2)}, u32[]{:S(2)}) collective-permute-start(bf16[256,1024]{1,0:T(8,128)(2,1)} %get-tuple-element.102), channel_id=1, source_target_pairs={{0,1},{1,0},{2,3},{3,2},{4,5},{5,4},{6,7},{7,6},{8,9},{9,8},{10,11... | collective-permute-start | bytes 1572872 | tf_op jit(solution)/shard_map/ppermute | solution.py:851
  213.8 19.1 %collective-permute-start.25 = (bf16[256,1024]{1,0:T(8,128)(2,1)S(1)}, bf16[256,1024]{1,0:T(8,128)(2,1)S(1)}, u32[]{:S(2)}, u32[]{:S(2)}) collective-permute-start(bf16[256,1024]{1,0:T(8,128)(2,1)S(1)} %copy-done.30), channel_id=1, source_target_pairs={{0,2},{1,3},{2,0},{3,1},{4,6},{5,7},{6,4},{7,5},{8,10},{9,11},{10,... | collective-permute-start | bytes 1572872 | tf_op jit(solution)/shard_map/ppermute | solution.py:851
  (42 other events, 412.3 us)
Sparse Core Ops, SparseCore 0:
  22.7 27.2 all-gather.4
  51.7 51.0 all-gather.6
  144.0 56.8 reduce-scatter.1

commit v9 on v8

--- a/solution.py
+++ b/solution.py
@@ -677,7 +677,7 @@
     model = x_pieces[0].shape[1]
     joined = len(mats) == 1
     plan, out_plan = plan_of(x_pieces, span), plan_of(out_shapes, span)
-    steps, many = len(plan), 4
+    steps, many = len(plan), 2
     count = len(x_pieces)
     there = lambda i, o: (o[jnp.minimum(i, steps - 1)], 0)
     later = lambda i, o: (jnp.maximum(i - steps, 0), 0)
@@ -760,7 +760,7 @@
     )(base, *vectors, *common, *parts)
 
 
-def cut_kernel(first, second, third, pieces, down, line):
+def cut_kernel(first, second, third, pieces, down, line, out):
     columns = first.shape[1]
     members, shard, _ = pieces.shape
     low = members * shard
@@ -773,6 +773,7 @@
         pieces[at, EXTRA:, both:] = (second[low:, :128].astype(F32) + third[low:, :128].astype(F32)).astype(LOW)
     down[...] = first[low : low + down.shape[0], :].astype(F32)
     line[...] = first[first.shape[0] - EXTRA :, :128].astype(F32)[3, :]
+    out[...] = first[low + down.shape[0] : low + down.shape[0] + shard, :]
 
 
 def call_cut(first, second, third, members, shard):
@@ -781,6 +782,7 @@
         jax.ShapeDtypeStruct((members, shard, columns + second.shape[1] + 128), LOW),
         jax.ShapeDtypeStruct((first.shape[0] - (members + 1) * shard - EXTRA, columns), F32),
         jax.ShapeDtypeStruct((128,), F32),
+        jax.ShapeDtypeStruct((shard, columns), LOW),
     ]
     return pl.pallas_call(
         cut_kernel,
@@ -1043,9 +1045,8 @@
     g_qkv = blocks[0], far[0]
     place = group * members + member
     if paired:
-        mixed_pieces, g_down, up_shift = call_cut(scattered, *g_qkv, members, shard)
-        g_out = scattered[scattered.shape[0] - shard - EXTRA : scattered.shape[0] - EXTRA]
-        g_out = swap_owner(behind(g_out, g_down), True)
+        mixed_pieces, g_down, up_shift, g_out = call_cut(scattered, *g_qkv, members, shard)
+        g_out = swap_owner(g_out, True)
         places = [(0, b * members * units_dev, units_dev) for b in range(groups)]
         places += [(1, part * model + low, width) for part in range(3) for low in range(0, width, 128)]
         arrived = lax.all_to_all(mixed_pieces, "fsdp", split_axis=0, concat_axis=0)

time: 252 us -> 252 us (level)
  Pallas kernels: 132 us -> 125 us
  starting transfers between devices: 34 us -> 38.4 us
    ppermute x3, waiting for transfers between devices: 10.4 us -> 3.85 us  [hop(): lax.ppermute(array, 'dp', [(i, i ^ bit) for i in range(lax.axis_size('dp'...]
    ppermute x24, waiting for transfers between devices: 41.5 us -> 47.7 us  [across(): return lax.ppermute(array, 'fsdp', [(i, i ^ bit) for i in range(size)])]
    pallas_call x1, Pallas kernels: 44.1 us -> 39.5 us  [call_bwd(): pl.pallas_call(functools.partial(bwd_kernel, plan, span // BLOCK, groups,...]
    ppermute x3, starting transfers between devices: 0.39 us -> 3.51 us  [hop(): lax.ppermute(array, 'dp', [(i, i ^ bit) for i in range(lax.axis_size('dp'...]
    all_gather x2, waiting for transfers between devices: 2.71 us -> 5.68 us  [gather_dp(): return lax.all_gather(array, 'dp', axis=0)]
    pallas_call x1, Pallas kernels: 20.4 us -> 17.4 us  [call_fwd(): pl.pallas_call(fwd_kernel, grid_spec=pltpu.PrefetchScalarGridSpec(num_sca...]
  transfers between devices with their start and end apart: 33 -> 33, of which waited for: 16 -> 18; matrix products, arithmetic and copies ran while one was open for 3% -> 2% of each run, Pallas kernels for 33% -> 30%
where the time goes in v9:
time: 252 us; the launch traced here: 248 us
  Pallas kernels  125 us (50%)
  waiting for transfers between devices  63.1 us (25%)
  starting transfers between devices  38.4 us (15%)
  between operations  14.1 us (6%)
  local copies, waits for them, and re-layouts  5.39 us (2%)
  other arithmetic  2.9 us (1%)
    ppermute x24, waiting for transfers between devices, across(): return lax.ppermute(array, 'fsdp', [(i, i ^ bit) for i in range(size)])  47.7 us
    pallas_call x1, Pallas kernels, call_mlp(): pl.pallas_call(functools.partial(mlp_kernel, plan, out_plan, count, len(o...  40.8 us
    pallas_call x1, Pallas kernels, call_bwd(): pl.pallas_call(functools.partial(bwd_kernel, plan, span // BLOCK, groups,...  39.5 us
    ppermute x24, starting transfers between devices, across(): return lax.ppermute(array, 'fsdp', [(i, i ^ bit) for i in range(size)])  29.1 us
    pallas_call x1, Pallas kernels, call_fwd(): pl.pallas_call(fwd_kernel, grid_spec=pltpu.PrefetchScalarGridSpec(num_sca...  17.4 us
    pallas_call x1, Pallas kernels, call_qkv(): pl.pallas_call(functools.partial(qkv_kernel, plan, len(pieces)), grid_spe...  11.2 us
    all_to_all x1, waiting for transfers between devices, local(): arrived = lax.all_to_all(mixed_pieces, 'fsdp', split_axis=0, concat_axis=0)  5.89 us
    all_gather x2, waiting for transfers between devices, gather_dp(): return lax.all_gather(array, 'dp', axis=0)  5.68 us
  transfers between devices with their start and end apart: 33, of which 18 were waited for; matrix products, arithmetic and copies ran while one was open for 2% of the time, Pallas kernels for 30%

profile of v9, /device:TPU:0, one launch (start us, length us, event | category | flops | bytes accessed | tf_op | source)
XLA Modules:
  0.0 248.5 jit_solution(7893668775160092624)
XLA Ops:
  7.3 2.0 pack.1
  9.3 3.0 %collective-permute-start = (bf16[32,1920]{1,0:T(8,128)(2,1)}, bf16[32,1920]{1,0:T(8,128)(2,1)S(1)}, u32[]{:S(2)}, u32[]{:S(2)}) collective-permute-start(bf16[32,1920]{1,0:T(8,128)(2,1)} %get-tuple-element.74), channel_id=1, source_target_pairs={{0,1},{1,0},{2,3},{3,2},{4,5},{5,4},{6,7},{7,6},{8,9},{9,8},{10,11... | collective-permute-start | bytes 368648 | tf_op jit(solution)/shard_map/ppermute | solution.py:853
  13.8 2.5 %collective-permute-done.refs_1_ = bf16[32,1920]{1,0:T(8,128)(2,1)S(1)} collective-permute-done((bf16[32,1920]{1,0:T(8,128)(2,1)}, bf16[32,1920]{1,0:T(8,128)(2,1)S(1)}, u32[]{:S(2)}, u32[]{:S(2)}) %collective-permute-start) | collective-permute-done | bytes 122912 | tf_op jit(solution)/shard_map/ppermute | solution.py:853
  16.3 3.7 %collective-permute-done.1.refs_2_ = bf16[32,1920]{1,0:T(8,128)(2,1)S(1)} collective-permute-done((bf16[32,1920]{1,0:T(8,128)(2,1)}, bf16[32,1920]{1,0:T(8,128)(2,1)S(1)}, u32[]{:S(2)}, u32[]{:S(2)}) %collective-permute-start.1) | collective-permute-done | bytes 122912 | tf_op jit(solution)/shard_map/ppermute | solution.py:853
  25.5 10.2 %collective-permute-done.3.refs_2_.rest_2_ = bf16[256,1024]{1,0:T(8,128)(2,1)S(1)} collective-permute-done((bf16[256,1024]{1,0:T(8,128)(2,1)S(1)}, bf16[256,1024]{1,0:T(8,128)(2,1)S(1)}, u32[]{:S(2)}, u32[]{:S(2)}) %collective-permute-start.3) | collective-permute-done | bytes 524320 | tf_op jit(solution)/shard_map/ppermute | solution.py:853
  39.8 2.3 fusion
  44.0 8.3 %collective-permute-done.5.refs_4_.rest_4_ = bf16[256,1024]{1,0:T(8,128)(2,1)S(1)} collective-permute-done((bf16[256,1024]{1,0:T(8,128)(2,1)S(1)}, bf16[256,1024]{1,0:T(8,128)(2,1)S(1)}, u32[]{:S(2)}, u32[]{:S(2)}) %collective-permute-start.5) | collective-permute-done | bytes 524320 | tf_op jit(solution)/shard_map/ppermute | solution.py:853
  52.3 2.0 collective-permute-done.4.refs_3_.rest_3_
  58.8 4.8 %collective-permute-done.7.refs_6_.rest_6_ = bf16[256,1024]{1,0:T(8,128)(2,1)} collective-permute-done((bf16[256,1024]{1,0:T(8,128)(2,1)S(1)}, bf16[256,1024]{1,0:T(8,128)(2,1)}, u32[]{:S(2)}, u32[]{:S(2)}) %collective-permute-start.7) | collective-permute-done | bytes 524320 | tf_op jit(solution)/shard_map/ppermute | solution.py:853
  65.6 11.2 %qkv.3 = (bf16[2048,256]{1,0:T(8,128)(2,1)}, bf16[2048,256]{1,0:T(8,128)(2,1)}, bf16[2048,256]{1,0:T(8,128)(2,1)}) custom-call(s32[4]{0:T(128)} %iota_xor_fusion.order, bf16[256,1024]{1,0:T(8,128)(2,1)} %copy-done.1, bf16[256,1024]{1,0:T(8,128)(2,1)} %copy-done, bf16[256,1024]{1,0:T(8,128)(2,1)} %copy-done.2, bf16[256,1024]{1,0:T(8,128)(2,1)} %copy-done.5, ...), custom_call_target="tpu_custom_call" | custom-call | tf_op jit(solution)/shard_map/qkv/pallas_call | solution.py:266
  79.7 17.4 %attend.1 = (f32[2048,256]{1,0:T(8,128)}, bf16[2048,256]{1,0:T(8,128)(2,1)}, f32[4,2048]{1,0:T(4,128)}) custom-call(s32[13]{0:T(128)} %pad_add_fusion.first, bf16[2048,256]{1,0:T(8,128)(2,1)} %get-tuple-element.82.q, bf16[2048,256]{1,0:T(8,128)(2,1)} %get-tuple-element.85.k, bf16[2048,256]{1,0:T(8,128)(2,1)} %get-tuple-element.86.v), custom_call_target="tpu_custom_call" | custom-call | tf_op jit(solution)/shard_map/attend/pallas_call | solution.py:358
  97.2 5.7 %all-gather.7.cloned.1.call-done = bf16[2304,1024]{1,0:T(8,128)(2,1)} async-done(((bf16[288,1024]{1,0:T(8,128)(2,1)}), bf16[2304,1024]{1,0:T(8,128)(2,1)}) %all-gather.7.cloned.1.call-update) | async-done | bytes 4718608 | tf_op jit(solution)/shard_map/all_gather | solution.py:926
  102.9 40.8 %mlp.1 = (bf16[512,1024]{1,0:T(8,128)(2,1)}, bf16[512,1024]{1,0:T(8,128)(2,1)}, bf16[512,1024]{1,0:T(8,128)(2,1)}, bf16[512,1024]{1,0:T(8,128)(2,1)}, bf16[2048,...) custom-call(s32[4]{0:T(128)} %iota_xor_fusion.order, ...), custom_call_target="tpu_custom_call" | custom-call | tf_op jit(solution)/shard_map/mlp/pallas_call | solution.py:692
  147.9 39.5 %attend_back.1 = (bf16[256,1024]{1,0:T(8,128)(2,1)}, bf16[256,1024]{1,0:T(8,128)(2,1)}, bf16[256,1024]{1,0:T(8,128)(2,1)}, bf16[256,1024]{1,0:T(8,128)(2,1)}, bf...) custom-call(s32[13]{0:T(128)} %pad_add_fusion.first, ...), custom_call_target="tpu_custom_call" | custom-call | tf_op jit(solution)/shard_map/attend_back/pallas_call | solution.py:537
  187.3 2.1 collective-permute-start.20
  193.6 3.8 %finish.1 = bf16[512,1024]{1,0:T(8,128)(2,1)} custom-call(bf16[512,1024]{1,0:T(8,128)(2,1)} %base.1, f32[16,1024]{1,0:T(8,128)} %vectors.1.refs_8_.refs_17_.refs_0_, bf16[512,1024]{1,0:T(8,128)(2,1)} %get-tuple-element.91.refs_1_, bf16[512,1024]{1,0:T(8,128)(2,1)} %collective-permute-done.16.refs_2_, bf16[512,1024]{1,0:T(8,128)(2,1)} %collective-permute-done.17.refs_3_, ...), custom_call_target="tpu_custom_call" | custom-call | flops 20000000000 | bytes 10000000 | tf_op jit(solution)/shard_map/finish/pallas_call | solution.py:751
  197.7 5.3 %collective-permute-done.23 = bf16[256,1024]{1,0:T(8,128)(2,1)S(1)} collective-permute-done((bf16[256,1024]{1,0:T(8,128)(2,1)}, bf16[256,1024]{1,0:T(8,128)(2,1)S(1)}, u32[]{:S(2)}, u32[]{:S(2)}) %collective-permute-start.23) | collective-permute-done | bytes 524320 | tf_op jit(solution)/shard_map/ppermute | solution.py:853
  209.7 3.4 %collective-permute-start.27 = (bf16[1,144,768]{2,1,0:T(8,128)(2,1)S(1)}, bf16[1,144,768]{2,1,0:T(8,128)(2,1)S(1)}, u32[]{:S(2)}, u32[]{:S(2)}) collective-permute-start(bf16[1,144,768]{2,1,0:T(8,128)(2,1)S(1)} %get-tuple-element.136), channel_id=1, source_target_pairs={{0,16},{4,20},{8,24},{12,28},{16,0},{20,4},{24,8},{28,12},{1,17},{... | collective-permute-start | bytes 663560 | tf_op jit(solution)/shard_map/ppermute | solution.py:892
  214.8 4.3 %collective-permute-done.22.refs_4_ = bf16[256,1024]{1,0:T(8,128)(2,1)S(1)} collective-permute-done((bf16[256,1024]{1,0:T(8,128)(2,1)S(1)}, bf16[256,1024]{1,0:T(8,128)(2,1)S(1)}, u32[]{:S(2)}, u32[]{:S(2)}) %collective-permute-start.22) | collective-permute-done | bytes 524320 | tf_op jit(solution)/shard_map/ppermute | solution.py:853
  220.8 2.4 collective-permute-done.27
  223.9 2.3 cut.1
  226.1 3.5 %all-to-all-start = ((bf16[4,32,1920]{2,1,0:T(8,128)(2,1)}), bf16[4,32,1920]{2,1,0:T(8,128)(2,1)S(1)}, u32[]{:S(2)}, u32[]{:S(2)}) async-start(bf16[4,32,1920]{2,1,0:T(8,128)(2,1)} %get-tuple-element.117), calls=%async_computation.1 | async-start | bytes 983040 | tf_op jit(solution)/shard_map/all_to_all | solution.py:1052
  231.2 5.9 %all-to-all-done.refs_7_ = bf16[4,32,1920]{2,1,0:T(8,128)(2,1)S(1)} async-done(((bf16[4,32,1920]{2,1,0:T(8,128)(2,1)}), bf16[4,32,1920]{2,1,0:T(8,128)(2,1)S(1)}, u32[]{:S(2)}, u32[]{:S(2)}) %all-to-all-start) | async-done | bytes 491552 | tf_op jit(solution)/shard_map/all_to_all | solution.py:1052
  237.8 4.1 %join.1 = (f32[32,4096]{1,0:T(8,128)}, f32[32,3072]{1,0:T(8,128)}, f32[32,1024]{1,0:T(8,128)}, f32[32]{0:T(128)}, f32[32]{0:T(128)}, /*index=5*/f32[32]{0:T(128)...) custom-call(s32[1]{0:T(128)} %bitcast.member, ...), custom_call_target="tpu_custom_call" | custom-call | tf_op jit(solution)/shard_map/join/pallas_call | solution.py:836
  (133 shorter events, 43.9 us)
Async XLA Ops:
  7.2 50.0 %all-gather.5.cloned.1.call-start = ((), (), s32[]{:S(2)}) async-start(), calls=%async_computation.3 | async-start | bytes 2064384 | tf_op jit(solution)/shard_map/all_gather | solution.py:926
  22.6 80.2 %all-gather.7.cloned.1.call-start = ((), (), s32[]{:S(2)}) async-start(), calls=%async_computation.4 | async-start | bytes 5308416 | tf_op jit(solution)/shard_map/all_gather | solution.py:926
  22.8 12.9 %collective-permute-start.3 = (bf16[256,1024]{1,0:T(8,128)(2,1)S(1)}, bf16[256,1024]{1,0:T(8,128)(2,1)S(1)}, u32[]{:S(2)}, u32[]{:S(2)}) collective-permute-start(bf16[256,1024]{1,0:T(8,128)(2,1)S(1)} %get-tuple-element.78.refs_0_.rest_0_), channel_id=1, source_target_pairs={{0,1},{1,0},{2,3},{3,2},{4,5},{5,4},{6,7},{7,6},{8,9},{9,8},{10,11... | collective-permute-start | bytes 1572872 | tf_op jit(solution)/shard_map/ppermute | solution.py:853
  37.4 185.8 %reduce-scatter.2.cloned.1.call-start = ((), (), s32[]{:S(2)}) async-start(), calls=%async_computation.2 | async-start | bytes 5603328 | tf_op jit(solution)/shard_map/reduce_scatter | solution.py:930
  37.4 14.8 %collective-permute-start.5 = (bf16[256,1024]{1,0:T(8,128)(2,1)S(1)}, bf16[256,1024]{1,0:T(8,128)(2,1)S(1)}, u32[]{:S(2)}, u32[]{:S(2)}) collective-permute-start(bf16[256,1024]{1,0:T(8,128)(2,1)S(1)} %get-tuple-element.78.refs_0_.rest_0_), channel_id=1, source_target_pairs={{0,2},{1,3},{2,0},{3,1},{4,6},{5,7},{6,4},{7,5},{8,10},{9,11},{10,... | collective-permute-start | bytes 1572872 | tf_op jit(solution)/shard_map/ppermute | solution.py:853
  39.4 14.9 %collective-permute-start.4 = (bf16[256,1024]{1,0:T(8,128)(2,1)S(1)}, bf16[256,1024]{1,0:T(8,128)(2,1)S(1)}, u32[]{:S(2)}, u32[]{:S(2)}) collective-permute-start(bf16[256,1024]{1,0:T(8,128)(2,1)S(1)} %get-tuple-element.79.refs_1_.rest_1_), channel_id=1, source_target_pairs={{0,1},{1,0},{2,3},{3,2},{4,5},{5,4},{6,7},{7,6},{8,9},{9,8},{10,11... | collective-permute-start | bytes 1572872 | tf_op jit(solution)/shard_map/ppermute | solution.py:853
  42.1 21.5 %collective-permute-start.7 = (bf16[256,1024]{1,0:T(8,128)(2,1)S(1)}, bf16[256,1024]{1,0:T(8,128)(2,1)}, u32[]{:S(2)}, u32[]{:S(2)}) collective-permute-start(bf16[256,1024]{1,0:T(8,128)(2,1)S(1)} %collective-permute-done.3.refs_2_.rest_2_), channel_id=1, source_target_pairs={{0,2},{1,3},{2,0},{3,1},{4,6},{5,7},{6,4},{7,5},{8,10},{9,11},{10,... | collective-permute-start | bytes 1572872 | tf_op jit(solution)/shard_map/ppermute | solution.py:853
  43.7 21.9 %collective-permute-start.8 = (bf16[256,1024]{1,0:T(8,128)(2,1)S(1)}, bf16[256,1024]{1,0:T(8,128)(2,1)}, u32[]{:S(2)}, u32[]{:S(2)}) collective-permute-start(bf16[256,1024]{1,0:T(8,128)(2,1)S(1)} %collective-permute-done.6.refs_5_.rest_5_), channel_id=1, source_target_pairs={{0,1},{1,0},{2,3},{3,2},{4,5},{5,4},{6,7},{7,6},{8,9},{9,8},{10,11... | collective-permute-start | bytes 1572872 | tf_op jit(solution)/shard_map/ppermute | solution.py:853
  54.3 22.5 %collective-permute-start.12 = (bf16[256,1024]{1,0:T(8,128)(2,1)}, bf16[256,1024]{1,0:T(8,128)(2,1)S(1)}, u32[]{:S(2)}, u32[]{:S(2)}) collective-permute-start(bf16[256,1024]{1,0:T(8,128)(2,1)} %get-tuple-element.81.refs_9_), channel_id=1, source_target_pairs={{0,2},{1,3},{2,0},{3,1},{4,6},{5,7},{6,4},{7,5},{8,10},{9,11},{10,... | collective-permute-start | bytes 1572872 | tf_op jit(solution)/shard_map/ppermute | solution.py:853
  54.4 22.5 %collective-permute-start.9 = (bf16[256,1024]{1,0:T(8,128)(2,1)}, bf16[256,1024]{1,0:T(8,128)(2,1)S(1)}, u32[]{:S(2)}, u32[]{:S(2)}) collective-permute-start(bf16[256,1024]{1,0:T(8,128)(2,1)} %get-tuple-element.80.refs_8_), channel_id=1, source_target_pairs={{0,1},{1,0},{2,3},{3,2},{4,5},{5,4},{6,7},{7,6},{8,9},{9,8},{10,11... | collective-permute-start | bytes 1572872 | tf_op jit(solution)/shard_map/ppermute | solution.py:853
  56.6 40.5 %collective-permute-start.11 = (bf16[256,1024]{1,0:T(8,128)(2,1)}, bf16[256,1024]{1,0:T(8,128)(2,1)}, u32[]{:S(2)}, u32[]{:S(2)}) collective-permute-start(bf16[256,1024]{1,0:T(8,128)(2,1)} %get-tuple-element.80.refs_8_), channel_id=1, source_target_pairs={{0,2},{1,3},{2,0},{3,1},{4,6},{5,7},{6,4},{7,5},{8,10},{9,11},{10,... | collective-permute-start | bytes 1572872 | tf_op jit(solution)/shard_map/ppermute | solution.py:853
  63.6 33.5 %collective-permute-start.10 = (bf16[256,1024]{1,0:T(8,128)(2,1)}, bf16[256,1024]{1,0:T(8,128)(2,1)S(1)}, u32[]{:S(2)}, u32[]{:S(2)}) collective-permute-start(bf16[256,1024]{1,0:T(8,128)(2,1)} %get-tuple-element.81.refs_9_), channel_id=1, source_target_pairs={{0,1},{1,0},{2,3},{3,2},{4,5},{5,4},{6,7},{7,6},{8,9},{9,8},{10,11... | collective-permute-start | bytes 1572872 | tf_op jit(solution)/shard_map/ppermute | solution.py:853
  76.8 20.3 %collective-permute-start.13 = (bf16[256,1024]{1,0:T(8,128)(2,1)S(1)}, bf16[256,1024]{1,0:T(8,128)(2,1)S(1)}, u32[]{:S(2)}, u32[]{:S(2)}) collective-permute-start(bf16[256,1024]{1,0:T(8,128)(2,1)S(1)} %collective-permute-done.9.refs_10_), channel_id=1, source_target_pairs={{0,2},{1,3},{2,0},{3,1},{4,6},{5,7},{6,4},{7,5},{8,10},{9,11},{10,... | collective-permute-start | bytes 1572872 | tf_op jit(solution)/shard_map/ppermute | solution.py:853
  77.3 19.9 %collective-permute-start.14 = (bf16[256,1024]{1,0:T(8,128)(2,1)S(1)}, bf16[256,1024]{1,0:T(8,128)(2,1)S(1)}, u32[]{:S(2)}, u32[]{:S(2)}) collective-permute-start(bf16[256,1024]{1,0:T(8,128)(2,1)S(1)} %collective-permute-done.12.refs_13_), channel_id=1, source_target_pairs={{0,1},{1,0},{2,3},{3,2},{4,5},{5,4},{6,7},{7,6},{8,9},{9,8},{10,11... | collective-permute-start | bytes 1572872 | tf_op jit(solution)/shard_map/ppermute | solution.py:853
  143.7 46.9 %collective-permute-start.16 = (bf16[512,1024]{1,0:T(8,128)(2,1)}, bf16[512,1024]{1,0:T(8,128)(2,1)}, u32[]{:S(2)}, u32[]{:S(2)}) collective-permute-start(bf16[512,1024]{1,0:T(8,128)(2,1)} %get-tuple-element.92), channel_id=1, source_target_pairs={{0,1},{1,0},{2,3},{3,2},{4,5},{5,4},{6,7},{7,6},{8,9},{9,8},{10,11... | collective-permute-start | bytes 3145736 | tf_op jit(solution)/shard_map/ppermute | solution.py:853
  145.3 47.3 %collective-permute-start.17 = (bf16[512,1024]{1,0:T(8,128)(2,1)S(1)}, bf16[512,1024]{1,0:T(8,128)(2,1)}, u32[]{:S(2)}, u32[]{:S(2)}) collective-permute-start(bf16[512,1024]{1,0:T(8,128)(2,1)S(1)} %copy-done.29), channel_id=1, source_target_pairs={{0,2},{1,3},{2,0},{3,1},{4,6},{5,7},{6,4},{7,5},{8,10},{9,11},{10,... | collective-permute-start | bytes 3145736 | tf_op jit(solution)/shard_map/ppermute | solution.py:853
  146.8 46.8 %collective-permute-start.18 = (bf16[512,1024]{1,0:T(8,128)(2,1)S(1)}, bf16[512,1024]{1,0:T(8,128)(2,1)}, u32[]{:S(2)}, u32[]{:S(2)}) collective-permute-start(bf16[512,1024]{1,0:T(8,128)(2,1)S(1)} %copy-done.28), channel_id=1, source_target_pairs={{0,3},{1,2},{2,1},{3,0},{4,7},{5,6},{6,5},{7,4},{8,11},{9,10},{10,... | collective-permute-start | bytes 3145736 | tf_op jit(solution)/shard_map/ppermute | solution.py:853
  187.3 16.7 %collective-permute-start.20 = (bf16[256,1024]{1,0:T(8,128)(2,1)}, bf16[256,1024]{1,0:T(8,128)(2,1)S(1)}, u32[]{:S(2)}, u32[]{:S(2)}) collective-permute-start(bf16[256,1024]{1,0:T(8,128)(2,1)} %get-tuple-element.104), channel_id=1, source_target_pairs={{0,2},{1,3},{2,0},{3,1},{4,6},{5,7},{6,4},{7,5},{8,10},{9,11},{10,... | collective-permute-start | bytes 1572872 | tf_op jit(solution)/shard_map/ppermute | solution.py:853
  189.4 13.7 %collective-permute-start.23 = (bf16[256,1024]{1,0:T(8,128)(2,1)}, bf16[256,1024]{1,0:T(8,128)(2,1)S(1)}, u32[]{:S(2)}, u32[]{:S(2)}) collective-permute-start(bf16[256,1024]{1,0:T(8,128)(2,1)} %get-tuple-element.110), channel_id=1, source_target_pairs={{0,1},{1,0},{2,3},{3,2},{4,5},{5,4},{6,7},{7,6},{8,9},{9,8},{10,11... | collective-permute-start | bytes 1572872 | tf_op jit(solution)/shard_map/ppermute | solution.py:853
  204.2 14.8 %collective-permute-start.22 = (bf16[256,1024]{1,0:T(8,128)(2,1)S(1)}, bf16[256,1024]{1,0:T(8,128)(2,1)S(1)}, u32[]{:S(2)}, u32[]{:S(2)}) collective-permute-start(bf16[256,1024]{1,0:T(8,128)(2,1)S(1)} %add_convert_fusion.2), channel_id=1, source_target_pairs={{0,1},{1,0},{2,3},{3,2},{4,5},{5,4},{6,7},{7,6},{8,9},{9,8},{10,11... | collective-permute-start | bytes 1572872 | tf_op jit(solution)/shard_map/ppermute | solution.py:853
  205.9 14.9 %collective-permute-start.24 = (bf16[256,1024]{1,0:T(8,128)(2,1)S(1)}, bf16[256,1024]{1,0:T(8,128)(2,1)S(1)}, u32[]{:S(2)}, u32[]{:S(2)}) collective-permute-start(bf16[256,1024]{1,0:T(8,128)(2,1)S(1)} %add_convert_fusion.1), channel_id=1, source_target_pairs={{0,2},{1,3},{2,0},{3,1},{4,6},{5,7},{6,4},{7,5},{8,10},{9,11},{10,... | collective-permute-start | bytes 1572872 | tf_op jit(solution)/shard_map/ppermute | solution.py:853
  209.7 13.5 %collective-permute-start.27 = (bf16[1,144,768]{2,1,0:T(8,128)(2,1)S(1)}, bf16[1,144,768]{2,1,0:T(8,128)(2,1)S(1)}, u32[]{:S(2)}, u32[]{:S(2)}) collective-permute-start(bf16[1,144,768]{2,1,0:T(8,128)(2,1)S(1)} %get-tuple-element.136), channel_id=1, source_target_pairs={{0,16},{4,20},{8,24},{12,28},{16,0},{20,4},{24,8},{28,12},{1,17},{... | collective-permute-start | bytes 663560 | tf_op jit(solution)/shard_map/ppermute | solution.py:892
  213.1 18.0 %collective-permute-start.19 = (bf16[256,1024]{1,0:T(8,128)(2,1)}, bf16[256,1024]{1,0:T(8,128)(2,1)S(1)}, u32[]{:S(2)}, u32[]{:S(2)}) collective-permute-start(bf16[256,1024]{1,0:T(8,128)(2,1)} %get-tuple-element.102), channel_id=1, source_target_pairs={{0,1},{1,0},{2,3},{3,2},{4,5},{5,4},{6,7},{7,6},{8,9},{9,8},{10,11... | collective-permute-start | bytes 1572872 | tf_op jit(solution)/shard_map/ppermute | solution.py:853
  214.3 16.8 %collective-permute-start.25 = (bf16[256,1024]{1,0:T(8,128)(2,1)S(1)}, bf16[256,1024]{1,0:T(8,128)(2,1)S(1)}, u32[]{:S(2)}, u32[]{:S(2)}) collective-permute-start(bf16[256,1024]{1,0:T(8,128)(2,1)S(1)} %copy-done.30), channel_id=1, source_target_pairs={{0,2},{1,3},{2,0},{3,1},{4,6},{5,7},{6,4},{7,5},{8,10},{9,11},{10,... | collective-permute-start | bytes 1572872 | tf_op jit(solution)/shard_map/ppermute | solution.py:853
  (42 other events, 417.8 us)
Sparse Core Ops, SparseCore 0:
  22.7 27.2 all-gather.4
  51.7 51.0 all-gather.6
  143.9 56.9 reduce-scatter.1
